TPU v7x, 32 devices: a whole 2x2x4 slice. The times are simulated.
32 devices in a mesh: dp: 16 (over z, x, core), mod: 2 (over y).
Axes of the slice: x: 2, y: 2, z: 4, core: 2. Of those that a mesh axis runs over, the one named last changes fastest.
Arguments:
- tokens: bfloat16 [32, 1024, 1152], P(('dp', 'mod')), may hold values from -6 to 6
- cond: float32 [32, 4, 1152], P(('dp', 'mod')), may hold values from -6 to 6
- segments: int32 [32, 1024], P(('dp', 'mod')), may hold values from 0 to 3, as said below
- coords: int32 [32, 2, 1024], P(('dp', 'mod')), may hold values from 0 to 31, as said below
- w_ada: bfloat16 [1152, 6912], P(None, 'mod'), may hold values from -0.1875 to 0.1875
- w_qkv: bfloat16 [1152, 3456], replicated, may hold values from -0.1875 to 0.1875
- q_gain: float32 [72], replicated, may hold values from 1 to 2
- k_gain: float32 [72], replicated, may hold values from 1 to 2
- w_out: bfloat16 [1152, 1152], replicated, may hold values from -1.5 to 1.5
- w_gate: bfloat16 [1152, 3072], replicated, may hold values from -0.1875 to 0.1875
- w_up: bfloat16 [1152, 3072], replicated, may hold values from -0.1875 to 0.1875
- w_down: bfloat16 [3072, 1152], replicated, may hold values from -0.109375 to 0.109375
- cotangent: bfloat16 [32, 1024, 1152], P(('dp', 'mod')), may hold values from -6 to 6
Outputs:
- output: bfloat16 [32, 1024, 1152], P(('dp', 'mod'))
- grad_tokens: bfloat16 [32, 1024, 1152], P(('dp', 'mod'))
- grad_cond: float32 [32, 4, 1152], P(('dp', 'mod'))
- grad_w_ada: float32 [1152, 6912], P('dp', 'mod')
- grad_w_qkv: float32 [1152, 3456], P(('dp', 'mod'))
- grad_q_gain: float32 [72], replicated
- grad_k_gain: float32 [72], replicated
- grad_w_out: float32 [1152, 1152], P(('dp', 'mod'))
- grad_w_gate: float32 [1152, 3072], P(('dp', 'mod'))
- grad_w_up: float32 [1152, 3072], P(('dp', 'mod'))
- grad_w_down: float32 [3072, 1152], P(('dp', 'mod'))
Inputs may be any that keep to these rules, and one draw needn't show every extreme that they name: `segments`: each packed row holds either one item of 1024 tokens, all in slot 0, or four items of 256 tokens in slots 0 to 3 in order; exactly half of the rows are of each kind. `coords`: coordinates of a token's patch on its item's square grid, 32 per side for a whole-row item and 16 for the others; each item's grid may be flipped along either side or transposed.
All inputs are finite; a program needn't handle non-finite values.
Results may differ from a plain program's by a relative error of at most 0.0131.
The roundings to bfloat16 on the way count: a program that leaves them out, or rounds other values in their place, can miss the bound.
Values may be sent and summed in bfloat16 or wider, within the bound.
No kernel may reach another device: no remote copies, remote signals or barrier semaphores. Data moves between devices by JAX's collectives and lax.ppermute only.
A program may use at most 576 MiB of HBM per device.

v0:
```python
import jax
import jax.numpy as jnp
from jax import lax
from jax.sharding import PartitionSpec as P

HEADS = 16
HD = 72


EPS_NORM = 1e-06
ROPE_BASE = 10000.0
MASKED = -1e30


def layer_norm(v):
    centred = v - jnp.mean(v, axis=-1, keepdims=True)
    variance = jnp.mean(centred * centred, axis=-1, keepdims=True)
    return centred * lax.rsqrt(variance + EPS_NORM)


def modulate(v, shift_part, scale_part):
    return layer_norm(v) * (1.0 + scale_part) + shift_part


def rms_norm(v, gain):
    return v * lax.rsqrt(jnp.mean(v * v, axis=-1, keepdims=True) + EPS_NORM) * gain


def rope_angles(coord_pair):
    quarter = HD // 4
    freqs = ROPE_BASE ** (-jnp.arange(quarter).astype(jnp.float32) / quarter)
    position = coord_pair.astype(jnp.float32)
    angle = position[:, :, None] * freqs[None, None, :]
    angle = jnp.transpose(angle, (1, 0, 2))[:, None, :, :]
    return (jnp.cos(angle), jnp.sin(angle))


def rotate(vectors, cosine_table, sine_table):
    shaped = vectors.reshape(vectors.shape[0], vectors.shape[1], 2, 2, HD // 4)
    lead = shaped[:, :, :, 0]
    trail = shaped[:, :, :, 1]
    new_lead = lead * cosine_table - trail * sine_table
    new_trail = lead * sine_table + trail * cosine_table
    return jnp.stack([new_lead, new_trail], axis=3).reshape(vectors.shape)


def silu_grad(v):
    sigmoid = jax.nn.sigmoid(v)
    return sigmoid * (1.0 + v * (1.0 - sigmoid))


def body(
    tokens,
    cond,
    segments,
    coords,
    w_ada,
    w_qkv,
    q_gain,
    k_gain,
    w_out,
    w_gate,
    w_up,
    w_down,
    cotangent,
):
    rows_here, row_len, width = tokens.shape
    slots = cond.shape[1]
    token_count = rows_here * row_len
    half_channels = w_ada.shape[1]
    score_scale = HD ** (-0.5)
    query_block = min(512, row_len)
    block_count = row_len // query_block
    cond_both = lax.all_gather(cond, "mod", axis=0, tiled=True)
    activated = jax.nn.silu(cond_both).astype(jnp.bfloat16).reshape(-1, width)
    mod_half = jnp.dot(activated, w_ada, preferred_element_type=jnp.float32).astype(jnp.bfloat16)
    mod_half = mod_half.reshape(cond_both.shape[0], slots, half_channels)
    modulation = lax.all_to_all(mod_half, "mod", split_axis=0, concat_axis=2, tiled=True)
    slot_onehot = (segments[:, :, None] == jnp.arange(slots)[None, None, :]).astype(jnp.float32)
    per_token = jnp.einsum(
        "rts,rsc->rtc", slot_onehot, modulation.astype(jnp.float32), precision=lax.Precision.HIGHEST
    )
    per_token = per_token.reshape(token_count, 6 * width)
    shift_attn, scale_attn, gate_attn, shift_ffn, scale_ffn, gate_ffn = jnp.split(
        per_token, 6, axis=1
    )
    stream = tokens.reshape(token_count, width).astype(jnp.float32)
    mod_attn, pull_attn_norm = jax.vjp(modulate, stream, shift_attn, scale_attn)
    mod_attn_low = mod_attn.astype(jnp.bfloat16)
    projected = jnp.dot(mod_attn_low, w_qkv, preferred_element_type=jnp.float32)
    cosine_table, sine_table = rope_angles(jnp.transpose(coords, (1, 0, 2)).reshape(2, token_count))

    def prepare(query_raw, key_raw, query_gain, key_gain):
        queries = rotate(
            rms_norm(query_raw.reshape(token_count, HEADS, HD), query_gain),
            cosine_table,
            sine_table,
        )
        key_vectors = rotate(
            rms_norm(key_raw.reshape(token_count, HEADS, HD), key_gain), cosine_table, sine_table
        )
        return (queries, key_vectors)

    (queries, key_vectors), pull_prepare = jax.vjp(
        prepare, projected[:, :width], projected[:, width : 2 * width], q_gain, k_gain
    )
    query_low = queries.astype(jnp.bfloat16)
    key_low = key_vectors.astype(jnp.bfloat16)
    value_low = projected[:, 2 * width :].astype(jnp.bfloat16).reshape(token_count, HEADS, HD)

    def block_scores(row_index, block_index):
        start_row = row_index * row_len + block_index * query_block
        query_part = query_low[start_row : start_row + query_block]
        seg_row = segments[row_index]
        seg_part = seg_row[block_index * query_block : (block_index + 1) * query_block]
        scores = (
            jnp.einsum("qhd,khd->hqk", query_part, key_low, preferred_element_type=jnp.float32)
            * score_scale
        )
        allowed = (seg_part[:, None] == seg_row[None, :])[None]
        return jnp.where(allowed, scores, MASKED)

    attended_parts = []
    log_totals = []
    row_index = 0
    for block_index in range(block_count):
        scores = block_scores(row_index, block_index)
        row_peak = jnp.max(scores, axis=-1, keepdims=True)
        exp_total = jnp.sum(jnp.exp(scores - row_peak), axis=-1, keepdims=True)
        log_total = row_peak + jnp.log(exp_total)
        probs_low = jnp.exp(scores - log_total).astype(jnp.bfloat16)
        attended_parts.append(
            jnp.einsum("hqk,khd->qhd", probs_low, value_low, preferred_element_type=jnp.float32)
        )
        log_totals.append(log_total)
    attended = (
        jnp.concatenate(attended_parts, axis=0).reshape(token_count, width).astype(jnp.bfloat16)
    )
    attn = jnp.dot(attended, w_out, preferred_element_type=jnp.float32)
    mid = stream + gate_attn * attn
    mod_ffn, pull_ffn_norm = jax.vjp(modulate, mid, shift_ffn, scale_ffn)
    mod_ffn_low = mod_ffn.astype(jnp.bfloat16)
    gate_h = jnp.dot(mod_ffn_low, w_gate, preferred_element_type=jnp.float32)
    up_h = jnp.dot(mod_ffn_low, w_up, preferred_element_type=jnp.float32)
    hidden = (jax.nn.silu(gate_h) * up_h).astype(jnp.bfloat16)
    ffn = jnp.dot(hidden, w_down, preferred_element_type=jnp.float32)
    output = (mid + gate_ffn * ffn).astype(jnp.bfloat16).reshape(rows_here, row_len, width)
    incoming = cotangent.reshape(token_count, width).astype(jnp.float32)
    grad_gate_ffn = incoming * ffn
    grad_ffn = (incoming * gate_ffn).astype(jnp.bfloat16)
    grad_w_down = jnp.einsum("nf,nd->fd", hidden, grad_ffn, preferred_element_type=jnp.float32)
    grad_hidden = jnp.einsum("nd,fd->nf", grad_ffn, w_down, preferred_element_type=jnp.float32)
    grad_gate_h = (grad_hidden * up_h * silu_grad(gate_h)).astype(jnp.bfloat16)
    grad_up_h = (grad_hidden * jax.nn.silu(gate_h)).astype(jnp.bfloat16)
    grad_w_gate = jnp.einsum(
        "nd,nf->df", mod_ffn_low, grad_gate_h, preferred_element_type=jnp.float32
    )
    grad_w_up = jnp.einsum("nd,nf->df", mod_ffn_low, grad_up_h, preferred_element_type=jnp.float32)
    grad_mod_ffn = jnp.einsum("nf,df->nd", grad_gate_h, w_gate, preferred_element_type=jnp.float32)
    grad_mod_ffn = grad_mod_ffn + jnp.einsum(
        "nf,df->nd", grad_up_h, w_up, preferred_element_type=jnp.float32
    )
    grad_mid_part, grad_shift_ffn, grad_scale_ffn = pull_ffn_norm(grad_mod_ffn)
    grad_mid = incoming + grad_mid_part
    grad_gate_attn = grad_mid * attn
    grad_attn = (grad_mid * gate_attn).astype(jnp.bfloat16)
    grad_w_out = jnp.einsum("nc,nd->cd", attended, grad_attn, preferred_element_type=jnp.float32)
    grad_attended = jnp.einsum("nd,cd->nc", grad_attn, w_out, preferred_element_type=jnp.float32)
    grad_attended = grad_attended.astype(jnp.bfloat16).reshape(token_count, HEADS, HD)
    grad_query_parts = []
    row_index = 0
    grad_key_row = jnp.zeros((row_len, HEADS, HD), jnp.float32)
    grad_value_row = jnp.zeros((row_len, HEADS, HD), jnp.float32)
    for block_index in range(block_count):
        start_row = row_index * row_len + block_index * query_block
        query_part = query_low[start_row : start_row + query_block]
        grad_out_part = grad_attended[start_row : start_row + query_block]
        scores = block_scores(row_index, block_index)
        attn_probs = jnp.exp(scores - log_totals[row_index * block_count + block_index])
        probs_low = attn_probs.astype(jnp.bfloat16)
        grad_value_row = grad_value_row + jnp.einsum(
            "hqk,qhd->khd", probs_low, grad_out_part, preferred_element_type=jnp.float32
        )
        grad_probs = jnp.einsum(
            "qhd,khd->hqk", grad_out_part, value_low, preferred_element_type=jnp.float32
        )
        dot_term = jnp.sum(attn_probs * grad_probs, axis=-1, keepdims=True)
        grad_scores = (attn_probs * (grad_probs - dot_term)).astype(jnp.bfloat16)
        grad_query_parts.append(
            jnp.einsum("hqk,khd->qhd", grad_scores, key_low, preferred_element_type=jnp.float32)
            * score_scale
        )
        grad_key_row = (
            grad_key_row
            + jnp.einsum(
                "hqk,qhd->khd", grad_scores, query_part, preferred_element_type=jnp.float32
            )
            * score_scale
        )
    grad_queries = jnp.concatenate(grad_query_parts, axis=0)
    grad_values = grad_value_row.reshape(token_count, width)
    grad_query_raw, grad_key_raw, grad_q_gain, grad_k_gain = pull_prepare(
        (grad_queries, grad_key_row)
    )
    grad_projected = jnp.concatenate([grad_query_raw, grad_key_raw, grad_values], axis=1).astype(
        jnp.bfloat16
    )
    grad_w_qkv = jnp.einsum(
        "nd,ne->de", mod_attn_low, grad_projected, preferred_element_type=jnp.float32
    )
    grad_mod_attn = jnp.einsum(
        "ne,de->nd", grad_projected, w_qkv, preferred_element_type=jnp.float32
    )
    grad_stream, grad_shift_attn, grad_scale_attn = pull_attn_norm(grad_mod_attn)
    grad_tokens = (grad_mid + grad_stream).astype(jnp.bfloat16).reshape(rows_here, row_len, width)
    grad_per_token = jnp.concatenate(
        [
            grad_shift_attn,
            grad_scale_attn,
            grad_gate_attn,
            grad_shift_ffn,
            grad_scale_ffn,
            grad_gate_ffn,
        ],
        axis=1,
    )
    grad_per_token = grad_per_token.reshape(rows_here, row_len, 6 * width)
    grad_modulation = jnp.einsum(
        "rts,rtc->rsc", slot_onehot, grad_per_token, precision=lax.Precision.HIGHEST
    ).astype(jnp.bfloat16)
    grad_mod_half = lax.all_to_all(grad_modulation, "mod", split_axis=2, concat_axis=0, tiled=True)
    grad_mod_flat = grad_mod_half.reshape(-1, half_channels)
    grad_ada_local = jnp.einsum(
        "nd,nc->dc", activated, grad_mod_flat, preferred_element_type=jnp.float32
    )
    grad_w_ada = lax.psum_scatter(grad_ada_local, "dp", scatter_dimension=0, tiled=True)
    grad_activated = jnp.einsum(
        "nc,dc->nd", grad_mod_flat, w_ada, preferred_element_type=jnp.float32
    )
    grad_activated = grad_activated.reshape(cond_both.shape[0], slots, width)
    grad_own = lax.psum_scatter(
        grad_activated.astype(jnp.bfloat16), "mod", scatter_dimension=0, tiled=True
    ).astype(jnp.float32)
    grad_cond = grad_own * silu_grad(cond)
    summed_q_gain, summed_k_gain = lax.psum((grad_q_gain, grad_k_gain), ("dp", "mod"))
    summed_qkv, summed_out, summed_gate, summed_up, summed_down = (
        lax.psum_scatter(grad_w_qkv, ("dp", "mod"), scatter_dimension=0, tiled=True),
        lax.psum_scatter(grad_w_out, ("dp", "mod"), scatter_dimension=0, tiled=True),
        lax.psum_scatter(grad_w_gate, ("dp", "mod"), scatter_dimension=0, tiled=True),
        lax.psum_scatter(grad_w_up, ("dp", "mod"), scatter_dimension=0, tiled=True),
        lax.psum_scatter(grad_w_down, ("dp", "mod"), scatter_dimension=0, tiled=True),
    )
    return (
        output,
        grad_tokens,
        grad_cond,
        grad_w_ada,
        summed_qkv,
        summed_q_gain,
        summed_k_gain,
        summed_out,
        summed_gate,
        summed_up,
        summed_down,
    )


def solution(mesh):
    in_specs = (
        P(("dp", "mod"), None, None),
        P(("dp", "mod"), None, None),
        P(("dp", "mod"), None),
        P(("dp", "mod"), None, None),
        P(None, "mod"),
        P(),
        P(),
        P(),
        P(),
        P(),
        P(),
        P(),
        P(("dp", "mod"), None, None),
    )
    out_specs = (
        P(("dp", "mod"), None, None),
        P(("dp", "mod"), None, None),
        P(("dp", "mod"), None, None),
        P("dp", "mod"),
        P(("dp", "mod"), None),
        P(),
        P(),
        P(("dp", "mod"), None),
        P(("dp", "mod"), None),
        P(("dp", "mod"), None),
        P(("dp", "mod"), None),
    )
    return jax.shard_map(body, mesh=mesh, in_specs=in_specs, out_specs=out_specs, check_vma=False)
```

profile of v0, /device:TPU:0, one launch (start us, length us, event | category | flops | bytes accessed | tf_op | source)
XLA Modules:
  0.0 2381.6 jit_solution(3017449772601050596)
XLA Ops:
  30.4 11.4 fusion.73
  47.7 12.3 fusion.102
  111.8 15.9 fusion.4
  127.7 15.0 exponential_reduce_fusion.1
  149.2 21.1 fusion.5
  170.3 15.0 exponential_reduce_fusion
  185.3 16.1 fusion.56
  201.4 16.2 fusion.57
  219.9 7.9 fusion.95
  234.1 14.0 fusion.103
  248.1 10.7 fusion.104
  258.8 27.6 %multiply_convert_fusion.2 = (bf16[1024,3072]{1,0:T(8,128)(2,1)}, bf16[1024,3072]{1,0:T(8,128)(2,1)}, bf16[1024,3072]{1,0:T(8,128)(2,1)}) fusion(f32[1024,3072]{1,0:T(8,128)} %fusion.103, f32[1024,3072]{1,0:T(8,128)} %fusion.104, bf16[3072,1152]{1,0:T(8,128)(2,1)} %param.24, f32[1024,6912]{1,0:T(8,128)} %fusion.73, bf16[1,1024,1152]{2,1,0:T(8,128)(2,1)} %param.25), kind=kOutput, calls=%fused_computation.14 | convolution fusion | flops 7298482176 | bytes 58195968 | tf_op jit(solution)/shard_map/nd,fd->nf/dot_general | solution.py:152
  286.4 14.0 fusion.106
  300.4 16.7 multiply_reduce_fusion.4
  317.2 14.5 fusion.105
  331.7 7.5 fusion.94
  352.0 25.7 %multiply_reduce_fusion.1 = (f32[16,512]{1,0:T(8,128)S(1)}, f32[16,512,1024]{2,1,0:T(8,128)}) fusion(f32[16,512,1024]{2,1,0:T(8,128)} %get-tuple-element.70, f32[16,512]{1,0:T(8,128)S(1)} %copy-done.49, pred[512,1024]{1,0:T(8,128)(4,1)} %get-tuple-element.63, bf16[512,16,72]{0,2,1:T(8,128)(2,1)} %bitcast.207, bf16[1024,16,72]{0,2,1:T(8,128)(2,1)S(1)} %bitcast.185), kind=kOutput, calls=%fused_computation.3 | convolution fusion | flops 1249894400 | bytes 71237632 | tf_op jit(solution)/shard_map/qhd,khd->hqk/dot_general | solution.py:184
  380.1 25.9 %multiply_reduce_fusion = (f32[16,512]{1,0:T(8,128)S(1)}, f32[16,512,1024]{2,1,0:T(8,128)}) fusion(f32[16,512,1024]{2,1,0:T(8,128)} %get-tuple-element.68, f32[16,512]{1,0:T(8,128)S(1)} %copy-done.51, pred[512,1024]{1,0:T(8,128)(4,1)S(1)} %copy-done.16, bf16[512,16,72]{0,2,1:T(8,128)(2,1)} %bitcast.209, bf16[1024,16,72]{0,2,1:T(8,128)(2,1)S(1)} %bitcast.186), kind=kOutput, calls=%fused_computation.1 | convolution fusion | flops 1249894400 | bytes 71237632 | tf_op jit(solution)/shard_map/qhd,khd->hqk/dot_general | solution.py:184
  406.1 54.1 %multiply_convert_fusion = (bf16[16,512,1024]{2,1,0:T(8,128)(2,1)}, bf16[16,512,1024]{2,1,0:T(8,128)(2,1)}) fusion(f32[16,512,1024]{2,1,0:T(8,128)} %get-tuple-element.75, f32[16,512,1024]{2,1,0:T(8,128)} %get-tuple-element.68, f32[16,512]{1,0:T(8,128)S(1)} %get-tuple-element.74, f32[16,512]{1,0:T(8,128)S(1)} %copy-done.51, ...), kind=kLoop, calls=%fused_computation | loop fusion | flops 100663296 | bytes 168951808 | tf_op jit(solution)/shard_map/convert_element_type | solution.py:188
  460.2 11.7 fusion.60
  471.8 12.9 multiply_bitcast_fusion.2
  484.8 15.9 fusion.88
  500.7 12.9 multiply_bitcast_fusion.1
  513.6 11.2 multiply_bitcast_fusion
  538.1 11.0 fusion.36
  650.1 17.3 fusion.66
  667.4 17.5 add_convert_fusion.1
  687.5 14.4 fusion.25
  701.9 16.9 constant_dynamic-update-slice_fusion.1
  742.8 13.6 fusion.11
  762.7 38.5 %reduce.3 = bf16[6912,4]{1,0:T(8,128)(2,1)S(1)} reduce(bf16[6912,1,4]{2,1,0:T(2,128)(2,1)} %bitcast.203, bf16[]{:T(256)} %broadcast.384), dimensions={1}, to_apply=%bitcast.116.reduce_sub_computation | reduce | bytes 110594
  804.5 7.3 all_to_all.30
  824.4 7.8 fusion.107
  840.5 13.3 fusion.42
  853.9 14.1 fusion.109
  868.0 913.1 %fusion.92 = (f32[48,3456]{1,0:T(8,128)S(1)}, f32[48,1152]{1,0:T(8,128)S(1)}, f32[40,3072]{1,0:T(8,128)}) fusion(f32[1152,3456]{1,0:T(8,128)} %fusion.42, f32[1152,1152]{1,0:T(8,128)} %fusion.108, f32[1152,3072]{1,0:T(8,128)} %fusion.109), kind=kCustom, calls=%all-reduce-scatter.4 | all-reduce-scatter fusion | flops 11010050 | bytes 36765696
  1781.8 13.4 collective-permute-start.10
  1798.7 13.0 fusion.110
  1811.7 331.6 %fusion.3 = f32[40,3072]{1,0:T(8,128)S(1)} fusion(f32[1152,3072]{1,0:T(8,128)} %fusion.110), kind=kCustom, calls=%all-reduce-scatter.3 | all-reduce-scatter fusion | flops 3932161 | bytes 14647296
  2170.1 38.1 %all-reduce.14 = (f32[72]{0:T(128)}, f32[72]{0:T(128)}) all-reduce(f32[72]{0:T(128)S(1)} %reduce_sum.215, f32[72]{0:T(128)S(1)} %reduce_sum.217), channel_id=1, replica_groups=mesh['dp'=16,'mod'=2] {'dp','mod'}, use_global_device_ids=true, to_apply=%region_22.23 | all-reduce | flops 144 | bytes 1152 | tf_op jit(solution)/shard_map/psum | solution.py:245
  2231.8 9.3 all-reduce.4
  2243.2 11.0 collective-permute-start.18
  2265.3 8.4 concatenate.19
  2274.4 7.2 concatenate.21
  2288.6 13.7 concatenate.20
  2305.9 9.8 collective-permute-start.6
  2318.7 10.2 collective-permute-done.5
  2335.9 36.7 %concatenate.18 = f32[420,3456]{1,0:T(8,128)} concatenate(f32[36,3456]{1,0:T(8,128)} %collective-permute-done.7, f32[48,3456]{1,0:T(8,128)} %collective-permute-done.6, f32[48,3456]{1,0:T(8,128)} %copy-done.53, f32[48,3456]{1,0:T(8,128)} %copy-done.52, f32[48,3456]{1,0:T(8,128)} %collective-permute-done.3, f32[48,3456]{1,0:T(8,128)} %collective-permute-done.2, ...), dimensions={0} | concatenate | bytes 11612160
  (383 shorter events, 372.4 us)
Async XLA Ops:
  7.2 212.5 %copy-start = (bf16[1152,1152]{1,0:T(8,128)(2,1)S(1)}, bf16[1152,1152]{1,0:T(8,128)(2,1)}, u32[]{:S(2)}) copy-start(bf16[1152,1152]{1,0:T(8,128)(2,1)} %param.21) | copy-start | bytes 7962628
  18.1 12.3 all-to-all-start
  21.4 2353.2 %reduce-scatter.13.cloned.1.call-start = ((), (), s32[]{:S(2)}) async-start(), calls=%async_computation.4 | async-start | bytes 14598144 | tf_op jit(solution)/shard_map/reduce_scatter | solution.py:251
  27.4 78.0 %copy-start.40 = (f32[1024,2,18]{0,2,1:T(8,128)}, f32[1024,2,18]{0,2,1:T(8,128)S(1)}, u32[]{:S(2)}) copy-start(f32[1024,2,18]{0,2,1:T(8,128)S(1)} %get-tuple-element.61) | copy-start | bytes 442372
  28.8 172.6 %copy-start.15 = (pred[512,1024]{1,0:T(8,128)(4,1)}, pred[512,1024]{1,0:T(8,128)(4,1)S(1)}, u32[]{:S(2)}) copy-start(pred[512,1024]{1,0:T(8,128)(4,1)S(1)} %get-tuple-element.64) | copy-start | bytes 1572868
  142.7 42.6 %copy-start.48 = (f32[16,512]{1,0:T(8,128)}, f32[16,512]{1,0:T(8,128)S(1)}, u32[]{:S(2)}) copy-start(f32[16,512]{1,0:T(8,128)S(1)} %log_add_fusion.1) | copy-start | bytes 98308
  149.2 21.1 copy-start.22
  227.9 103.8 %copy-start.68 = (f32[1024]{0:T(1024)}, f32[1024]{0:T(1024)S(1)}, u32[]{:S(2)}) copy-start(f32[1024]{0:T(1024)S(1)} %broadcast_multiply_fusion) | copy-start | bytes 12292
  228.5 103.2 %copy-start.73 = (f32[1024]{0:T(1024)}, f32[1024]{0:T(1024)S(1)}, u32[]{:S(2)}) copy-start(f32[1024]{0:T(1024)S(1)} %fusion.77) | copy-start | bytes 12292
  352.0 28.1 %copy-start.16 = (pred[512,1024]{1,0:T(8,128)(4,1)S(1)}, pred[512,1024]{1,0:T(8,128)(4,1)}, u32[]{:S(2)}) copy-start(pred[512,1024]{1,0:T(8,128)(4,1)} %copy-done.15) | copy-start | bytes 1572868
  352.0 28.1 %copy-start.51 = (f32[16,512]{1,0:T(8,128)S(1)}, f32[16,512]{1,0:T(8,128)}, u32[]{:S(2)}) copy-start(f32[16,512]{1,0:T(8,128)} %copy-done.50) | copy-start | bytes 98308
  380.1 25.9 %copy-start.18 = (pred[512,1024]{1,0:T(8,128)(4,1)S(1)}, pred[512,1024]{1,0:T(8,128)(4,1)}, u32[]{:S(2)}) copy-start(pred[512,1024]{1,0:T(8,128)(4,1)} %get-tuple-element.63) | copy-start | bytes 1572868
  406.1 54.1 %copy-start.25 = (bf16[512,16,2,2,18]{0,1,4,3,2:T(8,128)(2,1)S(1)}, bf16[512,16,2,2,18]{0,1,4,3,2:T(8,128)(2,1)}, u32[]{:S(2)}) copy-start(bf16[512,16,2,2,18]{0,1,4,3,2:T(8,128)(2,1)} %copy-done.24) | copy-start | bytes 3538948
  537.1 1837.5 %reduce-scatter.15.cloned.1.call-start = ((), (), s32[]{:S(2)}) async-start(), calls=%async_computation.5 | async-start | bytes 16920576
  801.2 23.2 copy-start.63
  1781.8 382.9 %collective-permute-start.10 = (f32[48,1152]{1,0:T(8,128)S(1)}, f32[48,1152]{1,0:T(8,128)}, u32[]{:S(2)}, u32[]{:S(2)}) collective-permute-start(f32[48,1152]{1,0:T(8,128)S(1)} %get-tuple-element.17), channel_id=1, source_target_pairs={{0,3},{1,4},{2,5},{3,6},{4,7},{5,8},{6,9},{7,10},{8,11},{9,12},{10... | collective-permute-start | bytes 663560
  1795.2 367.5 %collective-permute-start.15 = (f32[36,1152]{1,0:T(8,128)}, f32[36,1152]{1,0:T(8,128)}, u32[]{:S(2)}, u32[]{:S(2)}) collective-permute-start(f32[36,1152]{1,0:T(8,128)} %slice.89), channel_id=1, source_target_pairs={{0,8},{1,9},{2,10},{3,11},{4,12},{5,13},{6,14},{7,15},{8,16},{9,17... | collective-permute-start | bytes 497672
  1811.7 356.8 %copy-start.93 = (u32[32]{0:T(128)S(1)}, u32[32]{0:T(128)}, u32[]{:S(2)}) copy-start(u32[32]{0:T(128)} %constant.61) | copy-start | bytes 388
  1811.7 357.4 %copy-start.86 = (f32[2,2,18]{2,1,0:T(2,128)S(1)}, f32[2,2,18]{2,1,0:T(2,128)}, u32[]{:S(2)}) copy-start(f32[2,2,18]{2,1,0:T(2,128)} %get-tuple-element.41) | copy-start | bytes 868
  1811.7 357.4 %copy-start.87 = (f32[2,2,18]{2,1,0:T(2,128)S(1)}, f32[2,2,18]{2,1,0:T(2,128)}, u32[]{:S(2)}) copy-start(f32[2,2,18]{2,1,0:T(2,128)} %get-tuple-element.43) | copy-start | bytes 868
  2143.4 10.9 collective-permute-start.23
  2146.7 11.5 collective-permute-start.19
  2149.5 58.7 %collective-permute-start.11 = (f32[48,1152]{1,0:T(8,128)S(1)}, f32[48,1152]{1,0:T(8,128)}, u32[]{:S(2)}, u32[]{:S(2)}) collective-permute-start(f32[48,1152]{1,0:T(8,128)S(1)} %get-tuple-element.17), channel_id=1, source_target_pairs={{0,4},{1,5},{2,6},{3,7},{4,8},{5,9},{6,10},{7,11},{8,12},{9,13},{1... | collective-permute-start | bytes 663560
  2154.3 53.9 %copy-start.79 = (f32[4,3072]{1,0:T(4,128)}, f32[4,3072]{1,0:T(4,128)S(1)}, u32[]{:S(2)}) copy-start(f32[4,3072]{1,0:T(4,128)S(1)} %collective-permute-done.23) | copy-start | bytes 147460
  2154.3 58.3 %collective-permute-start.12 = (f32[48,1152]{1,0:T(8,128)S(1)}, f32[48,1152]{1,0:T(8,128)S(1)}, u32[]{:S(2)}, u32[]{:S(2)}) collective-permute-start(f32[48,1152]{1,0:T(8,128)S(1)} %get-tuple-element.17), channel_id=1, source_target_pairs={{0,5},{1,6},{2,7},{3,8},{4,9},{5,10},{6,11},{7,12},{8,13},{9,14},{... | collective-permute-start | bytes 663560
  2158.1 50.1 %copy-start.77 = (f32[4,3072]{1,0:T(4,128)}, f32[4,3072]{1,0:T(4,128)S(1)}, u32[]{:S(2)}) copy-start(f32[4,3072]{1,0:T(4,128)S(1)} %collective-permute-done.19) | copy-start | bytes 147460
  2158.1 55.8 %collective-permute-start.13 = (f32[48,1152]{1,0:T(8,128)S(1)}, f32[48,1152]{1,0:T(8,128)S(1)}, u32[]{:S(2)}, u32[]{:S(2)}) collective-permute-start(f32[48,1152]{1,0:T(8,128)S(1)} %get-tuple-element.17), channel_id=1, source_target_pairs={{0,6},{1,7},{2,8},{3,9},{4,10},{5,11},{6,12},{7,13},{8,14},{9,15},... | collective-permute-start | bytes 663560
  2162.7 54.8 %collective-permute-start.14 = (f32[48,1152]{1,0:T(8,128)S(1)}, f32[48,1152]{1,0:T(8,128)}, u32[]{:S(2)}, u32[]{:S(2)}) collective-permute-start(f32[48,1152]{1,0:T(8,128)S(1)} %get-tuple-element.17), channel_id=1, source_target_pairs={{0,7},{1,8},{2,9},{3,10},{4,11},{5,12},{6,13},{7,14},{8,15},{9,16}... | collective-permute-start | bytes 663560
  2164.7 55.2 %collective-permute-start.8 = (f32[48,1152]{1,0:T(8,128)S(1)}, f32[48,1152]{1,0:T(8,128)}, u32[]{:S(2)}, u32[]{:S(2)}) collective-permute-start(f32[48,1152]{1,0:T(8,128)S(1)} %get-tuple-element.17), channel_id=1, source_target_pairs={{0,1},{1,2},{2,3},{3,4},{4,5},{5,6},{6,7},{7,8},{8,9},{9,10},{10,1... | collective-permute-start | bytes 663560
  2208.2 35.0 %collective-permute-start.20 = (f32[40,3072]{1,0:T(8,128)S(1)}, f32[40,3072]{1,0:T(8,128)S(1)}, u32[]{:S(2)}, u32[]{:S(2)}) collective-permute-start(f32[40,3072]{1,0:T(8,128)S(1)} %fusion.3), channel_id=1, source_target_pairs={{0,1},{1,2},{2,3},{3,4},{4,5},{5,6},{6,7},{7,8},{8,9},{9,10},{10,1... | collective-permute-start | bytes 1474568
  2212.6 41.6 %collective-permute-start.21 = (f32[40,3072]{1,0:T(8,128)S(1)}, f32[40,3072]{1,0:T(8,128)S(1)}, u32[]{:S(2)}, u32[]{:S(2)}) collective-permute-start(f32[40,3072]{1,0:T(8,128)S(1)} %fusion.3), channel_id=1, source_target_pairs={{0,2},{1,3},{2,4},{3,5},{4,6},{5,7},{6,8},{7,9},{8,10},{9,11},{10,... | collective-permute-start | bytes 1474568
  2214.0 43.3 %collective-permute-start.22 = (f32[40,3072]{1,0:T(8,128)S(1)}, f32[40,3072]{1,0:T(8,128)S(1)}, u32[]{:S(2)}, u32[]{:S(2)}) collective-permute-start(f32[40,3072]{1,0:T(8,128)S(1)} %fusion.3), channel_id=1, source_target_pairs={{0,3},{1,4},{2,5},{3,6},{4,7},{5,8},{6,9},{7,10},{8,11},{9,12},{10... | collective-permute-start | bytes 1474568
  2217.5 43.9 %collective-permute-start.16 = (f32[40,3072]{1,0:T(8,128)}, f32[40,3072]{1,0:T(8,128)S(1)}, u32[]{:S(2)}, u32[]{:S(2)}) collective-permute-start(f32[40,3072]{1,0:T(8,128)} %get-tuple-element.18), channel_id=1, source_target_pairs={{0,1},{1,2},{2,3},{3,4},{4,5},{5,6},{6,7},{7,8},{8,9},{9,10},{10,1... | collective-permute-start | bytes 1474568
  2219.9 21.2 collective-permute-start.9
  2226.4 37.6 %copy-start.72 = (f32[1,4,1152]{2,1,0:T(4,128)S(1)}, f32[1,4,1152]{2,1,0:T(4,128)}, u32[]{:S(2)}) copy-start(f32[1,4,1152]{2,1,0:T(4,128)} %param.14) | copy-start | bytes 55300
  2231.8 56.7 %copy-start.78 = (f32[4,3072]{1,0:T(4,128)S(1)}, f32[4,3072]{1,0:T(4,128)}, u32[]{:S(2)}) copy-start(f32[4,3072]{1,0:T(4,128)} %copy-done.77) | copy-start | bytes 147460
  2241.1 40.5 %collective-permute-start.17 = (f32[40,3072]{1,0:T(8,128)}, f32[40,3072]{1,0:T(8,128)}, u32[]{:S(2)}, u32[]{:S(2)}) collective-permute-start(f32[40,3072]{1,0:T(8,128)} %get-tuple-element.18), channel_id=1, source_target_pairs={{0,2},{1,3},{2,4},{3,5},{4,6},{5,7},{6,8},{7,9},{8,10},{9,11},{10,... | collective-permute-start | bytes 1474568
  2243.2 20.8 copy-start.58
  2243.2 43.2 %collective-permute-start.18 = (f32[40,3072]{1,0:T(8,128)}, f32[40,3072]{1,0:T(8,128)}, u32[]{:S(2)}, u32[]{:S(2)}) collective-permute-start(f32[40,3072]{1,0:T(8,128)} %get-tuple-element.18), channel_id=1, source_target_pairs={{0,3},{1,4},{2,5},{3,6},{4,7},{5,8},{6,9},{7,10},{8,11},{9,12},{10... | collective-permute-start | bytes 1474568
  2254.2 49.7 %collective-permute-start = (f32[48,3456]{1,0:T(8,128)S(1)}, f32[48,3456]{1,0:T(8,128)}, u32[]{:S(2)}, u32[]{:S(2)}) collective-permute-start(f32[48,3456]{1,0:T(8,128)S(1)} %get-tuple-element.16), channel_id=1, source_target_pairs={{0,1},{1,2},{2,3},{3,4},{4,5},{5,6},{6,7},{7,8},{8,9},{9,10},{10,1... | collective-permute-start | bytes 1990664
  2257.3 48.6 %collective-permute-start.1 = (f32[48,3456]{1,0:T(8,128)S(1)}, f32[48,3456]{1,0:T(8,128)}, u32[]{:S(2)}, u32[]{:S(2)}) collective-permute-start(f32[48,3456]{1,0:T(8,128)S(1)} %get-tuple-element.16), channel_id=1, source_target_pairs={{0,2},{1,3},{2,4},{3,5},{4,6},{5,7},{6,8},{7,9},{8,10},{9,11},{10,... | collective-permute-start | bytes 1990664
  2261.4 40.9 %collective-permute-start.7 = (f32[36,3456]{1,0:T(8,128)}, f32[36,3456]{1,0:T(8,128)}, u32[]{:S(2)}, u32[]{:S(2)}) collective-permute-start(f32[36,3456]{1,0:T(8,128)} %slice.88), channel_id=1, source_target_pairs={{0,8},{1,9},{2,10},{3,11},{4,12},{5,13},{6,14},{7,15},{8,16},{9,17... | collective-permute-start | bytes 1493000
  2281.7 37.0 %collective-permute-start.2 = (f32[48,3456]{1,0:T(8,128)S(1)}, f32[48,3456]{1,0:T(8,128)}, u32[]{:S(2)}, u32[]{:S(2)}) collective-permute-start(f32[48,3456]{1,0:T(8,128)S(1)} %get-tuple-element.16), channel_id=1, source_target_pairs={{0,3},{1,4},{2,5},{3,6},{4,7},{5,8},{6,9},{7,10},{8,11},{9,12},{10... | collective-permute-start | bytes 1990664
  2286.4 32.3 %collective-permute-start.3 = (f32[48,3456]{1,0:T(8,128)S(1)}, f32[48,3456]{1,0:T(8,128)}, u32[]{:S(2)}, u32[]{:S(2)}) collective-permute-start(f32[48,3456]{1,0:T(8,128)S(1)} %get-tuple-element.16), channel_id=1, source_target_pairs={{0,4},{1,5},{2,6},{3,7},{4,8},{5,9},{6,10},{7,11},{8,12},{9,13},{1... | collective-permute-start | bytes 1990664
  2302.3 16.3 collective-permute-start.4
  2303.9 24.9 %collective-permute-start.5 = (f32[48,3456]{1,0:T(8,128)S(1)}, f32[48,3456]{1,0:T(8,128)S(1)}, u32[]{:S(2)}, u32[]{:S(2)}) collective-permute-start(f32[48,3456]{1,0:T(8,128)S(1)} %get-tuple-element.16), channel_id=1, source_target_pairs={{0,6},{1,7},{2,8},{3,9},{4,10},{5,11},{6,12},{7,13},{8,14},{9,15},... | collective-permute-start | bytes 1990664
  2305.9 30.0 %collective-permute-start.6 = (f32[48,3456]{1,0:T(8,128)S(1)}, f32[48,3456]{1,0:T(8,128)}, u32[]{:S(2)}, u32[]{:S(2)}) collective-permute-start(f32[48,3456]{1,0:T(8,128)S(1)} %get-tuple-element.16), channel_id=1, source_target_pairs={{0,7},{1,8},{2,9},{3,10},{4,11},{5,12},{6,13},{7,14},{8,15},{9,16}... | collective-permute-start | bytes 1990664
  2316.6 58.0 %copy-start.1 = (bf16[1152,1152]{1,0:T(8,128)(2,1)S(1)}, bf16[1152,1152]{1,0:T(8,128)(2,1)}, u32[]{:S(2)}) copy-start(bf16[1152,1152]{1,0:T(8,128)(2,1)} %param.21) | copy-start | bytes 7962628
  (87 other events, 648.5 us)
Sparse Core Ops, SparseCore 0:
  537.2 165.0 reduce-scatter.12
  832.3 219.6 reduce-scatter.14
where the time goes:
time: 2430 us; the launch traced here: 2380 us
  blocking collectives  1310 us (54%)
  matrix products  449 us (18%)
  local copies, waits for them, and re-layouts  245 us (10%)
  other arithmetic  245 us (10%)
  starting transfers between devices  106 us (4%)
    unnamed x3, blocking collectives  1250 us
    unnamed x233, local copies, waits for them, and re-layouts  103 us
    unnamed x25, starting transfers between devices  102 us
    convert_element_type x1, other arithmetic, body(): grad_scores = (attn_probs * (grad_probs - dot_term)).astype(jnp.bfloat16)  54.1 us
    dot_general x2, matrix products, body(): jnp.einsum('qhd,khd->hqk', grad_out_part, value_low, preferred_element_ty...  51.7 us
    unnamed x11, other arithmetic  51.4 us
  transfers between devices with their start and end apart: 27, of which 2 were waited for; matrix products, arithmetic and copies ran while one was open for 70% of the time, Pallas kernels for 0%

commit v1 on v0

--- a/solution.py
+++ b/solution.py
@@ -1,3 +1,5 @@
+import functools
+
 import jax
 import jax.numpy as jnp
 from jax import lax
@@ -49,7 +51,36 @@
     return sigmoid * (1.0 + v * (1.0 - sigmoid))
 
 
+def take_bit(arr, axis, bit):
+    return lax.dynamic_index_in_dim(arr, bit, axis=axis, keepdims=False)
+
+
+def reduce_rows(grad, n_dp, n_mod):
+    n_dev = n_dp * n_mod
+    bits = n_dp.bit_length() - 1
+    position = lax.axis_index("dp")
+    arr = grad.reshape((2,) * bits + (n_mod, grad.shape[0] // n_dev, grad.shape[1]))
+    order = [0] + ["mod"] + list(range(1, bits))
+    axes = list(range(bits - 1, -1, -1)) + ["mod"]
+    for step in order:
+        axis = axes.index(step)
+        if step == "mod":
+            mine = lax.axis_index("mod")
+            name, pairs = "mod", [(i, i ^ 1) for i in range(n_mod)]
+        else:
+            mine = lax.shift_right_logical(position, step) & 1
+            name, pairs = "dp", [(i, i ^ (1 << step)) for i in range(n_dp)]
+        sent = take_bit(arr, axis, 1 - mine).astype(jnp.bfloat16)
+        kept = take_bit(arr, axis, mine)
+        got = lax.ppermute(sent, name, pairs)
+        arr = kept + got.astype(jnp.float32)
+        axes.pop(axis)
+    return arr
+
+
 def body(
+    n_dp,
+    n_mod,
     tokens,
     cond,
     segments,
@@ -230,10 +261,15 @@
     ).astype(jnp.bfloat16)
     grad_mod_half = lax.all_to_all(grad_modulation, "mod", split_axis=2, concat_axis=0, tiled=True)
     grad_mod_flat = grad_mod_half.reshape(-1, half_channels)
-    grad_ada_local = jnp.einsum(
-        "nd,nc->dc", activated, grad_mod_flat, preferred_element_type=jnp.float32
-    )
-    grad_w_ada = lax.psum_scatter(grad_ada_local, "dp", scatter_dimension=0, tiled=True)
+    all_activated = lax.all_gather(activated, "dp", axis=0, tiled=True)
+    rows_ada = width // n_dp
+    own_activated = lax.dynamic_slice_in_dim(
+        all_activated, lax.axis_index("dp") * rows_ada, rows_ada, axis=1
+    )
+    all_grad_mod = lax.all_gather(grad_mod_flat, "dp", axis=0, tiled=True)
+    grad_w_ada = jnp.einsum(
+        "nd,nc->dc", own_activated, all_grad_mod, preferred_element_type=jnp.float32
+    )
     grad_activated = jnp.einsum(
         "nc,dc->nd", grad_mod_flat, w_ada, preferred_element_type=jnp.float32
     )
@@ -244,11 +280,11 @@
     grad_cond = grad_own * silu_grad(cond)
     summed_q_gain, summed_k_gain = lax.psum((grad_q_gain, grad_k_gain), ("dp", "mod"))
     summed_qkv, summed_out, summed_gate, summed_up, summed_down = (
-        lax.psum_scatter(grad_w_qkv, ("dp", "mod"), scatter_dimension=0, tiled=True),
-        lax.psum_scatter(grad_w_out, ("dp", "mod"), scatter_dimension=0, tiled=True),
-        lax.psum_scatter(grad_w_gate, ("dp", "mod"), scatter_dimension=0, tiled=True),
-        lax.psum_scatter(grad_w_up, ("dp", "mod"), scatter_dimension=0, tiled=True),
-        lax.psum_scatter(grad_w_down, ("dp", "mod"), scatter_dimension=0, tiled=True),
+        reduce_rows(grad_w_qkv, n_dp, n_mod),
+        reduce_rows(grad_w_out, n_dp, n_mod),
+        reduce_rows(grad_w_gate, n_dp, n_mod),
+        reduce_rows(grad_w_up, n_dp, n_mod),
+        reduce_rows(grad_w_down, n_dp, n_mod),
     )
     return (
         output,
@@ -294,4 +330,5 @@
         P(("dp", "mod"), None),
         P(("dp", "mod"), None),
     )
-    return jax.shard_map(body, mesh=mesh, in_specs=in_specs, out_specs=out_specs, check_vma=False)
+    return jax.shard_map(
+        functools.partial(body, mesh.shape['dp'], mesh.shape['mod']), mesh=mesh, in_specs=in_specs, out_specs=out_specs, check_vma=False)

time: 2430 us -> 1370 us (0.56); the launches traced: 2380 us -> 1360 us
  blocking collectives: 1310 us -> 102 us
  local copies, waits for them, and re-layouts: 245 us -> 382 us
  starting transfers between devices: 106 us -> 24.3 us
  waiting for transfers between devices: 16.5 us -> 94 us
  other arithmetic: 245 us -> 322 us
    unnamed x3 -> x1, blocking collectives: 1250 us -> 9.24 us
    unnamed x25 -> x0, starting transfers between devices: 102 us -> none
    convert_element_type x0 -> x41, local copies, waits for them, and re-layouts: none -> 99.8 us  [reduce_rows(): sent = take_bit(arr, axis, 1 - mine).astype(jnp.bfloat16)]
    ppermute x0 -> x25, waiting for transfers between devices: none -> 94 us  [reduce_rows(): got = lax.ppermute(sent, name, pairs)]
    add x0 -> x25, other arithmetic: none -> 80.9 us  [reduce_rows(): arr = kept + got.astype(jnp.float32)]
    unnamed x233 -> x245, local copies, waits for them, and re-layouts: 103 us -> 33.5 us
    dynamic_slice x0 -> x20, local copies, waits for them, and re-layouts: none -> 64.6 us  [take_bit(): return lax.dynamic_index_in_dim(arr, bit, axis=axis, keepdims=False)]
    all_gather x0 -> x2, blocking collectives: none -> 47.7 us  [the longest x1 24.5 us: body(): all_activated = lax.all_gather(activated, 'dp', axis=0, tiled=True)]
  transfers between devices with their start and end apart: 27 -> 27, of which waited for: 2 -> 11; matrix products, arithmetic and copies ran while one was open for 70% -> 23% of each run, Pallas kernels for 0% -> 0%
where the time goes in v1:
time: 1370 us; the launch traced here: 1360 us
  matrix products  432 us (32%)
  local copies, waits for them, and re-layouts  382 us (28%)
  other arithmetic  322 us (24%)
  blocking collectives  102 us (7%)
  waiting for transfers between devices  94 us (7%)
  starting transfers between devices  24.3 us (2%)
    convert_element_type x41, local copies, waits for them, and re-layouts, reduce_rows(): sent = take_bit(arr, axis, 1 - mine).astype(jnp.bfloat16)  99.8 us
    ppermute x25, waiting for transfers between devices, reduce_rows(): got = lax.ppermute(sent, name, pairs)  94 us
    add x25, other arithmetic, reduce_rows(): arr = kept + got.astype(jnp.float32)  80.9 us
    dynamic_slice x20, local copies, waits for them, and re-layouts, take_bit(): return lax.dynamic_index_in_dim(arr, bit, axis=axis, keepdims=False)  64.6 us
    convert_element_type x1, other arithmetic, body(): grad_scores = (attn_probs * (grad_probs - dot_term)).astype(jnp.bfloat16)  54.2 us
    unnamed x18, other arithmetic  52.6 us
    dot_general x2, matrix products, body(): jnp.einsum('qhd,khd->hqk', grad_out_part, value_low, preferred_element_ty...  51.6 us
    reshape x3, local copies, waits for them, and re-layouts, reduce_rows(): grad.reshape((2,) * bits + (n_mod, grad.shape[0] // n_dev, grad.shape[1]))  42.9 us
  transfers between devices with their start and end apart: 27, of which 11 were waited for; matrix products, arithmetic and copies ran while one was open for 23% of the time, Pallas kernels for 0%

profile of v1, /device:TPU:0, one launch (start us, length us, event | category | flops | bytes accessed | tf_op | source)
XLA Modules:
  0.0 1359.8 jit_solution(13589217506843282343)
XLA Ops:
  22.2 24.5 %all_gather.10 = bf16[128,1152]{1,0:T(8,128)(2,1)} all-gather(bf16[8,1152]{1,0:T(8,128)(2,1)S(1)} %reshape.426), channel_id=1, replica_groups=mesh['dp'=16,'mod'=2] {'dp'}, dimensions={0}, use_global_device_ids=true | all-gather | bytes 313344 | tf_op jit(solution)/shard_map/all_gather | solution.py:264
  48.9 11.6 fusion.82
  66.4 12.3 fusion.111
  130.6 15.9 %fusion = (f32[16,512]{1,0:T(8,128)S(1)}, f32[16,512,1024]{2,1,0:T(8,128)}) fusion(pred[512,1024]{1,0:T(8,128)(4,1)S(1)} %copy-done.15, bf16[1024,16,72]{0,1,2:T(8,128)(2,1)S(1)} %bitcast.292, bf16[512,16,72]{0,1,2:T(8,128)(2,1)S(1)} %bitcast.332), kind=kOutput, calls=%fused_computation.10 | convolution fusion | flops 1233117184 | bytes 37650432 | tf_op jit(solution)/shard_map/qhd,khd->hqk/dot_general | solution.py:148
  146.5 15.0 %exponential_reduce_fusion.1 = f32[16,512]{1,0:T(8,128)S(1)} fusion(f32[16,512,1024]{2,1,0:T(8,128)} %get-tuple-element.64, f32[16,512]{1,0:T(8,128)S(1)} %get-tuple-element.63, pred[512,1024]{1,0:T(8,128)(4,1)S(1)} %copy-done.15), kind=kLoop, calls=%fused_computation.8 | loop fusion | flops 33546240 | bytes 34144256 | tf_op jit(solution)/shard_map/reduce_sum | solution.py:160
  167.9 21.1 %fusion.1 = (f32[16,512]{1,0:T(8,128)S(1)}, f32[16,512,1024]{2,1,0:T(8,128)}) fusion(pred[512,1024]{1,0:T(8,128)(4,1)S(1)} %get-tuple-element.58, bf16[1024,16,72]{0,1,2:T(8,128)(2,1)} %bitcast.293, bf16[512,16,72]{0,1,2:T(8,128)(2,1)S(1)} %bitcast.318), kind=kOutput, calls=%fused_computation.11 | convolution fusion | flops 1233117184 | bytes 37650432 | tf_op jit(solution)/shard_map/qhd,khd->hqk/dot_general | solution.py:148
  189.0 15.0 %exponential_reduce_fusion = f32[16,512]{1,0:T(8,128)S(1)} fusion(f32[16,512,1024]{2,1,0:T(8,128)} %get-tuple-element.62, f32[16,512]{1,0:T(8,128)S(1)} %get-tuple-element.61, pred[512,1024]{1,0:T(8,128)(4,1)S(1)} %get-tuple-element.58), kind=kLoop, calls=%fused_computation.5 | loop fusion | flops 33546240 | bytes 34144256 | tf_op jit(solution)/shard_map/reduce_sum | solution.py:160
  204.1 16.1 %fusion.60 = bf16[512,16,72]{0,2,1:T(8,128)(2,1)} fusion(bf16[1024,16,72]{0,2,1:T(8,128)(2,1)} %bitcast.308, f32[16,512,1024]{2,1,0:T(8,128)} %get-tuple-element.64, f32[16,512]{1,0:T(8,128)S(1)} %log_add_fusion.1, pred[512,1024]{1,0:T(8,128)(4,1)} %get-tuple-element.57), kind=kOutput, calls=%fused_computation.160 | convolution fusion | flops 1242103808 | bytes 37650432 | tf_op jit(solution)/shard_map/hqk,khd->qhd/dot_general | solution.py:164
  220.2 16.2 %fusion.61 = bf16[512,16,72]{0,2,1:T(8,128)(2,1)} fusion(bf16[1024,16,72]{0,2,1:T(8,128)(2,1)} %bitcast.309, f32[16,512,1024]{2,1,0:T(8,128)} %get-tuple-element.62, f32[16,512]{1,0:T(8,128)S(1)} %log_add_fusion, pred[512,1024]{1,0:T(8,128)(4,1)S(1)} %get-tuple-element.58), kind=kOutput, calls=%fused_computation.161 | convolution fusion | flops 1242103808 | bytes 37650432 | tf_op jit(solution)/shard_map/hqk,khd->qhd/dot_general | solution.py:164
  253.5 14.1 %fusion.112 = f32[1024,3072]{1,0:T(8,128)} fusion(bf16[1024,1152]{1,0:T(8,128)(2,1)S(1)} %fusion.25, bf16[1152,3072]{1,0:T(8,128)(2,1)} %param.22), kind=kOutput, calls=%fused_computation.289 | convolution fusion | flops 7247757312 | bytes 22020096 | tf_op jit(solution)/shard_map/dot_general | solution.py:174
  267.6 10.6 fusion.113
  278.2 27.7 %multiply_convert_fusion.2 = (bf16[1024,3072]{1,0:T(8,128)(2,1)}, bf16[1024,3072]{1,0:T(8,128)(2,1)}, bf16[1024,3072]{1,0:T(8,128)(2,1)}) fusion(f32[1024,3072]{1,0:T(8,128)} %fusion.112, f32[1024,3072]{1,0:T(8,128)} %fusion.113, bf16[3072,1152]{1,0:T(8,128)(2,1)} %param.24, f32[1024,6912]{1,0:T(8,128)} %fusion.82, bf16[1,1024,1152]{2,1,0:T(8,128)(2,1)} %param.25), kind=kOutput, calls=%fused_computation.14 | convolution fusion | flops 7298482176 | bytes 58195968 | tf_op jit(solution)/shard_map/nd,fd->nf/dot_general | solution.py:183
  305.9 13.3 fusion.117
  319.3 12.7 reshape.446
  345.3 10.1 fusion.116
  355.4 12.9 reshape.445
  381.8 12.1 fusion.115
  393.9 15.0 %fusion.98 = f32[3072,1152]{1,0:T(8,128)} fusion(bf16[1024,3072]{1,0:T(8,128)(2,1)} %get-tuple-element.22, f32[1024,6912]{1,0:T(8,128)} %fusion.82, bf16[1,1024,1152]{2,1,0:T(8,128)(2,1)S(1)} %copy-done.21), kind=kOutput, calls=%fused_computation.278 | convolution fusion | flops 7251296256 | bytes 27525120 | tf_op jit(solution)/shard_map/nf,nd->fd/dot_general | solution.py:182
  408.9 11.9 fusion.114
  420.9 17.2 %multiply_reduce_fusion.4 = (f32[1024]{0:T(1024)S(1)}, f32[1024,1152]{1,0:T(8,128)}) fusion(f32[1024,1152]{1,0:T(8,128)S(1)} %bitcast.289, f32[1024]{0:T(1024)S(1)} %copy-done.64, f32[1024,6912]{1,0:T(8,128)} %fusion.82, f32[1024,1152]{1,0:T(8,128)} %fusion.115, bf16[1024,3072]{1,0:T(8,128)(2,1)} %get-tuple-element.20, bf16[1152,3072]{1,0:T(8,128)(2,1)} %param.23), kind=kOutput, calls=%fused_computation.82 | convolution fusion | flops 7254834176 | bytes 32251904 | tf_op jit(solution)/shard_map/nf,df->nd/dot_general | solution.py:191
  438.1 9.1 fusion.103
  460.1 25.8 %multiply_reduce_fusion.1 = (f32[16,512]{1,0:T(8,128)S(1)}, f32[16,512,1024]{2,1,0:T(8,128)}) fusion(f32[16,512,1024]{2,1,0:T(8,128)} %get-tuple-element.64, f32[16,512]{1,0:T(8,128)S(1)} %copy-done.56, pred[512,1024]{1,0:T(8,128)(4,1)} %get-tuple-element.57, bf16[512,16,72]{0,2,1:T(8,128)(2,1)} %bitcast.340, bf16[1024,16,72]{0,2,1:T(8,128)(2,1)S(1)} %bitcast.310), kind=kOutput, calls=%fused_computation.3 | convolution fusion | flops 1249894400 | bytes 71237632 | tf_op jit(solution)/shard_map/qhd,khd->hqk/dot_general | solution.py:215
  488.3 25.8 %multiply_reduce_fusion = (f32[16,512]{1,0:T(8,128)S(1)}, f32[16,512,1024]{2,1,0:T(8,128)}) fusion(f32[16,512,1024]{2,1,0:T(8,128)} %get-tuple-element.62, f32[16,512]{1,0:T(8,128)S(1)} %copy-done.54, pred[512,1024]{1,0:T(8,128)(4,1)S(1)} %copy-done.14, bf16[512,16,72]{0,2,1:T(8,128)(2,1)} %bitcast.338, bf16[1024,16,72]{0,2,1:T(8,128)(2,1)S(1)} %bitcast.311), kind=kOutput, calls=%fused_computation.1 | convolution fusion | flops 1249894400 | bytes 71237632 | tf_op jit(solution)/shard_map/qhd,khd->hqk/dot_general | solution.py:215
  514.1 54.2 %multiply_convert_fusion = (bf16[16,512,1024]{2,1,0:T(8,128)(2,1)}, bf16[16,512,1024]{2,1,0:T(8,128)(2,1)}) fusion(f32[16,512,1024]{2,1,0:T(8,128)} %get-tuple-element.69, f32[16,512,1024]{2,1,0:T(8,128)} %get-tuple-element.62, f32[16,512]{1,0:T(8,128)S(1)} %get-tuple-element.68, f32[16,512]{1,0:T(8,128)S(1)} %copy-done.54, ...), kind=kLoop, calls=%fused_computation | loop fusion | flops 100663296 | bytes 168951808 | tf_op jit(solution)/shard_map/convert_element_type | solution.py:219
  568.3 11.7 fusion.64
  580.1 12.9 multiply_bitcast_fusion.2
  593.0 13.1 multiply_bitcast_fusion.1
  606.1 11.2 multiply_bitcast_fusion
  626.7 9.5 fusion.36
  671.0 16.8 %fusion.73 = f32[16,72,1024]{2,1,0:T(8,128)} fusion(bf16[512,16,72]{0,2,1:T(8,128)(2,1)S(1)} %bitcast.341, f32[16,512,1024]{2,1,0:T(8,128)} %get-tuple-element.64, f32[16,512]{1,0:T(8,128)S(1)} %copy-done.56, pred[512,1024]{1,0:T(8,128)(4,1)S(1)} %copy-done.17), kind=kOutput, calls=%fused_computation.212 | convolution fusion | flops 1241513984 | bytes 40009728 | tf_op jit(solution)/shard_map/hqk,qhd->khd/dot_general | solution.py:212
  749.9 17.7 %add_convert_fusion.1 = bf16[16,72,1024]{2,1,0:T(8,128)(2,1)} fusion(f32[16,72,1024]{2,1,0:T(8,128)} %fusion.73, bf16[512,16,72]{0,2,1:T(8,128)(2,1)S(1)} %bitcast.339, f32[16,512,1024]{2,1,0:T(8,128)} %get-tuple-element.62, f32[16,512]{1,0:T(8,128)S(1)} %copy-done.54, pred[512,1024]{1,0:T(8,128)(4,1)S(1)} %copy-done.14), kind=kOutput, calls=%fused_computation.80 | convolution fusion | flops 1243873280 | bytes 42369024 | tf_op jit(solution)/shard_map/hqk,qhd->khd/dot_general | solution.py:212
  771.9 13.1 fusion.21
  786.3 12.6 fusion.42
  798.9 17.3 %reshape.444 = f32[2,2,2,2,2,36,3456]{6,5,4,3,2,1,0:T(8,128)} reshape(f32[1152,3456]{1,0:T(8,128)} %fusion.42) | data formatting | bytes 31850496 | tf_op jit(solution)/shard_map/reshape | solution.py:62
  830.1 16.0 %constant_dynamic-update-slice_fusion.1 = (f32[1024,6912]{1,0:T(8,128)}, f32[1024,1152]{1,0:T(8,128)}) fusion(bf16[1152,3456]{1,0:T(8,128)(2,1)} %param.18, bf16[1024,1152]{1,0:T(8,128)(2,1)} %copy.314, bf16[1024,1152]{1,0:T(8,128)(2,1)S(1)} %copy-done.38, bf16[1024,1152]{1,0:T(8,128)(2,1)S(1)} %get-tuple-element.23), kind=kOutput, calls=%fused_computation.231 | convolution fusion | flops 8174960640 | bytes 24477696 | tf_op jit(solution)/shard_map/ne,de->nd/dot_general | solution.py:242
  888.6 13.6 fusion.7
  908.5 38.5 %reduce.3 = bf16[6912,4]{1,0:T(8,128)(2,1)S(1)} reduce(bf16[6912,1,4]{2,1,0:T(2,128)(2,1)} %bitcast.334, bf16[]{:T(256)} %broadcast.384), dimensions={1}, to_apply=%bitcast.223.reduce_sub_computation | reduce | bytes 110594
  977.5 39.4 %all-reduce.5 = (f32[72]{0:T(128)}, f32[72]{0:T(128)}) all-reduce(f32[72]{0:T(128)S(1)} %reduce_sum.215, f32[72]{0:T(128)S(1)} %reduce_sum.217), channel_id=1, replica_groups=mesh['dp'=16,'mod'=2] {'dp','mod'}, use_global_device_ids=true, to_apply=%region_20.21 | all-reduce | flops 144 | bytes 1152 | tf_op jit(solution)/shard_map/psum | solution.py:281
  1034.8 9.2 all-reduce.4
  1051.3 23.2 %all_gather.11 = bf16[128,3456]{1,0:T(8,128)(2,1)S(1)} all-gather(bf16[8,3456]{1,0:T(8,128)(2,1)S(1)} %reshape.443), channel_id=1, replica_groups=mesh['dp'=16,'mod'=2] {'dp'}, dimensions={0}, use_global_device_ids=true | all-gather | bytes 940032 | tf_op jit(solution)/shard_map/all_gather | solution.py:269
  1110.6 9.9 bitcast_add_fusion.2
  1132.4 14.1 %bitcast_add_fusion.3 = f32[2,2,2,2,36,3072]{5,3,4,2,1,0:T(2,128)} fusion(f32[2,2,2,1,2,36,3072]{6,5,4,3,2,1,0:T(8,128)} %constant_dynamic-slice_fusion.11, bf16[2,2,2,2,36,3072]{5,3,4,2,1,0:T(2,128)(2,1)} %collective-permute-done.10), kind=kLoop, calls=%fused_computation.31 | loop fusion | flops 3538944 | bytes 17694720 | tf_op jit(solution)/shard_map/add | solution.py:76
  1174.1 12.9 bitcast_add_fusion
  1202.9 9.4 constant_dynamic-slice_fusion.20
  1241.3 25.8 %collective-permute-done.1 = bf16[2,2,2,36,3456]{4,2,3,1,0:T(2,128)(2,1)} collective-permute-done((bf16[2,2,2,36,3456]{4,2,3,1,0:T(2,128)(2,1)}, bf16[2,2,2,36,3456]{4,2,3,1,0:T(2,128)(2,1)}, u32[]{:S(2)}, u32[]{:S(2)}) %collective-permute-start.1) | collective-permute-done | bytes 1990688 | tf_op jit(solution)/shard_map/ppermute | solution.py:75
  1293.4 15.1 %collective-permute-done.18 = bf16[2,36,3072]{2,0,1:T(2,128)(2,1)S(1)} collective-permute-done((bf16[2,36,3072]{2,0,1:T(2,128)(2,1)S(1)}, bf16[2,36,3072]{2,0,1:T(2,128)(2,1)S(1)}, u32[]{:S(2)}, u32[]{:S(2)}) %collective-permute-start.18) | collective-permute-done | bytes 442400 | tf_op jit(solution)/shard_map/ppermute | solution.py:75
  1317.9 8.9 collective-permute-done.19
  1349.5 9.3 collective-permute-done.4
  (489 shorter events, 556.0 us)
Async XLA Ops:
  0.6 237.8 %copy-start = (bf16[1152,1152]{1,0:T(8,128)(2,1)S(1)}, bf16[1152,1152]{1,0:T(8,128)(2,1)}, u32[]{:S(2)}) copy-start(bf16[1152,1152]{1,0:T(8,128)(2,1)} %param.21) | copy-start | bytes 7962628
  10.8 35.9 %copy-start.85 = (f32[72]{0:T(128)S(1)}, f32[72]{0:T(128)}, u32[]{:S(2)}) copy-start(f32[72]{0:T(128)} %param.20) | copy-start | bytes 868
  10.9 35.9 %copy-start.87 = (f32[72]{0:T(128)S(1)}, f32[72]{0:T(128)}, u32[]{:S(2)}) copy-start(f32[72]{0:T(128)} %param.19) | copy-start | bytes 868
  10.9 37.4 %copy-start.89 = (u32[32]{0:T(128)S(1)}, u32[32]{0:T(128)}, u32[]{:S(2)}) copy-start(u32[32]{0:T(128)} %constant.226) | copy-start | bytes 388
  11.5 37.4 %all-to-all-start = ((bf16[2,4,3456]{2,1,0:T(4,128)(2,1)}), bf16[2,4,3456]{2,1,0:T(4,128)(2,1)S(1)}, u32[]{:S(2)}, u32[]{:S(2)}) async-start(bf16[2,4,3456]{2,1,0:T(4,128)(2,1)} %reshape.427), calls=%async_computation | async-start | bytes 110592 | tf_op jit(solution)/shard_map/all_to_all | solution.py:109
  16.9 43.6 %copy-start.66 = (f32[1024]{0:T(1024)}, f32[1024]{0:T(1024)S(1)}, u32[]{:S(2)}) copy-start(f32[1024]{0:T(1024)S(1)} %broadcast_multiply_fusion.1) | copy-start | bytes 12292
  19.3 27.4 %copy-start.74 = (f32[1024]{0:T(1024)}, f32[1024]{0:T(1024)S(1)}, u32[]{:S(2)}) copy-start(f32[1024]{0:T(1024)S(1)} %fusion.19) | copy-start | bytes 12292
  19.4 41.2 %copy-start.72 = (f32[1024]{0:T(1024)}, f32[1024]{0:T(1024)S(1)}, u32[]{:S(2)}) copy-start(f32[1024]{0:T(1024)S(1)} %fusion.86) | copy-start | bytes 12292
  20.8 103.1 %copy-start.45 = (f32[1024,2,18]{0,2,1:T(8,128)}, f32[1024,2,18]{0,2,1:T(8,128)S(1)}, u32[]{:S(2)}) copy-start(f32[1024,2,18]{0,2,1:T(8,128)S(1)} %get-tuple-element.55) | copy-start | bytes 442372
  22.2 197.9 %copy-start.13 = (pred[512,1024]{1,0:T(8,128)(4,1)}, pred[512,1024]{1,0:T(8,128)(4,1)S(1)}, u32[]{:S(2)}) copy-start(pred[512,1024]{1,0:T(8,128)(4,1)S(1)} %get-tuple-element.58) | copy-start | bytes 1572868
  161.5 42.5 %copy-start.55 = (f32[16,512]{1,0:T(8,128)}, f32[16,512]{1,0:T(8,128)S(1)}, u32[]{:S(2)}) copy-start(f32[16,512]{1,0:T(8,128)S(1)} %log_add_fusion.1) | copy-start | bytes 98308
  167.9 21.1 %copy-start.24 = (bf16[512,16,2,2,18]{0,1,4,3,2:T(8,128)(2,1)}, bf16[512,16,2,2,18]{0,1,4,3,2:T(8,128)(2,1)S(1)}, u32[]{:S(2)}) copy-start(bf16[512,16,2,2,18]{0,1,4,3,2:T(8,128)(2,1)S(1)} %copy.289) | copy-start | bytes 3538948
  248.9 18.7 %slice-start.24 = ((s8[7077888]{0:T(1024)(128)(4,1)}), s8[4194304]{0:T(1024)(128)(4,1)S(1)}, s32[]{:S(2)}) async-start(s8[7077888]{0:T(1024)(128)(4,1)} %bitcast.366), calls=%async_computation.26 | async-start | bytes 8388608
  381.7 27.2 %slice-start.22 = ((s8[7077888]{0:T(1024)(128)(4,1)}), s8[2883584]{0:T(1024)(128)(4,1)S(1)}, s32[]{:S(2)}) async-start(s8[7077888]{0:T(1024)(128)(4,1)} %bitcast.364), calls=%async_computation.24 | async-start | bytes 5767168
  381.8 39.1 %slice-start = ((s8[4718592]{0:T(1024)(128)(4,1)}), s8[4194304]{0:T(1024)(128)(4,1)S(1)}, s32[]{:S(2)}) async-start(s8[4718592]{0:T(1024)(128)(4,1)} %bitcast.288), calls=%async_computation.2 | async-start | bytes 8388608
  393.9 26.9 %slice-start.1 = ((s8[4718592]{0:T(1024)(128)(4,1)}), s8[524288]{0:T(1024)(128)(4,1)S(1)}, s32[]{:S(2)}) async-start(s8[4718592]{0:T(1024)(128)(4,1)} %bitcast.288), calls=%async_computation.3 | async-start | bytes 1048576
  460.1 28.2 %copy-start.14 = (pred[512,1024]{1,0:T(8,128)(4,1)S(1)}, pred[512,1024]{1,0:T(8,128)(4,1)}, u32[]{:S(2)}) copy-start(pred[512,1024]{1,0:T(8,128)(4,1)} %copy-done.13) | copy-start | bytes 1572868
  460.1 28.2 %copy-start.54 = (f32[16,512]{1,0:T(8,128)S(1)}, f32[16,512]{1,0:T(8,128)}, u32[]{:S(2)}) copy-start(f32[16,512]{1,0:T(8,128)} %copy-done.53) | copy-start | bytes 98308
  488.3 25.8 %copy-start.16 = (pred[512,1024]{1,0:T(8,128)(4,1)S(1)}, pred[512,1024]{1,0:T(8,128)(4,1)}, u32[]{:S(2)}) copy-start(pred[512,1024]{1,0:T(8,128)(4,1)} %get-tuple-element.57) | copy-start | bytes 1572868
  514.1 54.2 %copy-start.26 = (bf16[512,16,2,2,18]{0,1,4,3,2:T(8,128)(2,1)S(1)}, bf16[512,16,2,2,18]{0,1,4,3,2:T(8,128)(2,1)}, u32[]{:S(2)}) copy-start(bf16[512,16,2,2,18]{0,1,4,3,2:T(8,128)(2,1)} %copy-done.25) | copy-start | bytes 3538948
  862.2 183.1 %collective-permute-start.5 = (bf16[2,2,2,2,36,1152]{5,3,4,2,1,0:T(2,128)(2,1)}, bf16[2,2,2,2,36,1152]{5,3,4,2,1,0:T(2,128)(2,1)}, u32[]{:S(2)}, u32[]{:S(2)}) collective-permute-start(bf16[2,2,2,2,36,1152]{5,3,4,2,1,0:T(2,128)(2,1)} %copy.327), channel_id=1, source_target_pairs={{0,2},{2,0},{4,6},{6,4},{8,10},{10,8},{12,14},{14,12},{16,18},{18,... | collective-permute-start | bytes 3981320 | tf_op jit(solution)/shard_map/ppermute | solution.py:75
  950.9 66.0 %all-to-all-start.1 = ((bf16[2,2,6912]{2,1,0:T(2,128)(2,1)}), bf16[2,2,6912]{2,1,0:T(2,128)(2,1)S(1)}, u32[]{:S(2)}, u32[]{:S(2)}) async-start(bf16[2,2,6912]{2,1,0:T(2,128)(2,1)} %reshape.452), calls=%async_computation.1 | async-start | bytes 110592 | tf_op jit(solution)/shard_map/all_to_all | solution.py:262
  958.3 143.7 %collective-permute-start.20 = (bf16[2,2,2,2,96,1152]{5,4,0,1,2,3:T(8,128)(2,1)}, bf16[2,2,2,2,96,1152]{5,4,0,1,2,3:T(8,128)(2,1)}, u32[]{:S(2)}, u32[]{:S(2)}) collective-permute-start(bf16[2,2,2,2,96,1152]{5,4,0,1,2,3:T(8,128)(2,1)} %fusion.35), channel_id=1, source_target_pairs={{0,2},{2,0},{4,6},{6,4},{8,10},{10,8},{12,14},{14,12},{16,18},{18,... | collective-permute-start | bytes 10616840 | tf_op jit(solution)/shard_map/ppermute | solution.py:75
  964.0 146.6 %collective-permute-start.15 = (bf16[2,2,2,2,36,3072]{5,3,4,2,1,0:T(2,128)(2,1)}, bf16[2,2,2,2,36,3072]{5,3,4,2,1,0:T(2,128)(2,1)}, u32[]{:S(2)}, u32[]{:S(2)}) collective-permute-start(bf16[2,2,2,2,36,3072]{5,3,4,2,1,0:T(2,128)(2,1)} %copy.343), channel_id=1, source_target_pairs={{0,2},{2,0},{4,6},{6,4},{8,10},{10,8},{12,14},{14,12},{16,18},{18,... | collective-permute-start | bytes 10616840 | tf_op jit(solution)/shard_map/ppermute | solution.py:75
  969.6 162.8 %collective-permute-start.10 = (bf16[2,2,2,2,36,3072]{5,3,4,2,1,0:T(2,128)(2,1)}, bf16[2,2,2,2,36,3072]{5,3,4,2,1,0:T(2,128)(2,1)}, u32[]{:S(2)}, u32[]{:S(2)}) collective-permute-start(bf16[2,2,2,2,36,3072]{5,3,4,2,1,0:T(2,128)(2,1)} %copy.335), channel_id=1, source_target_pairs={{0,2},{2,0},{4,6},{6,4},{8,10},{10,8},{12,14},{14,12},{16,18},{18,... | collective-permute-start | bytes 10616840 | tf_op jit(solution)/shard_map/ppermute | solution.py:75
  977.3 196.8 %collective-permute-start = (bf16[2,2,2,2,36,3456]{5,3,4,2,1,0:T(2,128)(2,1)}, bf16[2,2,2,2,36,3456]{5,3,4,2,1,0:T(2,128)(2,1)}, u32[]{:S(2)}, u32[]{:S(2)}) collective-permute-start(bf16[2,2,2,2,36,3456]{5,3,4,2,1,0:T(2,128)(2,1)} %copy.319), channel_id=1, source_target_pairs={{0,2},{2,0},{4,6},{6,4},{8,10},{10,8},{12,14},{14,12},{16,18},{18,... | collective-permute-start | bytes 11943944 | tf_op jit(solution)/shard_map/ppermute | solution.py:75
  1051.2 24.7 %collective-permute-start.6 = (bf16[2,2,2,36,1152]{4,2,3,1,0:T(2,128)(2,1)S(1)}, bf16[2,2,2,36,1152]{4,2,3,1,0:T(2,128)(2,1)S(1)}, u32[]{:S(2)}, u32[]{:S(2)}) collective-permute-start(bf16[2,2,2,36,1152]{4,2,3,1,0:T(2,128)(2,1)S(1)} %bitcast.346), channel_id=1, source_target_pairs={{0,1},{1,0},{2,3},{3,2},{4,5},{5,4},{6,7},{7,6},{8,9},{9,8},{10,11... | collective-permute-start | bytes 1990664 | tf_op jit(solution)/shard_map/ppermute | solution.py:75
  1077.8 10.1 collective-permute-start.7
  1088.8 5.8 collective-permute-start.8
  1095.0 6.2 collective-permute-start.9
  1110.2 102.1 %collective-permute-start.21 = (bf16[2,2,2,96,1152]{4,3,0,1,2:T(8,128)(2,1)S(1)}, bf16[2,2,2,96,1152]{4,3,0,1,2:T(8,128)(2,1)}, u32[]{:S(2)}, u32[]{:S(2)}) collective-permute-start(bf16[2,2,2,96,1152]{4,3,0,1,2:T(8,128)(2,1)S(1)} %fusion.51), channel_id=1, source_target_pairs={{0,1},{1,0},{2,3},{3,2},{4,5},{5,4},{6,7},{7,6},{8,9},{9,8},{10,11... | collective-permute-start | bytes 5308424 | tf_op jit(solution)/shard_map/ppermute | solution.py:75
  1130.7 86.3 %collective-permute-start.16 = (bf16[2,2,2,36,3072]{4,2,3,1,0:T(2,128)(2,1)}, bf16[2,2,2,36,3072]{4,2,3,1,0:T(2,128)(2,1)}, u32[]{:S(2)}, u32[]{:S(2)}) collective-permute-start(bf16[2,2,2,36,3072]{4,2,3,1,0:T(2,128)(2,1)} %bitcast.273), channel_id=1, source_target_pairs={{0,1},{1,0},{2,3},{3,2},{4,5},{5,4},{6,7},{7,6},{8,9},{9,8},{10,11... | collective-permute-start | bytes 5308424 | tf_op jit(solution)/shard_map/ppermute | solution.py:75
  1156.6 71.1 %collective-permute-start.11 = (bf16[2,2,2,36,3072]{4,2,3,1,0:T(2,128)(2,1)}, bf16[2,2,2,36,3072]{4,2,3,1,0:T(2,128)(2,1)}, u32[]{:S(2)}, u32[]{:S(2)}) collective-permute-start(bf16[2,2,2,36,3072]{4,2,3,1,0:T(2,128)(2,1)} %bitcast.274), channel_id=1, source_target_pairs={{0,1},{1,0},{2,3},{3,2},{4,5},{5,4},{6,7},{7,6},{8,9},{9,8},{10,11... | collective-permute-start | bytes 5308424 | tf_op jit(solution)/shard_map/ppermute | solution.py:75
  1201.2 65.9 %collective-permute-start.1 = (bf16[2,2,2,36,3456]{4,2,3,1,0:T(2,128)(2,1)}, bf16[2,2,2,36,3456]{4,2,3,1,0:T(2,128)(2,1)}, u32[]{:S(2)}, u32[]{:S(2)}) collective-permute-start(bf16[2,2,2,36,3456]{4,2,3,1,0:T(2,128)(2,1)} %bitcast.272), channel_id=1, source_target_pairs={{0,1},{1,0},{2,3},{3,2},{4,5},{5,4},{6,7},{7,6},{8,9},{9,8},{10,11... | collective-permute-start | bytes 5971976 | tf_op jit(solution)/shard_map/ppermute | solution.py:75
  1216.3 62.3 %collective-permute-start.22 = (bf16[2,2,96,1152]{3,2,0,1:T(8,128)(2,1)}, bf16[2,2,96,1152]{3,2,0,1:T(8,128)(2,1)}, u32[]{:S(2)}, u32[]{:S(2)}) collective-permute-start(bf16[2,2,96,1152]{3,2,0,1:T(8,128)(2,1)} %fusion.67), channel_id=1, source_target_pairs={{0,4},{2,6},{4,0},{6,2},{8,12},{10,14},{12,8},{14,10},{16,20},{18,... | collective-permute-start | bytes 2654216 | tf_op jit(solution)/shard_map/ppermute | solution.py:75
  1226.4 53.7 %collective-permute-start.17 = (bf16[2,2,36,3072]{3,1,2,0:T(2,128)(2,1)}, bf16[2,2,36,3072]{3,1,2,0:T(2,128)(2,1)}, u32[]{:S(2)}, u32[]{:S(2)}) collective-permute-start(bf16[2,2,36,3072]{3,1,2,0:T(2,128)(2,1)} %bitcast.276), channel_id=1, source_target_pairs={{0,4},{2,6},{4,0},{6,2},{8,12},{10,14},{12,8},{14,10},{16,20},{18,... | collective-permute-start | bytes 2654216 | tf_op jit(solution)/shard_map/ppermute | solution.py:75
  1234.5 32.6 %copy-start.27 = (f32[2,2,2,1,36,3456]{5,3,4,2,1,0:T(1,128)S(1)}, f32[2,2,2,1,36,3456]{5,3,4,2,1,0:T(1,128)}, u32[]{:S(2)}) copy-start(f32[2,2,2,1,36,3456]{5,3,4,2,1,0:T(1,128)} %constant_dynamic-slice_fusion.20) | copy-start | bytes 11943940
  1237.0 50.4 %collective-permute-start.12 = (bf16[2,2,36,3072]{3,1,2,0:T(2,128)(2,1)}, bf16[2,2,36,3072]{3,1,2,0:T(2,128)(2,1)}, u32[]{:S(2)}, u32[]{:S(2)}) collective-permute-start(bf16[2,2,36,3072]{3,1,2,0:T(2,128)(2,1)} %bitcast.277), channel_id=1, source_target_pairs={{0,4},{2,6},{4,0},{6,2},{8,12},{10,14},{12,8},{14,10},{16,20},{18,... | collective-permute-start | bytes 2654216 | tf_op jit(solution)/shard_map/ppermute | solution.py:75
  1276.5 54.3 %collective-permute-start.2 = (bf16[2,2,36,3456]{3,1,2,0:T(2,128)(2,1)S(1)}, bf16[2,2,36,3456]{3,1,2,0:T(2,128)(2,1)S(1)}, u32[]{:S(2)}, u32[]{:S(2)}) collective-permute-start(bf16[2,2,36,3456]{3,1,2,0:T(2,128)(2,1)S(1)} %bitcast.343), channel_id=1, source_target_pairs={{0,4},{2,6},{4,0},{6,2},{8,12},{10,14},{12,8},{14,10},{16,20},{18,... | collective-permute-start | bytes 2985992 | tf_op jit(solution)/shard_map/ppermute | solution.py:75
  1280.1 13.2 collective-permute-start.23
  1284.4 24.1 %collective-permute-start.18 = (bf16[2,36,3072]{2,0,1:T(2,128)(2,1)S(1)}, bf16[2,36,3072]{2,0,1:T(2,128)(2,1)S(1)}, u32[]{:S(2)}, u32[]{:S(2)}) collective-permute-start(bf16[2,36,3072]{2,0,1:T(2,128)(2,1)S(1)} %bitcast.348), channel_id=1, source_target_pairs={{0,8},{2,10},{4,12},{6,14},{8,0},{10,2},{12,4},{14,6},{16,24},{18,... | collective-permute-start | bytes 1327112 | tf_op jit(solution)/shard_map/ppermute | solution.py:75
  1291.7 24.2 %collective-permute-start.13 = (bf16[2,36,3072]{2,0,1:T(2,128)(2,1)S(1)}, bf16[2,36,3072]{2,0,1:T(2,128)(2,1)S(1)}, u32[]{:S(2)}, u32[]{:S(2)}) collective-permute-start(bf16[2,36,3072]{2,0,1:T(2,128)(2,1)S(1)} %bitcast.349), channel_id=1, source_target_pairs={{0,8},{2,10},{4,12},{6,14},{8,0},{10,2},{12,4},{14,6},{16,24},{18,... | collective-permute-start | bytes 1327112 | tf_op jit(solution)/shard_map/ppermute | solution.py:75
  1293.4 41.9 %collective-permute-start.24 = (bf16[96,1152]{1,0:T(8,128)(2,1)S(1)}, bf16[96,1152]{1,0:T(8,128)(2,1)S(1)}, u32[]{:S(2)}, u32[]{:S(2)}) collective-permute-start(bf16[96,1152]{1,0:T(8,128)(2,1)S(1)} %fusion.70), channel_id=1, source_target_pairs={{0,16},{2,18},{4,20},{6,22},{8,24},{10,26},{12,28},{14,30},{16,0},... | collective-permute-start | bytes 663560 | tf_op jit(solution)/shard_map/ppermute | solution.py:75
  1310.0 16.8 %collective-permute-start.19 = (bf16[36,3072]{1,0:T(8,128)(2,1)S(1)}, bf16[36,3072]{1,0:T(8,128)(2,1)S(1)}, u32[]{:S(2)}, u32[]{:S(2)}) collective-permute-start(bf16[36,3072]{1,0:T(8,128)(2,1)S(1)} %bitcast.352), channel_id=1, source_target_pairs={{0,16},{2,18},{4,20},{6,22},{8,24},{10,26},{12,28},{14,30},{16,0},... | collective-permute-start | bytes 663560 | tf_op jit(solution)/shard_map/ppermute | solution.py:75
  1317.4 12.5 collective-permute-start.14
  1333.6 25.9 %copy-start.1 = (bf16[1152,1152]{1,0:T(8,128)(2,1)S(1)}, bf16[1152,1152]{1,0:T(8,128)(2,1)}, u32[]{:S(2)}) copy-start(bf16[1152,1152]{1,0:T(8,128)(2,1)} %param.21) | copy-start | bytes 7962628
  1333.7 11.3 collective-permute-start.3
  1346.2 12.5 collective-permute-start.4
  (97 other events, 708.1 us)

commit v2 on v0

v2 whole, which is shorter than its diff:
```python
import functools

import jax
import jax.numpy as jnp
import numpy as np
from jax import lax
from jax.experimental import pallas as pl
from jax.experimental.pallas import tpu as pltpu
from jax.sharding import PartitionSpec as P

HEADS = 16
HD = 72
GRID = 32
EPS = 1e-06
ROPE_BASE = 10000.0
TB = 256
WIN = 256
SCORE_SCALE = float(HD**-0.5)
SCORE_LOG2 = float(np.log2(np.e) * HD**-0.5)
VMEM = 60 * 2**20
f32 = jnp.float32
bf16 = jnp.bfloat16


def nn(a, b):
    return lax.dot_general(a, b, (((1,), (0,)), ((), ())), preferred_element_type=f32)


def nt(a, b):
    return lax.dot_general(a, b, (((1,), (1,)), ((), ())), preferred_element_type=f32)


def tn(a, b):
    return lax.dot_general(a, b, (((0,), (0,)), ((), ())), preferred_element_type=f32)


def split3(v):
    hi = v.astype(bf16).astype(f32)
    mid = (v - hi).astype(bf16).astype(f32)
    return hi, mid, v - hi - mid


def np_split3(v):
    v = v.astype(np.float32)
    hi = v.astype(jnp.bfloat16).astype(np.float32)
    mid = (v - hi).astype(jnp.bfloat16).astype(np.float32)
    return [part.astype(jnp.bfloat16) for part in (hi, mid, v - hi - mid)]


@functools.lru_cache(None)
def rope_tables(width):
    quarter = HD // 4
    freqs = ROPE_BASE ** (-np.arange(quarter, dtype=np.float64) / quarter)
    lane = np.arange(width) % HD
    group = lane // quarter
    angle = np.arange(GRID)[:, None] * freqs[lane % quarter][None, :]
    cosine, sine = np.cos(angle), np.sin(angle)
    sine = np.where((group % 2 == 0)[None, :], -sine, sine)
    uses_col = (group >= 2)[None, :]
    tables = []
    for table in (cosine, sine):
        whole = np.concatenate(
            [np.where(uses_col, 0.0, table), np.where(uses_col, table, 0.0)], axis=0
        )
        tables.append(np.concatenate(np_split3(whole), axis=0))
    return tables


@functools.lru_cache(None)
def head_tables(width):
    head = np.arange(width) // HD
    gather = np.zeros((width, 128), np.float32)
    for copy in range(3):
        gather[np.arange(width), copy * HEADS + head] = 1.0
    return gather.astype(jnp.bfloat16), gather.T.astype(jnp.bfloat16)


def unit_of(index, n_mod):
    mod = index % n_mod
    dp = index // n_mod
    return (dp % 2) * 2 * n_mod + mod * 2 + (dp // 2) % 2, dp // 4


@functools.lru_cache(None)
def unit_permutation(width, n_dp, n_mod):
    rows = width // (n_dp * n_mod)
    matrix = np.zeros((width, width), np.float32)
    for index in range(n_dp * n_mod):
        unit, rest = unit_of(index, n_mod)
        start = unit * (width // 8) + rest * rows
        matrix[start + np.arange(rows), index * rows + np.arange(rows)] = 1.0
    return matrix.astype(jnp.bfloat16)


def normed(v):
    centred = v - jnp.mean(v, axis=-1, keepdims=True)
    inverse = lax.rsqrt(jnp.mean(centred * centred, axis=-1, keepdims=True) + EPS)
    return centred * inverse, inverse


def norm_back(grad, scale_part, norm, inverse):
    e = grad * (1.0 + scale_part)
    return inverse * (
        e - jnp.mean(e, axis=-1, keepdims=True) - norm * jnp.mean(e * norm, axis=-1, keepdims=True)
    )


def part(mod_ref, slot, index, width):
    return mod_ref[pl.ds(slot, 1), index * width : (index + 1) * width]


def angles(coords_ref, cos_ref, sin_ref):
    value = lax.broadcasted_iota(jnp.int32, (GRID, 1), 0)
    hot = [(value == coords_ref[i : i + 1, :]).astype(f32) for i in range(2)]
    hot = jnp.concatenate(hot * 3, axis=0).astype(bf16)
    return tn(hot, cos_ref[...]), tn(hot, sin_ref[...])


def partner(v):
    width = v.shape[1]
    quarter = HD // 4
    lane = lax.broadcasted_iota(jnp.int32, (1, width), 1)
    leads = (lane // quarter) % 2 == 0
    return jnp.where(leads, pltpu.roll(v, width - quarter, 1), pltpu.roll(v, quarter, 1))


def head_sum(v, gather_ref):
    hi = v.astype(bf16)
    low = (v - hi.astype(f32)).astype(bf16)
    return nn(hi, gather_ref[...]) + nn(low, gather_ref[...])


def head_spread(v, spread_ref):
    hi, mid, low = split3(v)
    lane = lax.broadcasted_iota(jnp.int32, (1, 128), 1)
    chosen = jnp.where(lane < HEADS, hi, jnp.where(lane < 2 * HEADS, mid, low))
    return nn(chosen.astype(bf16), spread_ref[...])


def window(head, width):
    start = jnp.minimum((head * HD) // 128, width // 128 - WIN // 128) * 128
    return pl.multiple_of(start, 128), head * HD - start


def head_lanes(offset):
    lane = lax.broadcasted_iota(jnp.int32, (1, WIN), 1)
    return (lane >= offset) & (lane < offset + HD)


def project_kernel(
    slots, x_ref, mod_ref, w_ref, coords_ref, cos_ref, sin_ref, gain_ref, gather_ref, spread_ref,
    perm_ref, units_ref, raw_ref, inv_ref, q_ref, k_ref, v_ref, kt_ref,
):
    width = x_ref.shape[1]
    slot = slots[pl.program_id(0)]
    norm, _ = normed(x_ref[...].astype(f32))
    low = (norm * (1.0 + part(mod_ref, slot, 1, width)) + part(mod_ref, slot, 0, width)).astype(bf16)
    units_ref[...] = nt(perm_ref[...], low).astype(bf16).reshape(units_ref.shape)
    cosine, sine = angles(coords_ref, cos_ref, sin_ref)
    for index, out_ref in enumerate((q_ref, k_ref)):
        raw = nn(low, w_ref[:, index * width : (index + 1) * width])
        raw_ref[:, index * width : (index + 1) * width] = raw
        inverse = lax.rsqrt(head_sum(raw * raw, gather_ref) * (1.0 / HD) + EPS)
        inv_ref[:, index * 128 : (index + 1) * 128] = inverse
        scaled = raw * head_spread(inverse, spread_ref) * gain_ref[index : index + 1, :]
        turned = scaled * cosine + partner(scaled) * sine
        out_ref[...] = turned.astype(bf16)
        if index == 1:
            kt_ref[...] = turned.T.astype(bf16)
    v_ref[...] = nn(low, w_ref[:, 2 * width :]).astype(bf16)


def attend_kernel(
    slots, x_ref, cot_ref, mod_ref, q_ref, k_ref, v_ref, w_out_ref, perm_ref,
    o_ref, lse_ref, attn_ref, mid_ref, low_ref, gf_ref, att_units_ref, ffn_units_ref, lse_acc,
):
    block = pl.program_id(0)
    width = x_ref.shape[1]
    tokens = k_ref.shape[0]
    lane128 = lax.broadcasted_iota(jnp.int32, (1, 128), 1)
    lane = lax.broadcasted_iota(jnp.int32, (1, WIN), 1)
    o_ref[...] = jnp.zeros_like(o_ref)
    lse_acc[...] = jnp.zeros_like(lse_acc)

    def run(rows):
        def head(h, carry):
            start, offset = window(h, width)
            inside = head_lanes(offset)
            columns = pl.ds(start, WIN)
            query = jnp.where(inside, q_ref[:, columns], 0)
            value = jnp.where(inside, v_ref[rows, columns], 1)
            weight = jnp.exp2(nt(query, k_ref[rows, columns]) * SCORE_LOG2).astype(bf16)
            summed = nn(weight, value)
            free = jnp.where(offset > 0, 0, WIN - 1)
            total = jnp.sum(jnp.where(lane == free, summed, 0.0), axis=1, keepdims=True)
            o_ref[:, columns] += jnp.where(inside, summed * (1.0 / total), 0.0)
            lse_acc[...] += jnp.where(lane128 == h, jnp.log2(total), 0.0)
            return carry

        lax.fori_loop(0, HEADS, head, 0, unroll=2)

    whole = slots[tokens // TB - 1] == slots[0]

    @pl.when(whole)
    def _():
        run(slice(None))

    @pl.when(jnp.logical_not(whole))
    def _():
        run(pl.ds(pl.multiple_of(block * TB, TB), TB))

    lse_ref[...] = lse_acc[...].T
    slot = slots[block]
    attended = o_ref[...].astype(bf16)
    att_units_ref[...] = nt(perm_ref[...], attended).astype(bf16).reshape(att_units_ref.shape)
    attn = nn(attended, w_out_ref[...])
    attn_ref[...] = attn
    mid = x_ref[...].astype(f32) + part(mod_ref, slot, 2, width) * attn
    mid_ref[...] = mid
    norm, _ = normed(mid)
    low = (norm * (1.0 + part(mod_ref, slot, 4, width)) + part(mod_ref, slot, 3, width)).astype(bf16)
    low_ref[...] = low
    ffn_units_ref[...] = nt(perm_ref[...], low).astype(bf16).reshape(ffn_units_ref.shape)
    gf_ref[...] = (cot_ref[...].astype(f32) * part(mod_ref, slot, 5, width)).astype(bf16)


def ffn_kernel(
    x_ref, gf_ref, wg_ref, wu_ref, wd_ref, units_ref, dg_ref, du_ref, ffn_ref, dmod_ref, *, n_mod
):
    first = pl.program_id(0) == 0
    gate = nn(x_ref[...], wg_ref[...])
    up = nn(x_ref[...], wu_ref[...])
    grad_hidden = nt(gf_ref[...], wd_ref[...])
    sigmoid = 1.0 / (1.0 + jnp.exp(-gate))
    silu = gate * sigmoid
    hidden = silu * up
    rows = units_ref.shape[3]
    turned = hidden.T.astype(bf16)
    for index in range(turned.shape[0] // rows):
        unit, rest = unit_of(index, n_mod)
        nxt = unit % 2 if units_ref.shape[1] == 2 else 0
        units_ref[unit // 2, nxt, rest if units_ref.shape[1] == 2 else 0] = turned[
            index * rows : (index + 1) * rows
        ]
    dg = (grad_hidden * up * (sigmoid * (1.0 + gate * (1.0 - sigmoid)))).astype(bf16)
    du = (grad_hidden * silu).astype(bf16)
    dg_ref[...] = dg
    du_ref[...] = du

    @pl.when(first)
    def _():
        ffn_ref[...] = jnp.zeros_like(ffn_ref)
        dmod_ref[...] = jnp.zeros_like(dmod_ref)

    ffn_ref[...] += nn(hidden.astype(bf16), wd_ref[...])
    dmod_ref[...] += nt(dg, wg_ref[...]) + nt(du, wu_ref[...])


def middle_kernel(
    slots, mid_ref, ffn_ref, dmod_ref, cot_ref, attn_ref, o_ref, mod_ref, w_out_ref, gather_ref,
    out_ref, grad_mid_ref, ga_ref, do_ref, dot_ref, sums_ref,
):
    width = mid_ref.shape[1]
    slot = slots[pl.program_id(0)]
    incoming = cot_ref[...].astype(f32)
    mid = mid_ref[...]
    out_ref[...] = (mid + part(mod_ref, slot, 5, width) * ffn_ref[...]).astype(bf16)
    norm, inverse = normed(mid)
    dmod = dmod_ref[...]
    grad_mid = incoming + norm_back(dmod, part(mod_ref, slot, 4, width), norm, inverse)
    grad_mid_ref[...] = grad_mid
    ga = (grad_mid * part(mod_ref, slot, 2, width)).astype(bf16)
    ga_ref[...] = ga
    do = nt(ga, w_out_ref[...]).astype(bf16)
    do_ref[...] = do
    dot_ref[...] = head_sum(do.astype(f32) * o_ref[...], gather_ref).T
    sums_ref[0, 0:1, :] = jnp.sum(grad_mid * attn_ref[...], axis=0, keepdims=True)
    sums_ref[0, 1:2, :] = jnp.sum(dmod, axis=0, keepdims=True)
    sums_ref[0, 2:3, :] = jnp.sum(dmod * norm, axis=0, keepdims=True)
    sums_ref[0, 3:4, :] = jnp.sum(incoming * ffn_ref[...], axis=0, keepdims=True)


def attend_back_kernel(
    slots, q_ref, k_ref, v_ref, do_ref, lse_ref, dot_ref, kt_ref, dqt_ref, dk_ref, dv_ref
):
    h = pl.program_id(0)
    tokens, width = q_ref.shape

    @pl.when(h == 0)
    def _():
        dqt_ref[...] = jnp.zeros_like(dqt_ref)
        dk_ref[...] = jnp.zeros_like(dk_ref)
        dv_ref[...] = jnp.zeros_like(dv_ref)

    start, offset = window(h, width)
    inside = head_lanes(offset)
    columns = pl.ds(start, WIN)
    first_row = pl.multiple_of((h * HD) // 16 * 16, 16)
    row = lax.broadcasted_iota(jnp.int32, (HD + 8, 1), 0) + first_row
    own_rows = (row >= h * HD) & (row < h * HD + HD)

    def step(rows):
        query = q_ref[rows, columns]
        grad_out = do_ref[rows, columns]
        key = jnp.where(inside, k_ref[rows, columns], 0)
        value = jnp.where(inside, v_ref[rows, columns], 0)
        probs = jnp.exp2(nt(key, query) * SCORE_LOG2 - lse_ref[pl.ds(h, 1), rows])
        scores = (probs * (nt(value, grad_out) - dot_ref[pl.ds(h, 1), rows])).astype(bf16)
        dv_ref[rows, columns] += jnp.where(inside, nn(probs.astype(bf16), grad_out), 0.0)
        dk_ref[rows, columns] += jnp.where(inside, nn(scores, query) * SCORE_SCALE, 0.0)
        turned = nn(kt_ref[pl.ds(first_row, HD + 8), rows], scores) * SCORE_SCALE
        dqt_ref[pl.ds(first_row, HD + 8), rows] += jnp.where(own_rows, turned, 0.0)

    whole = slots[tokens // TB - 1] == slots[0]

    @pl.when(whole)
    def _():
        step(slice(None))

    @pl.when(jnp.logical_not(whole))
    def _():
        def block(i, carry):
            step(pl.ds(pl.multiple_of(i * TB, TB), TB))
            return carry

        lax.fori_loop(0, tokens // TB, block, 0)


def project_back_kernel(
    slots, dqt_ref, dk_ref, dv_ref, raw_ref, inv_ref, q_ref, k_ref, x_ref, grad_mid_ref, mod_ref,
    w_ref, coords_ref, cos_ref, sin_ref, gain_ref, gather_ref, spread_ref,
    gp_ref, grad_x_ref, sums_ref, gains_ref,
):
    width = x_ref.shape[1]
    slot = slots[pl.program_id(0)]

    @pl.when(pl.program_id(0) == 0)
    def _():
        gains_ref[...] = jnp.zeros_like(gains_ref)

    cosine, sine = angles(coords_ref, cos_ref, sin_ref)
    for index, low_ref in enumerate((q_ref, k_ref)):
        grad = dqt_ref[...].T if index == 0 else dk_ref[...]
        raw = raw_ref[:, index * width : (index + 1) * width]
        inverse = head_spread(inv_ref[:, index * 128 : (index + 1) * 128], spread_ref)
        mean = head_sum(grad * low_ref[...].astype(f32), gather_ref) * (1.0 / HD)
        norm = raw * inverse
        back = grad * cosine - partner(grad) * sine
        gains_ref[index : index + 1, :] += jnp.sum(back * norm, axis=0, keepdims=True)
        gp_ref[:, index * width : (index + 1) * width] = (
            inverse * (back * gain_ref[index : index + 1, :] - norm * head_spread(mean, spread_ref))
        ).astype(bf16)
    gp_ref[:, 2 * width :] = dv_ref[...].astype(bf16)
    dmod = nt(gp_ref[...], w_ref[...])
    norm, inverse = normed(x_ref[...].astype(f32))
    grad_x = grad_mid_ref[...] + norm_back(dmod, part(mod_ref, slot, 1, width), norm, inverse)
    grad_x_ref[...] = grad_x.astype(bf16)
    sums_ref[0, 0:1, :] = jnp.sum(dmod, axis=0, keepdims=True)
    sums_ref[0, 1:2, :] = jnp.sum(dmod * norm, axis=0, keepdims=True)


def send_kernel(where, units_ref, rhs_ref, out_ref):
    units, rows, _ = units_ref.shape
    result = nn(units_ref[...].reshape(units * rows, -1), rhs_ref[...])
    out_ref[...] = result.astype(bf16).reshape(out_ref.shape)


def keep_kernel(where, units_ref, rhs_ref, got_ref, send_ref, keep_ref, scratch):
    units, rows, _ = units_ref.shape
    result = nn(units_ref[...].reshape(units * rows, -1), rhs_ref[...])
    scratch[...] = result.reshape(scratch.shape)
    for i in range(units // 2):
        away, own = where[2 + i], where[4 + i]
        send_ref[i] = (scratch[away] + got_ref[away].astype(f32)).astype(bf16)
        keep_ref[i] = scratch[own] + got_ref[own].astype(f32)


def fold_kernel(where, keep_ref, got_ref, send_ref, own_ref):
    away, own = where[0], where[1]
    send_ref[...] = (keep_ref[away] + got_ref[away].astype(f32)).astype(bf16)
    own_ref[...] = keep_ref[own] + got_ref[own].astype(f32)


def call(kernel, grid, in_specs, out_specs, out_shape, args, scalars=None, scratch=(), cost=None, name=None):
    cost = cost or (0, 0)
    spec = pltpu.PrefetchScalarGridSpec(
        num_scalar_prefetch=0 if scalars is None else 1,
        grid=grid,
        in_specs=in_specs,
        out_specs=out_specs,
        scratch_shapes=scratch,
    )
    return pl.pallas_call(
        kernel,
        grid_spec=spec,
        out_shape=out_shape,
        compiler_params=pltpu.CompilerParams(vmem_limit_bytes=VMEM),
        cost_estimate=pl.CostEstimate(flops=int(cost[0]), bytes_accessed=int(cost[1]), transcendentals=0),
        name=name,
    )(*(() if scalars is None else (scalars,)), *args)


def shape(dims, dtype):
    return jax.ShapeDtypeStruct(dims, dtype)


def fixed(dims):
    return pl.BlockSpec(dims, lambda *_: (0,) * len(dims), pipeline_mode=pl.Buffered(1))


def rows_of(dims, axis=0):
    return pl.BlockSpec(dims, lambda b, *_: tuple(b if i == axis else 0 for i in range(len(dims))))


class Reducer:
    def __init__(self, n_dp, n_mod):
        self.n_dp, self.n_mod = n_dp, n_mod
        position = lax.axis_index("dp")
        self.core = position & 1
        self.nxt = lax.shift_right_logical(position, 1) & 1
        self.mod = lax.axis_index("mod")
        self.position = position

    def swap(self, arr, bit):
        if bit == "mod":
            return lax.ppermute(arr, "mod", [(i, i ^ 1) for i in range(self.n_mod)])
        return lax.ppermute(arr, "dp", [(i, i ^ (1 << bit)) for i in range(self.n_dp)])

    def start(self, units, rhs, name):
        _, rows, tokens = units.shape
        columns = rhs.shape[1]
        chunk = 384
        half = pl.BlockSpec((4, rows, tokens), lambda j, w: (w[0], 0, 0), pipeline_mode=pl.Buffered(1))
        sent = call(
            send_kernel,
            (columns // chunk,),
            [half, rows_of((tokens, chunk), 1)],
            rows_of((4, rows, chunk), 2),
            shape((4, rows, columns), bf16),
            (units, rhs),
            scalars=jnp.stack([1 - self.core]),
            cost=(8 * rows * tokens * columns, 2 * tokens * (columns + 4 * rows) + 8 * rows * columns),
            name=name + "_send",
        )
        return self.swap(sent, 0)

    def finish(self, units, rhs, got, mod_first, name):
        _, rows, tokens = units.shape
        columns = rhs.shape[1]
        chunk = 384
        if mod_first:
            where = [2 * (1 - self.mod), 2 * (1 - self.mod) + 1, 2 * self.mod, 2 * self.mod + 1]
            second, third, third_bit = "mod", 1, self.nxt
        else:
            where = [1 - self.nxt, 3 - self.nxt, self.nxt, 2 + self.nxt]
            second, third, third_bit = 1, "mod", self.mod
        half = pl.BlockSpec((4, rows, tokens), lambda j, w: (w[0], 0, 0), pipeline_mode=pl.Buffered(1))
        sent, kept = call(
            keep_kernel,
            (columns // chunk,),
            [half, rows_of((tokens, chunk), 1), rows_of((4, rows, chunk), 2)],
            [rows_of((2, rows, chunk), 2), rows_of((2, rows, chunk), 2)],
            [shape((2, rows, columns), bf16), shape((2, rows, columns), f32)],
            (units, rhs, got),
            scalars=jnp.stack([self.core, self.core] + where),
            scratch=[pltpu.VMEM((4, rows, chunk), f32)],
            cost=(8 * rows * tokens * columns, 2 * tokens * (columns + 4 * rows) + 20 * rows * columns),
            name=name + "_keep",
        )
        got = self.swap(sent, second)
        sent, kept = call(
            fold_kernel,
            (columns // chunk,),
            [rows_of((2, rows, chunk), 2), rows_of((2, rows, chunk), 2)],
            [rows_of((rows, chunk), 1), rows_of((rows, chunk), 1)],
            [shape((rows, columns), bf16), shape((rows, columns), f32)],
            (kept, got),
            scalars=jnp.stack([1 - third_bit, third_bit]),
            cost=(0, 18 * rows * columns),
            name=name + "_fold",
        )
        total = kept + self.swap(sent, third).astype(f32)
        bits = self.n_dp.bit_length() - 1
        total = total.reshape((2,) * (bits - 2) + (rows * 4 // self.n_dp, columns))
        for bit in range(2, bits):
            axis = bits - 1 - bit
            mine = lax.shift_right_logical(self.position, bit) & 1
            away = lax.dynamic_index_in_dim(total, 1 - mine, axis=axis, keepdims=False)
            own = lax.dynamic_index_in_dim(total, mine, axis=axis, keepdims=False)
            total = own + self.swap(away.astype(bf16), bit).astype(f32)
        return total


def silu_grad(v):
    sigmoid = jax.nn.sigmoid(v)
    return sigmoid * (1.0 + v * (1.0 - sigmoid))


def pair_order(own, other, mod):
    return jnp.where(mod == 0, jnp.stack([own, other]), jnp.stack([other, own]))


def body(
    n_dp, n_mod, tokens, cond, segments, coords, w_ada, w_qkv, q_gain, k_gain, w_out, w_gate, w_up,
    w_down, cotangent,
):
    _, count, width = tokens.shape
    slots_n = cond.shape[1]
    half = w_ada.shape[1]
    ff = w_gate.shape[1]
    blocks = count // TB
    n_dev = n_dp * n_mod
    reducer = Reducer(n_dp, n_mod)
    mod_index = lax.axis_index("mod")
    x = tokens[0]
    cot = cotangent[0]
    slots = segments[0, ::TB]
    coord = coords[0]
    cos_table, sin_table = (jnp.asarray(t) for t in rope_tables(width))
    gather, spread = (jnp.asarray(t) for t in head_tables(width))
    perm = jnp.asarray(unit_permutation(width, n_dp, n_mod))
    gains = jnp.stack([jnp.tile(q_gain, HEADS), jnp.tile(k_gain, HEADS)])

    cond_both = pair_order(cond[0], reducer.swap(cond[0], "mod"), mod_index)
    activated = jax.nn.silu(cond_both).astype(bf16).reshape(-1, width)
    mod_half = jnp.dot(activated, w_ada, preferred_element_type=f32).astype(bf16)
    mod_half = mod_half.reshape(n_mod, slots_n, half)
    own_half = lax.dynamic_index_in_dim(mod_half, mod_index, 0, keepdims=False)
    other_half = lax.dynamic_index_in_dim(mod_half, 1 - mod_index, 0, keepdims=False)
    pair = pair_order(own_half, reducer.swap(other_half, "mod"), mod_index)
    modulation = jnp.concatenate([pair[0], pair[1]], axis=1).astype(f32)

    token_f32 = shape((count, width), f32)
    token_bf16 = shape((count, width), bf16)
    units = shape((8, width // 8, count), bf16)
    units_spec = rows_of((8, width // 8, TB), 2)
    token_spec = rows_of((TB, width))
    mod_spec = fixed((slots_n, 6 * width))
    square = fixed((width, width))
    table_specs = [fixed(cos_table.shape), fixed(sin_table.shape), fixed((2, width)), fixed(gather.shape), fixed(spread.shape)]
    tables = (cos_table, sin_table, gains, gather, spread)
    lane_rows = shape((128, count), f32)
    macs = count * width * width

    attn_units, raw, inverse, query, key, value, key_t = call(
        project_kernel,
        (blocks,),
        [token_spec, mod_spec, fixed((width, 3 * width)), rows_of((2, TB), 1)] + table_specs + [square],
        [units_spec, rows_of((TB, 2 * width)), rows_of((TB, 256))] + [token_spec] * 3 + [rows_of((width, TB), 1)],
        [units, shape((count, 2 * width), f32), shape((count, 256), f32)] + [token_bf16] * 3
        + [shape((width, count), bf16)],
        (x, modulation, w_qkv, coord) + tables + (perm,),
        scalars=slots,
        cost=(2 * 5 * macs, 40e6),
        name="project",
    )
    attended, lse, attn, mid, ffn_in, grad_ffn, out_units, ffn_units = call(
        attend_kernel,
        (blocks,),
        [token_spec, token_spec, mod_spec, token_spec] + [fixed((count, width))] * 2 + [square, square],
        [token_spec, rows_of((128, TB), 1)] + [token_spec] * 4 + [units_spec] * 2,
        [token_f32, lane_rows, token_f32, token_f32, token_bf16, token_bf16, units, units],
        (x, cot, modulation, query, key, value, w_out, perm),
        scalars=slots,
        scratch=[pltpu.VMEM((TB, 128), f32)],
        cost=(2 * 10 * macs, 40e6),
        name="attend",
    )

    rows_ff = ff // n_dev
    rest = n_dp // 4
    chunk = 384
    group = chunk // rows_ff
    if group >= 8:
        unit_block = pl.BlockSpec((4, 2, group // 8, rows_ff, count), lambda i: (0, 0, i, 0, 0))
    else:
        unit_block = pl.BlockSpec((4, 1, 1, rows_ff, count), lambda i: (0, i % 2, i // 2, 0, 0))
    down_units, grad_gate, grad_up, ffn, grad_mod_ffn = call(
        functools.partial(ffn_kernel, n_mod=n_mod),
        (ff // chunk,),
        [fixed((count, width))] * 2 + [rows_of((width, chunk), 1)] * 2 + [rows_of((chunk, width))],
        [unit_block] + [rows_of((count, chunk), 1)] * 2 + [fixed((count, width))] * 2,
        [shape((4, 2, rest, rows_ff, count), bf16)] + [shape((count, ff), bf16)] * 2 + [token_f32] * 2,
        (ffn_in, grad_ffn, w_gate, w_up, w_down),
        cost=(2 * 6 * count * width * ff, 60e6),
        name="ffn",
    )
    down_units = down_units.reshape(8, rest * rows_ff, count)

    got_gate = reducer.start(ffn_units, grad_gate, "gate")
    got_up = reducer.start(ffn_units, grad_up, "up")
    got_down = reducer.start(down_units, grad_ffn, "down")
    summed_gate = reducer.finish(ffn_units, grad_gate, got_gate, True, "gate")
    summed_up = reducer.finish(ffn_units, grad_up, got_up, False, "up")
    summed_down = reducer.finish(down_units, grad_ffn, got_down, True, "down")

    output, grad_mid, grad_attn, grad_attended, dot_term, sums_b = call(
        middle_kernel,
        (blocks,),
        [token_spec] * 6 + [mod_spec, square, fixed(gather.shape)],
        [token_spec] * 4 + [rows_of((128, TB), 1), rows_of((1, 4, width))],
        [token_bf16, token_f32, token_bf16, token_bf16, lane_rows, shape((blocks, 4, width), f32)],
        (mid, ffn, grad_mod_ffn, cot, attn, attended, modulation, w_out, gather),
        scalars=slots,
        cost=(2 * macs, 40e6),
        name="middle",
    )
    got_out = reducer.start(out_units, grad_attn, "out")
    summed_out = reducer.finish(out_units, grad_attn, got_out, False, "out")

    grad_query_t, grad_key, grad_value = call(
        attend_back_kernel,
        (HEADS,),
        [fixed((count, width))] * 4 + [fixed((128, count))] * 2 + [fixed((width, count))],
        [fixed((width, count))] + [fixed((count, width))] * 2,
        [shape((width, count), f32), token_f32, token_f32],
        (query, key, value, grad_attended, lse, dot_term, key_t),
        scalars=slots,
        cost=(2 * 22 * macs, 40e6),
        name="attend_back",
    )
    grad_projected, grad_tokens, sums_a, gain_sums = call(
        project_back_kernel,
        (blocks,),
        [rows_of((width, TB), 1), token_spec, token_spec, rows_of((TB, 2 * width)), rows_of((TB, 256))]
        + [token_spec] * 4
        + [mod_spec, fixed((width, 3 * width)), rows_of((2, TB), 1)]
        + table_specs,
        [rows_of((TB, 3 * width)), token_spec, rows_of((1, 2, width)), fixed((2, width))],
        [shape((count, 3 * width), bf16), token_bf16, shape((blocks, 2, width), f32), shape((2, width), f32)],
        (grad_query_t, grad_key, grad_value, raw, inverse, query, key, x, grad_mid, modulation, w_qkv, coord)
        + tables,
        scalars=slots,
        cost=(2 * 4 * macs, 50e6),
        name="project_back",
    )
    got_qkv = reducer.start(attn_units, grad_projected, "qkv")
    summed_qkv = reducer.finish(attn_units, grad_projected, got_qkv, True, "qkv")

    sums = jnp.concatenate([sums_a, sums_b], axis=1).reshape(blocks, 6 * width)
    in_slot = slots[None, :, None] == jnp.arange(slots_n)[:, None, None]
    grad_modulation = jnp.sum(jnp.where(in_slot, sums[None], 0.0), axis=1).astype(bf16)
    halves = grad_modulation.reshape(slots_n, n_mod, half)
    own_half = lax.dynamic_index_in_dim(halves, mod_index, 1, keepdims=False)
    other_half = lax.dynamic_index_in_dim(halves, 1 - mod_index, 1, keepdims=False)
    grad_mod_flat = pair_order(own_half, reducer.swap(other_half, "mod"), mod_index).reshape(-1, half)
    all_activated = lax.all_gather(activated, "dp", axis=0, tiled=True)
    rows_ada = width // n_dp
    own_activated = lax.dynamic_slice_in_dim(
        all_activated, lax.axis_index("dp") * rows_ada, rows_ada, axis=1
    )
    all_grad_mod = lax.all_gather(grad_mod_flat, "dp", axis=0, tiled=True)
    grad_w_ada = jnp.einsum("nd,nc->dc", own_activated, all_grad_mod, preferred_element_type=f32)
    grad_activated = jnp.einsum("nc,dc->nd", grad_mod_flat, w_ada, preferred_element_type=f32)
    grad_activated = grad_activated.reshape(n_mod, slots_n, width)
    own_part = lax.dynamic_index_in_dim(grad_activated, mod_index, 0, keepdims=False)
    other_part = lax.dynamic_index_in_dim(grad_activated, 1 - mod_index, 0, keepdims=False)
    grad_own = own_part + reducer.swap(other_part.astype(bf16), "mod").astype(f32)
    grad_cond = grad_own[None] * silu_grad(cond)

    gain_grads = jnp.sum(gain_sums.reshape(2, HEADS, HD), axis=1)
    for bit in [0, "mod"] + list(range(1, n_dp.bit_length() - 1)):
        gain_grads = gain_grads + reducer.swap(gain_grads, bit)
    return (
        output[None],
        grad_tokens[None],
        grad_cond,
        grad_w_ada,
        summed_qkv,
        gain_grads[0],
        gain_grads[1],
        summed_out,
        summed_gate,
        summed_up,
        summed_down,
    )


def solution(mesh):
    rows = ("dp", "mod")
    in_specs = (
        P(rows, None, None),
        P(rows, None, None),
        P(rows, None),
        P(rows, None, None),
        P(None, "mod"),
        P(),
        P(),
        P(),
        P(),
        P(),
        P(),
        P(),
        P(rows, None, None),
    )
    out_specs = (
        P(rows, None, None),
        P(rows, None, None),
        P(rows, None, None),
        P("dp", "mod"),
        P(rows, None),
        P(),
        P(),
        P(rows, None),
        P(rows, None),
        P(rows, None),
        P(rows, None),
    )
    return jax.shard_map(
        functools.partial(body, mesh.shape["dp"], mesh.shape["mod"]),
        mesh=mesh,
        in_specs=in_specs,
        out_specs=out_specs,
        check_vma=False,
    )
```

time: 2430 us -> 688 us (0.28); the launches traced: 2380 us -> 677 us
  blocking collectives: 1310 us -> 46 us
  matrix products: 449 us -> 12.1 us
  Pallas kernels: 0 us -> 405 us
  other arithmetic: 245 us -> 18.1 us
  local copies, waits for them, and re-layouts: 245 us -> 19.9 us
  waiting for transfers between devices: 16.5 us -> 151 us
  starting transfers between devices: 106 us -> 22.7 us
    unnamed x3 -> x0, blocking collectives: 1250 us -> none
    dot_general x32 -> x3, matrix products: 449 us -> 12.1 us  [the longest x1 5.47 us: body(): jnp.einsum('nc,dc->nd', grad_mod_flat, w_ada, preferred_element_type=f32)]
    pallas_call x0 -> x21, Pallas kernels: none -> 405 us  [call(): pl.pallas_call(kernel, grid_spec=spec, out_shape=out_shape, compiler_para...]
    ppermute x0 -> x34, waiting for transfers between devices: none -> 151 us  [the longest x24 75.6 us: swap(): lax.ppermute(arr, 'dp', [(i, i ^ 1 << bit) for i in range(self.n_dp)])]
    unnamed x25 -> x0, starting transfers between devices: 102 us -> none
    unnamed x233 -> x36, local copies, waits for them, and re-layouts: 103 us -> 3.22 us
    reduce_sum x13 -> x2, other arithmetic: 79.4 us -> 0.37 us  [the longest x1 0.35 us: body(): jnp.sum(jnp.where(in_slot, sums[None], 0.0), axis=1).astype(bf16)]
    convert_element_type x5 -> x2, other arithmetic: 68.9 us -> 0.69 us  [the longest x1 0.67 us: body(): modulation = jnp.concatenate([pair[0], pair[1]], axis=1).astype(f32)]
  transfers between devices with their start and end apart: 27 -> 34, of which waited for: 2 -> 12; matrix products, arithmetic and copies ran while one was open for 70% -> 6% of each run, Pallas kernels for 0% -> 34%
where the time goes in v2:
time: 688 us; the launch traced here: 677 us
  Pallas kernels  405 us (59%)
  waiting for transfers between devices  151 us (22%)
  blocking collectives  46 us (7%)
  starting transfers between devices  22.7 us (3%)
  local copies, waits for them, and re-layouts  19.9 us (3%)
  other arithmetic  18.1 us (3%)
  matrix products  12.1 us (2%)
    pallas_call x21, Pallas kernels, call(): pl.pallas_call(kernel, grid_spec=spec, out_shape=out_shape, compiler_para...  405 us
    ppermute x24, waiting for transfers between devices, swap(): lax.ppermute(arr, 'dp', [(i, i ^ 1 << bit) for i in range(self.n_dp)])  75.6 us
    ppermute x10, waiting for transfers between devices, swap(): return lax.ppermute(arr, 'mod', [(i, i ^ 1) for i in range(self.n_mod)])  75.2 us
    all_gather x1, blocking collectives, body(): all_activated = lax.all_gather(activated, 'dp', axis=0, tiled=True)  24.4 us
    all_gather x1, blocking collectives, body(): all_grad_mod = lax.all_gather(grad_mod_flat, 'dp', axis=0, tiled=True)  21.6 us
  transfers between devices with their start and end apart: 34, of which 12 were waited for; matrix products, arithmetic and copies ran while one was open for 6% of the time, Pallas kernels for 34%

profile of v2, /device:TPU:0, one launch (start us, length us, event | category | flops | bytes accessed | tf_op | source)
XLA Modules:
  0.0 676.5 jit_solution(2561763988176367434)
XLA Ops:
  0.6 3.0 collective-permute-start
  10.4 4.4 convolution_convert_fusion
  14.9 24.4 %all_gather.6 = bf16[128,1152]{1,0:T(8,128)(2,1)} all-gather(bf16[8,1152]{1,0:T(8,128)(2,1)S(1)} %multiply_convert_fusion), channel_id=1, replica_groups=mesh['dp'=16,'mod'=2] {'dp'}, dimensions={0}, use_global_device_ids=true | all-gather | bytes 313344 | tf_op jit(solution)/shard_map/all_gather | solution.py:647
  40.1 29.1 %project.1 = (bf16[8,144,1024]{2,1,0:T(8,128)(2,1)}, f32[1024,2304]{1,0:T(8,128)}, f32[1024,256]{1,0:T(8,128)}, bf16[1024,1152]{1,0:T(8,128)(2,1)}, bf16[1024,11...) custom-call(s32[4]{0:T(128)} %bitcast.120, bf16[1024,1152]{1,0:T(8,128)(2,1)} %bitcast.105, ...), custom_call_target="tpu_custom_call" | custom-call | flops 13589544960 | bytes 40000000 | tf_op jit(solution)/shard_map/project/pallas_call | solution.py:393
  69.1 57.6 %attend.1 = (f32[1024,1152]{1,0:T(8,128)}, f32[128,1024]{1,0:T(8,128)}, f32[1024,1152]{1,0:T(8,128)}, f32[1024,1152]{1,0:T(8,128)}, bf16[1024,1152]{1,0:T(8,128)...) custom-call(s32[4]{0:T(128)} %bitcast.121, ...), custom_call_target="tpu_custom_call" | custom-call | flops 27179089920 | bytes 40000000 | tf_op jit(solution)/shard_map/attend/pallas_call | solution.py:393
  126.7 77.4 %ffn.1 = (bf16[4,2,4,96,1024]{4,3,2,1,0:T(8,128)(2,1)}, bf16[1024,3072]{1,0:T(8,128)(2,1)}, bf16[1024,3072]{1,0:T(8,128)(2,1)}, f32[1024,1152]{1,0:T(8,128)}, f32[1024,1152]{1,0:T(8,128)}) custom-call(bf16[1024,1152]{1,0:T(8,128)(2,1)} %get-tuple-element.68.x_ref, bf16[1024,1152]{1,0:T(8,128)(2,1)} %get-tuple-element.69.gf_ref.rhs_ref, ...), custom_call_target="tpu_custom_call" | custom-call | flops 43486543872 | bytes 60000000 | tf_op jit(solution)/shard_map/ffn/pallas_call | solution.py:393
  204.1 8.7 %down_send.1 = bf16[4,384,1152]{2,1,0:T(8,128)(2,1)} custom-call(s32[1]{0:T(128)} %bitcast.28.where, bf16[8,384,1024]{2,1,0:T(8,128)(2,1)} %bitcast.127, bf16[1024,1152]{1,0:T(8,128)(2,1)} %get-tuple-element.69.gf_ref.rhs_ref), custom_call_target="tpu_custom_call" | custom-call | flops 3623878656 | bytes 9043968 | tf_op jit(solution)/shard_map/down_send/pallas_call | solution.py:393
  213.1 10.3 %up_send.1 = bf16[4,144,3072]{2,1,0:T(8,128)(2,1)} custom-call(s32[1]{0:T(128)} %bitcast.28.where, bf16[8,144,1024]{2,1,0:T(8,128)(2,1)} %get-tuple-element.101.units_ref, bf16[1024,3072]{1,0:T(8,128)(2,1)} %get-tuple-element.107.rhs_ref), custom_call_target="tpu_custom_call" | custom-call | flops 3623878656 | bytes 11010048 | tf_op jit(solution)/shard_map/up_send/pallas_call | solution.py:393
  223.6 18.1 %middle.1 = (bf16[1024,1152]{1,0:T(8,128)(2,1)}, f32[1024,1152]{1,0:T(8,128)}, bf16[1024,1152]{1,0:T(8,128)(2,1)}, bf16[1024,1152]{1,0:T(8,128)(2,1)}, f32[128,1024]{1,0:T(8,128)}, /*index=5*/f32[4,4,1152]{2,1,0:T(4,128)}) custom-call(s32[4]{0:T(128)} %bitcast.122, f32[1024,1152]{1,0:T(8,128)} %get-tuple-element.67.mid_ref, ...), custom_call_target="tpu_custom_call" | custom-call | flops 2717908992 | bytes 40000000 | tf_op jit(solution)/shard_map/middle/pallas_call | solution.py:393
  241.8 5.2 out_send.1
  247.3 56.7 %attend_back.1 = (f32[1152,1024]{1,0:T(8,128)}, f32[1024,1152]{1,0:T(8,128)}, f32[1024,1152]{1,0:T(8,128)}) custom-call(s32[4]{0:T(128)} %bitcast.123, bf16[1024,1152]{1,0:T(8,128)(2,1)} %get-tuple-element.64.q_ref, bf16[1024,1152]{1,0:T(8,128)(2,1)} %get-tuple-element.65.k_ref, bf16[1024,1152]{1,0:T(8,128)(2,1)} %get-tuple-element.66.v_ref, ...), custom_call_target="tpu_custom_call" | custom-call | flops 59793997824 | bytes 40000000 | tf_op jit(solution)/shard_map/attend_back/pallas_call | solution.py:393
  304.0 33.3 %project_back.1 = (bf16[1024,3456]{1,0:T(8,128)(2,1)}, bf16[1024,1152]{1,0:T(8,128)(2,1)}, f32[4,2,1152]{2,1,0:T(2,128)}, f32[2,1152]{1,0:T(2,128)}) custom-call(s32[4]{0:T(128)} %bitcast.124, f32[1152,1024]{1,0:T(8,128)} %get-tuple-element.79.dqt_ref, f32[1024,1152]{1,0:T(8,128)} %get-tuple-element.80.dk_ref, f32[1024,1152]{1,0:T(8,128)} %get-tuple-element.81.dv_ref, ...), custom_call_target="tpu_custom_call" | custom-call | flops 10871635968 | bytes 50000000 | tf_op jit(solution)/shard_map/project_back/pallas_call | solution.py:393
  338.4 11.6 %qkv_send.1 = bf16[4,144,3456]{2,1,0:T(8,128)(2,1)} custom-call(s32[1]{0:T(128)} %bitcast.28.where, bf16[8,144,1024]{2,1,0:T(8,128)(2,1)} %get-tuple-element.88.units_ref, bf16[1024,3456]{1,0:T(8,128)(2,1)} %get-tuple-element.89.rhs_ref), custom_call_target="tpu_custom_call" | custom-call | flops 4076863488 | bytes 12238848 | tf_op jit(solution)/shard_map/qkv_send/pallas_call | solution.py:393
  351.5 2.4 collective-permute-done.10
  354.2 3.2 collective-permute-done.11
  357.4 3.5 collective-permute-done.12
  361.0 10.4 %gate_send.1 = bf16[4,144,3072]{2,1,0:T(8,128)(2,1)} custom-call(s32[1]{0:T(128)} %bitcast.28.where, bf16[8,144,1024]{2,1,0:T(8,128)(2,1)} %get-tuple-element.101.units_ref, bf16[1024,3072]{1,0:T(8,128)(2,1)} %get-tuple-element.102.rhs_ref), custom_call_target="tpu_custom_call" | custom-call | flops 3623878656 | bytes 11010048 | tf_op jit(solution)/shard_map/gate_send/pallas_call | solution.py:393
  373.0 6.7 out_keep.1
  379.8 5.5 fusion
  385.3 11.9 %collective-permute-done.15.got_ref = bf16[2,144,1152]{2,1,0:T(8,128)(2,1)S(1)} collective-permute-done((bf16[2,144,1152]{2,1,0:T(8,128)(2,1)}, bf16[2,144,1152]{2,1,0:T(8,128)(2,1)S(1)}, u32[]{:S(2)}, u32[]{:S(2)}) %collective-permute-start.15) | collective-permute-done | bytes 663584 | tf_op jit(solution)/shard_map/ppermute | solution.py:427
  398.0 3.9 out_fold.1
  403.1 21.6 %all_gather.7 = bf16[128,3456]{1,0:T(8,128)(2,1)S(1)} all-gather(bf16[8,3456]{1,0:T(8,128)(2,1)S(1)} %select_n.95), channel_id=1, replica_groups=mesh['dp'=16,'mod'=2] {'dp'}, dimensions={0}, use_global_device_ids=true | all-gather | bytes 940032 | tf_op jit(solution)/shard_map/all_gather | solution.py:652
  424.7 2.2 fusion.11
  427.2 10.7 %down_keep.1 = (bf16[2,384,1152]{2,1,0:T(8,128)(2,1)}, f32[2,384,1152]{2,1,0:T(8,128)}) custom-call(s32[6]{0:T(128)} %stack.145.where, bf16[8,384,1024]{2,1,0:T(8,128)(2,1)} %bitcast.128, bf16[1024,1152]{1,0:T(8,128)(2,1)} %get-tuple-element.69.gf_ref.rhs_ref, bf16[4,384,1152]{2,1,0:T(8,128)(2,1)} %collective-permute-done.29.got_ref), custom_call_target="tpu_custom_call" | custom-call | flops 3623878656 | bytes 14352384 | tf_op jit(solution)/shard_map/down_keep/pallas_call | solution.py:393
  438.8 12.2 %up_keep.1 = (bf16[2,144,3072]{2,1,0:T(8,128)(2,1)}, f32[2,144,3072]{2,1,0:T(8,128)}) custom-call(s32[6]{0:T(128)} %stack.152.where, bf16[8,144,1024]{2,1,0:T(8,128)(2,1)} %get-tuple-element.101.units_ref, bf16[1024,3072]{1,0:T(8,128)(2,1)} %get-tuple-element.107.rhs_ref, bf16[4,144,3072]{2,1,0:T(8,128)(2,1)} %collective-permute-done.24.got_ref), custom_call_target="tpu_custom_call" | custom-call | flops 3623878656 | bytes 16318464 | tf_op jit(solution)/shard_map/up_keep/pallas_call | solution.py:393
  451.1 13.5 %qkv_keep.1 = (bf16[2,144,3456]{2,1,0:T(8,128)(2,1)}, f32[2,144,3456]{2,1,0:T(8,128)}) custom-call(s32[6]{0:T(128)} %stack.145.where, bf16[8,144,1024]{2,1,0:T(8,128)(2,1)} %get-tuple-element.88.units_ref, bf16[1024,3456]{1,0:T(8,128)(2,1)} %get-tuple-element.89.rhs_ref, bf16[4,144,3456]{2,1,0:T(8,128)(2,1)} %collective-permute-done.4.got_ref), custom_call_target="tpu_custom_call" | custom-call | flops 4076863488 | bytes 18210816 | tf_op jit(solution)/shard_map/qkv_keep/pallas_call | solution.py:393
  465.7 12.2 %gate_keep.1 = (bf16[2,144,3072]{2,1,0:T(8,128)(2,1)}, f32[2,144,3072]{2,1,0:T(8,128)}) custom-call(s32[6]{0:T(128)} %stack.145.where, bf16[8,144,1024]{2,1,0:T(8,128)(2,1)} %get-tuple-element.101.units_ref, bf16[1024,3072]{1,0:T(8,128)(2,1)} %get-tuple-element.102.rhs_ref, bf16[4,144,3072]{2,1,0:T(8,128)(2,1)} %collective-permute-done.19.got_ref), custom_call_target="tpu_custom_call" | custom-call | flops 3623878656 | bytes 16318464 | tf_op jit(solution)/shard_map/gate_keep/pallas_call | solution.py:393
  481.3 5.6 down_fold.1
  486.9 72.8 %collective-permute-done.3 = bf16[4,1152]{1,0:T(4,128)(2,1)S(1)} collective-permute-done((bf16[4,1152]{1,0:T(4,128)(2,1)S(1)}, bf16[4,1152]{1,0:T(4,128)(2,1)S(1)}, u32[]{:S(2)}, u32[]{:S(2)}) %collective-permute-start.3) | collective-permute-done | bytes 9248 | tf_op jit(solution)/shard_map/ppermute | solution.py:426
  561.1 7.2 %up_fold.1 = (bf16[144,3072]{1,0:T(8,128)(2,1)}, f32[144,3072]{1,0:T(8,128)}) custom-call(s32[2]{0:T(128)} %pad_add_fusion.1.where, f32[2,144,3072]{2,1,0:T(8,128)} %get-tuple-element.108.keep_ref, bf16[2,144,3072]{2,1,0:T(8,128)(2,1)} %collective-permute-done.25.got_ref), custom_call_target="tpu_custom_call" | custom-call | bytes 7962624 | tf_op jit(solution)/shard_map/up_fold/pallas_call | solution.py:393
  569.3 7.1 %gate_fold.1 = (bf16[144,3072]{1,0:T(8,128)(2,1)}, f32[144,3072]{1,0:T(8,128)}) custom-call(s32[2]{0:T(128)} %pad_add_fusion.where, f32[2,144,3072]{2,1,0:T(8,128)} %get-tuple-element.103.keep_ref, bf16[2,144,3072]{2,1,0:T(8,128)(2,1)} %collective-permute-done.20.got_ref), custom_call_target="tpu_custom_call" | custom-call | bytes 7962624 | tf_op jit(solution)/shard_map/gate_fold/pallas_call | solution.py:393
  576.5 1.9 collective-permute-start.21
  579.7 8.0 %qkv_fold.1 = (bf16[144,3456]{1,0:T(8,128)(2,1)}, f32[144,3456]{1,0:T(8,128)}) custom-call(s32[2]{0:T(128)} %pad_add_fusion.where, f32[2,144,3456]{2,1,0:T(8,128)} %get-tuple-element.90.keep_ref, bf16[2,144,3456]{2,1,0:T(8,128)(2,1)} %copy-done.6), custom_call_target="tpu_custom_call" | custom-call | bytes 8957952 | tf_op jit(solution)/shard_map/qkv_fold/pallas_call | solution.py:393
  590.1 1.7 collective-permute-start.32
  593.3 1.5 reshape.106
  594.7 2.0 fusion.4
  597.1 4.5 collective-permute-done.21
  601.6 1.9 convert_add_fusion.3
  603.5 1.5 reshape.105
  606.3 1.8 collective-permute-start.22
  610.3 11.2 %collective-permute-done.27 = bf16[2,36,3072]{2,1,0:T(8,128)(2,1)} collective-permute-done((bf16[2,36,3072]{2,1,0:T(8,128)(2,1)}, bf16[2,36,3072]{2,1,0:T(8,128)(2,1)}, u32[]{:S(2)}, u32[]{:S(2)}) %collective-permute-start.27) | collective-permute-done | bytes 442400 | tf_op jit(solution)/shard_map/ppermute | solution.py:427
  622.7 6.9 %collective-permute-done.22 = bf16[2,36,3072]{2,1,0:T(8,128)(2,1)S(1)} collective-permute-done((bf16[2,36,3072]{2,1,0:T(8,128)(2,1)S(1)}, bf16[2,36,3072]{2,1,0:T(8,128)(2,1)S(1)}, u32[]{:S(2)}, u32[]{:S(2)}) %collective-permute-start.22) | collective-permute-done | bytes 442400 | tf_op jit(solution)/shard_map/ppermute | solution.py:427
  629.9 12.9 %collective-permute-done.28 = bf16[36,3072]{1,0:T(8,128)(2,1)S(1)} collective-permute-done((bf16[36,3072]{1,0:T(8,128)(2,1)S(1)}, bf16[36,3072]{1,0:T(8,128)(2,1)S(1)}, u32[]{:S(2)}, u32[]{:S(2)}) %collective-permute-start.28) | collective-permute-done | bytes 221216 | tf_op jit(solution)/shard_map/ppermute | solution.py:427
  643.6 1.9 collective-permute-done.23
  647.7 1.5 reshape.102
  652.2 9.7 %collective-permute-done.7 = bf16[2,36,3456]{2,0,1:T(2,128)(2,1)S(1)} collective-permute-done((bf16[2,36,3456]{2,0,1:T(2,128)(2,1)S(1)}, bf16[2,36,3456]{2,0,1:T(2,128)(2,1)S(1)}, u32[]{:S(2)}, u32[]{:S(2)}) %collective-permute-start.7) | collective-permute-done | bytes 497696 | tf_op jit(solution)/shard_map/ppermute | solution.py:427
  663.2 1.9 collective-permute-start.8
  665.5 9.7 %collective-permute-done.8 = bf16[36,3456]{1,0:T(8,128)(2,1)S(1)} collective-permute-done((bf16[36,3456]{1,0:T(8,128)(2,1)S(1)}, bf16[36,3456]{1,0:T(8,128)(2,1)S(1)}, u32[]{:S(2)}, u32[]{:S(2)}) %collective-permute-start.8) | collective-permute-done | bytes 248864 | tf_op jit(solution)/shard_map/ppermute | solution.py:427
  (148 shorter events, 42.1 us)
Async XLA Ops:
  0.6 8.8 %collective-permute-start = (f32[4,1152]{1,0:T(4,128)}, f32[4,1152]{1,0:T(4,128)S(1)}, u32[]{:S(2)}, u32[]{:S(2)}) collective-permute-start(f32[4,1152]{1,0:T(4,128)} %bitcast.113), channel_id=1, source_target_pairs={{0,1},{1,0},{2,3},{3,2},{4,5},{5,4},{6,7},{7,6},{8,9},{9,8},{10,11... | collective-permute-start | bytes 55304 | tf_op jit(solution)/shard_map/ppermute | solution.py:426
  4.5 10.3 %copy-start.15 = (s32[1,4]{1,0:T(1,128)}, s32[1,4]{1,0:T(1,128)S(1)}, u32[]{:S(2)}) copy-start(s32[1,4]{1,0:T(1,128)S(1)} %slice.15) | copy-start | bytes 52
  14.8 24.5 %collective-permute-start.1 = (bf16[4,3456]{1,0:T(4,128)(2,1)S(1)}, bf16[4,3456]{1,0:T(4,128)(2,1)S(1)}, u32[]{:S(2)}, u32[]{:S(2)}) collective-permute-start(bf16[4,3456]{1,0:T(4,128)(2,1)S(1)} %get-tuple-element.122), channel_id=1, source_target_pairs={{0,1},{1,0},{2,3},{3,2},{4,5},{5,4},{6,7},{7,6},{8,9},{9,8},{10,11... | collective-permute-start | bytes 82952 | tf_op jit(solution)/shard_map/ppermute | solution.py:426
  212.8 214.4 %collective-permute-start.29 = (bf16[4,384,1152]{2,1,0:T(8,128)(2,1)}, bf16[4,384,1152]{2,1,0:T(8,128)(2,1)}, u32[]{:S(2)}, u32[]{:S(2)}) collective-permute-start(bf16[4,384,1152]{2,1,0:T(8,128)(2,1)} %down_send.1), channel_id=1, source_target_pairs={{0,2},{2,0},{4,6},{6,4},{8,10},{10,8},{12,14},{14,12},{16,18},{18,... | collective-permute-start | bytes 10616840 | tf_op jit(solution)/shard_map/ppermute | solution.py:427
  223.4 215.3 %collective-permute-start.24 = (bf16[4,144,3072]{2,1,0:T(8,128)(2,1)}, bf16[4,144,3072]{2,1,0:T(8,128)(2,1)}, u32[]{:S(2)}, u32[]{:S(2)}) collective-permute-start(bf16[4,144,3072]{2,1,0:T(8,128)(2,1)} %up_send.1), channel_id=1, source_target_pairs={{0,2},{2,0},{4,6},{6,4},{8,10},{10,8},{12,14},{14,12},{16,18},{18,... | collective-permute-start | bytes 10616840 | tf_op jit(solution)/shard_map/ppermute | solution.py:427
  246.9 124.9 %collective-permute-start.14 = (bf16[4,144,1152]{2,1,0:T(8,128)(2,1)}, bf16[4,144,1152]{2,1,0:T(8,128)(2,1)S(1)}, u32[]{:S(2)}, u32[]{:S(2)}) collective-permute-start(bf16[4,144,1152]{2,1,0:T(8,128)(2,1)} %out_send.1), channel_id=1, source_target_pairs={{0,2},{2,0},{4,6},{6,4},{8,10},{10,8},{12,14},{14,12},{16,18},{18,... | collective-permute-start | bytes 3981320 | tf_op jit(solution)/shard_map/ppermute | solution.py:427
  338.1 12.1 %collective-permute-start.9 = (f32[2,72]{1,0:T(2,128)S(1)}, f32[2,72]{1,0:T(2,128)S(1)}, u32[]{:S(2)}, u32[]{:S(2)}) collective-permute-start(f32[2,72]{1,0:T(2,128)S(1)} %reduce_sum.19), channel_id=1, source_target_pairs={{0,2},{2,0},{4,6},{6,4},{8,10},{10,8},{12,14},{14,12},{16,18},{18,... | collective-permute-start | bytes 1736 | tf_op jit(solution)/shard_map/ppermute | solution.py:427
  338.4 13.0 %copy-start.12 = (f32[4,4,1152]{2,1,0:T(4,128)S(1)}, f32[4,4,1152]{2,1,0:T(4,128)}, u32[]{:S(2)}) copy-start(f32[4,4,1152]{2,1,0:T(4,128)} %get-tuple-element.87) | copy-start | bytes 221188
  338.4 13.0 %copy-start.14 = (f32[4,2,1152]{2,1,0:T(2,128)S(1)}, f32[4,2,1152]{2,1,0:T(2,128)}, u32[]{:S(2)}) copy-start(f32[4,2,1152]{2,1,0:T(2,128)} %get-tuple-element.86) | copy-start | bytes 110596
  338.4 15.5 %copy-start.16 = (pred[4,4]{1,0:T(4,128)(4,1)S(1)}, pred[4,4]{1,0:T(4,128)(4,1)}, u32[]{:S(2)}) copy-start(pred[4,4]{1,0:T(4,128)(4,1)} %iota_compare_fusion) | copy-start | bytes 52
  349.9 101.2 %collective-permute-start.4 = (bf16[4,144,3456]{2,1,0:T(8,128)(2,1)}, bf16[4,144,3456]{2,1,0:T(8,128)(2,1)}, u32[]{:S(2)}, u32[]{:S(2)}) collective-permute-start(bf16[4,144,3456]{2,1,0:T(8,128)(2,1)} %qkv_send.1), channel_id=1, source_target_pairs={{0,2},{2,0},{4,6},{6,4},{8,10},{10,8},{12,14},{14,12},{16,18},{18,... | collective-permute-start | bytes 11943944 | tf_op jit(solution)/shard_map/ppermute | solution.py:427
  350.2 3.6 collective-permute-start.10
  353.8 3.6 collective-permute-start.11
  357.4 3.6 collective-permute-start.12
  361.0 10.4 %collective-permute-start.13 = (f32[2,72]{1,0:T(2,128)S(1)}, f32[2,72]{1,0:T(2,128)S(1)}, u32[]{:S(2)}, u32[]{:S(2)}) collective-permute-start(f32[2,72]{1,0:T(2,128)S(1)} %add.162), channel_id=1, source_target_pairs={{0,16},{2,18},{4,20},{6,22},{8,24},{10,26},{12,28},{14,30},{16,0},... | collective-permute-start | bytes 1736 | tf_op jit(solution)/shard_map/ppermute | solution.py:427
  371.3 94.4 %collective-permute-start.19 = (bf16[4,144,3072]{2,1,0:T(8,128)(2,1)}, bf16[4,144,3072]{2,1,0:T(8,128)(2,1)}, u32[]{:S(2)}, u32[]{:S(2)}) collective-permute-start(bf16[4,144,3072]{2,1,0:T(8,128)(2,1)} %gate_send.1), channel_id=1, source_target_pairs={{0,2},{2,0},{4,6},{6,4},{8,10},{10,8},{12,14},{14,12},{16,18},{18,... | collective-permute-start | bytes 10616840 | tf_op jit(solution)/shard_map/ppermute | solution.py:427
  371.9 7.8 %collective-permute-start.2 = (bf16[4,3456]{1,0:T(4,128)(2,1)S(1)}, bf16[4,3456]{1,0:T(4,128)(2,1)S(1)}, u32[]{:S(2)}, u32[]{:S(2)}) collective-permute-start(bf16[4,3456]{1,0:T(4,128)(2,1)S(1)} %get-tuple-element.118), channel_id=1, source_target_pairs={{0,1},{1,0},{2,3},{3,2},{4,5},{5,4},{6,7},{7,6},{8,9},{9,8},{10,11... | collective-permute-start | bytes 82952 | tf_op jit(solution)/shard_map/ppermute | solution.py:426
  379.7 17.5 %collective-permute-start.15 = (bf16[2,144,1152]{2,1,0:T(8,128)(2,1)}, bf16[2,144,1152]{2,1,0:T(8,128)(2,1)S(1)}, u32[]{:S(2)}, u32[]{:S(2)}) collective-permute-start(bf16[2,144,1152]{2,1,0:T(8,128)(2,1)} %get-tuple-element.98), channel_id=1, source_target_pairs={{0,4},{2,6},{4,0},{6,2},{8,12},{10,14},{12,8},{14,10},{16,20},{18,... | collective-permute-start | bytes 1990664 | tf_op jit(solution)/shard_map/ppermute | solution.py:427
  402.0 24.9 %copy-start.10 = (f32[144,1152]{1,0:T(8,128)S(1)}, f32[144,1152]{1,0:T(8,128)}, u32[]{:S(2)}) copy-start(f32[144,1152]{1,0:T(8,128)} %get-tuple-element.99) | copy-start | bytes 1990660
  402.0 24.9 %collective-permute-start.16 = (bf16[144,1152]{1,0:T(8,128)(2,1)}, bf16[144,1152]{1,0:T(8,128)(2,1)S(1)}, u32[]{:S(2)}, u32[]{:S(2)}) collective-permute-start(bf16[144,1152]{1,0:T(8,128)(2,1)} %get-tuple-element.100), channel_id=1, source_target_pairs={{0,1},{1,0},{2,3},{3,2},{4,5},{5,4},{6,7},{7,6},{8,9},{9,8},{10,11... | collective-permute-start | bytes 995336 | tf_op jit(solution)/shard_map/ppermute | solution.py:426
  427.1 51.8 %collective-permute-start.17 = (bf16[2,36,1152]{2,1,0:T(8,128)(2,1)S(1)}, bf16[2,36,1152]{2,1,0:T(8,128)(2,1)S(1)}, u32[]{:S(2)}, u32[]{:S(2)}) collective-permute-start(bf16[2,36,1152]{2,1,0:T(8,128)(2,1)S(1)} %fusion.9), channel_id=1, source_target_pairs={{0,8},{2,10},{4,12},{6,14},{8,0},{10,2},{12,4},{14,6},{16,24},{18,... | collective-permute-start | bytes 497672 | tf_op jit(solution)/shard_map/ppermute | solution.py:427
  437.9 42.3 %collective-permute-start.30 = (bf16[2,384,1152]{2,1,0:T(8,128)(2,1)}, bf16[2,384,1152]{2,1,0:T(8,128)(2,1)}, u32[]{:S(2)}, u32[]{:S(2)}) collective-permute-start(bf16[2,384,1152]{2,1,0:T(8,128)(2,1)} %get-tuple-element.114), channel_id=1, source_target_pairs={{0,1},{1,0},{2,3},{3,2},{4,5},{5,4},{6,7},{7,6},{8,9},{9,8},{10,11... | collective-permute-start | bytes 5308424 | tf_op jit(solution)/shard_map/ppermute | solution.py:426
  451.0 110.1 %collective-permute-start.25 = (bf16[2,144,3072]{2,1,0:T(8,128)(2,1)}, bf16[2,144,3072]{2,1,0:T(8,128)(2,1)}, u32[]{:S(2)}, u32[]{:S(2)}) collective-permute-start(bf16[2,144,3072]{2,1,0:T(8,128)(2,1)} %get-tuple-element.109), channel_id=1, source_target_pairs={{0,4},{2,6},{4,0},{6,2},{8,12},{10,14},{12,8},{14,10},{16,20},{18,... | collective-permute-start | bytes 5308424 | tf_op jit(solution)/shard_map/ppermute | solution.py:427
  464.7 113.7 %collective-permute-start.5 = (bf16[2,144,3456]{2,1,0:T(8,128)(2,1)}, bf16[2,144,3456]{2,1,0:T(8,128)(2,1)S(1)}, u32[]{:S(2)}, u32[]{:S(2)}) collective-permute-start(bf16[2,144,3456]{2,1,0:T(8,128)(2,1)} %get-tuple-element.91), channel_id=1, source_target_pairs={{0,1},{1,0},{2,3},{3,2},{4,5},{5,4},{6,7},{7,6},{8,9},{9,8},{10,11... | collective-permute-start | bytes 5971976 | tf_op jit(solution)/shard_map/ppermute | solution.py:426
  478.0 91.3 %collective-permute-start.20 = (bf16[2,144,3072]{2,1,0:T(8,128)(2,1)}, bf16[2,144,3072]{2,1,0:T(8,128)(2,1)}, u32[]{:S(2)}, u32[]{:S(2)}) collective-permute-start(bf16[2,144,3072]{2,1,0:T(8,128)(2,1)} %get-tuple-element.104), channel_id=1, source_target_pairs={{0,1},{1,0},{2,3},{3,2},{4,5},{5,4},{6,7},{7,6},{8,9},{9,8},{10,11... | collective-permute-start | bytes 5308424 | tf_op jit(solution)/shard_map/ppermute | solution.py:426
  478.9 80.8 %collective-permute-start.3 = (bf16[4,1152]{1,0:T(4,128)(2,1)S(1)}, bf16[4,1152]{1,0:T(4,128)(2,1)S(1)}, u32[]{:S(2)}, u32[]{:S(2)}) collective-permute-start(bf16[4,1152]{1,0:T(4,128)(2,1)S(1)} %fusion.13), channel_id=1, source_target_pairs={{0,1},{1,0},{2,3},{3,2},{4,5},{5,4},{6,7},{7,6},{8,9},{9,8},{10,11... | collective-permute-start | bytes 27656 | tf_op jit(solution)/shard_map/ppermute | solution.py:426
  480.2 80.3 %collective-permute-start.18 = (bf16[36,1152]{1,0:T(8,128)(2,1)S(1)}, bf16[36,1152]{1,0:T(8,128)(2,1)S(1)}, u32[]{:S(2)}, u32[]{:S(2)}) collective-permute-start(bf16[36,1152]{1,0:T(8,128)(2,1)S(1)} %fusion.10), channel_id=1, source_target_pairs={{0,16},{2,18},{4,20},{6,22},{8,24},{10,26},{12,28},{14,30},{16,0},... | collective-permute-start | bytes 248840 | tf_op jit(solution)/shard_map/ppermute | solution.py:427
  481.3 78.5 %copy-start.13 = (f32[1,4,1152]{2,1,0:T(4,128)S(1)}, f32[1,4,1152]{2,1,0:T(4,128)}, u32[]{:S(2)}) copy-start(f32[1,4,1152]{2,1,0:T(4,128)} %param.19) | copy-start | bytes 55300
  559.7 28.1 %collective-permute-start.31 = (bf16[384,1152]{1,0:T(8,128)(2,1)}, bf16[384,1152]{1,0:T(8,128)(2,1)}, u32[]{:S(2)}, u32[]{:S(2)}) collective-permute-start(bf16[384,1152]{1,0:T(8,128)(2,1)} %get-tuple-element.116), channel_id=1, source_target_pairs={{0,4},{2,6},{4,0},{6,2},{8,12},{10,14},{12,8},{14,10},{16,20},{18,... | collective-permute-start | bytes 2654216 | tf_op jit(solution)/shard_map/ppermute | solution.py:427
  568.4 23.5 %collective-permute-start.26 = (bf16[144,3072]{1,0:T(8,128)(2,1)}, bf16[144,3072]{1,0:T(8,128)(2,1)}, u32[]{:S(2)}, u32[]{:S(2)}) collective-permute-start(bf16[144,3072]{1,0:T(8,128)(2,1)} %get-tuple-element.111), channel_id=1, source_target_pairs={{0,1},{1,0},{2,3},{3,2},{4,5},{5,4},{6,7},{7,6},{8,9},{9,8},{10,11... | collective-permute-start | bytes 2654216 | tf_op jit(solution)/shard_map/ppermute | solution.py:426
  576.5 25.1 %collective-permute-start.21 = (bf16[144,3072]{1,0:T(8,128)(2,1)}, bf16[144,3072]{1,0:T(8,128)(2,1)}, u32[]{:S(2)}, u32[]{:S(2)}) collective-permute-start(bf16[144,3072]{1,0:T(8,128)(2,1)} %get-tuple-element.106), channel_id=1, source_target_pairs={{0,4},{2,6},{4,0},{6,2},{8,12},{10,14},{12,8},{14,10},{16,20},{18,... | collective-permute-start | bytes 2654216 | tf_op jit(solution)/shard_map/ppermute | solution.py:427
  578.4 1.4 copy-start.6
  579.7 8.1 %copy-start.7 = (f32[384,1152]{1,0:T(8,128)S(1)}, f32[384,1152]{1,0:T(8,128)}, u32[]{:S(2)}) copy-start(f32[384,1152]{1,0:T(8,128)} %get-tuple-element.115) | copy-start | bytes 5308420
  587.7 58.6 %collective-permute-start.6 = (bf16[144,3456]{1,0:T(8,128)(2,1)}, bf16[144,3456]{1,0:T(8,128)(2,1)}, u32[]{:S(2)}, u32[]{:S(2)}) collective-permute-start(bf16[144,3456]{1,0:T(8,128)(2,1)} %get-tuple-element.93), channel_id=1, source_target_pairs={{0,4},{2,6},{4,0},{6,2},{8,12},{10,14},{12,8},{14,10},{16,20},{18,... | collective-permute-start | bytes 2985992 | tf_op jit(solution)/shard_map/ppermute | solution.py:427
  587.8 4.0 copy-start.8
  590.1 18.0 %collective-permute-start.32 = (bf16[2,96,1152]{2,1,0:T(8,128)(2,1)}, bf16[2,96,1152]{2,1,0:T(8,128)(2,1)}, u32[]{:S(2)}, u32[]{:S(2)}) collective-permute-start(bf16[2,96,1152]{2,1,0:T(8,128)(2,1)} %fusion.5), channel_id=1, source_target_pairs={{0,8},{2,10},{4,12},{6,14},{8,0},{10,2},{12,4},{14,6},{16,24},{18,... | collective-permute-start | bytes 1327112 | tf_op jit(solution)/shard_map/ppermute | solution.py:427
  596.8 24.7 %collective-permute-start.27 = (bf16[2,36,3072]{2,1,0:T(8,128)(2,1)}, bf16[2,36,3072]{2,1,0:T(8,128)(2,1)}, u32[]{:S(2)}, u32[]{:S(2)}) collective-permute-start(bf16[2,36,3072]{2,1,0:T(8,128)(2,1)} %fusion.4), channel_id=1, source_target_pairs={{0,8},{2,10},{4,12},{6,14},{8,0},{10,2},{12,4},{14,6},{16,24},{18,... | collective-permute-start | bytes 1327112 | tf_op jit(solution)/shard_map/ppermute | solution.py:427
  604.9 16.5 %copy-start.1 = (f32[2,2,36,3072]{3,2,1,0:T(8,128)S(1)}, f32[2,2,36,3072]{3,2,1,0:T(8,128)}, u32[]{:S(2)}) copy-start(f32[2,2,36,3072]{3,2,1,0:T(8,128)} %reshape.106) | copy-start | bytes 5308420
  606.3 23.3 %copy-start.2 = (f32[2,2,36,3072]{3,2,1,0:T(8,128)S(1)}, f32[2,2,36,3072]{3,2,1,0:T(8,128)}, u32[]{:S(2)}) copy-start(f32[2,2,36,3072]{3,2,1,0:T(8,128)} %reshape.105) | copy-start | bytes 5308420
  606.3 23.3 %collective-permute-start.22 = (bf16[2,36,3072]{2,1,0:T(8,128)(2,1)S(1)}, bf16[2,36,3072]{2,1,0:T(8,128)(2,1)S(1)}, u32[]{:S(2)}, u32[]{:S(2)}) collective-permute-start(bf16[2,36,3072]{2,1,0:T(8,128)(2,1)S(1)} %fusion.3), channel_id=1, source_target_pairs={{0,8},{2,10},{4,12},{6,14},{8,0},{10,2},{12,4},{14,6},{16,24},{18,... | collective-permute-start | bytes 1327112 | tf_op jit(solution)/shard_map/ppermute | solution.py:427
  609.3 42.0 %collective-permute-start.33 = (bf16[96,1152]{1,0:T(8,128)(2,1)S(1)}, bf16[96,1152]{1,0:T(8,128)(2,1)S(1)}, u32[]{:S(2)}, u32[]{:S(2)}) collective-permute-start(bf16[96,1152]{1,0:T(8,128)(2,1)S(1)} %fusion.8), channel_id=1, source_target_pairs={{0,16},{2,18},{4,20},{6,22},{8,24},{10,26},{12,28},{14,30},{16,0},... | collective-permute-start | bytes 663560 | tf_op jit(solution)/shard_map/ppermute | solution.py:427
  622.6 23.7 %copy-start.5 = (f32[144,3456]{1,0:T(8,128)S(1)}, f32[144,3456]{1,0:T(8,128)}, u32[]{:S(2)}) copy-start(f32[144,3456]{1,0:T(8,128)} %get-tuple-element.92) | copy-start | bytes 5971972
  622.6 20.2 %collective-permute-start.28 = (bf16[36,3072]{1,0:T(8,128)(2,1)S(1)}, bf16[36,3072]{1,0:T(8,128)(2,1)S(1)}, u32[]{:S(2)}, u32[]{:S(2)}) collective-permute-start(bf16[36,3072]{1,0:T(8,128)(2,1)S(1)} %fusion.7), channel_id=1, source_target_pairs={{0,16},{2,18},{4,20},{6,22},{8,24},{10,26},{12,28},{14,30},{16,0},... | collective-permute-start | bytes 663560 | tf_op jit(solution)/shard_map/ppermute | solution.py:427
  629.8 15.7 %collective-permute-start.23 = (bf16[36,3072]{1,0:T(8,128)(2,1)S(1)}, bf16[36,3072]{1,0:T(8,128)(2,1)S(1)}, u32[]{:S(2)}, u32[]{:S(2)}) collective-permute-start(bf16[36,3072]{1,0:T(8,128)(2,1)S(1)} %fusion.6), channel_id=1, source_target_pairs={{0,16},{2,18},{4,20},{6,22},{8,24},{10,26},{12,28},{14,30},{16,0},... | collective-permute-start | bytes 663560 | tf_op jit(solution)/shard_map/ppermute | solution.py:427
  647.7 3.6 copy-start.4
  649.2 2.9 copy-start
  651.1 10.9 %collective-permute-start.7 = (bf16[2,36,3456]{2,0,1:T(2,128)(2,1)S(1)}, bf16[2,36,3456]{2,0,1:T(2,128)(2,1)S(1)}, u32[]{:S(2)}, u32[]{:S(2)}) collective-permute-start(bf16[2,36,3456]{2,0,1:T(2,128)(2,1)S(1)} %copy.43), channel_id=1, source_target_pairs={{0,8},{2,10},{4,12},{6,14},{8,0},{10,2},{12,4},{14,6},{16,24},{18,... | collective-permute-start | bytes 1493000 | tf_op jit(solution)/shard_map/ppermute | solution.py:427
  663.2 12.1 %collective-permute-start.8 = (bf16[36,3456]{1,0:T(8,128)(2,1)S(1)}, bf16[36,3456]{1,0:T(8,128)(2,1)S(1)}, u32[]{:S(2)}, u32[]{:S(2)}) collective-permute-start(bf16[36,3456]{1,0:T(8,128)(2,1)S(1)} %bitcast.111), channel_id=1, source_target_pairs={{0,16},{2,18},{4,20},{6,22},{8,24},{10,26},{12,28},{14,30},{16,0},... | collective-permute-start | bytes 746504 | tf_op jit(solution)/shard_map/ppermute | solution.py:427
  (3 other events, 3.0 us)

commit v3 on v2

--- a/solution.py
+++ b/solution.py
@@ -281,7 +281,7 @@
 
 
 def attend_back_kernel(
-    slots, q_ref, k_ref, v_ref, do_ref, lse_ref, dot_ref, kt_ref, dqt_ref, dk_ref, dv_ref
+    slots, q_ref, k_ref, v_ref, do_ref, lse_ref, dot_ref, kt_ref, dqt_ref, dk_ref, dv_low_ref, dv_ref
 ):
     h = pl.program_id(0)
     tokens, width = q_ref.shape
@@ -325,11 +325,15 @@
 
         lax.fori_loop(0, tokens // TB, block, 0)
 
+    @pl.when(h == HEADS - 1)
+    def _():
+        dv_low_ref[...] = dv_ref[...].astype(bf16)
+
 
 def project_back_kernel(
     slots, dqt_ref, dk_ref, dv_ref, raw_ref, inv_ref, q_ref, k_ref, x_ref, grad_mid_ref, mod_ref,
     w_ref, coords_ref, cos_ref, sin_ref, gain_ref, gather_ref, spread_ref,
-    gp_ref, grad_x_ref, sums_ref, gains_ref,
+    gq_ref, gk_ref, grad_x_ref, sums_ref, gains_ref,
 ):
     width = x_ref.shape[1]
     slot = slots[pl.program_id(0)]
@@ -339,7 +343,7 @@
         gains_ref[...] = jnp.zeros_like(gains_ref)
 
     cosine, sine = angles(coords_ref, cos_ref, sin_ref)
-    for index, low_ref in enumerate((q_ref, k_ref)):
+    for index, (low_ref, gp_ref) in enumerate(((q_ref, gq_ref), (k_ref, gk_ref))):
         grad = dqt_ref[...].T if index == 0 else dk_ref[...]
         raw = raw_ref[:, index * width : (index + 1) * width]
         inverse = head_spread(inv_ref[:, index * 128 : (index + 1) * 128], spread_ref)
@@ -347,11 +351,11 @@
         norm = raw * inverse
         back = grad * cosine - partner(grad) * sine
         gains_ref[index : index + 1, :] += jnp.sum(back * norm, axis=0, keepdims=True)
-        gp_ref[:, index * width : (index + 1) * width] = (
+        gp_ref[...] = (
             inverse * (back * gain_ref[index : index + 1, :] - norm * head_spread(mean, spread_ref))
         ).astype(bf16)
-    gp_ref[:, 2 * width :] = dv_ref[...].astype(bf16)
-    dmod = nt(gp_ref[...], w_ref[...])
+    dmod = nt(gq_ref[...], w_ref[:, :width]) + nt(gk_ref[...], w_ref[:, width : 2 * width])
+    dmod = dmod + nt(dv_ref[...], w_ref[:, 2 * width :])
     norm, inverse = normed(x_ref[...].astype(f32))
     grad_x = grad_mid_ref[...] + norm_back(dmod, part(mod_ref, slot, 1, width), norm, inverse)
     grad_x_ref[...] = grad_x.astype(bf16)
@@ -381,23 +385,40 @@
     own_ref[...] = keep_ref[own] + got_ref[own].astype(f32)
 
 
-def call(kernel, grid, in_specs, out_specs, out_shape, args, scalars=None, scratch=(), cost=None, name=None):
-    cost = cost or (0, 0)
-    spec = pltpu.PrefetchScalarGridSpec(
-        num_scalar_prefetch=0 if scalars is None else 1,
-        grid=grid,
-        in_specs=in_specs,
-        out_specs=out_specs,
-        scratch_shapes=scratch,
-    )
-    return pl.pallas_call(
-        kernel,
-        grid_spec=spec,
-        out_shape=out_shape,
-        compiler_params=pltpu.CompilerParams(vmem_limit_bytes=VMEM),
-        cost_estimate=pl.CostEstimate(flops=int(cost[0]), bytes_accessed=int(cost[1]), transcendentals=0),
-        name=name,
-    )(*(() if scalars is None else (scalars,)), *args)
+class Chain:
+    def __init__(self):
+        self.last = None
+
+    def __call__(
+        self, kernel, grid, in_specs, out_specs, out_shape, args, scalars=None, scratch=(), cost=(0, 0), name=None
+    ):
+        ahead = 0 if scalars is None else 1
+        body = kernel
+        token = ()
+        if self.last is not None:
+            token = (self.last,)
+            in_specs = [pl.BlockSpec(memory_space=pl.ANY)] + list(in_specs)
+
+            def body(*refs):
+                kernel(*refs[:ahead], *refs[ahead + 1 :])
+
+        spec = pltpu.PrefetchScalarGridSpec(
+            num_scalar_prefetch=ahead,
+            grid=grid,
+            in_specs=in_specs,
+            out_specs=out_specs,
+            scratch_shapes=scratch,
+        )
+        outs = pl.pallas_call(
+            body,
+            grid_spec=spec,
+            out_shape=out_shape,
+            compiler_params=pltpu.CompilerParams(vmem_limit_bytes=VMEM),
+            cost_estimate=pl.CostEstimate(flops=int(cost[0]), bytes_accessed=int(cost[1]), transcendentals=0),
+            name=name,
+        )(*(() if scalars is None else (scalars,)), *token, *args)
+        self.last = outs[-1] if isinstance(outs, (list, tuple)) else outs
+        return outs
 
 
 def shape(dims, dtype):
@@ -413,81 +434,101 @@
 
 
 class Reducer:
-    def __init__(self, n_dp, n_mod):
-        self.n_dp, self.n_mod = n_dp, n_mod
-        position = lax.axis_index("dp")
-        self.core = position & 1
-        self.nxt = lax.shift_right_logical(position, 1) & 1
+    def __init__(self, n_dp, n_mod, call):
+        self.n_dp, self.n_mod, self.call = n_dp, n_mod, call
+        self.position = lax.axis_index("dp")
+        self.core = self.position & 1
+        self.nxt = lax.shift_right_logical(self.position, 1) & 1
         self.mod = lax.axis_index("mod")
-        self.position = position
 
     def swap(self, arr, bit):
         if bit == "mod":
             return lax.ppermute(arr, "mod", [(i, i ^ 1) for i in range(self.n_mod)])
         return lax.ppermute(arr, "dp", [(i, i ^ (1 << bit)) for i in range(self.n_dp)])
 
-    def start(self, units, rhs, name):
-        _, rows, tokens = units.shape
-        columns = rhs.shape[1]
-        chunk = 384
-        half = pl.BlockSpec((4, rows, tokens), lambda j, w: (w[0], 0, 0), pipeline_mode=pl.Buffered(1))
-        sent = call(
+    def stream(self, units, rhs, mod_first, name):
+        return Stream(self, units, rhs, mod_first, name)
+
+
+class Stream:
+    def __init__(self, reducer, units, rhs, mod_first, name):
+        self.r, self.units, self.rhs, self.mod_first, self.name = reducer, units, rhs, mod_first, name
+        _, self.rows, self.tokens = units.shape
+        self.columns = rhs.shape[1]
+        self.chunk = next(c for c in (1024, 1152) if self.columns % c == 0)
+        self.cost = (
+            8 * self.rows * self.tokens * self.columns,
+            2 * self.tokens * (self.columns + 4 * self.rows) + 8 * self.rows * self.columns,
+        )
+
+    def half(self):
+        return pl.BlockSpec(
+            (4, self.rows, self.tokens), lambda j, w: (w[0], 0, 0), pipeline_mode=pl.Buffered(1)
+        )
+
+    def send(self):
+        rows, columns, chunk = self.rows, self.columns, self.chunk
+        sent = self.r.call(
             send_kernel,
             (columns // chunk,),
-            [half, rows_of((tokens, chunk), 1)],
+            [self.half(), rows_of((self.tokens, chunk), 1)],
             rows_of((4, rows, chunk), 2),
             shape((4, rows, columns), bf16),
-            (units, rhs),
-            scalars=jnp.stack([1 - self.core]),
-            cost=(8 * rows * tokens * columns, 2 * tokens * (columns + 4 * rows) + 8 * rows * columns),
-            name=name + "_send",
+            (self.units, self.rhs),
+            scalars=jnp.stack([1 - self.r.core]),
+            cost=self.cost,
+            name=self.name + "_send",
         )
-        return self.swap(sent, 0)
-
-    def finish(self, units, rhs, got, mod_first, name):
-        _, rows, tokens = units.shape
-        columns = rhs.shape[1]
-        chunk = 384
-        if mod_first:
-            where = [2 * (1 - self.mod), 2 * (1 - self.mod) + 1, 2 * self.mod, 2 * self.mod + 1]
-            second, third, third_bit = "mod", 1, self.nxt
+        self.got = self.r.swap(sent, 0)
+
+    def keep(self):
+        rows, columns, chunk = self.rows, self.columns, self.chunk
+        mod, nxt = self.r.mod, self.r.nxt
+        if self.mod_first:
+            where = [2 * (1 - mod), 2 * (1 - mod) + 1, 2 * mod, 2 * mod + 1]
         else:
-            where = [1 - self.nxt, 3 - self.nxt, self.nxt, 2 + self.nxt]
-            second, third, third_bit = 1, "mod", self.mod
-        half = pl.BlockSpec((4, rows, tokens), lambda j, w: (w[0], 0, 0), pipeline_mode=pl.Buffered(1))
-        sent, kept = call(
+            where = [1 - nxt, 3 - nxt, nxt, 2 + nxt]
+        sent, self.kept = self.r.call(
             keep_kernel,
             (columns // chunk,),
-            [half, rows_of((tokens, chunk), 1), rows_of((4, rows, chunk), 2)],
+            [self.half(), rows_of((self.tokens, chunk), 1), rows_of((4, rows, chunk), 2)],
             [rows_of((2, rows, chunk), 2), rows_of((2, rows, chunk), 2)],
             [shape((2, rows, columns), bf16), shape((2, rows, columns), f32)],
-            (units, rhs, got),
-            scalars=jnp.stack([self.core, self.core] + where),
+            (self.units, self.rhs, self.got),
+            scalars=jnp.stack([self.r.core, self.r.core] + where),
             scratch=[pltpu.VMEM((4, rows, chunk), f32)],
-            cost=(8 * rows * tokens * columns, 2 * tokens * (columns + 4 * rows) + 20 * rows * columns),
-            name=name + "_keep",
+            cost=(self.cost[0], self.cost[1] + 12 * rows * columns),
+            name=self.name + "_keep",
         )
-        got = self.swap(sent, second)
-        sent, kept = call(
+        self.got = self.r.swap(sent, "mod" if self.mod_first else 1)
+
+    def fold(self):
+        rows, columns, chunk = self.rows, self.columns, self.chunk
+        bit = self.r.nxt if self.mod_first else self.r.mod
+        sent, self.kept = self.r.call(
             fold_kernel,
             (columns // chunk,),
             [rows_of((2, rows, chunk), 2), rows_of((2, rows, chunk), 2)],
             [rows_of((rows, chunk), 1), rows_of((rows, chunk), 1)],
             [shape((rows, columns), bf16), shape((rows, columns), f32)],
-            (kept, got),
-            scalars=jnp.stack([1 - third_bit, third_bit]),
+            (self.kept, self.got),
+            scalars=jnp.stack([1 - bit, bit]),
             cost=(0, 18 * rows * columns),
-            name=name + "_fold",
+            name=self.name + "_fold",
         )
-        total = kept + self.swap(sent, third).astype(f32)
-        bits = self.n_dp.bit_length() - 1
-        total = total.reshape((2,) * (bits - 2) + (rows * 4 // self.n_dp, columns))
+        self.got = self.r.swap(sent, 1 if self.mod_first else "mod")
+
+    def total(self):
+        n_dp = self.r.n_dp
+        total = self.kept + self.got.astype(f32)
+        bits = n_dp.bit_length() - 1
+        total = total.reshape((2,) * (bits - 2) + (self.rows * 4 // n_dp, self.columns))
         for bit in range(2, bits):
             axis = bits - 1 - bit
-            mine = lax.shift_right_logical(self.position, bit) & 1
+            mine = lax.shift_right_logical(self.r.position, bit) & 1
             away = lax.dynamic_index_in_dim(total, 1 - mine, axis=axis, keepdims=False)
             own = lax.dynamic_index_in_dim(total, mine, axis=axis, keepdims=False)
-            total = own + self.swap(away.astype(bf16), bit).astype(f32)
+            total = own + self.r.swap(away.astype(bf16), bit).astype(f32)
         return total
 
 
@@ -510,7 +551,8 @@
     ff = w_gate.shape[1]
     blocks = count // TB
     n_dev = n_dp * n_mod
-    reducer = Reducer(n_dp, n_mod)
+    call = Chain()
+    reducer = Reducer(n_dp, n_mod, call)
     mod_index = lax.axis_index("mod")
     x = tokens[0]
     cot = cotangent[0]
@@ -569,7 +611,7 @@
 
     rows_ff = ff // n_dev
     rest = n_dp // 4
-    chunk = 384
+    chunk = 768
     group = chunk // rows_ff
     if group >= 8:
         unit_block = pl.BlockSpec((4, 2, group // 8, rows_ff, count), lambda i: (0, 0, i, 0, 0))
@@ -587,12 +629,12 @@
     )
     down_units = down_units.reshape(8, rest * rows_ff, count)
 
-    got_gate = reducer.start(ffn_units, grad_gate, "gate")
-    got_up = reducer.start(ffn_units, grad_up, "up")
-    got_down = reducer.start(down_units, grad_ffn, "down")
-    summed_gate = reducer.finish(ffn_units, grad_gate, got_gate, True, "gate")
-    summed_up = reducer.finish(ffn_units, grad_up, got_up, False, "up")
-    summed_down = reducer.finish(down_units, grad_ffn, got_down, True, "down")
+    gate = reducer.stream(ffn_units, grad_gate, True, "gate")
+    up = reducer.stream(ffn_units, grad_up, False, "up")
+    down = reducer.stream(down_units, grad_ffn, True, "down")
+    gate.send()
+    up.send()
+    down.send()
 
     output, grad_mid, grad_attn, grad_attended, dot_term, sums_b = call(
         middle_kernel,
@@ -605,37 +647,57 @@
         cost=(2 * macs, 40e6),
         name="middle",
     )
-    got_out = reducer.start(out_units, grad_attn, "out")
-    summed_out = reducer.finish(out_units, grad_attn, got_out, False, "out")
+    out = reducer.stream(out_units, grad_attn, False, "out")
+    gate.keep()
+    up.keep()
+    out.send()
+    down.keep()
+    out.keep()
 
     grad_query_t, grad_key, grad_value = call(
         attend_back_kernel,
         (HEADS,),
         [fixed((count, width))] * 4 + [fixed((128, count))] * 2 + [fixed((width, count))],
         [fixed((width, count))] + [fixed((count, width))] * 2,
-        [shape((width, count), f32), token_f32, token_f32],
+        [shape((width, count), f32), token_f32, token_bf16],
         (query, key, value, grad_attended, lse, dot_term, key_t),
+        scratch=[pltpu.VMEM((count, width), f32)],
         scalars=slots,
         cost=(2 * 22 * macs, 40e6),
         name="attend_back",
     )
-    grad_projected, grad_tokens, sums_a, gain_sums = call(
+    v_part = reducer.stream(attn_units, grad_value, True, "v")
+    v_part.send()
+    gate.fold()
+    up.fold()
+    v_part.keep()
+    out.fold()
+    grad_q, grad_k, grad_tokens, sums_a, gain_sums = call(
         project_back_kernel,
         (blocks,),
         [rows_of((width, TB), 1), token_spec, token_spec, rows_of((TB, 2 * width)), rows_of((TB, 256))]
         + [token_spec] * 4
         + [mod_spec, fixed((width, 3 * width)), rows_of((2, TB), 1)]
         + table_specs,
-        [rows_of((TB, 3 * width)), token_spec, rows_of((1, 2, width)), fixed((2, width))],
-        [shape((count, 3 * width), bf16), token_bf16, shape((blocks, 2, width), f32), shape((2, width), f32)],
+        [token_spec, token_spec, token_spec, rows_of((1, 2, width)), fixed((2, width))],
+        [token_bf16, token_bf16, token_bf16, shape((blocks, 2, width), f32), shape((2, width), f32)],
         (grad_query_t, grad_key, grad_value, raw, inverse, query, key, x, grad_mid, modulation, w_qkv, coord)
         + tables,
         scalars=slots,
         cost=(2 * 4 * macs, 50e6),
         name="project_back",
     )
-    got_qkv = reducer.start(attn_units, grad_projected, "qkv")
-    summed_qkv = reducer.finish(attn_units, grad_projected, got_qkv, True, "qkv")
+    q_part = reducer.stream(attn_units, grad_q, False, "q")
+    k_part = reducer.stream(attn_units, grad_k, True, "k")
+    q_part.send()
+    k_part.send()
+    down.fold()
+    v_part.fold()
+    q_part.keep()
+    k_part.keep()
+    q_part.fold()
+    k_part.fold()
+    summed_qkv = jnp.concatenate([q_part.total(), k_part.total(), v_part.total()], axis=1)
 
     sums = jnp.concatenate([sums_a, sums_b], axis=1).reshape(blocks, 6 * width)
     in_slot = slots[None, :, None] == jnp.arange(slots_n)[:, None, None]
@@ -644,13 +706,18 @@
     own_half = lax.dynamic_index_in_dim(halves, mod_index, 1, keepdims=False)
     other_half = lax.dynamic_index_in_dim(halves, 1 - mod_index, 1, keepdims=False)
     grad_mod_flat = pair_order(own_half, reducer.swap(other_half, "mod"), mod_index).reshape(-1, half)
-    all_activated = lax.all_gather(activated, "dp", axis=0, tiled=True)
     rows_ada = width // n_dp
+    gathered = jnp.concatenate([activated, grad_mod_flat], axis=1)
+    for bit in range(n_dp.bit_length() - 1):
+        other = reducer.swap(gathered, bit)
+        second = (lax.shift_right_logical(reducer.position, bit) & 1) == 1
+        gathered = jnp.where(
+            second, jnp.concatenate([other, gathered]), jnp.concatenate([gathered, other])
+        )
     own_activated = lax.dynamic_slice_in_dim(
-        all_activated, lax.axis_index("dp") * rows_ada, rows_ada, axis=1
-    )
-    all_grad_mod = lax.all_gather(grad_mod_flat, "dp", axis=0, tiled=True)
-    grad_w_ada = jnp.einsum("nd,nc->dc", own_activated, all_grad_mod, preferred_element_type=f32)
+        gathered[:, :width], reducer.position * rows_ada, rows_ada, axis=1
+    )
+    grad_w_ada = jnp.einsum("nd,nc->dc", own_activated, gathered[:, width:], preferred_element_type=f32)
     grad_activated = jnp.einsum("nc,dc->nd", grad_mod_flat, w_ada, preferred_element_type=f32)
     grad_activated = grad_activated.reshape(n_mod, slots_n, width)
     own_part = lax.dynamic_index_in_dim(grad_activated, mod_index, 0, keepdims=False)
@@ -669,10 +736,10 @@
         summed_qkv,
         gain_grads[0],
         gain_grads[1],
-        summed_out,
-        summed_gate,
-        summed_up,
-        summed_down,
+        out.total(),
+        gate.total(),
+        up.total(),
+        down.total(),
     )
 
 

time: 688 us -> 608 us (0.88)
  blocking collectives: 46 us -> 0 us
  waiting for transfers between devices: 151 us -> 110 us
  starting transfers between devices: 22.7 us -> 42.4 us
  Pallas kernels: 405 us -> 391 us
    ppermute x10 -> x12, waiting for transfers between devices: 75.2 us -> 16.8 us  [swap(): return lax.ppermute(arr, 'mod', [(i, i ^ 1) for i in range(self.n_mod)])]
    all_gather x2 -> x0, blocking collectives: 46 us -> none  [the longest x1 24.4 us: body(): all_activated = lax.all_gather(activated, 'dp', axis=0, tiled=True)]
    ppermute x24 -> x36, starting transfers between devices: 11.2 us -> 29.4 us  [swap(): lax.ppermute(arr, 'dp', [(i, i ^ 1 << bit) for i in range(self.n_dp)])]
    ppermute x24 -> x36, waiting for transfers between devices: 75.6 us -> 92.7 us  [swap(): lax.ppermute(arr, 'dp', [(i, i ^ 1 << bit) for i in range(self.n_dp)])]
    pallas_call x21 -> x27, Pallas kernels: 405 us -> 391 us  [__call__(): pl.pallas_call(body, grid_spec=spec, out_shape=out_shape, compiler_params...]
  transfers between devices with their start and end apart: 34 -> 48, of which waited for: 12 -> 24; matrix products, arithmetic and copies ran while one was open for 6% -> 7% of each run, Pallas kernels for 34% -> 38%
where the time goes in v3:
time: 608 us; the launch traced here: 600 us
  Pallas kernels  391 us (64%)
  waiting for transfers between devices  110 us (18%)
  starting transfers between devices  42.4 us (7%)
  local copies, waits for them, and re-layouts  23.1 us (4%)
  other arithmetic  20.4 us (3%)
  matrix products  11.3 us (2%)
    pallas_call x27, Pallas kernels, __call__(): pl.pallas_call(body, grid_spec=spec, out_shape=out_shape, compiler_params...  391 us
    ppermute x36, waiting for transfers between devices, swap(): lax.ppermute(arr, 'dp', [(i, i ^ 1 << bit) for i in range(self.n_dp)])  92.7 us
    ppermute x36, starting transfers between devices, swap(): lax.ppermute(arr, 'dp', [(i, i ^ 1 << bit) for i in range(self.n_dp)])  29.4 us
    ppermute x12, waiting for transfers between devices, swap(): return lax.ppermute(arr, 'mod', [(i, i ^ 1) for i in range(self.n_mod)])  16.8 us
    ppermute x12, starting transfers between devices, swap(): return lax.ppermute(arr, 'mod', [(i, i ^ 1) for i in range(self.n_mod)])  13 us
  transfers between devices with their start and end apart: 48, of which 24 were waited for; matrix products, arithmetic and copies ran while one was open for 7% of the time, Pallas kernels for 38%

profile of v3, /device:TPU:0, one launch (start us, length us, event | category | flops | bytes accessed | tf_op | source)
XLA Modules:
  0.0 599.7 jit_solution(14310455900121513663)
XLA Ops:
  0.6 3.0 collective-permute-start
  7.1 4.4 convolution_convert_fusion
  16.3 29.1 %project.1 = (bf16[8,144,1024]{2,1,0:T(8,128)(2,1)}, f32[1024,2304]{1,0:T(8,128)}, f32[1024,256]{1,0:T(8,128)}, bf16[1024,1152]{1,0:T(8,128)(2,1)}, bf16[1024,11...) custom-call(s32[4]{0:T(128)} %bitcast.142, bf16[1024,1152]{1,0:T(8,128)(2,1)} %bitcast.131, ...), custom_call_target="tpu_custom_call" | custom-call | flops 13589544960 | bytes 40000000 | tf_op jit(solution)/shard_map/project/pallas_call | solution.py:412
  45.4 57.6 %attend.1 = (f32[1024,1152]{1,0:T(8,128)}, f32[128,1024]{1,0:T(8,128)}, f32[1024,1152]{1,0:T(8,128)}, f32[1024,1152]{1,0:T(8,128)}, bf16[1024,1152]{1,0:T(8,128)...) custom-call(s32[4]{0:T(128)} %bitcast.143, ...), custom_call_target="tpu_custom_call" | custom-call | flops 27179089920 | bytes 40000000 | tf_op jit(solution)/shard_map/attend/pallas_call | solution.py:412
  103.0 68.0 %ffn.1 = (bf16[4,2,4,96,1024]{4,3,2,1,0:T(8,128)(2,1)}, bf16[1024,3072]{1,0:T(8,128)(2,1)}, bf16[1024,3072]{1,0:T(8,128)(2,1)}, f32[1024,1152]{1,0:T(8,128)}, f32[1024,1152]{1,0:T(8,128)}) custom-call(bf16[8,144,1024]{2,1,0:T(8,128)(2,1)} %get-tuple-element.77.refs_0_.refs_2_, bf16[1024,1152]{1,0:T(8,128)(2,1)} %get-tuple-element.78.refs_1_, ...), custom_call_target="tpu_custom_call" | custom-call | flops 43486543872 | bytes 60000000 | tf_op jit(solution)/shard_map/ffn/pallas_call | solution.py:412
  171.0 8.2 %gate_send.1.refs_1_ = bf16[4,144,3072]{2,1,0:T(8,128)(2,1)} custom-call(s32[1]{0:T(128)} %bitcast.1.refs_0_, f32[1024,1152]{1,0:T(8,128)} %get-tuple-element.80.refs_1_.refs_4_, bf16[8,144,1024]{2,1,0:T(8,128)(2,1)} %get-tuple-element.77.refs_0_.refs_2_, bf16[1024,3072]{1,0:T(8,128)(2,1)} %get-tuple-element.81.refs_3_), custom_call_target="tpu_custom_call" | custom-call | flops 3623878656 | bytes 11010048 | tf_op jit(solution)/shard_map/gate_send/pallas_call | solution.py:412
  179.2 7.8 %up_send.1.refs_1_ = bf16[4,144,3072]{2,1,0:T(8,128)(2,1)} custom-call(s32[1]{0:T(128)} %bitcast.1.refs_0_, bf16[4,144,3072]{2,1,0:T(8,128)(2,1)} %gate_send.1.refs_1_, bf16[8,144,1024]{2,1,0:T(8,128)(2,1)} %get-tuple-element.77.refs_0_.refs_2_, bf16[1024,3072]{1,0:T(8,128)(2,1)} %get-tuple-element.82.refs_3_), custom_call_target="tpu_custom_call" | custom-call | flops 3623878656 | bytes 11010048 | tf_op jit(solution)/shard_map/up_send/pallas_call | solution.py:412
  187.5 8.8 %down_send.1.refs_1_ = bf16[4,384,1152]{2,1,0:T(8,128)(2,1)} custom-call(s32[1]{0:T(128)} %bitcast.1.refs_0_, bf16[4,144,3072]{2,1,0:T(8,128)(2,1)} %up_send.1.refs_1_, bf16[8,384,1024]{2,1,0:T(8,128)(2,1)} %bitcast.125, bf16[1024,1152]{1,0:T(8,128)(2,1)} %get-tuple-element.79.refs_2_.refs_3_), custom_call_target="tpu_custom_call" | custom-call | flops 3623878656 | bytes 9043968 | tf_op jit(solution)/shard_map/down_send/pallas_call | solution.py:412
  197.6 18.1 %middle.1 = (bf16[1024,1152]{1,0:T(8,128)(2,1)}, f32[1024,1152]{1,0:T(8,128)}, bf16[1024,1152]{1,0:T(8,128)(2,1)}, bf16[1024,1152]{1,0:T(8,128)(2,1)}, f32[128,1024]{1,0:T(8,128)}, /*index=5*/f32[4,4,1152]{2,1,0:T(4,128)}) custom-call(s32[4]{0:T(128)} %bitcast.144, bf16[4,384,1152]{2,1,0:T(8,128)(2,1)} %down_send.1.refs_1_, ...), custom_call_target="tpu_custom_call" | custom-call | flops 2717908992 | bytes 40000000 | tf_op jit(solution)/shard_map/middle/pallas_call | solution.py:412
  215.8 9.8 %gate_keep.1 = (bf16[2,144,3072]{2,1,0:T(8,128)(2,1)}, f32[2,144,3072]{2,1,0:T(8,128)}) custom-call(s32[6]{0:T(128)} %stack.70.refs_0_, f32[4,4,1152]{2,1,0:T(4,128)} %get-tuple-element.89.refs_1_, bf16[8,144,1024]{2,1,0:T(8,128)(2,1)} %get-tuple-element.77.refs_0_.refs_2_, bf16[1024,3072]{1,0:T(8,128)(2,1)} %get-tuple-element.81.refs_3_, ...), custom_call_target="tpu_custom_call" | custom-call | flops 3623878656 | bytes 16318464 | tf_op jit(solution)/shard_map/gate_keep/pallas_call | solution.py:412
  227.3 10.0 %up_keep.1 = (bf16[2,144,3072]{2,1,0:T(8,128)(2,1)}, f32[2,144,3072]{2,1,0:T(8,128)}) custom-call(s32[6]{0:T(128)} %stack.76.refs_0_, f32[2,144,3072]{2,1,0:T(8,128)} %get-tuple-element.90.refs_1_.refs_2_, bf16[8,144,1024]{2,1,0:T(8,128)(2,1)} %get-tuple-element.77.refs_0_.refs_2_, bf16[1024,3072]{1,0:T(8,128)(2,1)} %get-tuple-element.82.refs_3_, ...), custom_call_target="tpu_custom_call" | custom-call | flops 3623878656 | bytes 16318464 | tf_op jit(solution)/shard_map/up_keep/pallas_call | solution.py:412
  237.4 4.8 out_send.1.refs_1_
  242.5 3.5 collective-permute-start.7
  246.0 11.8 %down_keep.1 = (bf16[2,384,1152]{2,1,0:T(8,128)(2,1)}, f32[2,384,1152]{2,1,0:T(8,128)}) custom-call(s32[6]{0:T(128)} %stack.70.refs_0_, bf16[4,144,1152]{2,1,0:T(8,128)(2,1)} %out_send.1.refs_1_, bf16[8,384,1024]{2,1,0:T(8,128)(2,1)} %bitcast.126, bf16[1024,1152]{1,0:T(8,128)(2,1)} %get-tuple-element.79.refs_2_.refs_3_, ...), custom_call_target="tpu_custom_call" | custom-call | flops 3623878656 | bytes 14352384 | tf_op jit(solution)/shard_map/down_keep/pallas_call | solution.py:412
  258.9 6.3 %out_keep.1 = (bf16[2,144,1152]{2,1,0:T(8,128)(2,1)}, f32[2,144,1152]{2,1,0:T(8,128)}) custom-call(s32[6]{0:T(128)} %stack.76.refs_0_, f32[2,384,1152]{2,1,0:T(8,128)} %get-tuple-element.94.refs_1_.refs_2_, bf16[8,144,1024]{2,1,0:T(8,128)(2,1)} %get-tuple-element.92.refs_2_, bf16[1024,1152]{1,0:T(8,128)(2,1)} %get-tuple-element.93.refs_3_, ...), custom_call_target="tpu_custom_call" | custom-call | flops 1358954496 | bytes 6856704 | tf_op jit(solution)/shard_map/out_keep/pallas_call | solution.py:412
  265.1 56.3 %attend_back.1 = (f32[1152,1024]{1,0:T(8,128)}, f32[1024,1152]{1,0:T(8,128)}, bf16[1024,1152]{1,0:T(8,128)(2,1)}) custom-call(s32[4]{0:T(128)} %bitcast.145, f32[2,144,1152]{2,1,0:T(8,128)} %get-tuple-element.95.refs_1_.refs_2_, bf16[1024,1152]{1,0:T(8,128)(2,1)} %get-tuple-element.74.refs_5_.refs_2_.refs_7_, ...), custom_call_target="tpu_custom_call" | custom-call | flops 59793997824 | bytes 40000000 | tf_op jit(solution)/shard_map/attend_back/pallas_call | solution.py:412
  321.4 4.8 v_send.1.refs_1_
  328.5 5.5 gate_fold.1
  335.2 5.4 up_fold.1
  344.1 6.2 %v_keep.1 = (bf16[2,144,1152]{2,1,0:T(8,128)(2,1)}, f32[2,144,1152]{2,1,0:T(8,128)}) custom-call(s32[6]{0:T(128)} %stack.70.refs_0_, f32[144,3072]{1,0:T(8,128)} %get-tuple-element.104.refs_1_, bf16[8,144,1024]{2,1,0:T(8,128)(2,1)} %get-tuple-element.100.refs_2_, bf16[1024,1152]{1,0:T(8,128)(2,1)} %get-tuple-element.99.refs_1_.refs_3_.refs_4_, ...), custom_call_target="tpu_custom_call" | custom-call | flops 1358954496 | bytes 6856704 | tf_op jit(solution)/shard_map/v_keep/pallas_call | solution.py:412
  350.3 3.2 out_fold.1
  353.5 32.7 %project_back.1 = (bf16[1024,1152]{1,0:T(8,128)(2,1)}, bf16[1024,1152]{1,0:T(8,128)(2,1)}, bf16[1024,1152]{1,0:T(8,128)(2,1)}, f32[4,2,1152]{2,1,0:T(2,128)}, f32[2,1152]{1,0:T(2,128)}) custom-call(s32[4]{0:T(128)} %bitcast.146, f32[144,1152]{1,0:T(8,128)} %get-tuple-element.107.refs_1_, f32[1152,1024]{1,0:T(8,128)} %get-tuple-element.108.refs_2_, ...), custom_call_target="tpu_custom_call" | custom-call | flops 10871635968 | bytes 50000000 | tf_op jit(solution)/shard_map/project_back/pallas_call | solution.py:412
  387.0 4.8 q_send.1.refs_1_
  391.8 4.8 k_send.1.refs_1_
  398.4 5.0 down_fold.1
  416.9 8.3 %collective-permute-done.33 = f32[2,72]{1,0:T(2,128)S(1)} collective-permute-done((f32[2,72]{1,0:T(2,128)S(1)}, f32[2,72]{1,0:T(2,128)S(1)}, u32[]{:S(2)}, u32[]{:S(2)}) %collective-permute-start.33) | collective-permute-done | bytes 608 | tf_op jit(solution)/shard_map/ppermute | solution.py:447
  437.3 5.6 fusion
  444.9 3.0 collective-permute-done.11
  449.2 3.8 collective-permute-done.13
  454.5 6.1 %collective-permute-done.36 = bf16[144,1152]{1,0:T(8,128)(2,1)S(1)} collective-permute-done((bf16[144,1152]{1,0:T(8,128)(2,1)S(1)}, bf16[144,1152]{1,0:T(8,128)(2,1)S(1)}, u32[]{:S(2)}, u32[]{:S(2)}) %collective-permute-start.36) | collective-permute-done | bytes 331808 | tf_op jit(solution)/shard_map/ppermute | solution.py:446
  464.3 7.9 %collective-permute-done.40 = bf16[2,36,3072]{2,1,0:T(8,128)(2,1)} collective-permute-done((bf16[2,36,3072]{2,1,0:T(8,128)(2,1)}, bf16[2,36,3072]{2,1,0:T(8,128)(2,1)}, u32[]{:S(2)}, u32[]{:S(2)}) %collective-permute-start.40) | collective-permute-done | bytes 442400 | tf_op jit(solution)/shard_map/ppermute | solution.py:447
  474.6 5.2 collective-permute-done.37
  480.3 7.1 %collective-permute-done.14 = bf16[32,4608]{1,0:T(8,128)(2,1)S(1)} collective-permute-done((bf16[32,4608]{1,0:T(8,128)(2,1)S(1)}, bf16[32,4608]{1,0:T(8,128)(2,1)S(1)}, u32[]{:S(2)}, u32[]{:S(2)}) %collective-permute-start.14) | collective-permute-done | bytes 294944 | tf_op jit(solution)/shard_map/ppermute | solution.py:447
  488.8 6.0 %collective-permute-done.38 = bf16[36,1152]{1,0:T(8,128)(2,1)S(1)} collective-permute-done((bf16[36,1152]{1,0:T(8,128)(2,1)S(1)}, bf16[36,1152]{1,0:T(8,128)(2,1)S(1)}, u32[]{:S(2)}, u32[]{:S(2)}) %collective-permute-start.38) | collective-permute-done | bytes 82976 | tf_op jit(solution)/shard_map/ppermute | solution.py:447
  495.5 20.0 %collective-permute-done.44 = bf16[36,3072]{1,0:T(8,128)(2,1)S(1)} collective-permute-done((bf16[36,3072]{1,0:T(8,128)(2,1)S(1)}, bf16[36,3072]{1,0:T(8,128)(2,1)S(1)}, u32[]{:S(2)}, u32[]{:S(2)}) %collective-permute-start.44) | collective-permute-done | bytes 221216 | tf_op jit(solution)/shard_map/ppermute | solution.py:447
  516.4 2.9 collective-permute-start.15
  519.3 3.3 v_fold.1
  522.6 8.8 %collective-permute-done.41 = bf16[36,3072]{1,0:T(8,128)(2,1)S(1)} collective-permute-done((bf16[36,3072]{1,0:T(8,128)(2,1)}, bf16[36,3072]{1,0:T(8,128)(2,1)S(1)}, u32[]{:S(2)}, u32[]{:S(2)}) %collective-permute-start.41) | collective-permute-done | bytes 221216 | tf_op jit(solution)/shard_map/ppermute | solution.py:447
  535.8 2.9 collective-permute-done.28
  543.8 4.5 collective-permute-done.29
  548.5 6.2 %q_keep.1 = (bf16[2,144,1152]{2,1,0:T(8,128)(2,1)}, f32[2,144,1152]{2,1,0:T(8,128)}) custom-call(s32[6]{0:T(128)} %stack.76.refs_0_, f32[144,1152]{1,0:T(8,128)} %get-tuple-element.121.refs_1_, bf16[8,144,1024]{2,1,0:T(8,128)(2,1)} %get-tuple-element.100.refs_2_, bf16[1024,1152]{1,0:T(8,128)(2,1)} %get-tuple-element.116.refs_3_, ...), custom_call_target="tpu_custom_call" | custom-call | flops 1358954496 | bytes 6856704 | tf_op jit(solution)/shard_map/q_keep/pallas_call | solution.py:412
  556.1 6.3 %k_keep.1 = (bf16[2,144,1152]{2,1,0:T(8,128)(2,1)}, f32[2,144,1152]{2,1,0:T(8,128)}) custom-call(s32[6]{0:T(128)} %stack.70.refs_0_, f32[2,144,1152]{2,1,0:T(8,128)} %get-tuple-element.122.refs_1_.refs_2_, bf16[8,144,1024]{2,1,0:T(8,128)(2,1)} %get-tuple-element.100.refs_2_, bf16[1024,1152]{1,0:T(8,128)(2,1)} %get-tuple-element.117.refs_3_, ...), custom_call_target="tpu_custom_call" | custom-call | flops 1358954496 | bytes 6856704 | tf_op jit(solution)/shard_map/k_keep/pallas_call | solution.py:412
  563.4 3.0 collective-permute-start.47
  566.4 3.2 q_fold.1
  575.5 3.2 k_fold.1
  581.5 4.5 collective-permute-done.25
  589.1 3.7 collective-permute-done.26
  594.6 3.8 collective-permute-done.27
  (205 shorter events, 88.7 us)
Async XLA Ops:
  0.6 5.0 collective-permute-start
  11.6 4.0 collective-permute-start.1
  179.2 36.6 %collective-permute-start.2 = (bf16[4,144,3072]{2,1,0:T(8,128)(2,1)}, bf16[4,144,3072]{2,1,0:T(8,128)(2,1)}, u32[]{:S(2)}, u32[]{:S(2)}) collective-permute-start(bf16[4,144,3072]{2,1,0:T(8,128)(2,1)} %gate_send.1.refs_1_), channel_id=1, source_target_pairs={{0,2},{2,0},{4,6},{6,4},{8,10},{10,8},{12,14},{14,12},{16,18},{18,... | collective-permute-start | bytes 10616840 | tf_op jit(solution)/shard_map/ppermute | solution.py:447
  187.0 38.6 %collective-permute-start.3 = (bf16[4,144,3072]{2,1,0:T(8,128)(2,1)}, bf16[4,144,3072]{2,1,0:T(8,128)(2,1)S(1)}, u32[]{:S(2)}, u32[]{:S(2)}) collective-permute-start(bf16[4,144,3072]{2,1,0:T(8,128)(2,1)} %up_send.1.refs_1_), channel_id=1, source_target_pairs={{0,2},{2,0},{4,6},{6,4},{8,10},{10,8},{12,14},{14,12},{16,18},{18,... | collective-permute-start | bytes 10616840 | tf_op jit(solution)/shard_map/ppermute | solution.py:447
  196.3 49.7 %collective-permute-start.4 = (bf16[4,384,1152]{2,1,0:T(8,128)(2,1)}, bf16[4,384,1152]{2,1,0:T(8,128)(2,1)}, u32[]{:S(2)}, u32[]{:S(2)}) collective-permute-start(bf16[4,384,1152]{2,1,0:T(8,128)(2,1)} %down_send.1.refs_1_), channel_id=1, source_target_pairs={{0,2},{2,0},{4,6},{6,4},{8,10},{10,8},{12,14},{14,12},{16,18},{18,... | collective-permute-start | bytes 10616840 | tf_op jit(solution)/shard_map/ppermute | solution.py:447
  242.2 15.6 %collective-permute-start.5 = (bf16[4,144,1152]{2,1,0:T(8,128)(2,1)}, bf16[4,144,1152]{2,1,0:T(8,128)(2,1)S(1)}, u32[]{:S(2)}, u32[]{:S(2)}) collective-permute-start(bf16[4,144,1152]{2,1,0:T(8,128)(2,1)} %out_send.1.refs_1_), channel_id=1, source_target_pairs={{0,2},{2,0},{4,6},{6,4},{8,10},{10,8},{12,14},{14,12},{16,18},{18,... | collective-permute-start | bytes 3981320 | tf_op jit(solution)/shard_map/ppermute | solution.py:447
  242.5 86.0 %collective-permute-start.6 = (bf16[2,144,3072]{2,1,0:T(8,128)(2,1)}, bf16[2,144,3072]{2,1,0:T(8,128)(2,1)}, u32[]{:S(2)}, u32[]{:S(2)}) collective-permute-start(bf16[2,144,3072]{2,1,0:T(8,128)(2,1)} %get-tuple-element.101), channel_id=1, source_target_pairs={{0,1},{1,0},{2,3},{3,2},{4,5},{5,4},{6,7},{7,6},{8,9},{9,8},{10,11... | collective-permute-start | bytes 5308424 | tf_op jit(solution)/shard_map/ppermute | solution.py:446
  242.5 91.4 %collective-permute-start.7 = (bf16[2,144,3072]{2,1,0:T(8,128)(2,1)}, bf16[2,144,3072]{2,1,0:T(8,128)(2,1)S(1)}, u32[]{:S(2)}, u32[]{:S(2)}) collective-permute-start(bf16[2,144,3072]{2,1,0:T(8,128)(2,1)} %get-tuple-element.103), channel_id=1, source_target_pairs={{0,4},{2,6},{4,0},{6,2},{8,12},{10,14},{12,8},{14,10},{16,20},{18,... | collective-permute-start | bytes 5308424 | tf_op jit(solution)/shard_map/ppermute | solution.py:447
  326.3 17.8 %collective-permute-start.8 = (bf16[4,144,1152]{2,1,0:T(8,128)(2,1)}, bf16[4,144,1152]{2,1,0:T(8,128)(2,1)}, u32[]{:S(2)}, u32[]{:S(2)}) collective-permute-start(bf16[4,144,1152]{2,1,0:T(8,128)(2,1)} %v_send.1.refs_1_), channel_id=1, source_target_pairs={{0,2},{2,0},{4,6},{6,4},{8,10},{10,8},{12,14},{14,12},{16,18},{18,... | collective-permute-start | bytes 3981320 | tf_op jit(solution)/shard_map/ppermute | solution.py:447
  326.3 24.0 %collective-permute-start.9 = (bf16[2,144,1152]{2,1,0:T(8,128)(2,1)}, bf16[2,144,1152]{2,1,0:T(8,128)(2,1)}, u32[]{:S(2)}, u32[]{:S(2)}) collective-permute-start(bf16[2,144,1152]{2,1,0:T(8,128)(2,1)} %get-tuple-element.106), channel_id=1, source_target_pairs={{0,4},{2,6},{4,0},{6,2},{8,12},{10,14},{12,8},{14,10},{16,20},{18,... | collective-permute-start | bytes 1990664 | tf_op jit(solution)/shard_map/ppermute | solution.py:447
  326.3 70.8 %collective-permute-start.16 = (bf16[2,384,1152]{2,1,0:T(8,128)(2,1)}, bf16[2,384,1152]{2,1,0:T(8,128)(2,1)S(1)}, u32[]{:S(2)}, u32[]{:S(2)}) collective-permute-start(bf16[2,384,1152]{2,1,0:T(8,128)(2,1)} %get-tuple-element.118), channel_id=1, source_target_pairs={{0,1},{1,0},{2,3},{3,2},{4,5},{5,4},{6,7},{7,6},{8,9},{9,8},{10,11... | collective-permute-start | bytes 5308424 | tf_op jit(solution)/shard_map/ppermute | solution.py:446
  340.6 62.8 %collective-permute-start.42 = (bf16[144,3072]{1,0:T(8,128)(2,1)}, bf16[144,3072]{1,0:T(8,128)(2,1)}, u32[]{:S(2)}, u32[]{:S(2)}) collective-permute-start(bf16[144,3072]{1,0:T(8,128)(2,1)} %get-tuple-element.133), channel_id=1, source_target_pairs={{0,1},{1,0},{2,3},{3,2},{4,5},{5,4},{6,7},{7,6},{8,9},{9,8},{10,11... | collective-permute-start | bytes 2654216 | tf_op jit(solution)/shard_map/ppermute | solution.py:446
  342.1 68.9 %collective-permute-start.39 = (bf16[144,3072]{1,0:T(8,128)(2,1)}, bf16[144,3072]{1,0:T(8,128)(2,1)}, u32[]{:S(2)}, u32[]{:S(2)}) collective-permute-start(bf16[144,3072]{1,0:T(8,128)(2,1)} %get-tuple-element.132), channel_id=1, source_target_pairs={{0,4},{2,6},{4,0},{6,2},{8,12},{10,14},{12,8},{14,10},{16,20},{18,... | collective-permute-start | bytes 2654216 | tf_op jit(solution)/shard_map/ppermute | solution.py:447
  391.8 156.7 %collective-permute-start.18 = (bf16[4,144,1152]{2,1,0:T(8,128)(2,1)}, bf16[4,144,1152]{2,1,0:T(8,128)(2,1)}, u32[]{:S(2)}, u32[]{:S(2)}) collective-permute-start(bf16[4,144,1152]{2,1,0:T(8,128)(2,1)} %q_send.1.refs_1_), channel_id=1, source_target_pairs={{0,2},{2,0},{4,6},{6,4},{8,10},{10,8},{12,14},{14,12},{16,18},{18,... | collective-permute-start | bytes 3981320 | tf_op jit(solution)/shard_map/ppermute | solution.py:447
  396.6 159.4 %collective-permute-start.19 = (bf16[4,144,1152]{2,1,0:T(8,128)(2,1)}, bf16[4,144,1152]{2,1,0:T(8,128)(2,1)}, u32[]{:S(2)}, u32[]{:S(2)}) collective-permute-start(bf16[4,144,1152]{2,1,0:T(8,128)(2,1)} %k_send.1.refs_1_), channel_id=1, source_target_pairs={{0,2},{2,0},{4,6},{6,4},{8,10},{10,8},{12,14},{14,12},{16,18},{18,... | collective-permute-start | bytes 3981320 | tf_op jit(solution)/shard_map/ppermute | solution.py:447
  403.4 130.2 %collective-permute-start.45 = (bf16[384,1152]{1,0:T(8,128)(2,1)}, bf16[384,1152]{1,0:T(8,128)(2,1)}, u32[]{:S(2)}, u32[]{:S(2)}) collective-permute-start(bf16[384,1152]{1,0:T(8,128)(2,1)} %get-tuple-element.134), channel_id=1, source_target_pairs={{0,4},{2,6},{4,0},{6,2},{8,12},{10,14},{12,8},{14,10},{16,20},{18,... | collective-permute-start | bytes 2654216 | tf_op jit(solution)/shard_map/ppermute | solution.py:447
  408.2 53.1 %collective-permute-start.43 = (bf16[2,36,3072]{2,1,0:T(8,128)(2,1)}, bf16[2,36,3072]{2,1,0:T(8,128)(2,1)}, u32[]{:S(2)}, u32[]{:S(2)}) collective-permute-start(bf16[2,36,3072]{2,1,0:T(8,128)(2,1)} %fusion.5), channel_id=1, source_target_pairs={{0,8},{2,10},{4,12},{6,14},{8,0},{10,2},{12,4},{14,6},{16,24},{18,... | collective-permute-start | bytes 1327112 | tf_op jit(solution)/shard_map/ppermute | solution.py:447
  410.9 1.4 collective-permute-start.31
  413.0 3.6 collective-permute-start.32
  416.6 8.7 %collective-permute-start.33 = (f32[2,72]{1,0:T(2,128)S(1)}, f32[2,72]{1,0:T(2,128)S(1)}, u32[]{:S(2)}, u32[]{:S(2)}) collective-permute-start(f32[2,72]{1,0:T(2,128)S(1)} %add.194), channel_id=1, source_target_pairs={{0,4},{2,6},{4,0},{6,2},{8,12},{10,14},{12,8},{14,10},{16,20},{18,... | collective-permute-start | bytes 1736 | tf_op jit(solution)/shard_map/ppermute | solution.py:447
  425.3 3.6 collective-permute-start.34
  428.8 4.5 collective-permute-start.35
  433.3 3.9 collective-permute-start.10
  442.9 1.3 collective-permute-start.12
  444.2 3.7 collective-permute-start.11
  447.9 5.1 collective-permute-start.13
  453.0 7.6 %collective-permute-start.36 = (bf16[144,1152]{1,0:T(8,128)(2,1)S(1)}, bf16[144,1152]{1,0:T(8,128)(2,1)S(1)}, u32[]{:S(2)}, u32[]{:S(2)}) collective-permute-start(bf16[144,1152]{1,0:T(8,128)(2,1)S(1)} %copy-done.21), channel_id=1, source_target_pairs={{0,1},{1,0},{2,3},{3,2},{4,5},{5,4},{6,7},{7,6},{8,9},{9,8},{10,11... | collective-permute-start | bytes 995336 | tf_op jit(solution)/shard_map/ppermute | solution.py:446
  460.6 11.6 %collective-permute-start.40 = (bf16[2,36,3072]{2,1,0:T(8,128)(2,1)}, bf16[2,36,3072]{2,1,0:T(8,128)(2,1)}, u32[]{:S(2)}, u32[]{:S(2)}) collective-permute-start(bf16[2,36,3072]{2,1,0:T(8,128)(2,1)} %fusion.4), channel_id=1, source_target_pairs={{0,8},{2,10},{4,12},{6,14},{8,0},{10,2},{12,4},{14,6},{16,24},{18,... | collective-permute-start | bytes 1327112 | tf_op jit(solution)/shard_map/ppermute | solution.py:447
  461.3 55.0 %collective-permute-start.17 = (bf16[2,144,1152]{2,1,0:T(8,128)(2,1)}, bf16[2,144,1152]{2,1,0:T(8,128)(2,1)S(1)}, u32[]{:S(2)}, u32[]{:S(2)}) collective-permute-start(bf16[2,144,1152]{2,1,0:T(8,128)(2,1)} %get-tuple-element.120), channel_id=1, source_target_pairs={{0,1},{1,0},{2,3},{3,2},{4,5},{5,4},{6,7},{7,6},{8,9},{9,8},{10,11... | collective-permute-start | bytes 1990664 | tf_op jit(solution)/shard_map/ppermute | solution.py:446
  472.2 7.5 %collective-permute-start.37 = (bf16[2,36,1152]{2,1,0:T(8,128)(2,1)S(1)}, bf16[2,36,1152]{2,1,0:T(8,128)(2,1)S(1)}, u32[]{:S(2)}, u32[]{:S(2)}) collective-permute-start(bf16[2,36,1152]{2,1,0:T(8,128)(2,1)S(1)} %fusion.11), channel_id=1, source_target_pairs={{0,8},{2,10},{4,12},{6,14},{8,0},{10,2},{12,4},{14,6},{16,24},{18,... | collective-permute-start | bytes 497672 | tf_op jit(solution)/shard_map/ppermute | solution.py:447
  479.7 7.7 %collective-permute-start.14 = (bf16[32,4608]{1,0:T(8,128)(2,1)S(1)}, bf16[32,4608]{1,0:T(8,128)(2,1)S(1)}, u32[]{:S(2)}, u32[]{:S(2)}) collective-permute-start(bf16[32,4608]{1,0:T(8,128)(2,1)S(1)} %copy-done.13), channel_id=1, source_target_pairs={{0,8},{2,10},{4,12},{6,14},{8,0},{10,2},{12,4},{14,6},{16,24},{18,... | collective-permute-start | bytes 884744 | tf_op jit(solution)/shard_map/ppermute | solution.py:447
  487.4 7.4 %collective-permute-start.38 = (bf16[36,1152]{1,0:T(8,128)(2,1)S(1)}, bf16[36,1152]{1,0:T(8,128)(2,1)S(1)}, u32[]{:S(2)}, u32[]{:S(2)}) collective-permute-start(bf16[36,1152]{1,0:T(8,128)(2,1)S(1)} %fusion.17), channel_id=1, source_target_pairs={{0,16},{2,18},{4,20},{6,22},{8,24},{10,26},{12,28},{14,30},{16,0},... | collective-permute-start | bytes 248840 | tf_op jit(solution)/shard_map/ppermute | solution.py:447
  494.8 20.7 %collective-permute-start.44 = (bf16[36,3072]{1,0:T(8,128)(2,1)S(1)}, bf16[36,3072]{1,0:T(8,128)(2,1)S(1)}, u32[]{:S(2)}, u32[]{:S(2)}) collective-permute-start(bf16[36,3072]{1,0:T(8,128)(2,1)S(1)} %fusion.8), channel_id=1, source_target_pairs={{0,16},{2,18},{4,20},{6,22},{8,24},{10,26},{12,28},{14,30},{16,0},... | collective-permute-start | bytes 663560 | tf_op jit(solution)/shard_map/ppermute | solution.py:447
  515.5 15.9 %collective-permute-start.41 = (bf16[36,3072]{1,0:T(8,128)(2,1)}, bf16[36,3072]{1,0:T(8,128)(2,1)S(1)}, u32[]{:S(2)}, u32[]{:S(2)}) collective-permute-start(bf16[36,3072]{1,0:T(8,128)(2,1)} %fusion.7), channel_id=1, source_target_pairs={{0,16},{2,18},{4,20},{6,22},{8,24},{10,26},{12,28},{14,30},{16,0},... | collective-permute-start | bytes 663560 | tf_op jit(solution)/shard_map/ppermute | solution.py:447
  516.4 24.5 %collective-permute-start.15 = (bf16[64,4608]{1,0:T(8,128)(2,1)S(1)}, bf16[64,4608]{1,0:T(8,128)(2,1)}, u32[]{:S(2)}, u32[]{:S(2)}) collective-permute-start(bf16[64,4608]{1,0:T(8,128)(2,1)S(1)} %maximum_select_fusion.1), channel_id=1, source_target_pairs={{0,16},{2,18},{4,20},{6,22},{8,24},{10,26},{12,28},{14,30},{16,0},... | collective-permute-start | bytes 1769480 | tf_op jit(solution)/shard_map/ppermute | solution.py:447
  531.4 7.3 %collective-permute-start.28 = (bf16[144,1152]{1,0:T(8,128)(2,1)}, bf16[144,1152]{1,0:T(8,128)(2,1)S(1)}, u32[]{:S(2)}, u32[]{:S(2)}) collective-permute-start(bf16[144,1152]{1,0:T(8,128)(2,1)} %get-tuple-element.130), channel_id=1, source_target_pairs={{0,4},{2,6},{4,0},{6,2},{8,12},{10,14},{12,8},{14,10},{16,20},{18,... | collective-permute-start | bytes 995336 | tf_op jit(solution)/shard_map/ppermute | solution.py:447
  535.8 27.4 %collective-permute-start.46 = (bf16[2,96,1152]{2,1,0:T(8,128)(2,1)}, bf16[2,96,1152]{2,1,0:T(8,128)(2,1)S(1)}, u32[]{:S(2)}, u32[]{:S(2)}) collective-permute-start(bf16[2,96,1152]{2,1,0:T(8,128)(2,1)} %fusion.6), channel_id=1, source_target_pairs={{0,8},{2,10},{4,12},{6,14},{8,0},{10,2},{12,4},{14,6},{16,24},{18,... | collective-permute-start | bytes 1327112 | tf_op jit(solution)/shard_map/ppermute | solution.py:447
  540.8 7.5 %collective-permute-start.29 = (bf16[2,36,1152]{2,1,0:T(8,128)(2,1)S(1)}, bf16[2,36,1152]{2,1,0:T(8,128)(2,1)S(1)}, u32[]{:S(2)}, u32[]{:S(2)}) collective-permute-start(bf16[2,36,1152]{2,1,0:T(8,128)(2,1)S(1)} %fusion.13), channel_id=1, source_target_pairs={{0,8},{2,10},{4,12},{6,14},{8,0},{10,2},{12,4},{14,6},{16,24},{18,... | collective-permute-start | bytes 497672 | tf_op jit(solution)/shard_map/ppermute | solution.py:447
  548.4 18.0 %collective-permute-start.30 = (bf16[36,1152]{1,0:T(8,128)(2,1)S(1)}, bf16[36,1152]{1,0:T(8,128)(2,1)S(1)}, u32[]{:S(2)}, u32[]{:S(2)}) collective-permute-start(bf16[36,1152]{1,0:T(8,128)(2,1)S(1)} %fusion.16), channel_id=1, source_target_pairs={{0,16},{2,18},{4,20},{6,22},{8,24},{10,26},{12,28},{14,30},{16,0},... | collective-permute-start | bytes 248840 | tf_op jit(solution)/shard_map/ppermute | solution.py:447
  554.7 11.7 %collective-permute-start.20 = (bf16[2,144,1152]{2,1,0:T(8,128)(2,1)}, bf16[2,144,1152]{2,1,0:T(8,128)(2,1)}, u32[]{:S(2)}, u32[]{:S(2)}) collective-permute-start(bf16[2,144,1152]{2,1,0:T(8,128)(2,1)} %get-tuple-element.124), channel_id=1, source_target_pairs={{0,4},{2,6},{4,0},{6,2},{8,12},{10,14},{12,8},{14,10},{16,20},{18,... | collective-permute-start | bytes 1990664 | tf_op jit(solution)/shard_map/ppermute | solution.py:447
  562.4 13.1 %collective-permute-start.24 = (bf16[2,144,1152]{2,1,0:T(8,128)(2,1)}, bf16[2,144,1152]{2,1,0:T(8,128)(2,1)}, u32[]{:S(2)}, u32[]{:S(2)}) collective-permute-start(bf16[2,144,1152]{2,1,0:T(8,128)(2,1)} %get-tuple-element.127), channel_id=1, source_target_pairs={{0,1},{1,0},{2,3},{3,2},{4,5},{5,4},{6,7},{7,6},{8,9},{9,8},{10,11... | collective-permute-start | bytes 1990664 | tf_op jit(solution)/shard_map/ppermute | solution.py:446
  563.4 9.3 %collective-permute-start.47 = (bf16[96,1152]{1,0:T(8,128)(2,1)S(1)}, bf16[96,1152]{1,0:T(8,128)(2,1)S(1)}, u32[]{:S(2)}, u32[]{:S(2)}) collective-permute-start(bf16[96,1152]{1,0:T(8,128)(2,1)S(1)} %fusion.9), channel_id=1, source_target_pairs={{0,16},{2,18},{4,20},{6,22},{8,24},{10,26},{12,28},{14,30},{16,0},... | collective-permute-start | bytes 663560 | tf_op jit(solution)/shard_map/ppermute | solution.py:447
  569.6 10.2 %collective-permute-start.21 = (bf16[144,1152]{1,0:T(8,128)(2,1)}, bf16[144,1152]{1,0:T(8,128)(2,1)S(1)}, u32[]{:S(2)}, u32[]{:S(2)}) collective-permute-start(bf16[144,1152]{1,0:T(8,128)(2,1)} %get-tuple-element.126), channel_id=1, source_target_pairs={{0,1},{1,0},{2,3},{3,2},{4,5},{5,4},{6,7},{7,6},{8,9},{9,8},{10,11... | collective-permute-start | bytes 995336 | tf_op jit(solution)/shard_map/ppermute | solution.py:446
  578.7 7.3 %collective-permute-start.25 = (bf16[144,1152]{1,0:T(8,128)(2,1)}, bf16[144,1152]{1,0:T(8,128)(2,1)S(1)}, u32[]{:S(2)}, u32[]{:S(2)}) collective-permute-start(bf16[144,1152]{1,0:T(8,128)(2,1)} %get-tuple-element.129), channel_id=1, source_target_pairs={{0,4},{2,6},{4,0},{6,2},{8,12},{10,14},{12,8},{14,10},{16,20},{18,... | collective-permute-start | bytes 995336 | tf_op jit(solution)/shard_map/ppermute | solution.py:447
  580.6 6.1 %collective-permute-start.22 = (bf16[2,36,1152]{2,1,0:T(8,128)(2,1)}, bf16[2,36,1152]{2,1,0:T(8,128)(2,1)S(1)}, u32[]{:S(2)}, u32[]{:S(2)}) collective-permute-start(bf16[2,36,1152]{2,1,0:T(8,128)(2,1)} %fusion.10), channel_id=1, source_target_pairs={{0,8},{2,10},{4,12},{6,14},{8,0},{10,2},{12,4},{14,6},{16,24},{18,... | collective-permute-start | bytes 497672 | tf_op jit(solution)/shard_map/ppermute | solution.py:447
  586.2 6.6 %collective-permute-start.26 = (bf16[2,36,1152]{2,1,0:T(8,128)(2,1)S(1)}, bf16[2,36,1152]{2,1,0:T(8,128)(2,1)S(1)}, u32[]{:S(2)}, u32[]{:S(2)}) collective-permute-start(bf16[2,36,1152]{2,1,0:T(8,128)(2,1)S(1)} %fusion.12), channel_id=1, source_target_pairs={{0,8},{2,10},{4,12},{6,14},{8,0},{10,2},{12,4},{14,6},{16,24},{18,... | collective-permute-start | bytes 497672 | tf_op jit(solution)/shard_map/ppermute | solution.py:447
  586.8 7.8 %collective-permute-start.23 = (bf16[36,1152]{1,0:T(8,128)(2,1)S(1)}, bf16[36,1152]{1,0:T(8,128)(2,1)S(1)}, u32[]{:S(2)}, u32[]{:S(2)}) collective-permute-start(bf16[36,1152]{1,0:T(8,128)(2,1)S(1)} %fusion.14), channel_id=1, source_target_pairs={{0,16},{2,18},{4,20},{6,22},{8,24},{10,26},{12,28},{14,30},{16,0},... | collective-permute-start | bytes 248840 | tf_op jit(solution)/shard_map/ppermute | solution.py:447
  592.9 5.5 collective-permute-start.27
  (22 other events, 185.0 us)

commit v4 on v3

--- a/solution.py
+++ b/solution.py
@@ -81,13 +81,20 @@
     return (dp % 2) * 2 * n_mod + mod * 2 + (dp // 2) % 2, dp // 4
 
 
+def reversed_bits(value, size):
+    result = 0
+    for bit in range(size.bit_length() - 1):
+        result = 2 * result + (value >> bit) % 2
+    return result
+
+
 @functools.lru_cache(None)
 def unit_permutation(width, n_dp, n_mod):
     rows = width // (n_dp * n_mod)
     matrix = np.zeros((width, width), np.float32)
     for index in range(n_dp * n_mod):
         unit, rest = unit_of(index, n_mod)
-        start = unit * (width // 8) + rest * rows
+        start = unit * (width // 8) + reversed_bits(rest, n_dp // 4) * rows
         matrix[start + np.arange(rows), index * rows + np.arange(rows)] = 1.0
     return matrix.astype(jnp.bfloat16)
 
@@ -145,6 +152,19 @@
 def head_lanes(offset):
     lane = lax.broadcasted_iota(jnp.int32, (1, WIN), 1)
     return (lane >= offset) & (lane < offset + HD)
+
+
+def product(units_ref, half, rhs, out_ref):
+    _, rows, tokens = units_ref.shape
+    units = units_ref[pl.ds(4 * half, 4)].reshape(4 * rows, tokens)
+    out_ref[...] = nn(units, rhs).astype(bf16).reshape(out_ref.shape)
+
+
+def halves_out(acc_ref, core, send_ref, own_ref):
+    rows = acc_ref.shape[0] // 2
+    for half, out_ref in ((1 - core, send_ref), (core, own_ref)):
+        start = pl.multiple_of(half * rows, rows)
+        out_ref[...] = acc_ref[pl.ds(start, rows)].astype(bf16).reshape(out_ref.shape)
 
 
 def project_kernel(
@@ -225,43 +245,48 @@
 
 
 def ffn_kernel(
-    x_ref, gf_ref, wg_ref, wu_ref, wd_ref, units_ref, dg_ref, du_ref, ffn_ref, dmod_ref, *, n_mod
+    bits, x_ref, gf_ref, units_ref, wg_ref, wu_ref, wd_ref,
+    gate_send_ref, gate_own_ref, up_send_ref, up_own_ref, down_send_ref, down_own_ref, ffn_ref, dmod_ref,
+    turned_ref, *, n_mod, rows_ff,
 ):
-    first = pl.program_id(0) == 0
+    core = bits[0]
     gate = nn(x_ref[...], wg_ref[...])
     up = nn(x_ref[...], wu_ref[...])
     grad_hidden = nt(gf_ref[...], wd_ref[...])
     sigmoid = 1.0 / (1.0 + jnp.exp(-gate))
     silu = gate * sigmoid
-    hidden = silu * up
-    rows = units_ref.shape[3]
-    turned = hidden.T.astype(bf16)
-    for index in range(turned.shape[0] // rows):
+    hidden = (silu * up).astype(bf16)
+    turned = hidden.T
+    for index in range(turned.shape[0] // rows_ff):
         unit, rest = unit_of(index, n_mod)
-        nxt = unit % 2 if units_ref.shape[1] == 2 else 0
-        units_ref[unit // 2, nxt, rest if units_ref.shape[1] == 2 else 0] = turned[
-            index * rows : (index + 1) * rows
+        turned_ref[unit, rest * rows_ff : (rest + 1) * rows_ff] = turned[
+            index * rows_ff : (index + 1) * rows_ff
         ]
     dg = (grad_hidden * up * (sigmoid * (1.0 + gate * (1.0 - sigmoid)))).astype(bf16)
     du = (grad_hidden * silu).astype(bf16)
-    dg_ref[...] = dg
-    du_ref[...] = du
-
-    @pl.when(first)
+
+    @pl.when(pl.program_id(0) == 0)
     def _():
         ffn_ref[...] = jnp.zeros_like(ffn_ref)
         dmod_ref[...] = jnp.zeros_like(dmod_ref)
 
-    ffn_ref[...] += nn(hidden.astype(bf16), wd_ref[...])
+    ffn_ref[...] += nn(hidden, wd_ref[...])
     dmod_ref[...] += nt(dg, wg_ref[...]) + nt(du, wu_ref[...])
+    product(units_ref, 1 - core, dg, gate_send_ref)
+    product(units_ref, 1 - core, du, up_send_ref)
+    product(turned_ref, 1 - core, gf_ref[...], down_send_ref)
+    product(units_ref, core, dg, gate_own_ref)
+    product(units_ref, core, du, up_own_ref)
+    product(turned_ref, core, gf_ref[...], down_own_ref)
 
 
 def middle_kernel(
-    slots, mid_ref, ffn_ref, dmod_ref, cot_ref, attn_ref, o_ref, mod_ref, w_out_ref, gather_ref,
-    out_ref, grad_mid_ref, ga_ref, do_ref, dot_ref, sums_ref,
+    slots, mid_ref, ffn_ref, dmod_ref, cot_ref, attn_ref, o_ref, units_ref, mod_ref, w_out_ref, gather_ref,
+    out_ref, grad_mid_ref, do_ref, dot_ref, sums_ref, send_ref, own_ref, acc_ref,
 ):
     width = mid_ref.shape[1]
-    slot = slots[pl.program_id(0)]
+    block = pl.program_id(0)
+    slot = slots[block]
     incoming = cot_ref[...].astype(f32)
     mid = mid_ref[...]
     out_ref[...] = (mid + part(mod_ref, slot, 5, width) * ffn_ref[...]).astype(bf16)
@@ -270,7 +295,20 @@
     grad_mid = incoming + norm_back(dmod, part(mod_ref, slot, 4, width), norm, inverse)
     grad_mid_ref[...] = grad_mid
     ga = (grad_mid * part(mod_ref, slot, 2, width)).astype(bf16)
-    ga_ref[...] = ga
+    grow = nn(units_ref[...].reshape(width, TB), ga)
+
+    @pl.when(block == 0)
+    def _():
+        acc_ref[...] = grow
+
+    @pl.when(block > 0)
+    def _():
+        acc_ref[...] += grow
+
+    @pl.when(block == pl.num_programs(0) - 1)
+    def _():
+        halves_out(acc_ref, slots[pl.num_programs(0)], send_ref, own_ref)
+
     do = nt(ga, w_out_ref[...]).astype(bf16)
     do_ref[...] = do
     dot_ref[...] = head_sum(do.astype(f32) * o_ref[...], gather_ref).T
@@ -331,19 +369,24 @@
 
 
 def project_back_kernel(
-    slots, dqt_ref, dk_ref, dv_ref, raw_ref, inv_ref, q_ref, k_ref, x_ref, grad_mid_ref, mod_ref,
+    slots, dqt_ref, dk_ref, dv_ref, raw_ref, inv_ref, q_ref, k_ref, x_ref, grad_mid_ref, units_ref, mod_ref,
     w_ref, coords_ref, cos_ref, sin_ref, gain_ref, gather_ref, spread_ref,
-    gq_ref, gk_ref, grad_x_ref, sums_ref, gains_ref,
+    grad_x_ref, sums_ref, gains_ref, q_send_ref, q_own_ref, k_send_ref, k_own_ref, accq_ref, acck_ref,
 ):
     width = x_ref.shape[1]
-    slot = slots[pl.program_id(0)]
-
-    @pl.when(pl.program_id(0) == 0)
+    block = pl.program_id(0)
+    slot = slots[block]
+
+    @pl.when(block == 0)
     def _():
         gains_ref[...] = jnp.zeros_like(gains_ref)
+        accq_ref[...] = jnp.zeros_like(accq_ref)
+        acck_ref[...] = jnp.zeros_like(acck_ref)
+
+    dmod = nt(dv_ref[...], w_ref[:, 2 * width :])
 
     cosine, sine = angles(coords_ref, cos_ref, sin_ref)
-    for index, (low_ref, gp_ref) in enumerate(((q_ref, gq_ref), (k_ref, gk_ref))):
+    for index, (low_ref, acc_ref) in enumerate(((q_ref, accq_ref), (k_ref, acck_ref))):
         grad = dqt_ref[...].T if index == 0 else dk_ref[...]
         raw = raw_ref[:, index * width : (index + 1) * width]
         inverse = head_spread(inv_ref[:, index * 128 : (index + 1) * 128], spread_ref)
@@ -351,11 +394,17 @@
         norm = raw * inverse
         back = grad * cosine - partner(grad) * sine
         gains_ref[index : index + 1, :] += jnp.sum(back * norm, axis=0, keepdims=True)
-        gp_ref[...] = (
+        grad_raw = (
             inverse * (back * gain_ref[index : index + 1, :] - norm * head_spread(mean, spread_ref))
         ).astype(bf16)
-    dmod = nt(gq_ref[...], w_ref[:, :width]) + nt(gk_ref[...], w_ref[:, width : 2 * width])
-    dmod = dmod + nt(dv_ref[...], w_ref[:, 2 * width :])
+        acc_ref[...] += nn(units_ref[...].reshape(width, TB), grad_raw)
+        dmod = dmod + nt(grad_raw, w_ref[:, index * width : (index + 1) * width])
+
+    @pl.when(block == pl.num_programs(0) - 1)
+    def _():
+        halves_out(accq_ref, slots[pl.num_programs(0)], q_send_ref, q_own_ref)
+        halves_out(acck_ref, slots[pl.num_programs(0)], k_send_ref, k_own_ref)
+
     norm, inverse = normed(x_ref[...].astype(f32))
     grad_x = grad_mid_ref[...] + norm_back(dmod, part(mod_ref, slot, 1, width), norm, inverse)
     grad_x_ref[...] = grad_x.astype(bf16)
@@ -363,26 +412,39 @@
     sums_ref[0, 1:2, :] = jnp.sum(dmod * norm, axis=0, keepdims=True)
 
 
-def send_kernel(where, units_ref, rhs_ref, out_ref):
-    units, rows, _ = units_ref.shape
-    result = nn(units_ref[...].reshape(units * rows, -1), rhs_ref[...])
-    out_ref[...] = result.astype(bf16).reshape(out_ref.shape)
-
-
-def keep_kernel(where, units_ref, rhs_ref, got_ref, send_ref, keep_ref, scratch):
-    units, rows, _ = units_ref.shape
-    result = nn(units_ref[...].reshape(units * rows, -1), rhs_ref[...])
-    scratch[...] = result.reshape(scratch.shape)
-    for i in range(units // 2):
-        away, own = where[2 + i], where[4 + i]
-        send_ref[i] = (scratch[away] + got_ref[away].astype(f32)).astype(bf16)
-        keep_ref[i] = scratch[own] + got_ref[own].astype(f32)
-
-
-def fold_kernel(where, keep_ref, got_ref, send_ref, own_ref):
-    away, own = where[0], where[1]
-    send_ref[...] = (keep_ref[away] + got_ref[away].astype(f32)).astype(bf16)
-    own_ref[...] = keep_ref[own] + got_ref[own].astype(f32)
+def value_kernel(bits, units_ref, rhs_ref, send_ref, own_ref):
+    product(units_ref, 1 - bits[0], rhs_ref[...], send_ref)
+    product(units_ref, bits[0], rhs_ref[...], own_ref)
+
+
+def fold_kernel(bits, *refs, plans):
+    count = len(plans)
+    for i, (kind, bit, rows) in enumerate(plans):
+        own_ref, got_ref, send_ref, keep_ref = refs[2 * i], refs[2 * i + 1], refs[2 * count + 2 * i], refs[2 * count + 2 * i + 1]
+        mine = bits[bit]
+        if kind in ("outer", "inner"):
+            for j in range(2):
+                away = 2 * (1 - mine) + j if kind == "outer" else 2 * j + 1 - mine
+                own = 2 * mine + j if kind == "outer" else 2 * j + mine
+                send_ref[j] = (own_ref[away].astype(f32) + got_ref[away].astype(f32)).astype(bf16)
+                keep_ref[j] = own_ref[own].astype(f32) + got_ref[own].astype(f32)
+        elif kind == "unit":
+            send_ref[...] = (own_ref[1 - mine] + got_ref[1 - mine].astype(f32)).astype(bf16)
+            keep_ref[...] = own_ref[mine] + got_ref[mine].astype(f32)
+        else:
+            total = own_ref[...] + got_ref[...].astype(f32)
+            for j in range(total.shape[0] // (2 * rows)):
+                first = total[2 * j * rows : (2 * j + 1) * rows]
+                second = total[(2 * j + 1) * rows : (2 * j + 2) * rows]
+                place = slice(j * rows, (j + 1) * rows)
+                send_ref[place] = jnp.where(mine == 1, first, second).astype(bf16)
+                keep_ref[place] = jnp.where(mine == 1, second, first)
+
+
+def last_kernel(*refs):
+    count = len(refs) // 3
+    for i in range(count):
+        refs[2 * count + i][...] = refs[2 * i][...] + refs[2 * i + 1][...].astype(f32)
 
 
 class Chain:
@@ -390,7 +452,7 @@
         self.last = None
 
     def __call__(
-        self, kernel, grid, in_specs, out_specs, out_shape, args, scalars=None, scratch=(), cost=(0, 0), name=None
+        self, kernel, grid, in_specs, out_specs, out_shape, args, scalars=None, scratch=(), name=None
     ):
         ahead = 0 if scalars is None else 1
         body = kernel
@@ -414,10 +476,10 @@
             grid_spec=spec,
             out_shape=out_shape,
             compiler_params=pltpu.CompilerParams(vmem_limit_bytes=VMEM),
-            cost_estimate=pl.CostEstimate(flops=int(cost[0]), bytes_accessed=int(cost[1]), transcendentals=0),
+            cost_estimate=pl.CostEstimate(flops=1, bytes_accessed=1, transcendentals=0),
             name=name,
         )(*(() if scalars is None else (scalars,)), *token, *args)
-        self.last = outs[-1] if isinstance(outs, (list, tuple)) else outs
+        self.last = outs[-1]
         return outs
 
 
@@ -431,105 +493,86 @@
 
 def rows_of(dims, axis=0):
     return pl.BlockSpec(dims, lambda b, *_: tuple(b if i == axis else 0 for i in range(len(dims))))
+
+
+def whole(dims):
+    return rows_of(dims, None)
 
 
 class Reducer:
     def __init__(self, n_dp, n_mod, call):
         self.n_dp, self.n_mod, self.call = n_dp, n_mod, call
         self.position = lax.axis_index("dp")
-        self.core = self.position & 1
-        self.nxt = lax.shift_right_logical(self.position, 1) & 1
-        self.mod = lax.axis_index("mod")
+        steps = range(n_dp.bit_length() - 1)
+        dp_bits = [lax.shift_right_logical(self.position, step) & 1 for step in steps]
+        self.bits = jnp.stack([dp_bits[0], lax.axis_index("mod")] + dp_bits[1:]).astype(jnp.int32)
 
     def swap(self, arr, bit):
         if bit == "mod":
             return lax.ppermute(arr, "mod", [(i, i ^ 1) for i in range(self.n_mod)])
         return lax.ppermute(arr, "dp", [(i, i ^ (1 << bit)) for i in range(self.n_dp)])
 
-    def stream(self, units, rhs, mod_first, name):
-        return Stream(self, units, rhs, mod_first, name)
+    def bit_of(self, bit):
+        return 1 if bit == "mod" else bit + 1 if bit else 0
+
+    def stream(self, sent, own, mod_first, pair_rows=None):
+        return Stream(self, sent, own, mod_first, pair_rows)
+
+    def fold(self, streams, name):
+        plans, args, outs = [], [], []
+        for stream in streams:
+            plan, part_shape = stream.plan()
+            plans.append(plan)
+            args += [stream.own, stream.got]
+            outs += [shape(part_shape, bf16), shape(part_shape, f32)]
+        results = self.call(
+            functools.partial(fold_kernel, plans=plans),
+            (1,),
+            [whole(arg.shape) for arg in args],
+            [whole(out.shape) for out in outs],
+            outs,
+            args,
+            scalars=self.bits,
+            name=name + "_fold",
+        )
+        for i, stream in enumerate(streams):
+            stream.step(results[2 * i], results[2 * i + 1])
+
+    def last(self, streams, name):
+        args = [arr for stream in streams for arr in (stream.own, stream.got)]
+        outs = [shape(stream.own.shape, f32) for stream in streams]
+        return self.call(
+            last_kernel,
+            (1,),
+            [whole(arg.shape) for arg in args],
+            [whole(out.shape) for out in outs],
+            outs,
+            args,
+            name=name + "_last",
+        )
 
 
 class Stream:
-    def __init__(self, reducer, units, rhs, mod_first, name):
-        self.r, self.units, self.rhs, self.mod_first, self.name = reducer, units, rhs, mod_first, name
-        _, self.rows, self.tokens = units.shape
-        self.columns = rhs.shape[1]
-        self.chunk = next(c for c in (1024, 1152) if self.columns % c == 0)
-        self.cost = (
-            8 * self.rows * self.tokens * self.columns,
-            2 * self.tokens * (self.columns + 4 * self.rows) + 8 * self.rows * self.columns,
-        )
-
-    def half(self):
-        return pl.BlockSpec(
-            (4, self.rows, self.tokens), lambda j, w: (w[0], 0, 0), pipeline_mode=pl.Buffered(1)
-        )
-
-    def send(self):
-        rows, columns, chunk = self.rows, self.columns, self.chunk
-        sent = self.r.call(
-            send_kernel,
-            (columns // chunk,),
-            [self.half(), rows_of((self.tokens, chunk), 1)],
-            rows_of((4, rows, chunk), 2),
-            shape((4, rows, columns), bf16),
-            (self.units, self.rhs),
-            scalars=jnp.stack([1 - self.r.core]),
-            cost=self.cost,
-            name=self.name + "_send",
-        )
-        self.got = self.r.swap(sent, 0)
-
-    def keep(self):
-        rows, columns, chunk = self.rows, self.columns, self.chunk
-        mod, nxt = self.r.mod, self.r.nxt
-        if self.mod_first:
-            where = [2 * (1 - mod), 2 * (1 - mod) + 1, 2 * mod, 2 * mod + 1]
-        else:
-            where = [1 - nxt, 3 - nxt, nxt, 2 + nxt]
-        sent, self.kept = self.r.call(
-            keep_kernel,
-            (columns // chunk,),
-            [self.half(), rows_of((self.tokens, chunk), 1), rows_of((4, rows, chunk), 2)],
-            [rows_of((2, rows, chunk), 2), rows_of((2, rows, chunk), 2)],
-            [shape((2, rows, columns), bf16), shape((2, rows, columns), f32)],
-            (self.units, self.rhs, self.got),
-            scalars=jnp.stack([self.r.core, self.r.core] + where),
-            scratch=[pltpu.VMEM((4, rows, chunk), f32)],
-            cost=(self.cost[0], self.cost[1] + 12 * rows * columns),
-            name=self.name + "_keep",
-        )
-        self.got = self.r.swap(sent, "mod" if self.mod_first else 1)
-
-    def fold(self):
-        rows, columns, chunk = self.rows, self.columns, self.chunk
-        bit = self.r.nxt if self.mod_first else self.r.mod
-        sent, self.kept = self.r.call(
-            fold_kernel,
-            (columns // chunk,),
-            [rows_of((2, rows, chunk), 2), rows_of((2, rows, chunk), 2)],
-            [rows_of((rows, chunk), 1), rows_of((rows, chunk), 1)],
-            [shape((rows, columns), bf16), shape((rows, columns), f32)],
-            (self.kept, self.got),
-            scalars=jnp.stack([1 - bit, bit]),
-            cost=(0, 18 * rows * columns),
-            name=self.name + "_fold",
-        )
-        self.got = self.r.swap(sent, 1 if self.mod_first else "mod")
-
-    def total(self):
-        n_dp = self.r.n_dp
-        total = self.kept + self.got.astype(f32)
-        bits = n_dp.bit_length() - 1
-        total = total.reshape((2,) * (bits - 2) + (self.rows * 4 // n_dp, self.columns))
-        for bit in range(2, bits):
-            axis = bits - 1 - bit
-            mine = lax.shift_right_logical(self.r.position, bit) & 1
-            away = lax.dynamic_index_in_dim(total, 1 - mine, axis=axis, keepdims=False)
-            own = lax.dynamic_index_in_dim(total, mine, axis=axis, keepdims=False)
-            total = own + self.r.swap(away.astype(bf16), bit).astype(f32)
-        return total
+    def __init__(self, reducer, sent, own, mod_first, pair_rows):
+        self.r, self.own, self.pair_rows, self.mod_first = reducer, own, pair_rows, mod_first
+        self.steps = ["mod", 1] if mod_first else [1, "mod"]
+        self.steps += list(range(2, reducer.n_dp.bit_length() - 1))
+        self.at = 0
+        self.got = reducer.swap(sent, 0)
+
+    def plan(self):
+        bit = self.r.bit_of(self.steps[self.at])
+        dims = self.own.shape
+        if self.at == 0:
+            return ("outer" if self.mod_first else "inner", bit, 0), (2,) + dims[1:]
+        if self.at == 1:
+            return ("unit", bit, 0), dims[1:]
+        return ("rows", bit, self.pair_rows or dims[0] // 2), (dims[0] // 2, dims[1])
+
+    def step(self, sent, own):
+        self.own = own
+        self.got = self.r.swap(sent, self.steps[self.at])
+        self.at += 1
 
 
 def silu_grad(v):
@@ -593,7 +636,6 @@
         + [shape((width, count), bf16)],
         (x, modulation, w_qkv, coord) + tables + (perm,),
         scalars=slots,
-        cost=(2 * 5 * macs, 40e6),
         name="project",
     )
     attended, lse, attn, mid, ffn_in, grad_ffn, out_units, ffn_units = call(
@@ -605,54 +647,52 @@
         (x, cot, modulation, query, key, value, w_out, perm),
         scalars=slots,
         scratch=[pltpu.VMEM((TB, 128), f32)],
-        cost=(2 * 10 * macs, 40e6),
         name="attend",
     )
 
     rows_ff = ff // n_dev
-    rest = n_dp // 4
     chunk = 768
-    group = chunk // rows_ff
-    if group >= 8:
-        unit_block = pl.BlockSpec((4, 2, group // 8, rows_ff, count), lambda i: (0, 0, i, 0, 0))
-    else:
-        unit_block = pl.BlockSpec((4, 1, 1, rows_ff, count), lambda i: (0, i % 2, i // 2, 0, 0))
-    down_units, grad_gate, grad_up, ffn, grad_mod_ffn = call(
-        functools.partial(ffn_kernel, n_mod=n_mod),
+    piece = chunk // 8
+    half_units = lambda rows, columns: shape((4, rows, columns), bf16)
+    square_send = [fixed((4, width // 8, width))] * 2
+    square_shapes = [half_units(width // 8, width)] * 2
+    gate_send, gate_own, up_send, up_own, down_send, down_own, ffn, grad_mod_ffn = call(
+        functools.partial(ffn_kernel, n_mod=n_mod, rows_ff=rows_ff),
         (ff // chunk,),
-        [fixed((count, width))] * 2 + [rows_of((width, chunk), 1)] * 2 + [rows_of((chunk, width))],
-        [unit_block] + [rows_of((count, chunk), 1)] * 2 + [fixed((count, width))] * 2,
-        [shape((4, 2, rest, rows_ff, count), bf16)] + [shape((count, ff), bf16)] * 2 + [token_f32] * 2,
-        (ffn_in, grad_ffn, w_gate, w_up, w_down),
-        cost=(2 * 6 * count * width * ff, 60e6),
+        [fixed((count, width))] * 2 + [fixed(units.shape)]
+        + [rows_of((width, chunk), 1)] * 2 + [rows_of((chunk, width))],
+        [rows_of((4, width // 8, chunk), 2)] * 4
+        + [rows_of((4, 1, piece, width), 1)] * 2 + [fixed((count, width))] * 2,
+        [half_units(width // 8, ff)] * 4
+        + [shape((4, ff // chunk, piece, width), bf16)] * 2 + [token_f32] * 2,
+        (ffn_in, grad_ffn, ffn_units, w_gate, w_up, w_down),
+        scalars=reducer.bits,
+        scratch=[pltpu.VMEM((8, piece, count), bf16)],
         name="ffn",
     )
-    down_units = down_units.reshape(8, rest * rows_ff, count)
-
-    gate = reducer.stream(ffn_units, grad_gate, True, "gate")
-    up = reducer.stream(ffn_units, grad_up, False, "up")
-    down = reducer.stream(down_units, grad_ffn, True, "down")
-    gate.send()
-    up.send()
-    down.send()
-
-    output, grad_mid, grad_attn, grad_attended, dot_term, sums_b = call(
+    gate = reducer.stream(gate_send, gate_own, True)
+    up = reducer.stream(up_send, up_own, False)
+    down = reducer.stream(
+        down_send.reshape(4, ff // 8, width), down_own.reshape(4, ff // 8, width), True, rows_ff
+    )
+
+    slots_core = jnp.concatenate([slots, reducer.bits[:1]])
+    output, grad_mid, grad_attended, dot_term, sums_b, out_send, out_own = call(
         middle_kernel,
         (blocks,),
-        [token_spec] * 6 + [mod_spec, square, fixed(gather.shape)],
-        [token_spec] * 4 + [rows_of((128, TB), 1), rows_of((1, 4, width))],
-        [token_bf16, token_f32, token_bf16, token_bf16, lane_rows, shape((blocks, 4, width), f32)],
-        (mid, ffn, grad_mod_ffn, cot, attn, attended, modulation, w_out, gather),
-        scalars=slots,
-        cost=(2 * macs, 40e6),
+        [token_spec] * 6 + [units_spec, mod_spec, square, fixed(gather.shape)],
+        [token_spec] * 3 + [rows_of((128, TB), 1), rows_of((1, 4, width))] + square_send,
+        [token_bf16, token_f32, token_bf16, lane_rows, shape((blocks, 4, width), f32)] + square_shapes,
+        (mid, ffn, grad_mod_ffn, cot, attn, attended, out_units, modulation, w_out, gather),
+        scalars=slots_core,
+        scratch=[pltpu.VMEM((width, width), f32)],
         name="middle",
     )
-    out = reducer.stream(out_units, grad_attn, False, "out")
-    gate.keep()
-    up.keep()
-    out.send()
-    down.keep()
-    out.keep()
+    out = reducer.stream(out_send, out_own, False)
+    reducer.fold([gate], "gate")
+    reducer.fold([up], "up")
+    reducer.fold([down], "down")
+    reducer.fold([out], "out")
 
     grad_query_t, grad_key, grad_value = call(
         attend_back_kernel,
@@ -663,41 +703,52 @@
         (query, key, value, grad_attended, lse, dot_term, key_t),
         scratch=[pltpu.VMEM((count, width), f32)],
         scalars=slots,
-        cost=(2 * 22 * macs, 40e6),
         name="attend_back",
     )
-    v_part = reducer.stream(attn_units, grad_value, True, "v")
-    v_part.send()
-    gate.fold()
-    up.fold()
-    v_part.keep()
-    out.fold()
-    grad_q, grad_k, grad_tokens, sums_a, gain_sums = call(
+    v_send, v_own = call(
+        value_kernel,
+        (1,),
+        [whole(units.shape), whole((count, width))],
+        [whole((4, width // 8, width))] * 2,
+        square_shapes,
+        (attn_units, grad_value),
+        scalars=reducer.bits,
+        name="value",
+    )
+    v_part = reducer.stream(v_send, v_own, True)
+    reducer.fold([gate, up], "gate_up")
+    reducer.fold([out, v_part], "out_v")
+    reducer.fold([down], "down")
+    grad_tokens, sums_a, gain_sums, q_send, q_own, k_send, k_own = call(
         project_back_kernel,
         (blocks,),
         [rows_of((width, TB), 1), token_spec, token_spec, rows_of((TB, 2 * width)), rows_of((TB, 256))]
         + [token_spec] * 4
-        + [mod_spec, fixed((width, 3 * width)), rows_of((2, TB), 1)]
+        + [units_spec, mod_spec, fixed((width, 3 * width)), rows_of((2, TB), 1)]
         + table_specs,
-        [token_spec, token_spec, token_spec, rows_of((1, 2, width)), fixed((2, width))],
-        [token_bf16, token_bf16, token_bf16, shape((blocks, 2, width), f32), shape((2, width), f32)],
-        (grad_query_t, grad_key, grad_value, raw, inverse, query, key, x, grad_mid, modulation, w_qkv, coord)
+        [token_spec, rows_of((1, 2, width)), fixed((2, width))] + square_send * 2,
+        [token_bf16, shape((blocks, 2, width), f32), shape((2, width), f32)] + square_shapes * 2,
+        (grad_query_t, grad_key, grad_value, raw, inverse, query, key, x, grad_mid, attn_units, modulation,
+         w_qkv, coord)
         + tables,
-        scalars=slots,
-        cost=(2 * 4 * macs, 50e6),
+        scalars=slots_core,
+        scratch=[pltpu.VMEM((width, width), f32)] * 2,
         name="project_back",
     )
-    q_part = reducer.stream(attn_units, grad_q, False, "q")
-    k_part = reducer.stream(attn_units, grad_k, True, "k")
-    q_part.send()
-    k_part.send()
-    down.fold()
-    v_part.fold()
-    q_part.keep()
-    k_part.keep()
-    q_part.fold()
-    k_part.fold()
-    summed_qkv = jnp.concatenate([q_part.total(), k_part.total(), v_part.total()], axis=1)
+    q_part = reducer.stream(q_send, q_own, False)
+    k_part = reducer.stream(k_send, k_own, True)
+    reducer.fold([gate, up], "gate_up")
+    reducer.fold([down, out, v_part], "down_out_v")
+    reducer.fold([q_part, k_part], "q_k")
+    for _ in range(n_dp.bit_length() - 4):
+        reducer.fold([gate, up, down, out], "early")
+        reducer.fold([v_part], "v")
+        reducer.fold([q_part, k_part], "q_k")
+    summed_gate, summed_up, summed_down, summed_out = reducer.last([gate, up, down, out], "early")
+    reducer.fold([v_part, q_part, k_part], "v_q_k")
+    reducer.fold([q_part, k_part], "q_k")
+    summed = reducer.last([q_part, k_part, v_part], "q_k_v")
+    summed_qkv = jnp.concatenate(summed, axis=1)
 
     sums = jnp.concatenate([sums_a, sums_b], axis=1).reshape(blocks, 6 * width)
     in_slot = slots[None, :, None] == jnp.arange(slots_n)[:, None, None]
@@ -736,10 +787,10 @@
         summed_qkv,
         gain_grads[0],
         gain_grads[1],
-        out.total(),
-        gate.total(),
-        up.total(),
-        down.total(),
+        summed_out,
+        summed_gate,
+        summed_up,
+        summed_down,
     )
 
 

time: 608 us -> 627 us (1.031)
  waiting for transfers between devices: 110 us -> 131 us
  other arithmetic: 20.4 us -> 9.85 us
  starting transfers between devices: 42.4 us -> 51.6 us
  local copies, waits for them, and re-layouts: 23.1 us -> 14.4 us
  Pallas kernels: 391 us -> 398 us
    ppermute x12, waiting for transfers between devices: 16.8 us -> 35.9 us  [swap(): return lax.ppermute(arr, 'mod', [(i, i ^ 1) for i in range(self.n_mod)])]
    add x21 -> x0, other arithmetic: 10 us -> none  [the longest x14 5.68 us: total(): total = own + self.r.swap(away.astype(bf16), bit).astype(f32)]
    convert_element_type x14 -> x0, local copies, waits for them, and re-layouts: 7.54 us -> none  [total(): total = own + self.r.swap(away.astype(bf16), bit).astype(f32)]
    ppermute x36, starting transfers between devices: 29.4 us -> 36.1 us  [swap(): lax.ppermute(arr, 'dp', [(i, i ^ 1 << bit) for i in range(self.n_dp)])]
    pallas_call x27 -> x24, Pallas kernels: 391 us -> 398 us  [__call__(): pl.pallas_call(body, grid_spec=spec, out_shape=out_shape, compiler_params...]
  transfers between devices with their start and end apart: 48 -> 48, of which waited for: 24 -> 19; matrix products, arithmetic and copies ran while one was open for 7% -> 3% of each run, Pallas kernels for 38% -> 26%
where the time goes in v4:
time: 627 us; the launch traced here: 617 us
  Pallas kernels  398 us (63%)
  waiting for transfers between devices  131 us (21%)
  starting transfers between devices  51.6 us (8%)
  local copies, waits for them, and re-layouts  14.4 us (2%)
  matrix products  11.2 us (2%)
  other arithmetic  9.85 us (2%)
    pallas_call x24, Pallas kernels, __call__(): pl.pallas_call(body, grid_spec=spec, out_shape=out_shape, compiler_params...  398 us
    ppermute x36, waiting for transfers between devices, swap(): lax.ppermute(arr, 'dp', [(i, i ^ 1 << bit) for i in range(self.n_dp)])  95.5 us
    ppermute x36, starting transfers between devices, swap(): lax.ppermute(arr, 'dp', [(i, i ^ 1 << bit) for i in range(self.n_dp)])  36.1 us
    ppermute x12, waiting for transfers between devices, swap(): return lax.ppermute(arr, 'mod', [(i, i ^ 1) for i in range(self.n_mod)])  35.9 us
    ppermute x12, starting transfers between devices, swap(): return lax.ppermute(arr, 'mod', [(i, i ^ 1) for i in range(self.n_mod)])  15.5 us
  transfers between devices with their start and end apart: 48, of which 19 were waited for; matrix products, arithmetic and copies ran while one was open for 3% of the time, Pallas kernels for 26%

profile of v4, /device:TPU:0, one launch (start us, length us, event | category | flops | bytes accessed | tf_op | source)
XLA Modules:
  0.0 617.4 jit_solution(8482023026579432074)
XLA Ops:
  0.6 3.0 collective-permute-start
  6.5 4.4 convolution_convert_fusion
  11.0 2.1 collective-permute-start.1
  16.4 29.1 %project.1 = (bf16[8,144,1024]{2,1,0:T(8,128)(2,1)}, f32[1024,2304]{1,0:T(8,128)}, f32[1024,256]{1,0:T(8,128)}, bf16[1024,1152]{1,0:T(8,128)(2,1)}, bf16[1024,11...) custom-call(s32[4]{0:T(128)} %bitcast.64, bf16[1024,1152]{1,0:T(8,128)(2,1)} %bitcast.50, ...), custom_call_target="tpu_custom_call" | custom-call | flops 1 | bytes 1 | tf_op jit(solution)/shard_map/project/pallas_call | solution.py:474
  45.4 57.6 %attend.1 = (f32[1024,1152]{1,0:T(8,128)}, f32[128,1024]{1,0:T(8,128)}, f32[1024,1152]{1,0:T(8,128)}, f32[1024,1152]{1,0:T(8,128)}, bf16[1024,1152]{1,0:T(8,128)...) custom-call(s32[4]{0:T(128)} %bitcast.65, ...), custom_call_target="tpu_custom_call" | custom-call | flops 1 | bytes 1 | tf_op jit(solution)/shard_map/attend/pallas_call | solution.py:474
  103.0 99.7 %ffn.1 = (bf16[4,144,3072]{2,1,0:T(8,128)(2,1)}, bf16[4,144,3072]{2,1,0:T(8,128)(2,1)}, bf16[4,144,3072]{2,1,0:T(8,128)(2,1)}, bf16[4,144,3072]{2,1,0:T(8,128)(2...) custom-call(s32[5]{0:T(128)} %stack.62.refs_0_, ...), custom_call_target="tpu_custom_call" | custom-call | flops 1 | bytes 1 | tf_op jit(solution)/shard_map/ffn/pallas_call | solution.py:474
  203.9 24.6 %middle.1 = (bf16[1024,1152]{1,0:T(8,128)(2,1)}, f32[1024,1152]{1,0:T(8,128)}, bf16[1024,1152]{1,0:T(8,128)(2,1)}, f32[128,1024]{1,0:T(8,128)}, f32[4,4,1152]{2,...) custom-call(s32[5]{0:T(128)} %pad_add_fusion.refs_0_, ...), custom_call_target="tpu_custom_call" | custom-call | flops 1 | bytes 1 | tf_op jit(solution)/shard_map/middle/pallas_call | solution.py:474
  230.8 6.8 %gate_fold.1 = (bf16[2,144,3072]{2,1,0:T(8,128)(2,1)}, f32[2,144,3072]{2,1,0:T(8,128)}) custom-call(s32[5]{0:T(128)} %stack.62.refs_0_, bf16[4,144,1152]{2,1,0:T(8,128)(2,1)} %get-tuple-element.130.refs_1_.refs_2_, bf16[4,144,3072]{2,1,0:T(8,128)(2,1)} %get-tuple-element.131.refs_2_, bf16[4,144,3072]{2,1,0:T(8,128)(2,1)} %copy-done), custom_call_target="tpu_custom_call" | custom-call | flops 1 | bytes 1 | tf_op jit(solution)/shard_map/gate_fold/pallas_call | solution.py:474
  237.6 6.8 %up_fold.1 = (bf16[2,144,3072]{2,1,0:T(8,128)(2,1)}, f32[2,144,3072]{2,1,0:T(8,128)}) custom-call(s32[5]{0:T(128)} %stack.62.refs_0_, f32[2,144,3072]{2,1,0:T(8,128)} %get-tuple-element.133.refs_1_.refs_2_, bf16[4,144,3072]{2,1,0:T(8,128)(2,1)} %get-tuple-element.134.refs_2_, bf16[4,144,3072]{2,1,0:T(8,128)(2,1)} %collective-permute-done.3.refs_3_), custom_call_target="tpu_custom_call" | custom-call | flops 1 | bytes 1 | tf_op jit(solution)/shard_map/up_fold/pallas_call | solution.py:474
  244.4 2.8 collective-permute-start.6
  247.2 6.8 %down_fold.2 = (bf16[2,384,1152]{2,1,0:T(8,128)(2,1)}, f32[2,384,1152]{2,1,0:T(8,128)}) custom-call(s32[5]{0:T(128)} %stack.62.refs_0_, f32[2,144,3072]{2,1,0:T(8,128)} %get-tuple-element.136.refs_1_.refs_4_, bf16[4,384,1152]{2,1,0:T(8,128)(2,1)} %bitcast.55, bf16[4,384,1152]{2,1,0:T(8,128)(2,1)} %collective-permute-done.4.refs_3_), custom_call_target="tpu_custom_call" | custom-call | flops 1 | bytes 1 | tf_op jit(solution)/shard_map/down_fold/pallas_call | solution.py:474
  254.0 4.0 out_fold.1
  258.0 56.3 %attend_back.1 = (f32[1152,1024]{1,0:T(8,128)}, f32[1024,1152]{1,0:T(8,128)}, bf16[1024,1152]{1,0:T(8,128)(2,1)}) custom-call(s32[4]{0:T(128)} %bitcast.66, f32[2,144,1152]{2,1,0:T(8,128)} %get-tuple-element.141.refs_1_.refs_2_, bf16[1024,1152]{1,0:T(8,128)(2,1)} %get-tuple-element.117.refs_5_.refs_2_.refs_7_, ...), custom_call_target="tpu_custom_call" | custom-call | flops 1 | bytes 1 | tf_op jit(solution)/shard_map/attend_back/pallas_call | solution.py:474
  314.3 7.5 %value.1 = (bf16[4,144,1152]{2,1,0:T(8,128)(2,1)}, bf16[4,144,1152]{2,1,0:T(8,128)(2,1)}) custom-call(s32[5]{0:T(128)} %stack.62.refs_0_, bf16[1024,1152]{1,0:T(8,128)(2,1)} %get-tuple-element.145.refs_1_.refs_3_.refs_4_, bf16[8,144,1024]{2,1,0:T(8,128)(2,1)} %get-tuple-element.146.refs_2_.refs_11_, bf16[1024,1152]{1,0:T(8,128)(2,1)} %get-tuple-element.145.refs_1_.refs_3_.refs_4_), custom_call_target="tpu_custom_call" | custom-call | flops 1 | bytes 1 | tf_op jit(solution)/shard_map/value/pallas_call | solution.py:474
  323.5 7.6 %gate_up_fold.2 = (bf16[144,3072]{1,0:T(8,128)(2,1)}, f32[144,3072]{1,0:T(8,128)}, bf16[144,3072]{1,0:T(8,128)(2,1)}, f32[144,3072]{1,0:T(8,128)}) custom-call(s32[5]{0:T(128)} %stack.62.refs_0_, bf16[4,144,1152]{2,1,0:T(8,128)(2,1)} %get-tuple-element.147.refs_1_.refs_4_, f32[2,144,3072]{2,1,0:T(8,128)} %get-tuple-element.133.refs_1_.refs_2_, ...), custom_call_target="tpu_custom_call" | custom-call | flops 1 | bytes 1 | tf_op jit(solution)/shard_map/gate_up_fold/pallas_call | solution.py:474
  331.1 8.3 %collective-permute-done.8.refs_3_ = bf16[2,144,1152]{2,1,0:T(8,128)(2,1)} collective-permute-done((bf16[2,144,1152]{2,1,0:T(8,128)(2,1)}, bf16[2,144,1152]{2,1,0:T(8,128)(2,1)}, u32[]{:S(2)}, u32[]{:S(2)}) %collective-permute-start.8) | collective-permute-done | bytes 663584 | tf_op jit(solution)/shard_map/ppermute | solution.py:513
  339.5 4.7 out_v_fold.1
  345.4 5.1 down_fold.3
  350.5 43.2 %project_back.1 = (bf16[1024,1152]{1,0:T(8,128)(2,1)}, f32[4,2,1152]{2,1,0:T(2,128)}, f32[2,1152]{1,0:T(2,128)}, bf16[4,144,1152]{2,1,0:T(8,128)(2,1)}, bf16[4,1...) custom-call(s32[5]{0:T(128)} %pad_add_fusion.refs_0_, ...), custom_call_target="tpu_custom_call" | custom-call | flops 1 | bytes 1 | tf_op jit(solution)/shard_map/project_back/pallas_call | solution.py:474
  395.7 3.1 collective-permute-done.11
  406.1 15.3 %collective-permute-done.44 = f32[2,72]{1,0:T(2,128)S(1)} collective-permute-done((f32[2,72]{1,0:T(2,128)S(1)}, f32[2,72]{1,0:T(2,128)S(1)}, u32[]{:S(2)}, u32[]{:S(2)}) %collective-permute-start.44) | collective-permute-done | bytes 608 | tf_op jit(solution)/shard_map/ppermute | solution.py:512
  423.1 20.3 %collective-permute-done.45 = f32[2,72]{1,0:T(2,128)S(1)} collective-permute-done((f32[2,72]{1,0:T(2,128)S(1)}, f32[2,72]{1,0:T(2,128)S(1)}, u32[]{:S(2)}, u32[]{:S(2)}) %collective-permute-start.45) | collective-permute-done | bytes 608 | tf_op jit(solution)/shard_map/ppermute | solution.py:513
  443.5 2.3 collective-permute-start.46
  448.6 3.1 collective-permute-done.47
  455.5 4.8 gate_up_fold.3
  460.4 16.2 %collective-permute-done.20.refs_5_ = bf16[144,1152]{1,0:T(8,128)(2,1)} collective-permute-done((bf16[144,1152]{1,0:T(8,128)(2,1)}, bf16[144,1152]{1,0:T(8,128)(2,1)}, u32[]{:S(2)}, u32[]{:S(2)}) %collective-permute-start.20) | collective-permute-done | bytes 331808 | tf_op jit(solution)/shard_map/ppermute | solution.py:512
  476.6 2.0 collective-permute-start.15
  479.5 5.2 down_out_v_fold.1
  484.7 5.5 fusion
  490.2 2.1 collective-permute-start.27
  493.7 5.2 q_k_fold.3
  504.6 8.8 %collective-permute-done.24.refs_3_ = bf16[72,3072]{1,0:T(8,128)(2,1)S(1)} collective-permute-done((bf16[72,3072]{1,0:T(8,128)(2,1)}, bf16[72,3072]{1,0:T(8,128)(2,1)S(1)}, u32[]{:S(2)}, u32[]{:S(2)}) %collective-permute-start.24) | collective-permute-done | bytes 442400 | tf_op jit(solution)/shard_map/ppermute | solution.py:513
  514.9 4.8 collective-permute-done.25.refs_5_
  519.7 4.5 collective-permute-start.16
  524.2 4.4 early_fold.1
  528.7 2.9 collective-permute-start.32
  532.3 2.7 v_fold.1
  535.1 4.4 q_k_fold.4
  539.5 2.8 collective-permute-start.33
  542.3 34.9 %collective-permute-done.34.refs_8_ = bf16[36,1152]{1,0:T(8,128)(2,1)S(1)} collective-permute-done((bf16[36,1152]{1,0:T(8,128)(2,1)}, bf16[36,1152]{1,0:T(8,128)(2,1)S(1)}, u32[]{:S(2)}, u32[]{:S(2)}) %collective-permute-start.34) | collective-permute-done | bytes 82976 | tf_op jit(solution)/shard_map/ppermute | solution.py:513
  580.9 2.9 early_last.1
  586.6 3.5 v_q_k_fold.1
  594.3 2.4 collective-permute-done.38.refs_3_
  596.6 2.8 collective-permute-done.39.refs_5_
  600.1 2.7 q_k_fold.5
  607.1 3.3 collective-permute-done.40.refs_2_
  610.4 2.0 collective-permute-done.41.refs_4_
  613.0 2.0 q_k_v_last.1
  (181 shorter events, 58.8 us)
Async XLA Ops:
  0.6 5.0 collective-permute-start
  11.0 4.7 collective-permute-start.1
  202.7 26.3 %collective-permute-start.2 = (bf16[4,144,3072]{2,1,0:T(8,128)(2,1)}, bf16[4,144,3072]{2,1,0:T(8,128)(2,1)S(1)}, u32[]{:S(2)}, u32[]{:S(2)}) collective-permute-start(bf16[4,144,3072]{2,1,0:T(8,128)(2,1)} %get-tuple-element.132), channel_id=1, source_target_pairs={{0,2},{2,0},{4,6},{6,4},{8,10},{10,8},{12,14},{14,12},{16,18},{18,... | collective-permute-start | bytes 10616840 | tf_op jit(solution)/shard_map/ppermute | solution.py:513
  202.8 34.8 %collective-permute-start.3 = (bf16[4,144,3072]{2,1,0:T(8,128)(2,1)}, bf16[4,144,3072]{2,1,0:T(8,128)(2,1)}, u32[]{:S(2)}, u32[]{:S(2)}) collective-permute-start(bf16[4,144,3072]{2,1,0:T(8,128)(2,1)} %get-tuple-element.135), channel_id=1, source_target_pairs={{0,2},{2,0},{4,6},{6,4},{8,10},{10,8},{12,14},{14,12},{16,18},{18,... | collective-permute-start | bytes 10616840 | tf_op jit(solution)/shard_map/ppermute | solution.py:513
  203.3 44.0 %collective-permute-start.4 = (bf16[4,384,1152]{2,1,0:T(8,128)(2,1)}, bf16[4,384,1152]{2,1,0:T(8,128)(2,1)}, u32[]{:S(2)}, u32[]{:S(2)}) collective-permute-start(bf16[4,384,1152]{2,1,0:T(8,128)(2,1)} %bitcast.69), channel_id=1, source_target_pairs={{0,2},{2,0},{4,6},{6,4},{8,10},{10,8},{12,14},{14,12},{16,18},{18,... | collective-permute-start | bytes 10616840 | tf_op jit(solution)/shard_map/ppermute | solution.py:513
  228.6 25.4 %collective-permute-start.5 = (bf16[4,144,1152]{2,1,0:T(8,128)(2,1)}, bf16[4,144,1152]{2,1,0:T(8,128)(2,1)}, u32[]{:S(2)}, u32[]{:S(2)}) collective-permute-start(bf16[4,144,1152]{2,1,0:T(8,128)(2,1)} %get-tuple-element.140), channel_id=1, source_target_pairs={{0,2},{2,0},{4,6},{6,4},{8,10},{10,8},{12,14},{14,12},{16,18},{18,... | collective-permute-start | bytes 3981320 | tf_op jit(solution)/shard_map/ppermute | solution.py:513
  244.4 77.9 %collective-permute-start.7 = (bf16[2,144,3072]{2,1,0:T(8,128)(2,1)}, bf16[2,144,3072]{2,1,0:T(8,128)(2,1)S(1)}, u32[]{:S(2)}, u32[]{:S(2)}) collective-permute-start(bf16[2,144,3072]{2,1,0:T(8,128)(2,1)} %get-tuple-element.149), channel_id=1, source_target_pairs={{0,4},{2,6},{4,0},{6,2},{8,12},{10,14},{12,8},{14,10},{16,20},{18,... | collective-permute-start | bytes 5308424 | tf_op jit(solution)/shard_map/ppermute | solution.py:513
  244.4 77.9 %collective-permute-start.6 = (bf16[2,144,3072]{2,1,0:T(8,128)(2,1)}, bf16[2,144,3072]{2,1,0:T(8,128)(2,1)}, u32[]{:S(2)}, u32[]{:S(2)}) collective-permute-start(bf16[2,144,3072]{2,1,0:T(8,128)(2,1)} %get-tuple-element.148), channel_id=1, source_target_pairs={{0,1},{1,0},{2,3},{3,2},{4,5},{5,4},{6,7},{7,6},{8,9},{9,8},{10,11... | collective-permute-start | bytes 5308424 | tf_op jit(solution)/shard_map/ppermute | solution.py:512
  254.0 90.2 %collective-permute-start.10 = (bf16[2,384,1152]{2,1,0:T(8,128)(2,1)}, bf16[2,384,1152]{2,1,0:T(8,128)(2,1)S(1)}, u32[]{:S(2)}, u32[]{:S(2)}) collective-permute-start(bf16[2,384,1152]{2,1,0:T(8,128)(2,1)} %get-tuple-element.154), channel_id=1, source_target_pairs={{0,1},{1,0},{2,3},{3,2},{4,5},{5,4},{6,7},{7,6},{8,9},{9,8},{10,11... | collective-permute-start | bytes 5308424 | tf_op jit(solution)/shard_map/ppermute | solution.py:512
  321.8 17.6 %collective-permute-start.9 = (bf16[4,144,1152]{2,1,0:T(8,128)(2,1)}, bf16[4,144,1152]{2,1,0:T(8,128)(2,1)}, u32[]{:S(2)}, u32[]{:S(2)}) collective-permute-start(bf16[4,144,1152]{2,1,0:T(8,128)(2,1)} %get-tuple-element.152), channel_id=1, source_target_pairs={{0,2},{2,0},{4,6},{6,4},{8,10},{10,8},{12,14},{14,12},{16,18},{18,... | collective-permute-start | bytes 3981320 | tf_op jit(solution)/shard_map/ppermute | solution.py:513
  321.8 17.6 %collective-permute-start.8 = (bf16[2,144,1152]{2,1,0:T(8,128)(2,1)}, bf16[2,144,1152]{2,1,0:T(8,128)(2,1)}, u32[]{:S(2)}, u32[]{:S(2)}) collective-permute-start(bf16[2,144,1152]{2,1,0:T(8,128)(2,1)} %get-tuple-element.151), channel_id=1, source_target_pairs={{0,4},{2,6},{4,0},{6,2},{8,12},{10,14},{12,8},{14,10},{16,20},{18,... | collective-permute-start | bytes 1990664 | tf_op jit(solution)/shard_map/ppermute | solution.py:513
  394.9 3.9 collective-permute-start.11
  398.9 2.2 collective-permute-start.13
  399.0 53.3 %collective-permute-start.17 = (bf16[144,3072]{1,0:T(8,128)(2,1)}, bf16[144,3072]{1,0:T(8,128)(2,1)}, u32[]{:S(2)}, u32[]{:S(2)}) collective-permute-start(bf16[144,3072]{1,0:T(8,128)(2,1)} %get-tuple-element.166), channel_id=1, source_target_pairs={{0,4},{2,6},{4,0},{6,2},{8,12},{10,14},{12,8},{14,10},{16,20},{18,... | collective-permute-start | bytes 2654216 | tf_op jit(solution)/shard_map/ppermute | solution.py:513
  399.3 53.4 %collective-permute-start.18 = (bf16[144,3072]{1,0:T(8,128)(2,1)}, bf16[144,3072]{1,0:T(8,128)(2,1)}, u32[]{:S(2)}, u32[]{:S(2)}) collective-permute-start(bf16[144,3072]{1,0:T(8,128)(2,1)} %get-tuple-element.167), channel_id=1, source_target_pairs={{0,1},{1,0},{2,3},{3,2},{4,5},{5,4},{6,7},{7,6},{8,9},{9,8},{10,11... | collective-permute-start | bytes 2654216 | tf_op jit(solution)/shard_map/ppermute | solution.py:512
  401.8 50.0 %collective-permute-start.14 = (bf16[16,4608]{1,0:T(8,128)(2,1)}, bf16[16,4608]{1,0:T(8,128)(2,1)}, u32[]{:S(2)}, u32[]{:S(2)}) collective-permute-start(bf16[16,4608]{1,0:T(8,128)(2,1)} %maximum_select_fusion.3), channel_id=1, source_target_pairs={{0,4},{2,6},{4,0},{6,2},{8,12},{10,14},{12,8},{14,10},{16,20},{18,... | collective-permute-start | bytes 442376 | tf_op jit(solution)/shard_map/ppermute | solution.py:513
  402.5 76.1 %collective-permute-start.19 = (bf16[384,1152]{1,0:T(8,128)(2,1)}, bf16[384,1152]{1,0:T(8,128)(2,1)S(1)}, u32[]{:S(2)}, u32[]{:S(2)}) collective-permute-start(bf16[384,1152]{1,0:T(8,128)(2,1)} %get-tuple-element.169), channel_id=1, source_target_pairs={{0,4},{2,6},{4,0},{6,2},{8,12},{10,14},{12,8},{14,10},{16,20},{18,... | collective-permute-start | bytes 2654216 | tf_op jit(solution)/shard_map/ppermute | solution.py:513
  404.6 1.2 collective-permute-start.43
  405.8 15.6 %collective-permute-start.44 = (f32[2,72]{1,0:T(2,128)S(1)}, f32[2,72]{1,0:T(2,128)S(1)}, u32[]{:S(2)}, u32[]{:S(2)}) collective-permute-start(f32[2,72]{1,0:T(2,128)S(1)} %add.53), channel_id=1, source_target_pairs={{0,1},{1,0},{2,3},{3,2},{4,5},{5,4},{6,7},{7,6},{8,9},{9,8},{10,11... | collective-permute-start | bytes 1736 | tf_op jit(solution)/shard_map/ppermute | solution.py:512
  421.4 22.1 %collective-permute-start.45 = (f32[2,72]{1,0:T(2,128)S(1)}, f32[2,72]{1,0:T(2,128)S(1)}, u32[]{:S(2)}, u32[]{:S(2)}) collective-permute-start(f32[2,72]{1,0:T(2,128)S(1)} %add.54), channel_id=1, source_target_pairs={{0,4},{2,6},{4,0},{6,2},{8,12},{10,14},{12,8},{14,10},{16,20},{18,... | collective-permute-start | bytes 1736 | tf_op jit(solution)/shard_map/ppermute | solution.py:513
  443.5 3.9 collective-permute-start.46
  447.3 4.5 collective-permute-start.47
  451.8 40.5 %collective-permute-start.22 = (bf16[4,144,1152]{2,1,0:T(8,128)(2,1)}, bf16[4,144,1152]{2,1,0:T(8,128)(2,1)S(1)}, u32[]{:S(2)}, u32[]{:S(2)}) collective-permute-start(bf16[4,144,1152]{2,1,0:T(8,128)(2,1)} %get-tuple-element.175), channel_id=1, source_target_pairs={{0,2},{2,0},{4,6},{6,4},{8,10},{10,8},{12,14},{14,12},{16,18},{18,... | collective-permute-start | bytes 3981320 | tf_op jit(solution)/shard_map/ppermute | solution.py:513
  451.8 40.5 %collective-permute-start.23 = (bf16[4,144,1152]{2,1,0:T(8,128)(2,1)}, bf16[4,144,1152]{2,1,0:T(8,128)(2,1)S(1)}, u32[]{:S(2)}, u32[]{:S(2)}) collective-permute-start(bf16[4,144,1152]{2,1,0:T(8,128)(2,1)} %get-tuple-element.176), channel_id=1, source_target_pairs={{0,2},{2,0},{4,6},{6,4},{8,10},{10,8},{12,14},{14,12},{16,18},{18,... | collective-permute-start | bytes 3981320 | tf_op jit(solution)/shard_map/ppermute | solution.py:513
  452.3 26.3 %collective-permute-start.21 = (bf16[2,144,1152]{2,1,0:T(8,128)(2,1)}, bf16[2,144,1152]{2,1,0:T(8,128)(2,1)}, u32[]{:S(2)}, u32[]{:S(2)}) collective-permute-start(bf16[2,144,1152]{2,1,0:T(8,128)(2,1)} %get-tuple-element.172), channel_id=1, source_target_pairs={{0,1},{1,0},{2,3},{3,2},{4,5},{5,4},{6,7},{7,6},{8,9},{9,8},{10,11... | collective-permute-start | bytes 1990664 | tf_op jit(solution)/shard_map/ppermute | solution.py:512
  452.8 23.8 %collective-permute-start.20 = (bf16[144,1152]{1,0:T(8,128)(2,1)}, bf16[144,1152]{1,0:T(8,128)(2,1)}, u32[]{:S(2)}, u32[]{:S(2)}) collective-permute-start(bf16[144,1152]{1,0:T(8,128)(2,1)} %get-tuple-element.171), channel_id=1, source_target_pairs={{0,1},{1,0},{2,3},{3,2},{4,5},{5,4},{6,7},{7,6},{8,9},{9,8},{10,11... | collective-permute-start | bytes 995336 | tf_op jit(solution)/shard_map/ppermute | solution.py:512
  476.6 23.3 %collective-permute-start.15 = (bf16[32,4608]{1,0:T(8,128)(2,1)S(1)}, bf16[32,4608]{1,0:T(8,128)(2,1)}, u32[]{:S(2)}, u32[]{:S(2)}) collective-permute-start(bf16[32,4608]{1,0:T(8,128)(2,1)S(1)} %maximum_select_fusion.2), channel_id=1, source_target_pairs={{0,8},{2,10},{4,12},{6,14},{8,0},{10,2},{12,4},{14,6},{16,24},{18,... | collective-permute-start | bytes 884744 | tf_op jit(solution)/shard_map/ppermute | solution.py:513
  484.7 17.3 %collective-permute-start.26 = (bf16[192,1152]{1,0:T(8,128)(2,1)}, bf16[192,1152]{1,0:T(8,128)(2,1)S(1)}, u32[]{:S(2)}, u32[]{:S(2)}) collective-permute-start(bf16[192,1152]{1,0:T(8,128)(2,1)} %get-tuple-element.182), channel_id=1, source_target_pairs={{0,8},{2,10},{4,12},{6,14},{8,0},{10,2},{12,4},{14,6},{16,24},{18,... | collective-permute-start | bytes 1327112 | tf_op jit(solution)/shard_map/ppermute | solution.py:513
  490.2 10.6 %collective-permute-start.27 = (bf16[72,1152]{1,0:T(8,128)(2,1)}, bf16[72,1152]{1,0:T(8,128)(2,1)}, u32[]{:S(2)}, u32[]{:S(2)}) collective-permute-start(bf16[72,1152]{1,0:T(8,128)(2,1)} %get-tuple-element.184), channel_id=1, source_target_pairs={{0,8},{2,10},{4,12},{6,14},{8,0},{10,2},{12,4},{14,6},{16,24},{18,... | collective-permute-start | bytes 497672 | tf_op jit(solution)/shard_map/ppermute | solution.py:513
  498.9 29.8 %collective-permute-start.29 = (bf16[2,144,1152]{2,1,0:T(8,128)(2,1)}, bf16[2,144,1152]{2,1,0:T(8,128)(2,1)S(1)}, u32[]{:S(2)}, u32[]{:S(2)}) collective-permute-start(bf16[2,144,1152]{2,1,0:T(8,128)(2,1)} %get-tuple-element.189), channel_id=1, source_target_pairs={{0,4},{2,6},{4,0},{6,2},{8,12},{10,14},{12,8},{14,10},{16,20},{18,... | collective-permute-start | bytes 1990664 | tf_op jit(solution)/shard_map/ppermute | solution.py:513
  499.5 32.1 %collective-permute-start.30 = (bf16[2,144,1152]{2,1,0:T(8,128)(2,1)}, bf16[2,144,1152]{2,1,0:T(8,128)(2,1)S(1)}, u32[]{:S(2)}, u32[]{:S(2)}) collective-permute-start(bf16[2,144,1152]{2,1,0:T(8,128)(2,1)} %get-tuple-element.190), channel_id=1, source_target_pairs={{0,1},{1,0},{2,3},{3,2},{4,5},{5,4},{6,7},{7,6},{8,9},{9,8},{10,11... | collective-permute-start | bytes 1990664 | tf_op jit(solution)/shard_map/ppermute | solution.py:512
  499.9 13.4 %collective-permute-start.24 = (bf16[72,3072]{1,0:T(8,128)(2,1)}, bf16[72,3072]{1,0:T(8,128)(2,1)S(1)}, u32[]{:S(2)}, u32[]{:S(2)}) collective-permute-start(bf16[72,3072]{1,0:T(8,128)(2,1)} %get-tuple-element.179), channel_id=1, source_target_pairs={{0,8},{2,10},{4,12},{6,14},{8,0},{10,2},{12,4},{14,6},{16,24},{18,... | collective-permute-start | bytes 1327112 | tf_op jit(solution)/shard_map/ppermute | solution.py:513
  500.8 18.9 %collective-permute-start.25 = (bf16[72,3072]{1,0:T(8,128)(2,1)}, bf16[72,3072]{1,0:T(8,128)(2,1)}, u32[]{:S(2)}, u32[]{:S(2)}) collective-permute-start(bf16[72,3072]{1,0:T(8,128)(2,1)} %get-tuple-element.180), channel_id=1, source_target_pairs={{0,8},{2,10},{4,12},{6,14},{8,0},{10,2},{12,4},{14,6},{16,24},{18,... | collective-permute-start | bytes 1327112 | tf_op jit(solution)/shard_map/ppermute | solution.py:513
  502.0 26.6 %collective-permute-start.28 = (bf16[144,1152]{1,0:T(8,128)(2,1)}, bf16[144,1152]{1,0:T(8,128)(2,1)}, u32[]{:S(2)}, u32[]{:S(2)}) collective-permute-start(bf16[144,1152]{1,0:T(8,128)(2,1)} %get-tuple-element.186), channel_id=1, source_target_pairs={{0,4},{2,6},{4,0},{6,2},{8,12},{10,14},{12,8},{14,10},{16,20},{18,... | collective-permute-start | bytes 995336 | tf_op jit(solution)/shard_map/ppermute | solution.py:513
  513.3 26.2 %collective-permute-start.12 = (bf16[4,1152]{1,0:T(4,128)(2,1)S(1)}, bf16[4,1152]{1,0:T(4,128)(2,1)S(1)}, u32[]{:S(2)}, u32[]{:S(2)}) collective-permute-start(bf16[4,1152]{1,0:T(4,128)(2,1)S(1)} %fusion.5), channel_id=1, source_target_pairs={{0,1},{1,0},{2,3},{3,2},{4,5},{5,4},{6,7},{7,6},{8,9},{9,8},{10,11... | collective-permute-start | bytes 27656 | tf_op jit(solution)/shard_map/ppermute | solution.py:512
  519.7 72.4 %collective-permute-start.16 = (bf16[64,4608]{1,0:T(8,128)(2,1)S(1)}, bf16[64,4608]{1,0:T(8,128)(2,1)S(1)}, u32[]{:S(2)}, u32[]{:S(2)}) collective-permute-start(bf16[64,4608]{1,0:T(8,128)(2,1)S(1)} %maximum_select_fusion.1), channel_id=1, source_target_pairs={{0,16},{2,18},{4,20},{6,22},{8,24},{10,26},{12,28},{14,30},{16,0},... | collective-permute-start | bytes 1769480 | tf_op jit(solution)/shard_map/ppermute | solution.py:513
  528.6 48.6 %collective-permute-start.31 = (bf16[36,3072]{1,0:T(8,128)(2,1)}, bf16[36,3072]{1,0:T(8,128)(2,1)S(1)}, u32[]{:S(2)}, u32[]{:S(2)}) collective-permute-start(bf16[36,3072]{1,0:T(8,128)(2,1)} %get-tuple-element.193), channel_id=1, source_target_pairs={{0,16},{2,18},{4,20},{6,22},{8,24},{10,26},{12,28},{14,30},{16,0},... | collective-permute-start | bytes 663560 | tf_op jit(solution)/shard_map/ppermute | solution.py:513
  528.7 49.2 %collective-permute-start.32 = (bf16[36,3072]{1,0:T(8,128)(2,1)}, bf16[36,3072]{1,0:T(8,128)(2,1)S(1)}, u32[]{:S(2)}, u32[]{:S(2)}) collective-permute-start(bf16[36,3072]{1,0:T(8,128)(2,1)} %get-tuple-element.195), channel_id=1, source_target_pairs={{0,16},{2,18},{4,20},{6,22},{8,24},{10,26},{12,28},{14,30},{16,0},... | collective-permute-start | bytes 663560 | tf_op jit(solution)/shard_map/ppermute | solution.py:513
  531.6 45.6 %collective-permute-start.34 = (bf16[36,1152]{1,0:T(8,128)(2,1)}, bf16[36,1152]{1,0:T(8,128)(2,1)S(1)}, u32[]{:S(2)}, u32[]{:S(2)}) collective-permute-start(bf16[36,1152]{1,0:T(8,128)(2,1)} %get-tuple-element.198), channel_id=1, source_target_pairs={{0,16},{2,18},{4,20},{6,22},{8,24},{10,26},{12,28},{14,30},{16,0},... | collective-permute-start | bytes 248840 | tf_op jit(solution)/shard_map/ppermute | solution.py:513
  539.5 40.8 %collective-permute-start.33 = (bf16[96,1152]{1,0:T(8,128)(2,1)S(1)}, bf16[96,1152]{1,0:T(8,128)(2,1)S(1)}, u32[]{:S(2)}, u32[]{:S(2)}) collective-permute-start(bf16[96,1152]{1,0:T(8,128)(2,1)S(1)} %copy-done.30), channel_id=1, source_target_pairs={{0,16},{2,18},{4,20},{6,22},{8,24},{10,26},{12,28},{14,30},{16,0},... | collective-permute-start | bytes 663560 | tf_op jit(solution)/shard_map/ppermute | solution.py:513
  577.2 6.6 %collective-permute-start.35 = (bf16[72,1152]{1,0:T(8,128)(2,1)S(1)}, bf16[72,1152]{1,0:T(8,128)(2,1)S(1)}, u32[]{:S(2)}, u32[]{:S(2)}) collective-permute-start(bf16[72,1152]{1,0:T(8,128)(2,1)S(1)} %copy-done.31), channel_id=1, source_target_pairs={{0,8},{2,10},{4,12},{6,14},{8,0},{10,2},{12,4},{14,6},{16,24},{18,... | collective-permute-start | bytes 497672 | tf_op jit(solution)/shard_map/ppermute | solution.py:513
  577.3 7.4 %collective-permute-start.36 = (bf16[144,1152]{1,0:T(8,128)(2,1)}, bf16[144,1152]{1,0:T(8,128)(2,1)S(1)}, u32[]{:S(2)}, u32[]{:S(2)}) collective-permute-start(bf16[144,1152]{1,0:T(8,128)(2,1)} %get-tuple-element.202), channel_id=1, source_target_pairs={{0,1},{1,0},{2,3},{3,2},{4,5},{5,4},{6,7},{7,6},{8,9},{9,8},{10,11... | collective-permute-start | bytes 995336 | tf_op jit(solution)/shard_map/ppermute | solution.py:512
  578.0 7.9 %collective-permute-start.37 = (bf16[144,1152]{1,0:T(8,128)(2,1)}, bf16[144,1152]{1,0:T(8,128)(2,1)S(1)}, u32[]{:S(2)}, u32[]{:S(2)}) collective-permute-start(bf16[144,1152]{1,0:T(8,128)(2,1)} %get-tuple-element.203), channel_id=1, source_target_pairs={{0,4},{2,6},{4,0},{6,2},{8,12},{10,14},{12,8},{14,10},{16,20},{18,... | collective-permute-start | bytes 995336 | tf_op jit(solution)/shard_map/ppermute | solution.py:513
  590.1 6.6 %collective-permute-start.38 = (bf16[72,1152]{1,0:T(8,128)(2,1)}, bf16[72,1152]{1,0:T(8,128)(2,1)S(1)}, u32[]{:S(2)}, u32[]{:S(2)}) collective-permute-start(bf16[72,1152]{1,0:T(8,128)(2,1)} %get-tuple-element.206), channel_id=1, source_target_pairs={{0,8},{2,10},{4,12},{6,14},{8,0},{10,2},{12,4},{14,6},{16,24},{18,... | collective-permute-start | bytes 497672 | tf_op jit(solution)/shard_map/ppermute | solution.py:513
  591.7 7.7 %collective-permute-start.39 = (bf16[72,1152]{1,0:T(8,128)(2,1)}, bf16[72,1152]{1,0:T(8,128)(2,1)S(1)}, u32[]{:S(2)}, u32[]{:S(2)}) collective-permute-start(bf16[72,1152]{1,0:T(8,128)(2,1)} %get-tuple-element.207), channel_id=1, source_target_pairs={{0,8},{2,10},{4,12},{6,14},{8,0},{10,2},{12,4},{14,6},{16,24},{18,... | collective-permute-start | bytes 497672 | tf_op jit(solution)/shard_map/ppermute | solution.py:513
  592.4 14.7 %collective-permute-start.42 = (bf16[36,1152]{1,0:T(8,128)(2,1)S(1)}, bf16[36,1152]{1,0:T(8,128)(2,1)S(1)}, u32[]{:S(2)}, u32[]{:S(2)}) collective-permute-start(bf16[36,1152]{1,0:T(8,128)(2,1)S(1)} %copy-done.32), channel_id=1, source_target_pairs={{0,16},{2,18},{4,20},{6,22},{8,24},{10,26},{12,28},{14,30},{16,0},... | collective-permute-start | bytes 248840 | tf_op jit(solution)/shard_map/ppermute | solution.py:513
  602.8 7.6 %collective-permute-start.40 = (bf16[36,1152]{1,0:T(8,128)(2,1)}, bf16[36,1152]{1,0:T(8,128)(2,1)S(1)}, u32[]{:S(2)}, u32[]{:S(2)}) collective-permute-start(bf16[36,1152]{1,0:T(8,128)(2,1)} %get-tuple-element.210), channel_id=1, source_target_pairs={{0,16},{2,18},{4,20},{6,22},{8,24},{10,26},{12,28},{14,30},{16,0},... | collective-permute-start | bytes 248840 | tf_op jit(solution)/shard_map/ppermute | solution.py:513
  604.0 8.3 %collective-permute-start.41 = (bf16[36,1152]{1,0:T(8,128)(2,1)}, bf16[36,1152]{1,0:T(8,128)(2,1)S(1)}, u32[]{:S(2)}, u32[]{:S(2)}) collective-permute-start(bf16[36,1152]{1,0:T(8,128)(2,1)} %get-tuple-element.211), channel_id=1, source_target_pairs={{0,16},{2,18},{4,20},{6,22},{8,24},{10,26},{12,28},{14,30},{16,0},... | collective-permute-start | bytes 248840 | tf_op jit(solution)/shard_map/ppermute | solution.py:513
  (33 other events, 430.5 us)

commit v5 on v4

--- a/solution.py
+++ b/solution.py
@@ -312,10 +312,14 @@
     do = nt(ga, w_out_ref[...]).astype(bf16)
     do_ref[...] = do
     dot_ref[...] = head_sum(do.astype(f32) * o_ref[...], gather_ref).T
-    sums_ref[0, 0:1, :] = jnp.sum(grad_mid * attn_ref[...], axis=0, keepdims=True)
-    sums_ref[0, 1:2, :] = jnp.sum(dmod, axis=0, keepdims=True)
-    sums_ref[0, 2:3, :] = jnp.sum(dmod * norm, axis=0, keepdims=True)
-    sums_ref[0, 3:4, :] = jnp.sum(incoming * ffn_ref[...], axis=0, keepdims=True)
+
+    @pl.when(block == 0)
+    def _():
+        sums_ref[...] = jnp.zeros_like(sums_ref)
+
+    for index, term in enumerate((grad_mid * attn_ref[...], dmod, dmod * norm, incoming * ffn_ref[...])):
+        columns = slice(index * width, (index + 1) * width)
+        sums_ref[pl.ds(slot, 1), columns] += jnp.sum(term, axis=0, keepdims=True)
 
 
 def attend_back_kernel(
@@ -370,11 +374,13 @@
 
 def project_back_kernel(
     slots, dqt_ref, dk_ref, dv_ref, raw_ref, inv_ref, q_ref, k_ref, x_ref, grad_mid_ref, units_ref, mod_ref,
-    w_ref, coords_ref, cos_ref, sin_ref, gain_ref, gather_ref, spread_ref,
-    grad_x_ref, sums_ref, gains_ref, q_send_ref, q_own_ref, k_send_ref, k_own_ref, accq_ref, acck_ref,
+    w_ref, coords_ref, cos_ref, sin_ref, gain_ref, gather_ref, spread_ref, other_sums_ref,
+    grad_x_ref, gains_ref, grad_own_ref, grad_other_ref, q_send_ref, q_own_ref, k_send_ref, k_own_ref,
+    accq_ref, acck_ref, sums_ref,
 ):
     width = x_ref.shape[1]
     block = pl.program_id(0)
+    last_block = pl.num_programs(0) - 1
     slot = slots[block]
 
     @pl.when(block == 0)
@@ -408,8 +414,26 @@
     norm, inverse = normed(x_ref[...].astype(f32))
     grad_x = grad_mid_ref[...] + norm_back(dmod, part(mod_ref, slot, 1, width), norm, inverse)
     grad_x_ref[...] = grad_x.astype(bf16)
-    sums_ref[0, 0:1, :] = jnp.sum(dmod, axis=0, keepdims=True)
-    sums_ref[0, 1:2, :] = jnp.sum(dmod * norm, axis=0, keepdims=True)
+
+    @pl.when(block == 0)
+    def _():
+        sums_ref[...] = jnp.zeros_like(sums_ref)
+
+    for index, term in enumerate((dmod, dmod * norm)):
+        columns = slice(index * width, (index + 1) * width)
+        sums_ref[pl.ds(slot, 1), columns] += jnp.sum(term, axis=0, keepdims=True)
+
+    @pl.when(block == last_block)
+    def _():
+        mod = slots[last_block + 2]
+        count = sums_ref.shape[0]
+        mine = jnp.concatenate([sums_ref[...]] * 2, axis=0)
+        rest = jnp.concatenate([other_sums_ref[...]] * 2, axis=0)
+        row = lax.broadcasted_iota(jnp.int32, (2 * count, 1), 0) // count
+        attn_part = jnp.where(row == mod, jnp.concatenate([mine, rest[:, :width]], axis=1), 0.0)
+        ffn_part = jnp.where(row == mod, rest[:, width:], 0.0)
+        grad_own_ref[...] = jnp.where(mod == 0, attn_part, ffn_part).astype(bf16)
+        grad_other_ref[...] = jnp.where(mod == 0, ffn_part, attn_part).astype(bf16)
 
 
 def value_kernel(bits, units_ref, rhs_ref, send_ref, own_ref):
@@ -417,34 +441,74 @@
     product(units_ref, bits[0], rhs_ref[...], own_ref)
 
 
-def fold_kernel(bits, *refs, plans):
-    count = len(plans)
-    for i, (kind, bit, rows) in enumerate(plans):
-        own_ref, got_ref, send_ref, keep_ref = refs[2 * i], refs[2 * i + 1], refs[2 * count + 2 * i], refs[2 * count + 2 * i + 1]
-        mine = bits[bit]
-        if kind in ("outer", "inner"):
-            for j in range(2):
-                away = 2 * (1 - mine) + j if kind == "outer" else 2 * j + 1 - mine
-                own = 2 * mine + j if kind == "outer" else 2 * j + mine
-                send_ref[j] = (own_ref[away].astype(f32) + got_ref[away].astype(f32)).astype(bf16)
-                keep_ref[j] = own_ref[own].astype(f32) + got_ref[own].astype(f32)
-        elif kind == "unit":
-            send_ref[...] = (own_ref[1 - mine] + got_ref[1 - mine].astype(f32)).astype(bf16)
-            keep_ref[...] = own_ref[mine] + got_ref[mine].astype(f32)
-        else:
-            total = own_ref[...] + got_ref[...].astype(f32)
-            for j in range(total.shape[0] // (2 * rows)):
-                first = total[2 * j * rows : (2 * j + 1) * rows]
-                second = total[(2 * j + 1) * rows : (2 * j + 2) * rows]
-                place = slice(j * rows, (j + 1) * rows)
+def split_step(bits, ins, outs, *, lead, at, bit, pair_rows):
+    own_ref, got_ref = ins
+    send_ref, keep_ref = outs
+    mine = bits[bit]
+
+    def total(*index):
+        return own_ref[index].astype(f32) + got_ref[index].astype(f32)
+
+    if at is None:
+        for j in range(max(lead, 1)):
+            index = (j,) if lead else ()
+            value = total(*index) if lead else own_ref[...].astype(f32) + got_ref[...].astype(f32)
+            rows = pair_rows or value.shape[0] // 2
+            for p in range(value.shape[0] // (2 * rows)):
+                first = value[2 * p * rows : (2 * p + 1) * rows]
+                second = value[(2 * p + 1) * rows : (2 * p + 2) * rows]
+                place = index + (slice(p * rows, (p + 1) * rows),)
                 send_ref[place] = jnp.where(mine == 1, first, second).astype(bf16)
                 keep_ref[place] = jnp.where(mine == 1, second, first)
-
-
-def last_kernel(*refs):
-    count = len(refs) // 3
-    for i in range(count):
-        refs[2 * count + i][...] = refs[2 * i][...] + refs[2 * i + 1][...].astype(f32)
+        return
+    for j in range(lead // 2):
+        place = (j,) if lead > 2 else (Ellipsis,)
+        away = 1 - mine if lead == 2 else 2 * (1 - mine) + j if at == 0 else 2 * j + 1 - mine
+        own = mine if lead == 2 else 2 * mine + j if at == 0 else 2 * j + mine
+        send_ref[place] = total(away).astype(bf16)
+        keep_ref[place] = total(own)
+
+
+def sum_step(bits, ins, outs):
+    outs[0][...] = ins[0][...] + ins[1][...]
+
+
+def pair_step(bits, ins, outs):
+    own_ref, got_ref, activated_ref = ins
+    width = activated_ref.shape[1]
+    outs[0][:, :width] = activated_ref[...]
+    outs[0][:, width:] = (own_ref[...].astype(f32) + got_ref[...].astype(f32)).astype(bf16)
+
+
+def joined(ins):
+    return jnp.concatenate([ref[...].astype(f32) for ref in ins], axis=0).astype(bf16)
+
+
+def join_step(bits, ins, outs):
+    outs[0][...] = joined(ins)
+
+
+def last_step(bits, ins, outs):
+    outs[0][...] = ins[0][...] + ins[1][...].astype(f32)
+
+
+def ada_step(bits, ins, outs, *, width):
+    rows = outs[0].shape[0]
+    every = joined(ins)
+    position = bits[0] + sum(bits[1 + k] * 2**k for k in range(1, (width // rows).bit_length() - 1))
+    feature = lax.broadcasted_iota(jnp.int32, (width, 128), 0)
+    place = lax.broadcasted_iota(jnp.int32, (width, 128), 1)
+    chosen = (feature == position * rows + place) & (place < rows)
+    own = nn(every[:, :width], chosen.astype(f32).astype(bf16)).astype(bf16)
+    outs[0][...] = tn(own, every[:, width:])[:rows]
+
+
+def step_kernel(bits, *refs, plans):
+    n_in = sum(plan[1] for plan in plans)
+    ins, outs = refs[:n_in], refs[n_in:]
+    for function, takes, gives in plans:
+        function(bits, ins[:takes], outs[:gives])
+        ins, outs = ins[takes:], outs[gives:]
 
 
 class Chain:
@@ -452,7 +516,7 @@
         self.last = None
 
     def __call__(
-        self, kernel, grid, in_specs, out_specs, out_shape, args, scalars=None, scratch=(), name=None
+        self, kernel, grid, in_specs, out_specs, out_shape, args, scalars=None, scratch=(), name=None, aliases=None
     ):
         ahead = 0 if scalars is None else 1
         body = kernel
@@ -474,12 +538,13 @@
         outs = pl.pallas_call(
             body,
             grid_spec=spec,
+            input_output_aliases=aliases or {},
             out_shape=out_shape,
             compiler_params=pltpu.CompilerParams(vmem_limit_bytes=VMEM),
             cost_estimate=pl.CostEstimate(flops=1, bytes_accessed=1, transcendentals=0),
             name=name,
         )(*(() if scalars is None else (scalars,)), *token, *args)
-        self.last = outs[-1]
+        self.last = outs[0]
         return outs
 
 
@@ -497,6 +562,10 @@
 
 def whole(dims):
     return rows_of(dims, None)
+
+
+def column_parts(dims, steps):
+    return rows_of(dims[:-1] + (dims[-1] // steps,), len(dims) - 1)
 
 
 class Reducer:
@@ -515,64 +584,127 @@
     def bit_of(self, bit):
         return 1 if bit == "mod" else bit + 1 if bit else 0
 
-    def stream(self, sent, own, mod_first, pair_rows=None):
-        return Stream(self, sent, own, mod_first, pair_rows)
-
-    def fold(self, streams, name):
+    def fold(self, streams, name, last=False):
         plans, args, outs = [], [], []
         for stream in streams:
-            plan, part_shape = stream.plan()
-            plans.append(plan)
-            args += [stream.own, stream.got]
-            outs += [shape(part_shape, bf16), shape(part_shape, f32)]
+            function, shapes = stream.last_plan() if last else stream.plan()
+            inputs = stream.inputs()
+            plans.append((function, len(inputs), len(shapes)))
+            args += inputs
+            outs += shapes
+        steps = 3 if not last and len(streams) == 1 and args[0].ndim == 3 and args[0].shape[-1] % 384 == 0 else 1
         results = self.call(
-            functools.partial(fold_kernel, plans=plans),
-            (1,),
-            [whole(arg.shape) for arg in args],
-            [whole(out.shape) for out in outs],
+            functools.partial(step_kernel, plans=plans),
+            (steps,),
+            [column_parts(arg.shape, steps) for arg in args],
+            [column_parts(out.shape, steps) for out in outs],
             outs,
             args,
             scalars=self.bits,
-            name=name + "_fold",
+            name=name,
         )
-        for i, stream in enumerate(streams):
-            stream.step(results[2 * i], results[2 * i + 1])
-
-    def last(self, streams, name):
-        args = [arr for stream in streams for arr in (stream.own, stream.got)]
-        outs = [shape(stream.own.shape, f32) for stream in streams]
+        results = list(results)
+        if last:
+            return results
+        for stream, plan in zip(streams, plans):
+            stream.step(results[: plan[2]])
+            results = results[plan[2] :]
+
+    def pass_on(self, arrays):
+        anywhere = [pl.BlockSpec(memory_space=pl.ANY)] * len(arrays)
         return self.call(
-            last_kernel,
+            lambda *refs: None,
             (1,),
-            [whole(arg.shape) for arg in args],
-            [whole(out.shape) for out in outs],
-            outs,
-            args,
-            name=name + "_last",
+            anywhere,
+            anywhere,
+            [shape(arr.shape, arr.dtype) for arr in arrays],
+            arrays,
+            name="pass_on",
+            aliases={i + 1: i for i in range(len(arrays))},
         )
 
 
 class Stream:
-    def __init__(self, reducer, sent, own, mod_first, pair_rows):
-        self.r, self.own, self.pair_rows, self.mod_first = reducer, own, pair_rows, mod_first
-        self.steps = ["mod", 1] if mod_first else [1, "mod"]
-        self.steps += list(range(2, reducer.n_dp.bit_length() - 1))
-        self.at = 0
+    def __init__(self, reducer, sent, own, first, pair_rows=None):
+        self.r, self.own, self.pair_rows = reducer, own, pair_rows
+        order = ["mod", 1, 2]
+        self.steps = order[first:] + order[:first] + list(range(3, reducer.n_dp.bit_length() - 1))
+        self.lead = ["mod", 1]
         self.got = reducer.swap(sent, 0)
 
+    def inputs(self):
+        return [self.own, self.got]
+
     def plan(self):
-        bit = self.r.bit_of(self.steps[self.at])
+        bit = self.steps[0]
         dims = self.own.shape
-        if self.at == 0:
-            return ("outer" if self.mod_first else "inner", bit, 0), (2,) + dims[1:]
-        if self.at == 1:
-            return ("unit", bit, 0), dims[1:]
-        return ("rows", bit, self.pair_rows or dims[0] // 2), (dims[0] // 2, dims[1])
-
-    def step(self, sent, own):
-        self.own = own
-        self.got = self.r.swap(sent, self.steps[self.at])
-        self.at += 1
+        at = self.lead.index(bit) if bit in self.lead else None
+        function = functools.partial(
+            split_step, lead=dims[0] if self.lead else 0, at=at, bit=self.r.bit_of(bit), pair_rows=self.pair_rows
+        )
+        if at is None:
+            dims = dims[:-2] + (dims[-2] // 2, dims[-1])
+        else:
+            dims = dims[1:] if len(self.lead) == 1 else (2,) + dims[1:]
+        return function, [shape(dims, bf16), shape(dims, f32)]
+
+    def step(self, results):
+        bit = self.steps.pop(0)
+        if bit in self.lead:
+            self.lead.remove(bit)
+        sent, self.own = results
+        self.got = self.r.swap(sent, bit)
+
+    def last_plan(self):
+        return last_step, [shape(self.own.shape, f32)]
+
+
+class Total:
+    def __init__(self, reducer, own):
+        self.r, self.own = reducer, own
+        self.steps = ["mod"] + list(range(1, reducer.n_dp.bit_length() - 1))
+        self.got = reducer.swap(own, 0)
+
+    def inputs(self):
+        return [self.own, self.got]
+
+    def plan(self):
+        return sum_step, [shape(self.own.shape, f32)]
+
+    def step(self, results):
+        (self.own,) = results
+        self.got = self.r.swap(self.own, self.steps.pop(0))
+
+    def last_plan(self):
+        return self.plan()
+
+
+class Gather:
+    def __init__(self, reducer, sent, own, activated):
+        self.r, self.own, self.activated = reducer, own, activated
+        self.steps = list(range(reducer.n_dp.bit_length() - 2, -1, -1))
+        self.got = reducer.swap(sent, "mod")
+        self.pair = None
+
+    def inputs(self):
+        return [self.own, self.got] + ([self.activated] if self.pair is None else [])
+
+    def plan(self):
+        rows, columns = self.own.shape
+        if self.pair is None:
+            return pair_step, [shape((rows, columns + self.activated.shape[1]), bf16)]
+        return join_step, [shape((2 * rows, columns), bf16)]
+
+    def step(self, results):
+        (self.own,) = results
+        if self.pair is None:
+            self.pair = self.own
+        self.got = self.r.swap(self.own, self.steps.pop(0))
+
+    def last_plan(self):
+        width = self.activated.shape[1]
+        function = functools.partial(ada_step, width=width)
+        return function, [shape((width // self.r.n_dp, self.own.shape[1] - width), f32)]
 
 
 def silu_grad(v):
@@ -670,25 +802,25 @@
         scratch=[pltpu.VMEM((8, piece, count), bf16)],
         name="ffn",
     )
-    gate = reducer.stream(gate_send, gate_own, True)
-    up = reducer.stream(up_send, up_own, False)
-    down = reducer.stream(
-        down_send.reshape(4, ff // 8, width), down_own.reshape(4, ff // 8, width), True, rows_ff
-    )
-
-    slots_core = jnp.concatenate([slots, reducer.bits[:1]])
+    gate = Stream(reducer, gate_send, gate_own, 0)
+    up = Stream(reducer, up_send, up_own, 1)
+    down = Stream(
+        reducer, down_send.reshape(4, ff // 8, width), down_own.reshape(4, ff // 8, width), 2, rows_ff
+    )
+
+    slots_core = jnp.concatenate([slots, reducer.bits[:2]])
     output, grad_mid, grad_attended, dot_term, sums_b, out_send, out_own = call(
         middle_kernel,
         (blocks,),
         [token_spec] * 6 + [units_spec, mod_spec, square, fixed(gather.shape)],
-        [token_spec] * 3 + [rows_of((128, TB), 1), rows_of((1, 4, width))] + square_send,
-        [token_bf16, token_f32, token_bf16, lane_rows, shape((blocks, 4, width), f32)] + square_shapes,
+        [token_spec] * 3 + [rows_of((128, TB), 1), fixed((slots_n, 4 * width))] + square_send,
+        [token_bf16, token_f32, token_bf16, lane_rows, shape((slots_n, 4 * width), f32)] + square_shapes,
         (mid, ffn, grad_mod_ffn, cot, attn, attended, out_units, modulation, w_out, gather),
         scalars=slots_core,
         scratch=[pltpu.VMEM((width, width), f32)],
         name="middle",
     )
-    out = reducer.stream(out_send, out_own, False)
+    out = Stream(reducer, out_send, out_own, 1)
     reducer.fold([gate], "gate")
     reducer.fold([up], "up")
     reducer.fold([down], "down")
@@ -705,6 +837,10 @@
         scalars=slots,
         name="attend_back",
     )
+    reducer.fold([gate], "gate")
+    reducer.fold([up], "up")
+    reducer.fold([down], "down")
+    reducer.fold([out], "out")
     v_send, v_own = call(
         value_kernel,
         (1,),
@@ -715,70 +851,54 @@
         scalars=reducer.bits,
         name="value",
     )
-    v_part = reducer.stream(v_send, v_own, True)
-    reducer.fold([gate, up], "gate_up")
-    reducer.fold([out, v_part], "out_v")
-    reducer.fold([down], "down")
-    grad_tokens, sums_a, gain_sums, q_send, q_own, k_send, k_own = call(
+    v_part = Stream(reducer, v_send, v_own, 2)
+    grad_tokens, gain_sums, mod_own, mod_other, q_send, q_own, k_send, k_own = call(
         project_back_kernel,
         (blocks,),
         [rows_of((width, TB), 1), token_spec, token_spec, rows_of((TB, 2 * width)), rows_of((TB, 256))]
         + [token_spec] * 4
         + [units_spec, mod_spec, fixed((width, 3 * width)), rows_of((2, TB), 1)]
-        + table_specs,
-        [token_spec, rows_of((1, 2, width)), fixed((2, width))] + square_send * 2,
-        [token_bf16, shape((blocks, 2, width), f32), shape((2, width), f32)] + square_shapes * 2,
+        + table_specs + [fixed((slots_n, 4 * width))],
+        [token_spec, fixed((2, width))] + [fixed((2 * slots_n, half))] * 2 + square_send * 2,
+        [token_bf16, shape((2, width), f32)] + [shape((2 * slots_n, half), bf16)] * 2 + square_shapes * 2,
         (grad_query_t, grad_key, grad_value, raw, inverse, query, key, x, grad_mid, attn_units, modulation,
          w_qkv, coord)
-        + tables,
+        + tables + (sums_b,),
         scalars=slots_core,
-        scratch=[pltpu.VMEM((width, width), f32)] * 2,
+        scratch=[pltpu.VMEM((width, width), f32)] * 2 + [pltpu.VMEM((slots_n, 2 * width), f32)],
         name="project_back",
     )
-    q_part = reducer.stream(q_send, q_own, False)
-    k_part = reducer.stream(k_send, k_own, True)
-    reducer.fold([gate, up], "gate_up")
-    reducer.fold([down, out, v_part], "down_out_v")
-    reducer.fold([q_part, k_part], "q_k")
+    early = [gate, up, down, out]
+    arrived = [stream.got for stream in early + [v_part]]
+    *arrived, q_send, k_send, mod_other, gain_sums = reducer.pass_on(
+        arrived + [q_send, k_send, mod_other, gain_sums]
+    )
+    for stream, got in zip(early + [v_part], arrived):
+        stream.got = got
+    q_part = Stream(reducer, q_send, q_own, 1)
+    k_part = Stream(reducer, k_send, k_own, 0)
+    gains_total = Total(reducer, gain_sums)
+    every_mod = Gather(reducer, mod_other, mod_own, activated)
+    late = [q_part, k_part, gains_total, every_mod]
+    reducer.fold([v_part], "v")
+    reducer.fold(early, "early")
+    reducer.fold(late, "late")
     for _ in range(n_dp.bit_length() - 4):
-        reducer.fold([gate, up, down, out], "early")
-        reducer.fold([v_part], "v")
-        reducer.fold([q_part, k_part], "q_k")
-    summed_gate, summed_up, summed_down, summed_out = reducer.last([gate, up, down, out], "early")
-    reducer.fold([v_part, q_part, k_part], "v_q_k")
-    reducer.fold([q_part, k_part], "q_k")
-    summed = reducer.last([q_part, k_part, v_part], "q_k_v")
-    summed_qkv = jnp.concatenate(summed, axis=1)
-
-    sums = jnp.concatenate([sums_a, sums_b], axis=1).reshape(blocks, 6 * width)
-    in_slot = slots[None, :, None] == jnp.arange(slots_n)[:, None, None]
-    grad_modulation = jnp.sum(jnp.where(in_slot, sums[None], 0.0), axis=1).astype(bf16)
-    halves = grad_modulation.reshape(slots_n, n_mod, half)
-    own_half = lax.dynamic_index_in_dim(halves, mod_index, 1, keepdims=False)
-    other_half = lax.dynamic_index_in_dim(halves, 1 - mod_index, 1, keepdims=False)
-    grad_mod_flat = pair_order(own_half, reducer.swap(other_half, "mod"), mod_index).reshape(-1, half)
-    rows_ada = width // n_dp
-    gathered = jnp.concatenate([activated, grad_mod_flat], axis=1)
-    for bit in range(n_dp.bit_length() - 1):
-        other = reducer.swap(gathered, bit)
-        second = (lax.shift_right_logical(reducer.position, bit) & 1) == 1
-        gathered = jnp.where(
-            second, jnp.concatenate([other, gathered]), jnp.concatenate([gathered, other])
-        )
-    own_activated = lax.dynamic_slice_in_dim(
-        gathered[:, :width], reducer.position * rows_ada, rows_ada, axis=1
-    )
-    grad_w_ada = jnp.einsum("nd,nc->dc", own_activated, gathered[:, width:], preferred_element_type=f32)
-    grad_activated = jnp.einsum("nc,dc->nd", grad_mod_flat, w_ada, preferred_element_type=f32)
+        reducer.fold(early, "early")
+        reducer.fold([v_part] + late, "late")
+    summed_gate, summed_up, summed_down, summed_out = reducer.fold(early, "early", last=True)
+    reducer.fold([v_part] + late, "late")
+    reducer.fold([v_part] + late, "late")
+    *summed, gain_sums, grad_w_ada = reducer.fold([v_part] + late, "late", last=True)
+    summed_qkv = jnp.concatenate([summed[1], summed[2], summed[0]], axis=1)
+
+    grad_activated = jnp.einsum("nc,dc->nd", every_mod.pair[:, width:], w_ada, preferred_element_type=f32)
     grad_activated = grad_activated.reshape(n_mod, slots_n, width)
     own_part = lax.dynamic_index_in_dim(grad_activated, mod_index, 0, keepdims=False)
     other_part = lax.dynamic_index_in_dim(grad_activated, 1 - mod_index, 0, keepdims=False)
     grad_own = own_part + reducer.swap(other_part.astype(bf16), "mod").astype(f32)
     grad_cond = grad_own[None] * silu_grad(cond)
-
     gain_grads = jnp.sum(gain_sums.reshape(2, HEADS, HD), axis=1)
-    for bit in [0, "mod"] + list(range(1, n_dp.bit_length() - 1)):
-        gain_grads = gain_grads + reducer.swap(gain_grads, bit)
     return (
         output[None],
         grad_tokens[None],

time: 627 us -> 559 us (0.89)
  waiting for transfers between devices: 131 us -> 71.1 us
  Pallas kernels: 398 us -> 373 us
  starting transfers between devices: 51.6 us -> 72.9 us
    ppermute x36, waiting for transfers between devices: 95.5 us -> 57.5 us  [swap(): lax.ppermute(arr, 'dp', [(i, i ^ 1 << bit) for i in range(self.n_dp)])]
    pallas_call x24 -> x25, Pallas kernels: 398 us -> 373 us  [__call__(): pl.pallas_call(body, grid_spec=spec, input_output_aliases=aliases or {},...]
    ppermute x12, waiting for transfers between devices: 35.9 us -> 13.6 us  [swap(): return lax.ppermute(arr, 'mod', [(i, i ^ 1) for i in range(self.n_mod)])]
    ppermute x36, starting transfers between devices: 36.1 us -> 53.8 us  [swap(): lax.ppermute(arr, 'dp', [(i, i ^ 1 << bit) for i in range(self.n_dp)])]
  transfers between devices with their start and end apart: 48 -> 48, of which waited for: 19 -> 13; matrix products, arithmetic and copies ran while one was open for 3% -> 2% of each run, Pallas kernels for 26% -> 33%
where the time goes in v5:
time: 559 us; the launch traced here: 550 us
  Pallas kernels  373 us (67%)
  starting transfers between devices  72.9 us (13%)
  waiting for transfers between devices  71.1 us (13%)
  local copies, waits for them, and re-layouts  16.5 us (3%)
  matrix products  9.81 us (2%)
    pallas_call x25, Pallas kernels, __call__(): pl.pallas_call(body, grid_spec=spec, input_output_aliases=aliases or {},...  373 us
    ppermute x36, waiting for transfers between devices, swap(): lax.ppermute(arr, 'dp', [(i, i ^ 1 << bit) for i in range(self.n_dp)])  57.5 us
    ppermute x36, starting transfers between devices, swap(): lax.ppermute(arr, 'dp', [(i, i ^ 1 << bit) for i in range(self.n_dp)])  53.8 us
    ppermute x12, starting transfers between devices, swap(): return lax.ppermute(arr, 'mod', [(i, i ^ 1) for i in range(self.n_mod)])  19.2 us
    ppermute x12, waiting for transfers between devices, swap(): return lax.ppermute(arr, 'mod', [(i, i ^ 1) for i in range(self.n_mod)])  13.6 us
    unnamed x94, local copies, waits for them, and re-layouts  11.6 us
  transfers between devices with their start and end apart: 48, of which 13 were waited for; matrix products, arithmetic and copies ran while one was open for 2% of the time, Pallas kernels for 33%

profile of v5, /device:TPU:0, one launch (start us, length us, event | category | flops | bytes accessed | tf_op | source)
XLA Modules:
  0.0 549.8 jit_solution(1675757078574651057)
XLA Ops:
  0.6 3.0 collective-permute-start
  6.5 4.4 convolution_convert_fusion
  11.0 2.1 collective-permute-start.1
  16.3 29.1 %project.1 = (bf16[8,144,1024]{2,1,0:T(8,128)(2,1)}, f32[1024,2304]{1,0:T(8,128)}, f32[1024,256]{1,0:T(8,128)}, bf16[1024,1152]{1,0:T(8,128)(2,1)}, bf16[1024,11...) custom-call(s32[4]{0:T(128)} %bitcast.50, bf16[1024,1152]{1,0:T(8,128)(2,1)} %bitcast.37, ...), custom_call_target="tpu_custom_call" | custom-call | flops 1 | bytes 1 | tf_op jit(solution)/shard_map/project/pallas_call | solution.py:538
  45.4 48.2 %attend.1 = (f32[1024,1152]{1,0:T(8,128)}, f32[128,1024]{1,0:T(8,128)}, f32[1024,1152]{1,0:T(8,128)}, f32[1024,1152]{1,0:T(8,128)}, bf16[1024,1152]{1,0:T(8,128)...) custom-call(s32[4]{0:T(128)} %bitcast.51, ...), custom_call_target="tpu_custom_call" | custom-call | flops 1 | bytes 1 | tf_op jit(solution)/shard_map/attend/pallas_call | solution.py:538
  93.6 91.2 %ffn.1 = (bf16[4,144,3072]{2,1,0:T(8,128)(2,1)}, bf16[4,144,3072]{2,1,0:T(8,128)(2,1)}, bf16[4,144,3072]{2,1,0:T(8,128)(2,1)}, bf16[4,144,3072]{2,1,0:T(8,128)(2...) custom-call(s32[5]{0:T(128)} %stack.48.refs_0_, ...), custom_call_target="tpu_custom_call" | custom-call | flops 1 | bytes 1 | tf_op jit(solution)/shard_map/ffn/pallas_call | solution.py:538
  184.9 7.9 %collective-permute-start.2 = (bf16[4,144,3072]{2,1,0:T(8,128)(2,1)}, bf16[4,144,3072]{2,1,0:T(8,128)(2,1)}, u32[]{:S(2)}, u32[]{:S(2)}) collective-permute-start(bf16[4,144,3072]{2,1,0:T(8,128)(2,1)} %get-tuple-element.144.refs_1_), channel_id=1, source_target_pairs={{0,2},{2,0},{4,6},{6,4},{8,10},{10,8},{12,14},{14,12},{16,18},{18,... | collective-permute-start | bytes 10616840 | tf_op jit(solution)/shard_map/ppermute | solution.py:582
  193.9 25.2 %middle.1 = (bf16[1024,1152]{1,0:T(8,128)(2,1)}, f32[1024,1152]{1,0:T(8,128)}, bf16[1024,1152]{1,0:T(8,128)(2,1)}, f32[128,1024]{1,0:T(8,128)}, f32[4,4608]{1,0:...) custom-call(s32[6]{0:T(128)} %pad_add_fusion.refs_0_, ...), custom_call_target="tpu_custom_call" | custom-call | flops 1 | bytes 1 | tf_op jit(solution)/shard_map/middle/pallas_call | solution.py:538
  219.2 7.0 %gate.2 = (bf16[2,144,3072]{2,1,0:T(8,128)(2,1)}, f32[2,144,3072]{2,1,0:T(8,128)}) custom-call(s32[5]{0:T(128)} %stack.48.refs_0_, bf16[1024,1152]{1,0:T(8,128)(2,1)} %get-tuple-element.150.refs_1_, bf16[4,144,3072]{2,1,0:T(8,128)(2,1)} %get-tuple-element.151.refs_2_, bf16[4,144,3072]{2,1,0:T(8,128)(2,1)} %collective-permute-done.2.refs_3_), custom_call_target="tpu_custom_call" | custom-call | flops 1 | bytes 1 | tf_op jit(solution)/shard_map/gate/pallas_call | solution.py:538
  226.3 3.4 collective-permute-start.6
  229.7 7.1 %up.2 = (bf16[2,144,3072]{2,1,0:T(8,128)(2,1)}, f32[2,144,3072]{2,1,0:T(8,128)}) custom-call(s32[5]{0:T(128)} %stack.48.refs_0_, bf16[2,144,3072]{2,1,0:T(8,128)(2,1)} %get-tuple-element.152.refs_1_, bf16[4,144,3072]{2,1,0:T(8,128)(2,1)} %get-tuple-element.153.refs_2_, bf16[4,144,3072]{2,1,0:T(8,128)(2,1)} %collective-permute-done.3.refs_3_), custom_call_target="tpu_custom_call" | custom-call | flops 1 | bytes 1 | tf_op jit(solution)/shard_map/up/pallas_call | solution.py:538
  238.5 7.2 %down.2 = (bf16[4,192,1152]{2,1,0:T(8,128)(2,1)}, f32[4,192,1152]{2,1,0:T(8,128)}) custom-call(s32[5]{0:T(128)} %stack.48.refs_0_, bf16[2,144,3072]{2,1,0:T(8,128)(2,1)} %get-tuple-element.155.refs_1_, bf16[4,384,1152]{2,1,0:T(8,128)(2,1)} %bitcast.42, bf16[4,384,1152]{2,1,0:T(8,128)(2,1)} %copy-done.2), custom_call_target="tpu_custom_call" | custom-call | flops 1 | bytes 1 | tf_op jit(solution)/shard_map/down/pallas_call | solution.py:538
  246.0 4.5 out.2
  250.6 2.0 collective-permute-start.9
  252.6 39.0 %attend_back.1 = (f32[1152,1024]{1,0:T(8,128)}, f32[1024,1152]{1,0:T(8,128)}, bf16[1024,1152]{1,0:T(8,128)(2,1)}) custom-call(s32[4]{0:T(128)} %bitcast.52, bf16[2,144,1152]{2,1,0:T(8,128)(2,1)} %get-tuple-element.161.refs_1_, bf16[1024,1152]{1,0:T(8,128)(2,1)} %get-tuple-element.137.refs_5_.refs_2_.refs_7_, ...), custom_call_target="tpu_custom_call" | custom-call | flops 1 | bytes 1 | tf_op jit(solution)/shard_map/attend_back/pallas_call | solution.py:538
  291.6 5.4 gate.3
  296.9 5.5 %up.3 = (bf16[2,72,3072]{2,1,0:T(8,128)(2,1)}, f32[2,72,3072]{2,1,0:T(8,128)}) custom-call(s32[5]{0:T(128)} %stack.48.refs_0_, bf16[144,3072]{1,0:T(8,128)(2,1)} %get-tuple-element.168.refs_1_, f32[2,144,3072]{2,1,0:T(8,128)} %get-tuple-element.169.refs_2_, bf16[2,144,3072]{2,1,0:T(8,128)(2,1)} %collective-permute-done.7.refs_3_), custom_call_target="tpu_custom_call" | custom-call | flops 1 | bytes 1 | tf_op jit(solution)/shard_map/up/pallas_call | solution.py:538
  303.7 5.5 down.3
  310.0 4.2 out.3
  314.2 7.3 %value.1 = (bf16[4,144,1152]{2,1,0:T(8,128)(2,1)}, bf16[4,144,1152]{2,1,0:T(8,128)(2,1)}) custom-call(s32[5]{0:T(128)} %stack.48.refs_0_, bf16[2,72,1152]{2,1,0:T(8,128)(2,1)} %get-tuple-element.174.refs_1_, bf16[8,144,1024]{2,1,0:T(8,128)(2,1)} %get-tuple-element.136.refs_1_.refs_2_.refs_11_, bf16[1024,1152]{1,0:T(8,128)(2,1)} %get-tuple-element.175.refs_3_.refs_4_), custom_call_target="tpu_custom_call" | custom-call | flops 1 | bytes 1 | tf_op jit(solution)/shard_map/value/pallas_call | solution.py:538
  321.5 16.4 %collective-permute-start.14 = (bf16[4,144,1152]{2,1,0:T(8,128)(2,1)}, bf16[4,144,1152]{2,1,0:T(8,128)(2,1)S(1)}, u32[]{:S(2)}, u32[]{:S(2)}) collective-permute-start(bf16[4,144,1152]{2,1,0:T(8,128)(2,1)} %get-tuple-element.176.refs_1_), channel_id=1, source_target_pairs={{0,2},{2,0},{4,6},{6,4},{8,10},{10,8},{12,14},{14,12},{16,18},{18,... | collective-permute-start | bytes 3981320 | tf_op jit(solution)/shard_map/ppermute | solution.py:582
  337.9 2.8 collective-permute-start.12
  340.7 2.0 collective-permute-start.13
  342.7 44.1 %project_back.1 = (bf16[1024,1152]{1,0:T(8,128)(2,1)}, f32[2,1152]{1,0:T(2,128)}, bf16[8,3456]{1,0:T(8,128)(2,1)}, bf16[8,3456]{1,0:T(8,128)(2,1)}, bf16[4,144,1...) custom-call(s32[6]{0:T(128)} %pad_add_fusion.refs_0_, ...), custom_call_target="tpu_custom_call" | custom-call | flops 1 | bytes 1 | tf_op jit(solution)/shard_map/project_back/pallas_call | solution.py:538
  389.3 4.9 v.1
  394.2 6.7 %early.3 = (bf16[72,3072]{1,0:T(8,128)(2,1)}, f32[72,3072]{1,0:T(8,128)}, bf16[72,3072]{1,0:T(8,128)(2,1)}, f32[72,3072]{1,0:T(8,128)}, bf16[192,1152]{1,0:T(8,1...) custom-call(s32[5]{0:T(128)} %stack.48.refs_0_, ...), custom_call_target="tpu_custom_call" | custom-call | flops 1 | bytes 1 | tf_op jit(solution)/shard_map/early/pallas_call | solution.py:538
  404.2 10.2 %collective-permute-done.18.refs_9_ = bf16[8,3456]{1,0:T(8,128)(2,1)S(1)} collective-permute-done((bf16[8,3456]{1,0:T(8,128)(2,1)S(1)}, bf16[8,3456]{1,0:T(8,128)(2,1)S(1)}, u32[]{:S(2)}, u32[]{:S(2)}) %collective-permute-start.18) | collective-permute-done | bytes 55328 | tf_op jit(solution)/shard_map/ppermute | solution.py:581
  416.2 5.4 late.5
  423.4 2.0 collective-permute-start.25
  425.5 23.3 %collective-permute-done.22.refs_7_ = bf16[192,1152]{1,0:T(8,128)(2,1)S(1)} collective-permute-done((bf16[192,1152]{1,0:T(8,128)(2,1)}, bf16[192,1152]{1,0:T(8,128)(2,1)S(1)}, u32[]{:S(2)}, u32[]{:S(2)}) %collective-permute-start.22) | collective-permute-done | bytes 442400 | tf_op jit(solution)/shard_map/ppermute | solution.py:582
  449.8 4.6 early.4
  454.3 2.2 collective-permute-start.31
  458.1 2.9 collective-permute-done.27.refs_9_
  461.0 2.2 collective-permute-start.32
  463.2 7.5 %collective-permute-done.28.refs_11_ = bf16[8,4608]{1,0:T(8,128)(2,1)S(1)} collective-permute-done((bf16[8,4608]{1,0:T(8,128)(2,1)S(1)}, bf16[8,4608]{1,0:T(8,128)(2,1)S(1)}, u32[]{:S(2)}, u32[]{:S(2)}) %collective-permute-start.28) | collective-permute-done | bytes 73760 | tf_op jit(solution)/shard_map/ppermute | solution.py:582
  471.8 5.4 late.6
  477.2 3.6 collective-permute-start.34
  485.1 10.0 %collective-permute-done.29.refs_3_ = bf16[36,3072]{1,0:T(8,128)(2,1)S(1)} collective-permute-done((bf16[36,3072]{1,0:T(8,128)(2,1)S(1)}, bf16[36,3072]{1,0:T(8,128)(2,1)S(1)}, u32[]{:S(2)}, u32[]{:S(2)}) %collective-permute-start.29) | collective-permute-done | bytes 221216 | tf_op jit(solution)/shard_map/ppermute | solution.py:582
  496.3 3.6 early.5
  501.0 3.8 late.7
  509.8 5.4 fusion
  515.3 4.3 collective-permute-done.42.refs_11_
  520.3 3.5 late.8
  525.6 2.5 collective-permute-start.44
  528.5 2.5 collective-permute-start.43
  531.6 6.5 %collective-permute-done.44.refs_5_ = bf16[36,1152]{1,0:T(8,128)(2,1)S(1)} collective-permute-done((bf16[36,1152]{1,0:T(8,128)(2,1)}, bf16[36,1152]{1,0:T(8,128)(2,1)S(1)}, u32[]{:S(2)}, u32[]{:S(2)}) %collective-permute-start.44) | collective-permute-done | bytes 82976 | tf_op jit(solution)/shard_map/ppermute | solution.py:582
  538.2 2.0 collective-permute-done.45.refs_7_
  542.1 4.1 late.9
  (192 shorter events, 44.7 us)
Async XLA Ops:
  0.6 5.0 collective-permute-start
  11.0 4.6 collective-permute-start.1
  184.9 34.4 %collective-permute-start.2 = (bf16[4,144,3072]{2,1,0:T(8,128)(2,1)}, bf16[4,144,3072]{2,1,0:T(8,128)(2,1)}, u32[]{:S(2)}, u32[]{:S(2)}) collective-permute-start(bf16[4,144,3072]{2,1,0:T(8,128)(2,1)} %get-tuple-element.144.refs_1_), channel_id=1, source_target_pairs={{0,2},{2,0},{4,6},{6,4},{8,10},{10,8},{12,14},{14,12},{16,18},{18,... | collective-permute-start | bytes 10616840 | tf_op jit(solution)/shard_map/ppermute | solution.py:582
  192.7 36.9 %collective-permute-start.3 = (bf16[4,144,3072]{2,1,0:T(8,128)(2,1)}, bf16[4,144,3072]{2,1,0:T(8,128)(2,1)}, u32[]{:S(2)}, u32[]{:S(2)}) collective-permute-start(bf16[4,144,3072]{2,1,0:T(8,128)(2,1)} %get-tuple-element.154), channel_id=1, source_target_pairs={{0,2},{2,0},{4,6},{6,4},{8,10},{10,8},{12,14},{14,12},{16,18},{18,... | collective-permute-start | bytes 10616840 | tf_op jit(solution)/shard_map/ppermute | solution.py:582
  192.8 43.9 %collective-permute-start.4 = (bf16[4,384,1152]{2,1,0:T(8,128)(2,1)}, bf16[4,384,1152]{2,1,0:T(8,128)(2,1)S(1)}, u32[]{:S(2)}, u32[]{:S(2)}) collective-permute-start(bf16[4,384,1152]{2,1,0:T(8,128)(2,1)} %bitcast.54), channel_id=1, source_target_pairs={{0,2},{2,0},{4,6},{6,4},{8,10},{10,8},{12,14},{14,12},{16,18},{18,... | collective-permute-start | bytes 10616840 | tf_op jit(solution)/shard_map/ppermute | solution.py:582
  219.1 26.9 %collective-permute-start.5 = (bf16[4,144,1152]{2,1,0:T(8,128)(2,1)}, bf16[4,144,1152]{2,1,0:T(8,128)(2,1)}, u32[]{:S(2)}, u32[]{:S(2)}) collective-permute-start(bf16[4,144,1152]{2,1,0:T(8,128)(2,1)} %get-tuple-element.160), channel_id=1, source_target_pairs={{0,2},{2,0},{4,6},{6,4},{8,10},{10,8},{12,14},{14,12},{16,18},{18,... | collective-permute-start | bytes 3981320 | tf_op jit(solution)/shard_map/ppermute | solution.py:582
  226.3 65.3 %collective-permute-start.6 = (bf16[2,144,3072]{2,1,0:T(8,128)(2,1)}, bf16[2,144,3072]{2,1,0:T(8,128)(2,1)}, u32[]{:S(2)}, u32[]{:S(2)}) collective-permute-start(bf16[2,144,3072]{2,1,0:T(8,128)(2,1)} %get-tuple-element.152.refs_1_), channel_id=1, source_target_pairs={{0,1},{1,0},{2,3},{3,2},{4,5},{5,4},{6,7},{7,6},{8,9},{9,8},{10,11... | collective-permute-start | bytes 5308424 | tf_op jit(solution)/shard_map/ppermute | solution.py:581
  236.7 60.2 %collective-permute-start.7 = (bf16[2,144,3072]{2,1,0:T(8,128)(2,1)}, bf16[2,144,3072]{2,1,0:T(8,128)(2,1)}, u32[]{:S(2)}, u32[]{:S(2)}) collective-permute-start(bf16[2,144,3072]{2,1,0:T(8,128)(2,1)} %get-tuple-element.155.refs_1_), channel_id=1, source_target_pairs={{0,4},{2,6},{4,0},{6,2},{8,12},{10,14},{12,8},{14,10},{16,20},{18,... | collective-permute-start | bytes 5308424 | tf_op jit(solution)/shard_map/ppermute | solution.py:582
  245.8 56.7 %collective-permute-start.8 = (bf16[4,192,1152]{2,1,0:T(8,128)(2,1)}, bf16[4,192,1152]{2,1,0:T(8,128)(2,1)S(1)}, u32[]{:S(2)}, u32[]{:S(2)}) collective-permute-start(bf16[4,192,1152]{2,1,0:T(8,128)(2,1)} %get-tuple-element.158.refs_1_), channel_id=1, source_target_pairs={{0,8},{2,10},{4,12},{6,14},{8,0},{10,2},{12,4},{14,6},{16,24},{18,... | collective-permute-start | bytes 5308424 | tf_op jit(solution)/shard_map/ppermute | solution.py:582
  250.6 58.6 %collective-permute-start.9 = (bf16[2,144,1152]{2,1,0:T(8,128)(2,1)}, bf16[2,144,1152]{2,1,0:T(8,128)(2,1)S(1)}, u32[]{:S(2)}, u32[]{:S(2)}) collective-permute-start(bf16[2,144,1152]{2,1,0:T(8,128)(2,1)} %get-tuple-element.161.refs_1_), channel_id=1, source_target_pairs={{0,4},{2,6},{4,0},{6,2},{8,12},{10,14},{12,8},{14,10},{16,20},{18,... | collective-permute-start | bytes 1990664 | tf_op jit(solution)/shard_map/ppermute | solution.py:582
  321.5 65.4 %collective-permute-start.14 = (bf16[4,144,1152]{2,1,0:T(8,128)(2,1)}, bf16[4,144,1152]{2,1,0:T(8,128)(2,1)S(1)}, u32[]{:S(2)}, u32[]{:S(2)}) collective-permute-start(bf16[4,144,1152]{2,1,0:T(8,128)(2,1)} %get-tuple-element.176.refs_1_), channel_id=1, source_target_pairs={{0,2},{2,0},{4,6},{6,4},{8,10},{10,8},{12,14},{14,12},{16,18},{18,... | collective-permute-start | bytes 3981320 | tf_op jit(solution)/shard_map/ppermute | solution.py:582
  337.9 49.0 %collective-permute-start.12 = (bf16[2,192,1152]{2,1,0:T(8,128)(2,1)}, bf16[2,192,1152]{2,1,0:T(8,128)(2,1)S(1)}, u32[]{:S(2)}, u32[]{:S(2)}) collective-permute-start(bf16[2,192,1152]{2,1,0:T(8,128)(2,1)} %get-tuple-element.172.refs_1_), channel_id=1, source_target_pairs={{0,1},{1,0},{2,3},{3,2},{4,5},{5,4},{6,7},{7,6},{8,9},{9,8},{10,11... | collective-permute-start | bytes 2654216 | tf_op jit(solution)/shard_map/ppermute | solution.py:581
  340.7 46.2 %collective-permute-start.11 = (bf16[2,72,3072]{2,1,0:T(8,128)(2,1)}, bf16[2,72,3072]{2,1,0:T(8,128)(2,1)S(1)}, u32[]{:S(2)}, u32[]{:S(2)}) collective-permute-start(bf16[2,72,3072]{2,1,0:T(8,128)(2,1)} %get-tuple-element.170.refs_1_), channel_id=1, source_target_pairs={{0,8},{2,10},{4,12},{6,14},{8,0},{10,2},{12,4},{14,6},{16,24},{18,... | collective-permute-start | bytes 2654216 | tf_op jit(solution)/shard_map/ppermute | solution.py:582
  340.7 46.2 %collective-permute-start.10 = (bf16[144,3072]{1,0:T(8,128)(2,1)}, bf16[144,3072]{1,0:T(8,128)(2,1)S(1)}, u32[]{:S(2)}, u32[]{:S(2)}) collective-permute-start(bf16[144,3072]{1,0:T(8,128)(2,1)} %get-tuple-element.168.refs_1_), channel_id=1, source_target_pairs={{0,4},{2,6},{4,0},{6,2},{8,12},{10,14},{12,8},{14,10},{16,20},{18,... | collective-permute-start | bytes 2654216 | tf_op jit(solution)/shard_map/ppermute | solution.py:582
  340.7 46.2 %collective-permute-start.13 = (bf16[2,72,1152]{2,1,0:T(8,128)(2,1)}, bf16[2,72,1152]{2,1,0:T(8,128)(2,1)}, u32[]{:S(2)}, u32[]{:S(2)}) collective-permute-start(bf16[2,72,1152]{2,1,0:T(8,128)(2,1)} %get-tuple-element.174.refs_1_), channel_id=1, source_target_pairs={{0,8},{2,10},{4,12},{6,14},{8,0},{10,2},{12,4},{14,6},{16,24},{18,... | collective-permute-start | bytes 995336 | tf_op jit(solution)/shard_map/ppermute | solution.py:582
  388.8 25.9 %collective-permute-start.15 = (bf16[4,144,1152]{2,1,0:T(8,128)(2,1)}, bf16[4,144,1152]{2,1,0:T(8,128)(2,1)S(1)}, u32[]{:S(2)}, u32[]{:S(2)}) collective-permute-start(bf16[4,144,1152]{2,1,0:T(8,128)(2,1)} %get-tuple-element.200), channel_id=1, source_target_pairs={{0,2},{2,0},{4,6},{6,4},{8,10},{10,8},{12,14},{14,12},{16,18},{18,... | collective-permute-start | bytes 3981320 | tf_op jit(solution)/shard_map/ppermute | solution.py:582
  388.8 25.9 %collective-permute-start.16 = (bf16[4,144,1152]{2,1,0:T(8,128)(2,1)}, bf16[4,144,1152]{2,1,0:T(8,128)(2,1)S(1)}, u32[]{:S(2)}, u32[]{:S(2)}) collective-permute-start(bf16[4,144,1152]{2,1,0:T(8,128)(2,1)} %get-tuple-element.202), channel_id=1, source_target_pairs={{0,2},{2,0},{4,6},{6,4},{8,10},{10,8},{12,14},{14,12},{16,18},{18,... | collective-permute-start | bytes 3981320 | tf_op jit(solution)/shard_map/ppermute | solution.py:582
  400.9 24.5 %collective-permute-start.21 = (bf16[72,3072]{1,0:T(8,128)(2,1)}, bf16[72,3072]{1,0:T(8,128)(2,1)}, u32[]{:S(2)}, u32[]{:S(2)}) collective-permute-start(bf16[72,3072]{1,0:T(8,128)(2,1)} %get-tuple-element.210), channel_id=1, source_target_pairs={{0,1},{1,0},{2,3},{3,2},{4,5},{5,4},{6,7},{7,6},{8,9},{9,8},{10,11... | collective-permute-start | bytes 1327112 | tf_op jit(solution)/shard_map/ppermute | solution.py:581
  401.0 13.4 %collective-permute-start.18 = (bf16[8,3456]{1,0:T(8,128)(2,1)S(1)}, bf16[8,3456]{1,0:T(8,128)(2,1)S(1)}, u32[]{:S(2)}, u32[]{:S(2)}) collective-permute-start(bf16[8,3456]{1,0:T(8,128)(2,1)S(1)} %copy-done.37), channel_id=1, source_target_pairs={{0,1},{1,0},{2,3},{3,2},{4,5},{5,4},{6,7},{7,6},{8,9},{9,8},{10,11... | collective-permute-start | bytes 165896 | tf_op jit(solution)/shard_map/ppermute | solution.py:581
  403.0 1.2 collective-permute-start.17
  404.2 53.1 %collective-permute-start.24 = (bf16[4,72,1152]{2,1,0:T(8,128)(2,1)S(1)}, bf16[4,72,1152]{2,1,0:T(8,128)(2,1)S(1)}, u32[]{:S(2)}, u32[]{:S(2)}) collective-permute-start(bf16[4,72,1152]{2,1,0:T(8,128)(2,1)S(1)} %copy-done.12), channel_id=1, source_target_pairs={{0,8},{2,10},{4,12},{6,14},{8,0},{10,2},{12,4},{14,6},{16,24},{18,... | collective-permute-start | bytes 1990664 | tf_op jit(solution)/shard_map/ppermute | solution.py:582
  414.4 11.0 %collective-permute-start.23 = (bf16[72,1152]{1,0:T(8,128)(2,1)}, bf16[72,1152]{1,0:T(8,128)(2,1)}, u32[]{:S(2)}, u32[]{:S(2)}) collective-permute-start(bf16[72,1152]{1,0:T(8,128)(2,1)} %get-tuple-element.214), channel_id=1, source_target_pairs={{0,1},{1,0},{2,3},{3,2},{4,5},{5,4},{6,7},{7,6},{8,9},{9,8},{10,11... | collective-permute-start | bytes 497672 | tf_op jit(solution)/shard_map/ppermute | solution.py:581
  421.6 49.1 %collective-permute-start.26 = (bf16[2,144,1152]{2,1,0:T(8,128)(2,1)}, bf16[2,144,1152]{2,1,0:T(8,128)(2,1)S(1)}, u32[]{:S(2)}, u32[]{:S(2)}) collective-permute-start(bf16[2,144,1152]{2,1,0:T(8,128)(2,1)} %get-tuple-element.219), channel_id=1, source_target_pairs={{0,1},{1,0},{2,3},{3,2},{4,5},{5,4},{6,7},{7,6},{8,9},{9,8},{10,11... | collective-permute-start | bytes 1990664 | tf_op jit(solution)/shard_map/ppermute | solution.py:581
  423.4 47.4 %collective-permute-start.25 = (bf16[2,144,1152]{2,1,0:T(8,128)(2,1)}, bf16[2,144,1152]{2,1,0:T(8,128)(2,1)S(1)}, u32[]{:S(2)}, u32[]{:S(2)}) collective-permute-start(bf16[2,144,1152]{2,1,0:T(8,128)(2,1)} %get-tuple-element.207.refs_1_), channel_id=1, source_target_pairs={{0,4},{2,6},{4,0},{6,2},{8,12},{10,14},{12,8},{14,10},{16,20},{18,... | collective-permute-start | bytes 1990664 | tf_op jit(solution)/shard_map/ppermute | solution.py:582
  425.4 23.5 %collective-permute-start.22 = (bf16[192,1152]{1,0:T(8,128)(2,1)}, bf16[192,1152]{1,0:T(8,128)(2,1)S(1)}, u32[]{:S(2)}, u32[]{:S(2)}) collective-permute-start(bf16[192,1152]{1,0:T(8,128)(2,1)} %get-tuple-element.212), channel_id=1, source_target_pairs={{0,4},{2,6},{4,0},{6,2},{8,12},{10,14},{12,8},{14,10},{16,20},{18,... | collective-permute-start | bytes 1327112 | tf_op jit(solution)/shard_map/ppermute | solution.py:582
  425.4 23.4 %collective-permute-start.20 = (bf16[72,3072]{1,0:T(8,128)(2,1)}, bf16[72,3072]{1,0:T(8,128)(2,1)S(1)}, u32[]{:S(2)}, u32[]{:S(2)}) collective-permute-start(bf16[72,3072]{1,0:T(8,128)(2,1)} %get-tuple-element.198.refs_1_), channel_id=1, source_target_pairs={{0,8},{2,10},{4,12},{6,14},{8,0},{10,2},{12,4},{14,6},{16,24},{18,... | collective-permute-start | bytes 1327112 | tf_op jit(solution)/shard_map/ppermute | solution.py:582
  454.3 28.6 %collective-permute-start.31 = (bf16[96,1152]{1,0:T(8,128)(2,1)}, bf16[96,1152]{1,0:T(8,128)(2,1)S(1)}, u32[]{:S(2)}, u32[]{:S(2)}) collective-permute-start(bf16[96,1152]{1,0:T(8,128)(2,1)} %get-tuple-element.226), channel_id=1, source_target_pairs={{0,16},{2,18},{4,20},{6,22},{8,24},{10,26},{12,28},{14,30},{16,0},... | collective-permute-start | bytes 663560 | tf_op jit(solution)/shard_map/ppermute | solution.py:582
  456.6 14.1 %collective-permute-start.28 = (bf16[8,4608]{1,0:T(8,128)(2,1)S(1)}, bf16[8,4608]{1,0:T(8,128)(2,1)S(1)}, u32[]{:S(2)}, u32[]{:S(2)}) collective-permute-start(bf16[8,4608]{1,0:T(8,128)(2,1)S(1)} %copy-done.24), channel_id=1, source_target_pairs={{0,16},{2,18},{4,20},{6,22},{8,24},{10,26},{12,28},{14,30},{16,0},... | collective-permute-start | bytes 221192 | tf_op jit(solution)/shard_map/ppermute | solution.py:582
  457.3 3.7 collective-permute-start.27
  461.0 21.2 %collective-permute-start.32 = (bf16[36,1152]{1,0:T(8,128)(2,1)}, bf16[36,1152]{1,0:T(8,128)(2,1)S(1)}, u32[]{:S(2)}, u32[]{:S(2)}) collective-permute-start(bf16[36,1152]{1,0:T(8,128)(2,1)} %get-tuple-element.228), channel_id=1, source_target_pairs={{0,16},{2,18},{4,20},{6,22},{8,24},{10,26},{12,28},{14,30},{16,0},... | collective-permute-start | bytes 248840 | tf_op jit(solution)/shard_map/ppermute | solution.py:582
  470.7 14.0 %collective-permute-start.30 = (bf16[36,3072]{1,0:T(8,128)(2,1)}, bf16[36,3072]{1,0:T(8,128)(2,1)S(1)}, u32[]{:S(2)}, u32[]{:S(2)}) collective-permute-start(bf16[36,3072]{1,0:T(8,128)(2,1)} %get-tuple-element.224), channel_id=1, source_target_pairs={{0,16},{2,18},{4,20},{6,22},{8,24},{10,26},{12,28},{14,30},{16,0},... | collective-permute-start | bytes 663560 | tf_op jit(solution)/shard_map/ppermute | solution.py:582
  477.2 22.9 %collective-permute-start.34 = (bf16[2,72,1152]{2,1,0:T(8,128)(2,1)}, bf16[2,72,1152]{2,1,0:T(8,128)(2,1)S(1)}, u32[]{:S(2)}, u32[]{:S(2)}) collective-permute-start(bf16[2,72,1152]{2,1,0:T(8,128)(2,1)} %get-tuple-element.232), channel_id=1, source_target_pairs={{0,8},{2,10},{4,12},{6,14},{8,0},{10,2},{12,4},{14,6},{16,24},{18,... | collective-permute-start | bytes 995336 | tf_op jit(solution)/shard_map/ppermute | solution.py:582
  480.8 19.3 %collective-permute-start.35 = (bf16[144,1152]{1,0:T(8,128)(2,1)}, bf16[144,1152]{1,0:T(8,128)(2,1)S(1)}, u32[]{:S(2)}, u32[]{:S(2)}) collective-permute-start(bf16[144,1152]{1,0:T(8,128)(2,1)} %get-tuple-element.234), channel_id=1, source_target_pairs={{0,4},{2,6},{4,0},{6,2},{8,12},{10,14},{12,8},{14,10},{16,20},{18,... | collective-permute-start | bytes 995336 | tf_op jit(solution)/shard_map/ppermute | solution.py:582
  482.2 17.9 %collective-permute-start.33 = (bf16[2,72,1152]{2,1,0:T(8,128)(2,1)}, bf16[2,72,1152]{2,1,0:T(8,128)(2,1)S(1)}, u32[]{:S(2)}, u32[]{:S(2)}) collective-permute-start(bf16[2,72,1152]{2,1,0:T(8,128)(2,1)} %get-tuple-element.221.refs_1_), channel_id=1, source_target_pairs={{0,1},{1,0},{2,3},{3,2},{4,5},{5,4},{6,7},{7,6},{8,9},{9,8},{10,11... | collective-permute-start | bytes 995336 | tf_op jit(solution)/shard_map/ppermute | solution.py:581
  483.0 12.1 %collective-permute-start.29 = (bf16[36,3072]{1,0:T(8,128)(2,1)S(1)}, bf16[36,3072]{1,0:T(8,128)(2,1)S(1)}, u32[]{:S(2)}, u32[]{:S(2)}) collective-permute-start(bf16[36,3072]{1,0:T(8,128)(2,1)S(1)} %copy-done.21), channel_id=1, source_target_pairs={{0,16},{2,18},{4,20},{6,22},{8,24},{10,26},{12,28},{14,30},{16,0},... | collective-permute-start | bytes 663560 | tf_op jit(solution)/shard_map/ppermute | solution.py:582
  484.7 15.3 %collective-permute-start.37 = (bf16[16,4608]{1,0:T(8,128)(2,1)}, bf16[16,4608]{1,0:T(8,128)(2,1)S(1)}, u32[]{:S(2)}, u32[]{:S(2)}) collective-permute-start(bf16[16,4608]{1,0:T(8,128)(2,1)} %get-tuple-element.236.refs_10_), channel_id=1, source_target_pairs={{0,8},{2,10},{4,12},{6,14},{8,0},{10,2},{12,4},{14,6},{16,24},{18,... | collective-permute-start | bytes 442376 | tf_op jit(solution)/shard_map/ppermute | solution.py:582
  495.0 4.9 collective-permute-start.36
  504.9 10.4 %collective-permute-start.41 = (f32[2,1152]{1,0:T(2,128)}, f32[2,1152]{1,0:T(2,128)S(1)}, u32[]{:S(2)}, u32[]{:S(2)}) collective-permute-start(f32[2,1152]{1,0:T(2,128)} %get-tuple-element.243.refs_8_), channel_id=1, source_target_pairs={{0,8},{2,10},{4,12},{6,14},{8,0},{10,2},{12,4},{14,6},{16,24},{18,... | collective-permute-start | bytes 27656 | tf_op jit(solution)/shard_map/ppermute | solution.py:582
  506.0 9.2 %collective-permute-start.39 = (bf16[72,1152]{1,0:T(8,128)(2,1)}, bf16[72,1152]{1,0:T(8,128)(2,1)S(1)}, u32[]{:S(2)}, u32[]{:S(2)}) collective-permute-start(bf16[72,1152]{1,0:T(8,128)(2,1)} %get-tuple-element.240), channel_id=1, source_target_pairs={{0,1},{1,0},{2,3},{3,2},{4,5},{5,4},{6,7},{7,6},{8,9},{9,8},{10,11... | collective-permute-start | bytes 497672 | tf_op jit(solution)/shard_map/ppermute | solution.py:581
  506.9 8.3 %collective-permute-start.40 = (bf16[72,1152]{1,0:T(8,128)(2,1)}, bf16[72,1152]{1,0:T(8,128)(2,1)S(1)}, u32[]{:S(2)}, u32[]{:S(2)}) collective-permute-start(bf16[72,1152]{1,0:T(8,128)(2,1)} %get-tuple-element.242), channel_id=1, source_target_pairs={{0,8},{2,10},{4,12},{6,14},{8,0},{10,2},{12,4},{14,6},{16,24},{18,... | collective-permute-start | bytes 497672 | tf_op jit(solution)/shard_map/ppermute | solution.py:582
  507.7 7.5 %collective-permute-start.38 = (bf16[72,1152]{1,0:T(8,128)(2,1)}, bf16[72,1152]{1,0:T(8,128)(2,1)S(1)}, u32[]{:S(2)}, u32[]{:S(2)}) collective-permute-start(bf16[72,1152]{1,0:T(8,128)(2,1)} %get-tuple-element.237.refs_1_), channel_id=1, source_target_pairs={{0,4},{2,6},{4,0},{6,2},{8,12},{10,14},{12,8},{14,10},{16,20},{18,... | collective-permute-start | bytes 497672 | tf_op jit(solution)/shard_map/ppermute | solution.py:582
  508.0 11.6 %collective-permute-start.42 = (bf16[32,4608]{1,0:T(8,128)(2,1)}, bf16[32,4608]{1,0:T(8,128)(2,1)S(1)}, u32[]{:S(2)}, u32[]{:S(2)}) collective-permute-start(bf16[32,4608]{1,0:T(8,128)(2,1)} %get-tuple-element.244.refs_10_), channel_id=1, source_target_pairs={{0,4},{2,6},{4,0},{6,2},{8,12},{10,14},{12,8},{14,10},{16,20},{18,... | collective-permute-start | bytes 884744 | tf_op jit(solution)/shard_map/ppermute | solution.py:582
  523.8 17.4 %collective-permute-start.47 = (bf16[64,4608]{1,0:T(8,128)(2,1)}, bf16[64,4608]{1,0:T(8,128)(2,1)S(1)}, u32[]{:S(2)}, u32[]{:S(2)}) collective-permute-start(bf16[64,4608]{1,0:T(8,128)(2,1)} %get-tuple-element.252.refs_10_), channel_id=1, source_target_pairs={{0,2},{2,0},{4,6},{6,4},{8,10},{10,8},{12,14},{14,12},{16,18},{18,... | collective-permute-start | bytes 1769480 | tf_op jit(solution)/shard_map/ppermute | solution.py:582
  523.9 4.7 collective-permute-start.19
  525.1 6.5 %collective-permute-start.46 = (f32[2,1152]{1,0:T(2,128)}, f32[2,1152]{1,0:T(2,128)S(1)}, u32[]{:S(2)}, u32[]{:S(2)}) collective-permute-start(f32[2,1152]{1,0:T(2,128)} %get-tuple-element.251.refs_8_), channel_id=1, source_target_pairs={{0,16},{2,18},{4,20},{6,22},{8,24},{10,26},{12,28},{14,30},{16,0},... | collective-permute-start | bytes 27656 | tf_op jit(solution)/shard_map/ppermute | solution.py:582
  525.6 12.6 %collective-permute-start.44 = (bf16[36,1152]{1,0:T(8,128)(2,1)}, bf16[36,1152]{1,0:T(8,128)(2,1)S(1)}, u32[]{:S(2)}, u32[]{:S(2)}) collective-permute-start(bf16[36,1152]{1,0:T(8,128)(2,1)} %get-tuple-element.248), channel_id=1, source_target_pairs={{0,16},{2,18},{4,20},{6,22},{8,24},{10,26},{12,28},{14,30},{16,0},... | collective-permute-start | bytes 248840 | tf_op jit(solution)/shard_map/ppermute | solution.py:582
  528.1 12.1 %collective-permute-start.45 = (bf16[36,1152]{1,0:T(8,128)(2,1)}, bf16[36,1152]{1,0:T(8,128)(2,1)S(1)}, u32[]{:S(2)}, u32[]{:S(2)}) collective-permute-start(bf16[36,1152]{1,0:T(8,128)(2,1)} %get-tuple-element.250), channel_id=1, source_target_pairs={{0,16},{2,18},{4,20},{6,22},{8,24},{10,26},{12,28},{14,30},{16,0},... | collective-permute-start | bytes 248840 | tf_op jit(solution)/shard_map/ppermute | solution.py:582
  528.5 12.7 %collective-permute-start.43 = (bf16[36,1152]{1,0:T(8,128)(2,1)}, bf16[36,1152]{1,0:T(8,128)(2,1)S(1)}, u32[]{:S(2)}, u32[]{:S(2)}) collective-permute-start(bf16[36,1152]{1,0:T(8,128)(2,1)} %get-tuple-element.245.refs_1_), channel_id=1, source_target_pairs={{0,16},{2,18},{4,20},{6,22},{8,24},{10,26},{12,28},{14,30},{16,0},... | collective-permute-start | bytes 248840 | tf_op jit(solution)/shard_map/ppermute | solution.py:582
  (47 other events, 309.0 us)

commit v6 on v5

--- a/solution.py
+++ b/solution.py
@@ -72,7 +72,9 @@
     gather = np.zeros((width, 128), np.float32)
     for copy in range(3):
         gather[np.arange(width), copy * HEADS + head] = 1.0
-    return gather.astype(jnp.bfloat16), gather.T.astype(jnp.bfloat16)
+    fold = np.zeros((width, 128), np.float32)
+    fold[np.arange(width), np.arange(width) % HD] = 1.0
+    return gather.astype(jnp.bfloat16), gather.T.astype(jnp.bfloat16), fold.astype(jnp.bfloat16)
 
 
 def unit_of(index, n_mod):
@@ -323,21 +325,24 @@
 
 
 def attend_back_kernel(
-    slots, q_ref, k_ref, v_ref, do_ref, lse_ref, dot_ref, kt_ref, dqt_ref, dk_ref, dv_low_ref, dv_ref
+    slots, q_ref, k_ref, v_ref, do_ref, lse_ref, dot_ref, kt_ref, dqt_ref, dk_ref, dv_low_ref, dv_ref,
+    *, first, base, base_row,
 ):
-    h = pl.program_id(0)
+    h = pl.program_id(0) + first
     tokens, width = q_ref.shape
 
-    @pl.when(h == 0)
+    @pl.when(pl.program_id(0) == 0)
     def _():
         dqt_ref[...] = jnp.zeros_like(dqt_ref)
         dk_ref[...] = jnp.zeros_like(dk_ref)
         dv_ref[...] = jnp.zeros_like(dv_ref)
 
-    start, offset = window(h, width)
+    start, offset = window(h, kt_ref.shape[0])
     inside = head_lanes(offset)
     columns = pl.ds(start, WIN)
+    out_columns = pl.ds(pl.multiple_of(start - base, 128), WIN)
     first_row = pl.multiple_of((h * HD) // 16 * 16, 16)
+    out_rows = pl.ds(pl.multiple_of(first_row - base_row, 16), HD + 8)
     row = lax.broadcasted_iota(jnp.int32, (HD + 8, 1), 0) + first_row
     own_rows = (row >= h * HD) & (row < h * HD + HD)
 
@@ -348,10 +353,10 @@
         value = jnp.where(inside, v_ref[rows, columns], 0)
         probs = jnp.exp2(nt(key, query) * SCORE_LOG2 - lse_ref[pl.ds(h, 1), rows])
         scores = (probs * (nt(value, grad_out) - dot_ref[pl.ds(h, 1), rows])).astype(bf16)
-        dv_ref[rows, columns] += jnp.where(inside, nn(probs.astype(bf16), grad_out), 0.0)
-        dk_ref[rows, columns] += jnp.where(inside, nn(scores, query) * SCORE_SCALE, 0.0)
+        dv_ref[rows, out_columns] += jnp.where(inside, nn(probs.astype(bf16), grad_out), 0.0)
+        dk_ref[rows, out_columns] += jnp.where(inside, nn(scores, query) * SCORE_SCALE, 0.0)
         turned = nn(kt_ref[pl.ds(first_row, HD + 8), rows], scores) * SCORE_SCALE
-        dqt_ref[pl.ds(first_row, HD + 8), rows] += jnp.where(own_rows, turned, 0.0)
+        dqt_ref[out_rows, rows] += jnp.where(own_rows, turned, 0.0)
 
     whole = slots[tokens // TB - 1] == slots[0]
 
@@ -367,21 +372,31 @@
 
         lax.fori_loop(0, tokens // TB, block, 0)
 
-    @pl.when(h == HEADS - 1)
+    @pl.when(pl.program_id(0) == pl.num_programs(0) - 1)
     def _():
         dv_low_ref[...] = dv_ref[...].astype(bf16)
 
 
+def head_span(first, end, width):
+    begin = lambda head: min(head * HD // 128, width // 128 - WIN // 128) * 128
+    return begin(first), begin(end - 1) + WIN, first * HD // 16 * 16, (end - 1) * HD // 16 * 16 + HD + 8
+
+
+def join_spans(low, high, begin, axis):
+    size = low.shape[axis] - begin
+    cut = lambda arr, start, stop: lax.slice_in_dim(arr, start, stop, axis=axis)
+    middle = cut(low, begin, begin + size) + cut(high, 0, size)
+    return jnp.concatenate([cut(low, 0, begin), middle, cut(high, size, high.shape[axis])], axis=axis)
+
+
 def project_back_kernel(
-    slots, dqt_ref, dk_ref, dv_ref, raw_ref, inv_ref, q_ref, k_ref, x_ref, grad_mid_ref, units_ref, mod_ref,
-    w_ref, coords_ref, cos_ref, sin_ref, gain_ref, gather_ref, spread_ref, other_sums_ref,
-    grad_x_ref, gains_ref, grad_own_ref, grad_other_ref, q_send_ref, q_own_ref, k_send_ref, k_own_ref,
-    accq_ref, acck_ref, sums_ref,
+    bits, dqt0_ref, dqt1_ref, dk0_ref, dk1_ref, raw_ref, inv_ref, q_ref, k_ref, units_ref,
+    coords_ref, cos_ref, sin_ref, gain_ref, gather_ref, spread_ref, fold_ref,
+    gq_ref, gk_ref, gains_low_ref, q_send_ref, q_own_ref, k_send_ref, k_own_ref, accq_ref, acck_ref, gains_ref,
+    *, base, base_row,
 ):
-    width = x_ref.shape[1]
+    width = q_ref.shape[1]
     block = pl.program_id(0)
-    last_block = pl.num_programs(0) - 1
-    slot = slots[block]
 
     @pl.when(block == 0)
     def _():
@@ -389,11 +404,13 @@
         accq_ref[...] = jnp.zeros_like(accq_ref)
         acck_ref[...] = jnp.zeros_like(acck_ref)
 
-    dmod = nt(dv_ref[...], w_ref[:, 2 * width :])
-
     cosine, sine = angles(coords_ref, cos_ref, sin_ref)
-    for index, (low_ref, acc_ref) in enumerate(((q_ref, accq_ref), (k_ref, acck_ref))):
-        grad = dqt_ref[...].T if index == 0 else dk_ref[...]
+    parts = ((q_ref, gq_ref, accq_ref), (k_ref, gk_ref, acck_ref))
+    for index, (low_ref, out_ref, acc_ref) in enumerate(parts):
+        if index == 0:
+            grad = join_spans(dqt0_ref[...], dqt1_ref[...], base_row, 0).T
+        else:
+            grad = join_spans(dk0_ref[...], dk1_ref[...], base, 1)
         raw = raw_ref[:, index * width : (index + 1) * width]
         inverse = head_spread(inv_ref[:, index * 128 : (index + 1) * 128], spread_ref)
         mean = head_sum(grad * low_ref[...].astype(f32), gather_ref) * (1.0 / HD)
@@ -403,14 +420,34 @@
         grad_raw = (
             inverse * (back * gain_ref[index : index + 1, :] - norm * head_spread(mean, spread_ref))
         ).astype(bf16)
+        out_ref[...] = grad_raw
         acc_ref[...] += nn(units_ref[...].reshape(width, TB), grad_raw)
-        dmod = dmod + nt(grad_raw, w_ref[:, index * width : (index + 1) * width])
 
     @pl.when(block == pl.num_programs(0) - 1)
     def _():
-        halves_out(accq_ref, slots[pl.num_programs(0)], q_send_ref, q_own_ref)
-        halves_out(acck_ref, slots[pl.num_programs(0)], k_send_ref, k_own_ref)
-
+        halves_out(accq_ref, bits[0], q_send_ref, q_own_ref)
+        halves_out(acck_ref, bits[0], k_send_ref, k_own_ref)
+        terms = split3(gains_ref[...])
+        sums = sum(nn(term.astype(bf16), fold_ref[...]) for term in terms)
+        high = sums.astype(bf16).astype(f32)
+        row = lax.broadcasted_iota(jnp.int32, (8, 1), 0)
+        mine = 4 * bits[1]
+        placed = jnp.zeros((8, 128), f32)
+        for index, term in enumerate((high[0:1], (sums - high)[0:1], high[1:2], (sums - high)[1:2])):
+            placed = jnp.where(row == mine + index, term, placed)
+        gains_low_ref[...] = placed.astype(bf16)
+
+
+def input_back_kernel(
+    slots, gq_ref, gk_ref, dv0_ref, dv1_ref, x_ref, grad_mid_ref, mod_ref, w_ref, other_sums_ref, gains_ref,
+    grad_x_ref, grad_own_ref, grad_other_ref, sums_ref, *, base,
+):
+    width = x_ref.shape[1]
+    block = pl.program_id(0)
+    slot = slots[block]
+    last_block = pl.num_programs(0) - 1
+    dmod = nt(gq_ref[...], w_ref[:, :width]) + nt(gk_ref[...], w_ref[:, width : 2 * width])
+    dmod = dmod + nt(join_spans(dv0_ref[...], dv1_ref[...], base, 1), w_ref[:, 2 * width :])
     norm, inverse = normed(x_ref[...].astype(f32))
     grad_x = grad_mid_ref[...] + norm_back(dmod, part(mod_ref, slot, 1, width), norm, inverse)
     grad_x_ref[...] = grad_x.astype(bf16)
@@ -427,18 +464,22 @@
     def _():
         mod = slots[last_block + 2]
         count = sums_ref.shape[0]
+        half = 3 * width
         mine = jnp.concatenate([sums_ref[...]] * 2, axis=0)
         rest = jnp.concatenate([other_sums_ref[...]] * 2, axis=0)
         row = lax.broadcasted_iota(jnp.int32, (2 * count, 1), 0) // count
         attn_part = jnp.where(row == mod, jnp.concatenate([mine, rest[:, :width]], axis=1), 0.0)
         ffn_part = jnp.where(row == mod, rest[:, width:], 0.0)
-        grad_own_ref[...] = jnp.where(mod == 0, attn_part, ffn_part).astype(bf16)
-        grad_other_ref[...] = jnp.where(mod == 0, ffn_part, attn_part).astype(bf16)
-
-
-def value_kernel(bits, units_ref, rhs_ref, send_ref, own_ref):
-    product(units_ref, 1 - bits[0], rhs_ref[...], send_ref)
-    product(units_ref, bits[0], rhs_ref[...], own_ref)
+        grad_own_ref[:, :half] = jnp.where(mod == 0, attn_part, ffn_part).astype(bf16)
+        grad_other_ref[:, :half] = jnp.where(mod == 0, ffn_part, attn_part).astype(bf16)
+        grad_own_ref[:, half:] = gains_ref[...]
+        grad_other_ref[:, half:] = gains_ref[...]
+
+
+def value_kernel(bits, units_ref, dv0_ref, dv1_ref, send_ref, own_ref, *, base):
+    rhs = join_spans(dv0_ref[...], dv1_ref[...], base, 1)
+    product(units_ref, 1 - bits[0], rhs, send_ref)
+    product(units_ref, bits[0], rhs, own_ref)
 
 
 def split_step(bits, ins, outs, *, lead, at, bit, pair_rows):
@@ -459,18 +500,27 @@
                 second = value[(2 * p + 1) * rows : (2 * p + 2) * rows]
                 place = index + (slice(p * rows, (p + 1) * rows),)
                 send_ref[place] = jnp.where(mine == 1, first, second).astype(bf16)
-                keep_ref[place] = jnp.where(mine == 1, second, first)
+                keep_ref[place] = jnp.where(mine == 1, second, first).astype(keep_ref.dtype)
         return
     for j in range(lead // 2):
         place = (j,) if lead > 2 else (Ellipsis,)
         away = 1 - mine if lead == 2 else 2 * (1 - mine) + j if at == 0 else 2 * j + 1 - mine
         own = mine if lead == 2 else 2 * mine + j if at == 0 else 2 * j + mine
         send_ref[place] = total(away).astype(bf16)
-        keep_ref[place] = total(own)
-
-
-def sum_step(bits, ins, outs):
-    outs[0][...] = ins[0][...] + ins[1][...]
+        keep_ref[place] = total(own).astype(keep_ref.dtype)
+
+
+def merge_step(bits, ins, outs, *, bit):
+    send_ref, keep_ref = outs
+    start = 0
+    for own_ref, got_ref in zip(ins[::2], ins[1::2]):
+        value = own_ref[...].astype(f32) + got_ref[...].astype(f32)
+        rows = value.shape[0] // 2
+        place = slice(start, start + value.shape[1])
+        first, second = value[:rows], value[rows:]
+        send_ref[:, place] = jnp.where(bits[bit] == 1, first, second).astype(bf16)
+        keep_ref[:, place] = jnp.where(bits[bit] == 1, second, first)
+        start += value.shape[1]
 
 
 def pair_step(bits, ins, outs):
@@ -500,7 +550,12 @@
     place = lax.broadcasted_iota(jnp.int32, (width, 128), 1)
     chosen = (feature == position * rows + place) & (place < rows)
     own = nn(every[:, :width], chosen.astype(f32).astype(bf16)).astype(bf16)
-    outs[0][...] = tn(own, every[:, width:])[:rows]
+    half = outs[0].shape[1]
+    outs[0][...] = tn(own, every[:, width : width + half])[:rows]
+    terms = every[:, width + half :].astype(f32)
+    kind = lax.broadcasted_iota(jnp.int32, (terms.shape[0], 1), 0) // 2 % 2
+    for index in range(2):
+        outs[1][index : index + 1, :] = jnp.sum(jnp.where(kind == index, terms, 0.0), axis=0, keepdims=True)
 
 
 def step_kernel(bits, *refs, plans):
@@ -592,7 +647,9 @@
             plans.append((function, len(inputs), len(shapes)))
             args += inputs
             outs += shapes
-        steps = 3 if not last and len(streams) == 1 and args[0].ndim == 3 and args[0].shape[-1] % 384 == 0 else 1
+        size = sum(arg.size for arg in args)
+        split = all(isinstance(stream, Stream) and stream.own.shape[-1] % 384 == 0 for stream in streams)
+        steps = 3 if split and size > 2**20 else 1
         results = self.call(
             functools.partial(step_kernel, plans=plans),
             (steps,),
@@ -646,7 +703,7 @@
             dims = dims[:-2] + (dims[-2] // 2, dims[-1])
         else:
             dims = dims[1:] if len(self.lead) == 1 else (2,) + dims[1:]
-        return function, [shape(dims, bf16), shape(dims, f32)]
+        return function, [shape(dims, bf16), shape(dims, bf16 if len(self.lead) == 2 else f32)]
 
     def step(self, results):
         bit = self.steps.pop(0)
@@ -659,24 +716,28 @@
         return last_step, [shape(self.own.shape, f32)]
 
 
-class Total:
-    def __init__(self, reducer, own):
-        self.r, self.own = reducer, own
-        self.steps = ["mod"] + list(range(1, reducer.n_dp.bit_length() - 1))
-        self.got = reducer.swap(own, 0)
+class Merged:
+    def __init__(self, streams):
+        self.streams, self.r, self.bit = streams, streams[0].r, streams[0].steps[0]
+        self.own = None
 
     def inputs(self):
-        return [self.own, self.got]
+        if self.own is not None:
+            return [self.own, self.got]
+        return [arr for stream in self.streams for arr in (stream.own, stream.got)]
 
     def plan(self):
-        return sum_step, [shape(self.own.shape, f32)]
+        columns = sum(stream.own.shape[1] for stream in self.streams)
+        dims = (self.streams[0].own.shape[0] // 2, columns)
+        function = functools.partial(merge_step, bit=self.r.bit_of(self.bit))
+        return function, [shape(dims, bf16), shape(dims, f32)]
 
     def step(self, results):
-        (self.own,) = results
-        self.got = self.r.swap(self.own, self.steps.pop(0))
+        sent, self.own = results
+        self.got = self.r.swap(sent, self.bit)
 
     def last_plan(self):
-        return self.plan()
+        return last_step, [shape(self.own.shape, f32)]
 
 
 class Gather:
@@ -704,7 +765,8 @@
     def last_plan(self):
         width = self.activated.shape[1]
         function = functools.partial(ada_step, width=width)
-        return function, [shape((width // self.r.n_dp, self.own.shape[1] - width), f32)]
+        dims = (width // self.r.n_dp, self.own.shape[1] - width - 128)
+        return function, [shape(dims, f32), shape((2, 128), f32)]
 
 
 def silu_grad(v):
@@ -734,7 +796,7 @@
     slots = segments[0, ::TB]
     coord = coords[0]
     cos_table, sin_table = (jnp.asarray(t) for t in rope_tables(width))
-    gather, spread = (jnp.asarray(t) for t in head_tables(width))
+    gather, spread, head_fold = (jnp.asarray(t) for t in head_tables(width))
     perm = jnp.asarray(unit_permutation(width, n_dp, n_mod))
     gains = jnp.stack([jnp.tile(q_gain, HEADS), jnp.tile(k_gain, HEADS)])
 
@@ -821,92 +883,110 @@
         name="middle",
     )
     out = Stream(reducer, out_send, out_own, 1)
-    reducer.fold([gate], "gate")
-    reducer.fold([up], "up")
-    reducer.fold([down], "down")
-    reducer.fold([out], "out")
-
-    grad_query_t, grad_key, grad_value = call(
-        attend_back_kernel,
-        (HEADS,),
-        [fixed((count, width))] * 4 + [fixed((128, count))] * 2 + [fixed((width, count))],
-        [fixed((width, count))] + [fixed((count, width))] * 2,
-        [shape((width, count), f32), token_f32, token_bf16],
-        (query, key, value, grad_attended, lse, dot_term, key_t),
-        scratch=[pltpu.VMEM((count, width), f32)],
-        scalars=slots,
-        name="attend_back",
-    )
-    reducer.fold([gate], "gate")
-    reducer.fold([up], "up")
-    reducer.fold([down], "down")
-    reducer.fold([out], "out")
+    early = [gate, up, down, out]
+    reducer.fold(early, "early")
+
+    def attend_back(first, end, name):
+        begin, stop, begin_row, stop_row = head_span(first, end, width)
+        columns, rows = stop - begin, stop_row - begin_row
+        used = fixed((count, stop))
+        return call(
+            functools.partial(attend_back_kernel, first=first, base=begin, base_row=begin_row),
+            (end - first,),
+            [used] * 4 + [fixed((128, count))] * 2 + [fixed((width, count))],
+            [fixed((rows, count))] + [fixed((count, columns))] * 2,
+            [shape((rows, count), f32), shape((count, columns), f32), shape((count, columns), bf16)],
+            (query, key, value, grad_attended, lse, dot_term, key_t),
+            scratch=[pltpu.VMEM((count, columns), f32)],
+            scalars=slots,
+            name=name,
+        )
+
+    cut = HEADS // 2 + 1
+    dqt0, dk0, dv0 = attend_back(0, cut, "attend_back_0")
+    reducer.fold(early, "early")
+    dqt1, dk1, dv1 = attend_back(cut, HEADS, "attend_back_1")
+    reducer.fold(early, "early")
+    base, _, base_row, _ = head_span(cut, HEADS, width)
     v_send, v_own = call(
-        value_kernel,
+        functools.partial(value_kernel, base=base),
         (1,),
-        [whole(units.shape), whole((count, width))],
+        [whole(units.shape), whole(dv0.shape), whole(dv1.shape)],
         [whole((4, width // 8, width))] * 2,
         square_shapes,
-        (attn_units, grad_value),
+        (attn_units, dv0, dv1),
         scalars=reducer.bits,
         name="value",
     )
     v_part = Stream(reducer, v_send, v_own, 2)
-    grad_tokens, gain_sums, mod_own, mod_other, q_send, q_own, k_send, k_own = call(
-        project_back_kernel,
+    grad_q, grad_k, gains_low, q_send, q_own, k_send, k_own = call(
+        functools.partial(project_back_kernel, base=base, base_row=base_row),
         (blocks,),
-        [rows_of((width, TB), 1), token_spec, token_spec, rows_of((TB, 2 * width)), rows_of((TB, 256))]
-        + [token_spec] * 4
-        + [units_spec, mod_spec, fixed((width, 3 * width)), rows_of((2, TB), 1)]
-        + table_specs + [fixed((slots_n, 4 * width))],
-        [token_spec, fixed((2, width))] + [fixed((2 * slots_n, half))] * 2 + square_send * 2,
-        [token_bf16, shape((2, width), f32)] + [shape((2 * slots_n, half), bf16)] * 2 + square_shapes * 2,
-        (grad_query_t, grad_key, grad_value, raw, inverse, query, key, x, grad_mid, attn_units, modulation,
-         w_qkv, coord)
-        + tables + (sums_b,),
-        scalars=slots_core,
-        scratch=[pltpu.VMEM((width, width), f32)] * 2 + [pltpu.VMEM((slots_n, 2 * width), f32)],
+        [rows_of((dqt0.shape[0], TB), 1), rows_of((dqt1.shape[0], TB), 1)]
+        + [rows_of((TB, dk0.shape[1])), rows_of((TB, dk1.shape[1]))]
+        + [rows_of((TB, 2 * width)), rows_of((TB, 256)), token_spec, token_spec, units_spec, rows_of((2, TB), 1)]
+        + table_specs + [fixed(head_fold.shape)],
+        [token_spec] * 2 + [fixed((8, 128))] + square_send * 2,
+        [token_bf16] * 2 + [shape((8, 128), bf16)] + square_shapes * 2,
+        (dqt0, dqt1, dk0, dk1, raw, inverse, query, key, attn_units, coord) + tables + (head_fold,),
+        scalars=reducer.bits,
+        scratch=[pltpu.VMEM((width, width), f32)] * 2 + [pltpu.VMEM((2, width), f32)],
         name="project_back",
     )
-    early = [gate, up, down, out]
-    arrived = [stream.got for stream in early + [v_part]]
-    *arrived, q_send, k_send, mod_other, gain_sums = reducer.pass_on(
-        arrived + [q_send, k_send, mod_other, gain_sums]
-    )
-    for stream, got in zip(early + [v_part], arrived):
+    waiting = early + [v_part]
+    *arrived, q_send, k_send = reducer.pass_on([stream.got for stream in waiting] + [q_send, k_send])
+    for stream, got in zip(waiting, arrived):
         stream.got = got
     q_part = Stream(reducer, q_send, q_own, 1)
     k_part = Stream(reducer, k_send, k_own, 0)
-    gains_total = Total(reducer, gain_sums)
+    late = [q_part, k_part, v_part]
+    extra = n_dp.bit_length() - 5
+    reducer.fold([v_part], "v")
+    for _ in range(extra):
+        reducer.fold(early, "early")
+    early = [Merged([gate, up, out]), down]
+    reducer.fold(early, "early")
+    reducer.fold([q_part, k_part], "late")
+    grad_tokens, mod_own, mod_other = call(
+        functools.partial(input_back_kernel, base=base),
+        (blocks,),
+        [token_spec] * 2 + [rows_of((TB, dv0.shape[1])), rows_of((TB, dv1.shape[1]))] + [token_spec] * 2
+        + [mod_spec, fixed((width, 3 * width)), fixed((slots_n, 4 * width)), fixed((8, 128))],
+        [token_spec] + [fixed((2 * slots_n, half + 128))] * 2,
+        [token_bf16] + [shape((2 * slots_n, half + 128), bf16)] * 2,
+        (grad_q, grad_k, dv0, dv1, x, grad_mid, modulation, w_qkv, sums_b, gains_low),
+        scalars=slots_core,
+        scratch=[pltpu.VMEM((slots_n, 2 * width), f32)],
+        name="input_back",
+    )
     every_mod = Gather(reducer, mod_other, mod_own, activated)
-    late = [q_part, k_part, gains_total, every_mod]
-    reducer.fold([v_part], "v")
-    reducer.fold(early, "early")
     reducer.fold(late, "late")
-    for _ in range(n_dp.bit_length() - 4):
-        reducer.fold(early, "early")
-        reducer.fold([v_part] + late, "late")
-    summed_gate, summed_up, summed_down, summed_out = reducer.fold(early, "early", last=True)
-    reducer.fold([v_part] + late, "late")
-    reducer.fold([v_part] + late, "late")
-    *summed, gain_sums, grad_w_ada = reducer.fold([v_part] + late, "late", last=True)
-    summed_qkv = jnp.concatenate([summed[1], summed[2], summed[0]], axis=1)
-
-    grad_activated = jnp.einsum("nc,dc->nd", every_mod.pair[:, width:], w_ada, preferred_element_type=f32)
+    reducer.fold([every_mod], "pair")
+    summed_early, summed_down = reducer.fold(early, "early_last", last=True)
+    for _ in range(1 + extra):
+        reducer.fold(late + [every_mod], "late")
+    late = [Merged(late)]
+    reducer.fold(late + [every_mod], "late")
+    while every_mod.steps:
+        reducer.fold([every_mod], "every")
+    summed_qkv, grad_w_ada, gain_grads = reducer.fold(late + [every_mod], "late_last", last=True)
+    summed_gate, summed_up = summed_early[:, :ff], summed_early[:, ff : 2 * ff]
+    summed_out = summed_early[:, 2 * ff :]
+
+    grad_activated = jnp.einsum("nc,dc->nd", every_mod.pair[:, width : width + half], w_ada, preferred_element_type=f32)
     grad_activated = grad_activated.reshape(n_mod, slots_n, width)
     own_part = lax.dynamic_index_in_dim(grad_activated, mod_index, 0, keepdims=False)
     other_part = lax.dynamic_index_in_dim(grad_activated, 1 - mod_index, 0, keepdims=False)
     grad_own = own_part + reducer.swap(other_part.astype(bf16), "mod").astype(f32)
     grad_cond = grad_own[None] * silu_grad(cond)
-    gain_grads = jnp.sum(gain_sums.reshape(2, HEADS, HD), axis=1)
     return (
         output[None],
         grad_tokens[None],
         grad_cond,
         grad_w_ada,
         summed_qkv,
-        gain_grads[0],
-        gain_grads[1],
+        gain_grads[0, :HD],
+        gain_grads[1, :HD],
         summed_out,
         summed_gate,
         summed_up,

time: 559 us -> 534 us (0.955)
  waiting for transfers between devices: 71.1 us -> 55 us
  starting transfers between devices: 72.9 us -> 58.3 us
    ppermute x36 -> x28, starting transfers between devices: 53.8 us -> 40.4 us  [swap(): lax.ppermute(arr, 'dp', [(i, i ^ 1 << bit) for i in range(self.n_dp)])]
    ppermute x12 -> x11, waiting for transfers between devices: 13.6 us -> 0.48 us  [swap(): return lax.ppermute(arr, 'mod', [(i, i ^ 1) for i in range(self.n_mod)])]
    unnamed x94 -> x86, local copies, waits for them, and re-layouts: 11.6 us -> 15.2 us
    ppermute x36 -> x28, waiting for transfers between devices: 57.5 us -> 54.6 us  [swap(): lax.ppermute(arr, 'dp', [(i, i ^ 1 << bit) for i in range(self.n_dp)])]
    pallas_call x25 -> x23, Pallas kernels: 373 us -> 375 us  [__call__(): pl.pallas_call(body, grid_spec=spec, input_output_aliases=aliases or {},...]
    ppermute x12 -> x11, starting transfers between devices: 19.2 us -> 17.9 us  [swap(): return lax.ppermute(arr, 'mod', [(i, i ^ 1) for i in range(self.n_mod)])]
  transfers between devices with their start and end apart: 48 -> 39, of which waited for: 13 -> 7; matrix products, arithmetic and copies ran while one was open for 2% -> 2% of each run, Pallas kernels for 33% -> 28%
where the time goes in v6:
time: 534 us; the launch traced here: 525 us
  Pallas kernels  375 us (70%)
  starting transfers between devices  58.3 us (11%)
  waiting for transfers between devices  55 us (10%)
  local copies, waits for them, and re-layouts  21.7 us (4%)
  matrix products  9.81 us (2%)
    pallas_call x23, Pallas kernels, __call__(): pl.pallas_call(body, grid_spec=spec, input_output_aliases=aliases or {},...  375 us
    ppermute x28, waiting for transfers between devices, swap(): lax.ppermute(arr, 'dp', [(i, i ^ 1 << bit) for i in range(self.n_dp)])  54.6 us
    ppermute x28, starting transfers between devices, swap(): lax.ppermute(arr, 'dp', [(i, i ^ 1 << bit) for i in range(self.n_dp)])  40.4 us
    ppermute x11, starting transfers between devices, swap(): return lax.ppermute(arr, 'mod', [(i, i ^ 1) for i in range(self.n_mod)])  17.9 us
    unnamed x86, local copies, waits for them, and re-layouts  15.2 us
  transfers between devices with their start and end apart: 39, of which 7 were waited for; matrix products, arithmetic and copies ran while one was open for 2% of the time, Pallas kernels for 28%

profile of v6, /device:TPU:0, one launch (start us, length us, event | category | flops | bytes accessed | tf_op | source)
XLA Modules:
  0.0 524.7 jit_solution(6522700981704877140)
XLA Ops:
  0.6 3.0 collective-permute-start
  6.5 4.4 convolution_convert_fusion
  11.0 2.1 collective-permute-start.1
  16.3 29.1 %project.1 = (bf16[8,144,1024]{2,1,0:T(8,128)(2,1)}, f32[1024,2304]{1,0:T(8,128)}, f32[1024,256]{1,0:T(8,128)}, bf16[1024,1152]{1,0:T(8,128)(2,1)}, bf16[1024,11...) custom-call(s32[4]{0:T(128)} %bitcast.50, bf16[1024,1152]{1,0:T(8,128)(2,1)} %bitcast.37, ...), custom_call_target="tpu_custom_call" | custom-call | flops 1 | bytes 1 | tf_op jit(solution)/shard_map/project/pallas_call | solution.py:593
  45.4 48.2 %attend.1 = (f32[1024,1152]{1,0:T(8,128)}, f32[128,1024]{1,0:T(8,128)}, f32[1024,1152]{1,0:T(8,128)}, f32[1024,1152]{1,0:T(8,128)}, bf16[1024,1152]{1,0:T(8,128)...) custom-call(s32[4]{0:T(128)} %bitcast.51, ...), custom_call_target="tpu_custom_call" | custom-call | flops 1 | bytes 1 | tf_op jit(solution)/shard_map/attend/pallas_call | solution.py:593
  93.6 102.9 %ffn.1 = (bf16[4,144,3072]{2,1,0:T(8,128)(2,1)}, bf16[4,144,3072]{2,1,0:T(8,128)(2,1)}, bf16[4,144,3072]{2,1,0:T(8,128)(2,1)}, bf16[4,144,3072]{2,1,0:T(8,128)(2...) custom-call(s32[5]{0:T(128)} %stack.48.refs_0_, ...), custom_call_target="tpu_custom_call" | custom-call | flops 1 | bytes 1 | tf_op jit(solution)/shard_map/ffn/pallas_call | solution.py:593
  196.5 7.9 %collective-permute-start.3 = (bf16[4,144,3072]{2,1,0:T(8,128)(2,1)}, bf16[4,144,3072]{2,1,0:T(8,128)(2,1)S(1)}, u32[]{:S(2)}, u32[]{:S(2)}) collective-permute-start(bf16[4,144,3072]{2,1,0:T(8,128)(2,1)} %get-tuple-element.138), channel_id=1, source_target_pairs={{0,2},{2,0},{4,6},{6,4},{8,10},{10,8},{12,14},{14,12},{16,18},{18,... | collective-permute-start | bytes 10616840 | tf_op jit(solution)/shard_map/ppermute | solution.py:637
  205.6 25.2 %middle.1 = (bf16[1024,1152]{1,0:T(8,128)(2,1)}, f32[1024,1152]{1,0:T(8,128)}, bf16[1024,1152]{1,0:T(8,128)(2,1)}, f32[128,1024]{1,0:T(8,128)}, f32[4,4608]{1,0:...) custom-call(s32[6]{0:T(128)} %pad_add_fusion.refs_0_, ...), custom_call_target="tpu_custom_call" | custom-call | flops 1 | bytes 1 | tf_op jit(solution)/shard_map/middle/pallas_call | solution.py:593
  230.9 3.2 collective-permute-done.5.refs_9_
  235.3 1.8 copy-done.3
  237.0 14.5 %early.4 = (bf16[2,144,3072]{2,1,0:T(8,128)(2,1)}, bf16[2,144,3072]{2,1,0:T(8,128)(2,1)}, bf16[2,144,3072]{2,1,0:T(8,128)(2,1)}, bf16[2,144,3072]{2,1,0:T(8,128)...) custom-call(s32[5]{0:T(128)} %stack.48.refs_0_, ...), custom_call_target="tpu_custom_call" | custom-call | flops 1 | bytes 1 | tf_op jit(solution)/shard_map/early/pallas_call | solution.py:593
  251.6 1.6 collective-permute-start.7
  253.1 1.6 collective-permute-start.8
  254.7 3.1 collective-permute-start.6
  258.4 24.0 %attend_back_0.1 = (f32[656,1024]{1,0:T(8,128)}, f32[1024,768]{1,0:T(8,128)}, bf16[1024,768]{1,0:T(8,128)(2,1)}) custom-call(s32[4]{0:T(128)} %bitcast.52, bf16[2,144,3072]{2,1,0:T(8,128)(2,1)} %get-tuple-element.143.refs_1_, bf16[1024,1152]{1,0:T(8,128)(2,1)} %get-tuple-element.122.refs_5_.refs_2_.refs_8_, ...), custom_call_target="tpu_custom_call" | custom-call | flops 1 | bytes 1 | tf_op jit(solution)/shard_map/attend_back_0/pallas_call | solution.py:593
  282.4 24.5 %collective-permute-done.9.refs_9_ = bf16[2,144,1152]{2,1,0:T(8,128)(2,1)} collective-permute-done((bf16[2,144,1152]{2,1,0:T(8,128)(2,1)}, bf16[2,144,1152]{2,1,0:T(8,128)(2,1)}, u32[]{:S(2)}, u32[]{:S(2)}) %collective-permute-start.9) | collective-permute-done | bytes 663584 | tf_op jit(solution)/shard_map/ppermute | solution.py:637
  308.6 9.1 %early.5 = (bf16[144,3072]{1,0:T(8,128)(2,1)}, f32[144,3072]{1,0:T(8,128)}, bf16[2,72,3072]{2,1,0:T(8,128)(2,1)}, f32[2,72,3072]{2,1,0:T(8,128)}, bf16[2,192,115...) custom-call(s32[5]{0:T(128)} %stack.48.refs_0_, ...), custom_call_target="tpu_custom_call" | custom-call | flops 1 | bytes 1 | tf_op jit(solution)/shard_map/early/pallas_call | solution.py:593
  317.7 1.6 collective-permute-start.11
  319.4 3.3 collective-permute-start.12
  322.7 1.5 collective-permute-start.10
  324.2 20.6 %attend_back_1.1 = (f32[512,1024]{1,0:T(8,128)}, f32[1024,512]{1,0:T(8,128)}, bf16[1024,512]{1,0:T(8,128)(2,1)}) custom-call(s32[4]{0:T(128)} %bitcast.53, bf16[144,3072]{1,0:T(8,128)(2,1)} %get-tuple-element.156.refs_1_, bf16[1024,1152]{1,0:T(8,128)(2,1)} %get-tuple-element.122.refs_5_.refs_2_.refs_8_, ...), custom_call_target="tpu_custom_call" | custom-call | flops 1 | bytes 1 | tf_op jit(solution)/shard_map/attend_back_1/pallas_call | solution.py:593
  347.6 6.6 %early.6 = (bf16[72,3072]{1,0:T(8,128)(2,1)}, f32[72,3072]{1,0:T(8,128)}, bf16[72,3072]{1,0:T(8,128)(2,1)}, f32[72,3072]{1,0:T(8,128)}, bf16[192,1152]{1,0:T(8,1...) custom-call(s32[5]{0:T(128)} %stack.48.refs_0_, ...), custom_call_target="tpu_custom_call" | custom-call | flops 1 | bytes 1 | tf_op jit(solution)/shard_map/early/pallas_call | solution.py:593
  354.2 7.5 %value.1 = (bf16[4,144,1152]{2,1,0:T(8,128)(2,1)}, bf16[4,144,1152]{2,1,0:T(8,128)(2,1)}) custom-call(s32[5]{0:T(128)} %stack.48.refs_0_, bf16[72,3072]{1,0:T(8,128)(2,1)} %get-tuple-element.165.refs_1_, bf16[8,144,1024]{2,1,0:T(8,128)(2,1)} %get-tuple-element.121.refs_1_.refs_2_.refs_10_, bf16[1024,768]{1,0:T(8,128)(2,1)} %get-tuple-element.166.refs_3_.refs_4_, ...), custom_call_target="tpu_custom_call" | custom-call | flops 1 | bytes 1 | tf_op jit(solution)/shard_map/value/pallas_call | solution.py:593
  361.7 5.0 collective-permute-start.18
  367.3 3.2 collective-permute-start.14
  371.0 28.0 %project_back.1 = (bf16[1024,1152]{1,0:T(8,128)(2,1)}, bf16[1024,1152]{1,0:T(8,128)(2,1)}, bf16[8,128]{1,0:T(8,128)(2,1)}, bf16[4,144,1152]{2,1,0:T(8,128)(2,1)}...) custom-call(s32[5]{0:T(128)} %stack.48.refs_0_, ...), custom_call_target="tpu_custom_call" | custom-call | flops 1 | bytes 1 | tf_op jit(solution)/shard_map/project_back/pallas_call | solution.py:593
  401.1 4.4 v.1
  405.8 4.7 early.7
  412.0 5.5 %late.4 = (bf16[2,144,1152]{2,1,0:T(8,128)(2,1)}, bf16[2,144,1152]{2,1,0:T(8,128)(2,1)}, bf16[2,144,1152]{2,1,0:T(8,128)(2,1)}, bf16[2,144,1152]{2,1,0:T(8,128)(2,1)}) custom-call(s32[5]{0:T(128)} %stack.48.refs_0_, bf16[36,7296]{1,0:T(8,128)(2,1)} %get-tuple-element.190.refs_1_, bf16[4,144,1152]{2,1,0:T(8,128)(2,1)} %get-tuple-element.191.refs_2_, ...), custom_call_target="tpu_custom_call" | custom-call | flops 1 | bytes 1 | tf_op jit(solution)/shard_map/late/pallas_call | solution.py:593
  418.8 1.5 collective-permute-start.21
  420.3 3.6 collective-permute-start.26
  424.0 19.7 %input_back.1 = (bf16[1024,1152]{1,0:T(8,128)(2,1)}, bf16[8,3584]{1,0:T(8,128)(2,1)}, bf16[8,3584]{1,0:T(8,128)(2,1)}) custom-call(s32[6]{0:T(128)} %pad_add_fusion.refs_0_, bf16[2,144,1152]{2,1,0:T(8,128)(2,1)} %get-tuple-element.195.refs_1_, bf16[1024,1152]{1,0:T(8,128)(2,1)} %get-tuple-element.173.refs_0_.refs_2_, ...), custom_call_target="tpu_custom_call" | custom-call | flops 1 | bytes 1 | tf_op jit(solution)/shard_map/input_back/pallas_call | solution.py:593
  446.0 5.5 %late.5 = (bf16[2,72,1152]{2,1,0:T(8,128)(2,1)}, f32[2,72,1152]{2,1,0:T(8,128)}, bf16[144,1152]{1,0:T(8,128)(2,1)}, f32[144,1152]{1,0:T(8,128)}, bf16[2,72,1152]...) custom-call(s32[5]{0:T(128)} %stack.48.refs_0_, bf16[1024,1152]{1,0:T(8,128)(2,1)} %get-tuple-element.200.refs_1_, ...), custom_call_target="tpu_custom_call" | custom-call | flops 1 | bytes 1 | tf_op jit(solution)/shard_map/late/pallas_call | solution.py:593
  452.9 1.8 collective-permute-start.28
  455.4 2.2 pair.1.refs_1_.refs_8_
  457.6 8.2 %collective-permute-done.27.refs_5_ = bf16[96,1152]{1,0:T(8,128)(2,1)S(1)} collective-permute-done((bf16[96,1152]{1,0:T(8,128)(2,1)S(1)}, bf16[96,1152]{1,0:T(8,128)(2,1)S(1)}, u32[]{:S(2)}, u32[]{:S(2)}) %collective-permute-start.27) | collective-permute-done | bytes 221216 | tf_op jit(solution)/shard_map/ppermute | solution.py:637
  465.8 2.7 collective-permute-start.31
  469.3 3.5 early_last.1
  473.8 3.7 late.6
  478.7 1.7 collective-permute-start.32
  480.4 2.0 collective-permute-start.35
  482.4 3.4 collective-permute-done.35.refs_9_
  486.6 3.3 late.7
  490.3 5.4 %fusion = f32[8,1152]{1,0:T(8,128)S(1)} fusion(bf16[1152,3456]{1,0:T(8,128)(2,1)} %param.23, bf16[8,4736]{1,0:T(8,128)(2,1)S(1)} %copy-done.11), kind=kOutput, calls=%fused_computation.1 | convolution fusion | flops 63700992 | bytes 8054784 | tf_op jit(solution)/shard_map/nc,dc->nd/dot_general | solution.py:976
  495.8 1.4 collective-permute-start.25
  497.9 2.6 every.1.refs_1_.refs_4_
  504.0 14.1 %collective-permute-done.37.refs_3_ = bf16[36,3456]{1,0:T(8,128)(2,1)S(1)} collective-permute-done((bf16[36,3456]{1,0:T(8,128)(2,1)S(1)}, bf16[36,3456]{1,0:T(8,128)(2,1)S(1)}, u32[]{:S(2)}, u32[]{:S(2)}) %collective-permute-start.37) | collective-permute-done | bytes 248864 | tf_op jit(solution)/shard_map/ppermute | solution.py:637
  519.0 4.0 late_last.1
  (163 shorter events, 34.7 us)
Async XLA Ops:
  0.6 5.0 collective-permute-start
  11.0 4.6 collective-permute-start.1
  93.6 111.4 %copy-start.39 = (s32[1,4]{1,0:T(1,128)S(1)}, s32[1,4]{1,0:T(1,128)}, u32[]{:S(2)}) copy-start(s32[1,4]{1,0:T(1,128)} %slice.29) | copy-start | bytes 52
  196.5 37.6 %collective-permute-start.3 = (bf16[4,144,3072]{2,1,0:T(8,128)(2,1)}, bf16[4,144,3072]{2,1,0:T(8,128)(2,1)S(1)}, u32[]{:S(2)}, u32[]{:S(2)}) collective-permute-start(bf16[4,144,3072]{2,1,0:T(8,128)(2,1)} %get-tuple-element.138), channel_id=1, source_target_pairs={{0,2},{2,0},{4,6},{6,4},{8,10},{10,8},{12,14},{14,12},{16,18},{18,... | collective-permute-start | bytes 10616840 | tf_op jit(solution)/shard_map/ppermute | solution.py:637
  204.4 30.8 %collective-permute-start.4 = (bf16[4,384,1152]{2,1,0:T(8,128)(2,1)}, bf16[4,384,1152]{2,1,0:T(8,128)(2,1)}, u32[]{:S(2)}, u32[]{:S(2)}) collective-permute-start(bf16[4,384,1152]{2,1,0:T(8,128)(2,1)} %bitcast.55), channel_id=1, source_target_pairs={{0,2},{2,0},{4,6},{6,4},{8,10},{10,8},{12,14},{14,12},{16,18},{18,... | collective-permute-start | bytes 10616840 | tf_op jit(solution)/shard_map/ppermute | solution.py:637
  204.5 30.8 %collective-permute-start.2 = (bf16[4,144,3072]{2,1,0:T(8,128)(2,1)}, bf16[4,144,3072]{2,1,0:T(8,128)(2,1)}, u32[]{:S(2)}, u32[]{:S(2)}) collective-permute-start(bf16[4,144,3072]{2,1,0:T(8,128)(2,1)} %get-tuple-element.129.refs_1_), channel_id=1, source_target_pairs={{0,2},{2,0},{4,6},{6,4},{8,10},{10,8},{12,14},{14,12},{16,18},{18,... | collective-permute-start | bytes 10616840 | tf_op jit(solution)/shard_map/ppermute | solution.py:637
  230.8 3.3 collective-permute-start.5
  251.6 55.3 %collective-permute-start.7 = (bf16[2,144,3072]{2,1,0:T(8,128)(2,1)}, bf16[2,144,3072]{2,1,0:T(8,128)(2,1)S(1)}, u32[]{:S(2)}, u32[]{:S(2)}) collective-permute-start(bf16[2,144,3072]{2,1,0:T(8,128)(2,1)} %get-tuple-element.151), channel_id=1, source_target_pairs={{0,4},{2,6},{4,0},{6,2},{8,12},{10,14},{12,8},{14,10},{16,20},{18,... | collective-permute-start | bytes 5308424 | tf_op jit(solution)/shard_map/ppermute | solution.py:637
  253.1 53.7 %collective-permute-start.8 = (bf16[4,192,1152]{2,1,0:T(8,128)(2,1)}, bf16[4,192,1152]{2,1,0:T(8,128)(2,1)S(1)}, u32[]{:S(2)}, u32[]{:S(2)}) collective-permute-start(bf16[4,192,1152]{2,1,0:T(8,128)(2,1)} %get-tuple-element.153), channel_id=1, source_target_pairs={{0,8},{2,10},{4,12},{6,14},{8,0},{10,2},{12,4},{14,6},{16,24},{18,... | collective-permute-start | bytes 5308424 | tf_op jit(solution)/shard_map/ppermute | solution.py:637
  254.7 52.1 %collective-permute-start.6 = (bf16[2,144,3072]{2,1,0:T(8,128)(2,1)}, bf16[2,144,3072]{2,1,0:T(8,128)(2,1)}, u32[]{:S(2)}, u32[]{:S(2)}) collective-permute-start(bf16[2,144,3072]{2,1,0:T(8,128)(2,1)} %get-tuple-element.143.refs_1_), channel_id=1, source_target_pairs={{0,1},{1,0},{2,3},{3,2},{4,5},{5,4},{6,7},{7,6},{8,9},{9,8},{10,11... | collective-permute-start | bytes 5308424 | tf_op jit(solution)/shard_map/ppermute | solution.py:636
  257.8 49.0 %collective-permute-start.9 = (bf16[2,144,1152]{2,1,0:T(8,128)(2,1)}, bf16[2,144,1152]{2,1,0:T(8,128)(2,1)}, u32[]{:S(2)}, u32[]{:S(2)}) collective-permute-start(bf16[2,144,1152]{2,1,0:T(8,128)(2,1)} %get-tuple-element.155), channel_id=1, source_target_pairs={{0,4},{2,6},{4,0},{6,2},{8,12},{10,14},{12,8},{14,10},{16,20},{18,... | collective-permute-start | bytes 1990664 | tf_op jit(solution)/shard_map/ppermute | solution.py:637
  317.7 28.3 %collective-permute-start.11 = (bf16[2,72,3072]{2,1,0:T(8,128)(2,1)}, bf16[2,72,3072]{2,1,0:T(8,128)(2,1)S(1)}, u32[]{:S(2)}, u32[]{:S(2)}) collective-permute-start(bf16[2,72,3072]{2,1,0:T(8,128)(2,1)} %get-tuple-element.160), channel_id=1, source_target_pairs={{0,8},{2,10},{4,12},{6,14},{8,0},{10,2},{12,4},{14,6},{16,24},{18,... | collective-permute-start | bytes 2654216 | tf_op jit(solution)/shard_map/ppermute | solution.py:637
  319.4 26.6 %collective-permute-start.12 = (bf16[2,192,1152]{2,1,0:T(8,128)(2,1)}, bf16[2,192,1152]{2,1,0:T(8,128)(2,1)S(1)}, u32[]{:S(2)}, u32[]{:S(2)}) collective-permute-start(bf16[2,192,1152]{2,1,0:T(8,128)(2,1)} %get-tuple-element.162), channel_id=1, source_target_pairs={{0,1},{1,0},{2,3},{3,2},{4,5},{5,4},{6,7},{7,6},{8,9},{9,8},{10,11... | collective-permute-start | bytes 2654216 | tf_op jit(solution)/shard_map/ppermute | solution.py:636
  322.7 23.3 %collective-permute-start.10 = (bf16[144,3072]{1,0:T(8,128)(2,1)}, bf16[144,3072]{1,0:T(8,128)(2,1)S(1)}, u32[]{:S(2)}, u32[]{:S(2)}) collective-permute-start(bf16[144,3072]{1,0:T(8,128)(2,1)} %get-tuple-element.156.refs_1_), channel_id=1, source_target_pairs={{0,4},{2,6},{4,0},{6,2},{8,12},{10,14},{12,8},{14,10},{16,20},{18,... | collective-permute-start | bytes 2654216 | tf_op jit(solution)/shard_map/ppermute | solution.py:637
  324.2 21.8 %collective-permute-start.13 = (bf16[2,72,1152]{2,1,0:T(8,128)(2,1)}, bf16[2,72,1152]{2,1,0:T(8,128)(2,1)S(1)}, u32[]{:S(2)}, u32[]{:S(2)}) collective-permute-start(bf16[2,72,1152]{2,1,0:T(8,128)(2,1)} %get-tuple-element.164), channel_id=1, source_target_pairs={{0,8},{2,10},{4,12},{6,14},{8,0},{10,2},{12,4},{14,6},{16,24},{18,... | collective-permute-start | bytes 995336 | tf_op jit(solution)/shard_map/ppermute | solution.py:637
  354.2 12.5 %copy-start.40 = (bf16[192,1152]{1,0:T(8,128)(2,1)S(1)}, bf16[192,1152]{1,0:T(8,128)(2,1)}, u32[]{:S(2)}) copy-start(bf16[192,1152]{1,0:T(8,128)(2,1)} %get-tuple-element.175) | copy-start | bytes 1327108
  354.2 13.1 %copy-start.22 = (bf16[72,3072]{1,0:T(8,128)(2,1)S(1)}, bf16[72,3072]{1,0:T(8,128)(2,1)}, u32[]{:S(2)}) copy-start(bf16[72,3072]{1,0:T(8,128)(2,1)} %get-tuple-element.165.refs_1_) | copy-start | bytes 1327108
  354.2 16.3 %copy-start.42 = (bf16[72,1152]{1,0:T(8,128)(2,1)S(1)}, bf16[72,1152]{1,0:T(8,128)(2,1)}, u32[]{:S(2)}) copy-start(bf16[72,1152]{1,0:T(8,128)(2,1)} %get-tuple-element.176) | copy-start | bytes 497668
  361.7 37.4 %collective-permute-start.18 = (bf16[4,144,1152]{2,1,0:T(8,128)(2,1)}, bf16[4,144,1152]{2,1,0:T(8,128)(2,1)S(1)}, u32[]{:S(2)}, u32[]{:S(2)}) collective-permute-start(bf16[4,144,1152]{2,1,0:T(8,128)(2,1)} %get-tuple-element.168.refs_1_), channel_id=1, source_target_pairs={{0,2},{2,0},{4,6},{6,4},{8,10},{10,8},{12,14},{14,12},{16,18},{18,... | collective-permute-start | bytes 3981320 | tf_op jit(solution)/shard_map/ppermute | solution.py:637
  366.7 32.3 %collective-permute-start.15 = (bf16[72,3072]{1,0:T(8,128)(2,1)}, bf16[72,3072]{1,0:T(8,128)(2,1)S(1)}, u32[]{:S(2)}, u32[]{:S(2)}) collective-permute-start(bf16[72,3072]{1,0:T(8,128)(2,1)} %get-tuple-element.174), channel_id=1, source_target_pairs={{0,1},{1,0},{2,3},{3,2},{4,5},{5,4},{6,7},{7,6},{8,9},{9,8},{10,11... | collective-permute-start | bytes 1327112 | tf_op jit(solution)/shard_map/ppermute | solution.py:636
  366.7 32.3 %collective-permute-start.16 = (bf16[192,1152]{1,0:T(8,128)(2,1)S(1)}, bf16[192,1152]{1,0:T(8,128)(2,1)S(1)}, u32[]{:S(2)}, u32[]{:S(2)}) collective-permute-start(bf16[192,1152]{1,0:T(8,128)(2,1)S(1)} %copy-done.40), channel_id=1, source_target_pairs={{0,4},{2,6},{4,0},{6,2},{8,12},{10,14},{12,8},{14,10},{16,20},{18,... | collective-permute-start | bytes 1327112 | tf_op jit(solution)/shard_map/ppermute | solution.py:637
  367.3 31.8 %collective-permute-start.14 = (bf16[72,3072]{1,0:T(8,128)(2,1)S(1)}, bf16[72,3072]{1,0:T(8,128)(2,1)S(1)}, u32[]{:S(2)}, u32[]{:S(2)}) collective-permute-start(bf16[72,3072]{1,0:T(8,128)(2,1)S(1)} %copy-done.22), channel_id=1, source_target_pairs={{0,8},{2,10},{4,12},{6,14},{8,0},{10,2},{12,4},{14,6},{16,24},{18,... | collective-permute-start | bytes 1327112 | tf_op jit(solution)/shard_map/ppermute | solution.py:637
  370.5 28.5 %collective-permute-start.17 = (bf16[72,1152]{1,0:T(8,128)(2,1)S(1)}, bf16[72,1152]{1,0:T(8,128)(2,1)S(1)}, u32[]{:S(2)}, u32[]{:S(2)}) collective-permute-start(bf16[72,1152]{1,0:T(8,128)(2,1)S(1)} %copy-done.42), channel_id=1, source_target_pairs={{0,1},{1,0},{2,3},{3,2},{4,5},{5,4},{6,7},{7,6},{8,9},{9,8},{10,11... | collective-permute-start | bytes 497672 | tf_op jit(solution)/shard_map/ppermute | solution.py:636
  400.6 9.9 %collective-permute-start.19 = (bf16[4,144,1152]{2,1,0:T(8,128)(2,1)}, bf16[4,144,1152]{2,1,0:T(8,128)(2,1)S(1)}, u32[]{:S(2)}, u32[]{:S(2)}) collective-permute-start(bf16[4,144,1152]{2,1,0:T(8,128)(2,1)} %get-tuple-element.192), channel_id=1, source_target_pairs={{0,2},{2,0},{4,6},{6,4},{8,10},{10,8},{12,14},{14,12},{16,18},{18,... | collective-permute-start | bytes 3981320 | tf_op jit(solution)/shard_map/ppermute | solution.py:637
  400.6 9.9 %collective-permute-start.20 = (bf16[4,144,1152]{2,1,0:T(8,128)(2,1)}, bf16[4,144,1152]{2,1,0:T(8,128)(2,1)S(1)}, u32[]{:S(2)}, u32[]{:S(2)}) collective-permute-start(bf16[4,144,1152]{2,1,0:T(8,128)(2,1)} %get-tuple-element.194), channel_id=1, source_target_pairs={{0,2},{2,0},{4,6},{6,4},{8,10},{10,8},{12,14},{14,12},{16,18},{18,... | collective-permute-start | bytes 3981320 | tf_op jit(solution)/shard_map/ppermute | solution.py:637
  405.5 39.3 %collective-permute-start.23 = (bf16[4,72,1152]{2,1,0:T(8,128)(2,1)}, bf16[4,72,1152]{2,1,0:T(8,128)(2,1)S(1)}, u32[]{:S(2)}, u32[]{:S(2)}) collective-permute-start(bf16[4,72,1152]{2,1,0:T(8,128)(2,1)} %get-tuple-element.182.refs_1_), channel_id=1, source_target_pairs={{0,8},{2,10},{4,12},{6,14},{8,0},{10,2},{12,4},{14,6},{16,24},{18,... | collective-permute-start | bytes 1990664 | tf_op jit(solution)/shard_map/ppermute | solution.py:637
  412.0 8.3 %copy-start.20 = (bf16[36,7296]{1,0:T(8,128)(2,1)S(1)}, bf16[36,7296]{1,0:T(8,128)(2,1)}, u32[]{:S(2)}) copy-start(bf16[36,7296]{1,0:T(8,128)(2,1)} %get-tuple-element.190.refs_1_) | copy-start | bytes 1575940
  417.5 27.2 %collective-permute-start.22 = (bf16[2,144,1152]{2,1,0:T(8,128)(2,1)}, bf16[2,144,1152]{2,1,0:T(8,128)(2,1)S(1)}, u32[]{:S(2)}, u32[]{:S(2)}) collective-permute-start(bf16[2,144,1152]{2,1,0:T(8,128)(2,1)} %get-tuple-element.203), channel_id=1, source_target_pairs={{0,1},{1,0},{2,3},{3,2},{4,5},{5,4},{6,7},{7,6},{8,9},{9,8},{10,11... | collective-permute-start | bytes 1990664 | tf_op jit(solution)/shard_map/ppermute | solution.py:636
  418.8 26.0 %collective-permute-start.21 = (bf16[2,144,1152]{2,1,0:T(8,128)(2,1)}, bf16[2,144,1152]{2,1,0:T(8,128)(2,1)S(1)}, u32[]{:S(2)}, u32[]{:S(2)}) collective-permute-start(bf16[2,144,1152]{2,1,0:T(8,128)(2,1)} %get-tuple-element.195.refs_1_), channel_id=1, source_target_pairs={{0,4},{2,6},{4,0},{6,2},{8,12},{10,14},{12,8},{14,10},{16,20},{18,... | collective-permute-start | bytes 1990664 | tf_op jit(solution)/shard_map/ppermute | solution.py:637
  420.3 48.1 %collective-permute-start.26 = (bf16[36,7296]{1,0:T(8,128)(2,1)S(1)}, bf16[36,7296]{1,0:T(8,128)(2,1)S(1)}, u32[]{:S(2)}, u32[]{:S(2)}) collective-permute-start(bf16[36,7296]{1,0:T(8,128)(2,1)S(1)} %copy-done.20), channel_id=1, source_target_pairs={{0,16},{2,18},{4,20},{6,22},{8,24},{10,26},{12,28},{14,30},{16,0},... | collective-permute-start | bytes 1575944 | tf_op jit(solution)/shard_map/ppermute | solution.py:637
  443.7 11.1 %collective-permute-start.24 = (bf16[8,3584]{1,0:T(8,128)(2,1)}, bf16[8,3584]{1,0:T(8,128)(2,1)S(1)}, u32[]{:S(2)}, u32[]{:S(2)}) collective-permute-start(bf16[8,3584]{1,0:T(8,128)(2,1)} %get-tuple-element.207), channel_id=1, source_target_pairs={{0,1},{1,0},{2,3},{3,2},{4,5},{5,4},{6,7},{7,6},{8,9},{9,8},{10,11... | collective-permute-start | bytes 172040 | tf_op jit(solution)/shard_map/ppermute | solution.py:636
  446.0 8.7 %copy-start.41 = (bf16[96,1152]{1,0:T(8,128)(2,1)S(1)}, bf16[96,1152]{1,0:T(8,128)(2,1)}, u32[]{:S(2)}) copy-start(bf16[96,1152]{1,0:T(8,128)(2,1)} %get-tuple-element.210) | copy-start | bytes 663556
  451.6 21.2 %collective-permute-start.29 = (bf16[144,1152]{1,0:T(8,128)(2,1)}, bf16[144,1152]{1,0:T(8,128)(2,1)S(1)}, u32[]{:S(2)}, u32[]{:S(2)}) collective-permute-start(bf16[144,1152]{1,0:T(8,128)(2,1)} %get-tuple-element.214), channel_id=1, source_target_pairs={{0,4},{2,6},{4,0},{6,2},{8,12},{10,14},{12,8},{14,10},{16,20},{18,... | collective-permute-start | bytes 995336 | tf_op jit(solution)/shard_map/ppermute | solution.py:637
  452.5 20.3 %collective-permute-start.30 = (bf16[2,72,1152]{2,1,0:T(8,128)(2,1)}, bf16[2,72,1152]{2,1,0:T(8,128)(2,1)S(1)}, u32[]{:S(2)}, u32[]{:S(2)}) collective-permute-start(bf16[2,72,1152]{2,1,0:T(8,128)(2,1)} %get-tuple-element.216), channel_id=1, source_target_pairs={{0,1},{1,0},{2,3},{3,2},{4,5},{5,4},{6,7},{7,6},{8,9},{9,8},{10,11... | collective-permute-start | bytes 995336 | tf_op jit(solution)/shard_map/ppermute | solution.py:636
  452.9 19.9 %collective-permute-start.28 = (bf16[2,72,1152]{2,1,0:T(8,128)(2,1)}, bf16[2,72,1152]{2,1,0:T(8,128)(2,1)S(1)}, u32[]{:S(2)}, u32[]{:S(2)}) collective-permute-start(bf16[2,72,1152]{2,1,0:T(8,128)(2,1)} %get-tuple-element.205.refs_1_), channel_id=1, source_target_pairs={{0,8},{2,10},{4,12},{6,14},{8,0},{10,2},{12,4},{14,6},{16,24},{18,... | collective-permute-start | bytes 995336 | tf_op jit(solution)/shard_map/ppermute | solution.py:637
  454.8 11.0 %collective-permute-start.27 = (bf16[96,1152]{1,0:T(8,128)(2,1)S(1)}, bf16[96,1152]{1,0:T(8,128)(2,1)S(1)}, u32[]{:S(2)}, u32[]{:S(2)}) collective-permute-start(bf16[96,1152]{1,0:T(8,128)(2,1)S(1)} %copy-done.41), channel_id=1, source_target_pairs={{0,16},{2,18},{4,20},{6,22},{8,24},{10,26},{12,28},{14,30},{16,0},... | collective-permute-start | bytes 663560 | tf_op jit(solution)/shard_map/ppermute | solution.py:637
  465.8 7.0 %collective-permute-start.31 = (bf16[8,4736]{1,0:T(8,128)(2,1)}, bf16[8,4736]{1,0:T(8,128)(2,1)S(1)}, u32[]{:S(2)}, u32[]{:S(2)}) collective-permute-start(bf16[8,4736]{1,0:T(8,128)(2,1)} %pair.1.refs_1_.refs_8_), channel_id=1, source_target_pairs={{0,16},{2,18},{4,20},{6,22},{8,24},{10,26},{12,28},{14,30},{16,0},... | collective-permute-start | bytes 227336 | tf_op jit(solution)/shard_map/ppermute | solution.py:637
  473.8 16.6 %copy-start.11 = (bf16[8,4736]{1,0:T(8,128)(2,1)S(1)}, bf16[8,4736]{1,0:T(8,128)(2,1)}, u32[]{:S(2)}) copy-start(bf16[8,4736]{1,0:T(8,128)(2,1)} %pair.1.refs_1_.refs_8_) | copy-start | bytes 227332
  477.5 8.3 %collective-permute-start.33 = (bf16[72,1152]{1,0:T(8,128)(2,1)}, bf16[72,1152]{1,0:T(8,128)(2,1)S(1)}, u32[]{:S(2)}, u32[]{:S(2)}) collective-permute-start(bf16[72,1152]{1,0:T(8,128)(2,1)} %get-tuple-element.220), channel_id=1, source_target_pairs={{0,8},{2,10},{4,12},{6,14},{8,0},{10,2},{12,4},{14,6},{16,24},{18,... | collective-permute-start | bytes 497672 | tf_op jit(solution)/shard_map/ppermute | solution.py:637
  477.5 8.3 %collective-permute-start.34 = (bf16[72,1152]{1,0:T(8,128)(2,1)}, bf16[72,1152]{1,0:T(8,128)(2,1)S(1)}, u32[]{:S(2)}, u32[]{:S(2)}) collective-permute-start(bf16[72,1152]{1,0:T(8,128)(2,1)} %get-tuple-element.222), channel_id=1, source_target_pairs={{0,4},{2,6},{4,0},{6,2},{8,12},{10,14},{12,8},{14,10},{16,20},{18,... | collective-permute-start | bytes 497672 | tf_op jit(solution)/shard_map/ppermute | solution.py:637
  478.7 7.1 %collective-permute-start.32 = (bf16[72,1152]{1,0:T(8,128)(2,1)}, bf16[72,1152]{1,0:T(8,128)(2,1)S(1)}, u32[]{:S(2)}, u32[]{:S(2)}) collective-permute-start(bf16[72,1152]{1,0:T(8,128)(2,1)} %get-tuple-element.217.refs_1_), channel_id=1, source_target_pairs={{0,1},{1,0},{2,3},{3,2},{4,5},{5,4},{6,7},{7,6},{8,9},{9,8},{10,11... | collective-permute-start | bytes 497672 | tf_op jit(solution)/shard_map/ppermute | solution.py:636
  480.4 5.4 %collective-permute-start.35 = (bf16[16,4736]{1,0:T(8,128)(2,1)}, bf16[16,4736]{1,0:T(8,128)(2,1)S(1)}, u32[]{:S(2)}, u32[]{:S(2)}) collective-permute-start(bf16[16,4736]{1,0:T(8,128)(2,1)} %get-tuple-element.223.refs_8_), channel_id=1, source_target_pairs={{0,8},{2,10},{4,12},{6,14},{8,0},{10,2},{12,4},{14,6},{16,24},{18,... | collective-permute-start | bytes 454664 | tf_op jit(solution)/shard_map/ppermute | solution.py:637
  490.0 10.6 %copy-start.1 = (f32[36,7296]{1,0:T(8,128)S(1)}, f32[36,7296]{1,0:T(8,128)}, u32[]{:S(2)}) copy-start(f32[36,7296]{1,0:T(8,128)} %get-tuple-element.211.refs_1_) | copy-start | bytes 3151876
  490.0 7.2 %collective-permute-start.36 = (bf16[32,4736]{1,0:T(8,128)(2,1)}, bf16[32,4736]{1,0:T(8,128)(2,1)S(1)}, u32[]{:S(2)}, u32[]{:S(2)}) collective-permute-start(bf16[32,4736]{1,0:T(8,128)(2,1)} %get-tuple-element.225.refs_2_), channel_id=1, source_target_pairs={{0,4},{2,6},{4,0},{6,2},{8,12},{10,14},{12,8},{14,10},{16,20},{18,... | collective-permute-start | bytes 909320 | tf_op jit(solution)/shard_map/ppermute | solution.py:637
  495.7 7.7 %copy-start.37 = (f32[1,4,1152]{2,1,0:T(4,128)S(1)}, f32[1,4,1152]{2,1,0:T(4,128)}, u32[]{:S(2)}) copy-start(f32[1,4,1152]{2,1,0:T(4,128)} %param.20) | copy-start | bytes 55300
  495.8 7.6 %collective-permute-start.25 = (bf16[4,1152]{1,0:T(4,128)(2,1)S(1)}, bf16[4,1152]{1,0:T(4,128)(2,1)S(1)}, u32[]{:S(2)}, u32[]{:S(2)}) collective-permute-start(bf16[4,1152]{1,0:T(4,128)(2,1)S(1)} %fusion.2), channel_id=1, source_target_pairs={{0,1},{1,0},{2,3},{3,2},{4,5},{5,4},{6,7},{7,6},{8,9},{9,8},{10,11... | collective-permute-start | bytes 27656 | tf_op jit(solution)/shard_map/ppermute | solution.py:636
  500.5 17.6 %collective-permute-start.38 = (bf16[64,4736]{1,0:T(8,128)(2,1)}, bf16[64,4736]{1,0:T(8,128)(2,1)S(1)}, u32[]{:S(2)}, u32[]{:S(2)}) collective-permute-start(bf16[64,4736]{1,0:T(8,128)(2,1)} %every.1.refs_1_.refs_4_), channel_id=1, source_target_pairs={{0,2},{2,0},{4,6},{6,4},{8,10},{10,8},{12,14},{14,12},{16,18},{18,... | collective-permute-start | bytes 1818632 | tf_op jit(solution)/shard_map/ppermute | solution.py:637
  502.2 15.8 %collective-permute-start.37 = (bf16[36,3456]{1,0:T(8,128)(2,1)S(1)}, bf16[36,3456]{1,0:T(8,128)(2,1)S(1)}, u32[]{:S(2)}, u32[]{:S(2)}) collective-permute-start(bf16[36,3456]{1,0:T(8,128)(2,1)S(1)} %copy-done.29), channel_id=1, source_target_pairs={{0,16},{2,18},{4,20},{6,22},{8,24},{10,26},{12,28},{14,30},{16,0},... | collective-permute-start | bytes 746504 | tf_op jit(solution)/shard_map/ppermute | solution.py:637
  (34 other events, 44.7 us)

commit v7 on v6

--- a/solution.py
+++ b/solution.py
@@ -13,8 +13,10 @@
 GRID = 32
 EPS = 1e-06
 ROPE_BASE = 10000.0
-TB = 256
+SEG = 256
+TB = 512
 WIN = 256
+TOGETHER = 4
 SCORE_SCALE = float(HD**-0.5)
 SCORE_LOG2 = float(np.log2(np.e) * HD**-0.5)
 VMEM = 60 * 2**20
@@ -107,8 +109,7 @@
     return centred * inverse, inverse
 
 
-def norm_back(grad, scale_part, norm, inverse):
-    e = grad * (1.0 + scale_part)
+def norm_back(e, norm, inverse):
     return inverse * (
         e - jnp.mean(e, axis=-1, keepdims=True) - norm * jnp.mean(e * norm, axis=-1, keepdims=True)
     )
@@ -116,6 +117,17 @@
 
 def part(mod_ref, slot, index, width):
     return mod_ref[pl.ds(slot, 1), index * width : (index + 1) * width]
+
+
+def slots_here(slots, rows):
+    return [slots[pl.program_id(0) * (rows // SEG) + i] for i in range(rows // SEG)]
+
+
+def by_slot(function, here, *values):
+    done = [
+        function(slot, *(value[i * SEG : (i + 1) * SEG] for value in values)) for i, slot in enumerate(here)
+    ]
+    return jnp.concatenate(done, axis=0)
 
 
 def angles(coords_ref, cos_ref, sin_ref):
@@ -169,14 +181,24 @@
         out_ref[...] = acc_ref[pl.ds(start, rows)].astype(bf16).reshape(out_ref.shape)
 
 
+def add_by_slot(sums_ref, here, index, term):
+    width = term.shape[1]
+    for i, slot in enumerate(here):
+        rows = term[i * SEG : (i + 1) * SEG]
+        sums_ref[pl.ds(slot, 1), index * width : (index + 1) * width] += jnp.sum(rows, axis=0, keepdims=True)
+
+
 def project_kernel(
     slots, x_ref, mod_ref, w_ref, coords_ref, cos_ref, sin_ref, gain_ref, gather_ref, spread_ref,
     perm_ref, units_ref, raw_ref, inv_ref, q_ref, k_ref, v_ref, kt_ref,
 ):
     width = x_ref.shape[1]
-    slot = slots[pl.program_id(0)]
     norm, _ = normed(x_ref[...].astype(f32))
-    low = (norm * (1.0 + part(mod_ref, slot, 1, width)) + part(mod_ref, slot, 0, width)).astype(bf16)
+
+    def modulate(slot, rows):
+        return (rows * (1.0 + part(mod_ref, slot, 1, width)) + part(mod_ref, slot, 0, width)).astype(bf16)
+
+    low = by_slot(modulate, slots_here(slots, x_ref.shape[0]), norm)
     units_ref[...] = nt(perm_ref[...], low).astype(bf16).reshape(units_ref.shape)
     cosine, sine = angles(coords_ref, cos_ref, sin_ref)
     for index, out_ref in enumerate((q_ref, k_ref)):
@@ -192,68 +214,100 @@
     v_ref[...] = nn(low, w_ref[:, 2 * width :]).astype(bf16)
 
 
-def attend_kernel(
-    slots, x_ref, cot_ref, mod_ref, q_ref, k_ref, v_ref, w_out_ref, perm_ref,
-    o_ref, lse_ref, attn_ref, mid_ref, low_ref, gf_ref, att_units_ref, ffn_units_ref, lse_acc,
-):
-    block = pl.program_id(0)
-    width = x_ref.shape[1]
-    tokens = k_ref.shape[0]
+def attend_kernel(slots, q_ref, k_ref, v_ref, o_ref, lse_ref):
+    step = pl.program_id(0)
+    tokens, width = q_ref.shape
     lane128 = lax.broadcasted_iota(jnp.int32, (1, 128), 1)
     lane = lax.broadcasted_iota(jnp.int32, (1, WIN), 1)
-    o_ref[...] = jnp.zeros_like(o_ref)
-    lse_acc[...] = jnp.zeros_like(lse_acc)
-
-    def run(rows):
-        def head(h, carry):
-            start, offset = window(h, width)
-            inside = head_lanes(offset)
-            columns = pl.ds(start, WIN)
-            query = jnp.where(inside, q_ref[:, columns], 0)
-            value = jnp.where(inside, v_ref[rows, columns], 1)
-            weight = jnp.exp2(nt(query, k_ref[rows, columns]) * SCORE_LOG2).astype(bf16)
-            summed = nn(weight, value)
-            free = jnp.where(offset > 0, 0, WIN - 1)
-            total = jnp.sum(jnp.where(lane == free, summed, 0.0), axis=1, keepdims=True)
-            o_ref[:, columns] += jnp.where(inside, summed * (1.0 / total), 0.0)
-            lse_acc[...] += jnp.where(lane128 == h, jnp.log2(total), 0.0)
-            return carry
-
-        lax.fori_loop(0, HEADS, head, 0, unroll=2)
-
-    whole = slots[tokens // TB - 1] == slots[0]
+
+    @pl.when(step == 0)
+    def _():
+        o_ref[...] = jnp.zeros_like(o_ref)
+        lse_ref[...] = jnp.zeros_like(lse_ref)
+
+    def head(h, rows):
+        start, offset = window(h, width)
+        inside = head_lanes(offset)
+        columns = pl.ds(start, WIN)
+        query = jnp.where(inside, q_ref[rows, columns], 0)
+        value = jnp.where(inside, v_ref[rows, columns], 1)
+        weight = jnp.exp2(nt(query, k_ref[rows, columns]) * SCORE_LOG2).astype(bf16)
+        summed = nn(weight, value)
+        free = jnp.where(offset > 0, 0, WIN - 1)
+        total = jnp.sum(jnp.where(lane == free, summed, 0.0), axis=1, keepdims=True)
+        o_ref[rows, columns] += jnp.where(inside, summed * (1.0 / total), 0.0)
+        lse_ref[rows, :] += jnp.where(lane128 == h, jnp.log2(total), 0.0)
+
+    whole = slots[tokens // SEG - 1] == slots[0]
 
     @pl.when(whole)
     def _():
-        run(slice(None))
+        for i in range(TOGETHER):
+            head(step * TOGETHER + i, slice(None))
 
     @pl.when(jnp.logical_not(whole))
     def _():
-        run(pl.ds(pl.multiple_of(block * TB, TB), TB))
-
-    lse_ref[...] = lse_acc[...].T
-    slot = slots[block]
+        for i in range(TOGETHER):
+            for b in range(tokens // SEG):
+                head(step * TOGETHER + i, slice(b * SEG, (b + 1) * SEG))
+
+
+def mix_kernel(
+    slots, x_ref, cot_ref, mod_ref, o_ref, lse_ref, w_out_ref, perm_ref,
+    lse_out_ref, attn_ref, mid_ref, low_ref, gf_ref, att_units_ref, ffn_units_ref,
+):
+    width = x_ref.shape[1]
+    here = slots_here(slots, x_ref.shape[0])
+    lse_out_ref[...] = lse_ref[...].T
     attended = o_ref[...].astype(bf16)
     att_units_ref[...] = nt(perm_ref[...], attended).astype(bf16).reshape(att_units_ref.shape)
     attn = nn(attended, w_out_ref[...])
     attn_ref[...] = attn
-    mid = x_ref[...].astype(f32) + part(mod_ref, slot, 2, width) * attn
+    mid = by_slot(
+        lambda slot, x, rows: x.astype(f32) + part(mod_ref, slot, 2, width) * rows, here, x_ref[...], attn
+    )
     mid_ref[...] = mid
     norm, _ = normed(mid)
-    low = (norm * (1.0 + part(mod_ref, slot, 4, width)) + part(mod_ref, slot, 3, width)).astype(bf16)
+
+    def modulate(slot, rows):
+        return (rows * (1.0 + part(mod_ref, slot, 4, width)) + part(mod_ref, slot, 3, width)).astype(bf16)
+
+    low = by_slot(modulate, here, norm)
     low_ref[...] = low
     ffn_units_ref[...] = nt(perm_ref[...], low).astype(bf16).reshape(ffn_units_ref.shape)
-    gf_ref[...] = (cot_ref[...].astype(f32) * part(mod_ref, slot, 5, width)).astype(bf16)
+    gf_ref[...] = by_slot(
+        lambda slot, rows: (rows.astype(f32) * part(mod_ref, slot, 5, width)).astype(bf16), here, cot_ref[...]
+    )
 
 
 def ffn_kernel(
-    bits, x_ref, gf_ref, units_ref, wg_ref, wu_ref, wd_ref,
-    gate_send_ref, gate_own_ref, up_send_ref, up_own_ref, down_send_ref, down_own_ref, ffn_ref, dmod_ref,
-    turned_ref, *, n_mod, rows_ff,
+    bits, x_ref, gf_hbm, units_hbm, wg_ref, wu_ref, wd_ref,
+    gate_send_ref, gate_own_ref, up_send_ref, up_own_ref, down_send_ref, down_own_ref, ffn_hbm, dmod_hbm,
+    turned_ref, gf_ref, units_ref, ffn_ref, dmod_ref, sems, *, n_mod, rows_ff,
 ):
     core = bits[0]
+    first = pl.program_id(0) == 0
+    last = pl.program_id(0) == pl.num_programs(0) - 1
+    load_gf = pltpu.make_async_copy(gf_hbm, gf_ref, sems.at[0])
+    load_units = pltpu.make_async_copy(units_hbm, units_ref, sems.at[1])
+    store_ffn = pltpu.make_async_copy(ffn_ref, ffn_hbm, sems.at[2])
+    store_dmod = pltpu.make_async_copy(dmod_ref, dmod_hbm, sems.at[3])
+
+    @pl.when(first)
+    def _():
+        load_gf.start()
+        load_units.start()
+        ffn_ref[...] = jnp.zeros_like(ffn_ref)
+        dmod_ref[...] = jnp.zeros_like(dmod_ref)
+
     gate = nn(x_ref[...], wg_ref[...])
     up = nn(x_ref[...], wu_ref[...])
+
+    @pl.when(first)
+    def _():
+        load_gf.wait()
+        load_units.wait()
+
     grad_hidden = nt(gf_ref[...], wd_ref[...])
     sigmoid = 1.0 / (1.0 + jnp.exp(-gate))
     silu = gate * sigmoid
@@ -267,13 +321,14 @@
     dg = (grad_hidden * up * (sigmoid * (1.0 + gate * (1.0 - sigmoid)))).astype(bf16)
     du = (grad_hidden * silu).astype(bf16)
 
-    @pl.when(pl.program_id(0) == 0)
-    def _():
-        ffn_ref[...] = jnp.zeros_like(ffn_ref)
-        dmod_ref[...] = jnp.zeros_like(dmod_ref)
-
     ffn_ref[...] += nn(hidden, wd_ref[...])
     dmod_ref[...] += nt(dg, wg_ref[...]) + nt(du, wu_ref[...])
+
+    @pl.when(last)
+    def _():
+        store_ffn.start()
+        store_dmod.start()
+
     product(units_ref, 1 - core, dg, gate_send_ref)
     product(units_ref, 1 - core, du, up_send_ref)
     product(turned_ref, 1 - core, gf_ref[...], down_send_ref)
@@ -281,6 +336,11 @@
     product(units_ref, core, du, up_own_ref)
     product(turned_ref, core, gf_ref[...], down_own_ref)
 
+    @pl.when(last)
+    def _():
+        store_ffn.wait()
+        store_dmod.wait()
+
 
 def middle_kernel(
     slots, mid_ref, ffn_ref, dmod_ref, cot_ref, attn_ref, o_ref, units_ref, mod_ref, w_out_ref, gather_ref,
@@ -288,16 +348,20 @@
 ):
     width = mid_ref.shape[1]
     block = pl.program_id(0)
-    slot = slots[block]
+    here = slots_here(slots, mid_ref.shape[0])
+    segments = pl.num_programs(0) * len(here)
     incoming = cot_ref[...].astype(f32)
     mid = mid_ref[...]
-    out_ref[...] = (mid + part(mod_ref, slot, 5, width) * ffn_ref[...]).astype(bf16)
+    out_ref[...] = by_slot(
+        lambda slot, rows, ffn: (rows + part(mod_ref, slot, 5, width) * ffn).astype(bf16), here, mid, ffn_ref[...]
+    )
     norm, inverse = normed(mid)
     dmod = dmod_ref[...]
-    grad_mid = incoming + norm_back(dmod, part(mod_ref, slot, 4, width), norm, inverse)
+    scaled = by_slot(lambda slot, rows: rows * (1.0 + part(mod_ref, slot, 4, width)), here, dmod)
+    grad_mid = incoming + norm_back(scaled, norm, inverse)
     grad_mid_ref[...] = grad_mid
-    ga = (grad_mid * part(mod_ref, slot, 2, width)).astype(bf16)
-    grow = nn(units_ref[...].reshape(width, TB), ga)
+    ga = by_slot(lambda slot, rows: (rows * part(mod_ref, slot, 2, width)).astype(bf16), here, grad_mid)
+    grow = nn(units_ref[...].reshape(width, -1), ga)
 
     @pl.when(block == 0)
     def _():
@@ -309,7 +373,7 @@
 
     @pl.when(block == pl.num_programs(0) - 1)
     def _():
-        halves_out(acc_ref, slots[pl.num_programs(0)], send_ref, own_ref)
+        halves_out(acc_ref, slots[segments], send_ref, own_ref)
 
     do = nt(ga, w_out_ref[...]).astype(bf16)
     do_ref[...] = do
@@ -320,16 +384,14 @@
         sums_ref[...] = jnp.zeros_like(sums_ref)
 
     for index, term in enumerate((grad_mid * attn_ref[...], dmod, dmod * norm, incoming * ffn_ref[...])):
-        columns = slice(index * width, (index + 1) * width)
-        sums_ref[pl.ds(slot, 1), columns] += jnp.sum(term, axis=0, keepdims=True)
+        add_by_slot(sums_ref, here, index, term)
 
 
 def attend_back_kernel(
     slots, q_ref, k_ref, v_ref, do_ref, lse_ref, dot_ref, kt_ref, dqt_ref, dk_ref, dv_low_ref, dv_ref,
     *, first, base, base_row,
 ):
-    h = pl.program_id(0) + first
-    tokens, width = q_ref.shape
+    tokens = q_ref.shape[0]
 
     @pl.when(pl.program_id(0) == 0)
     def _():
@@ -337,16 +399,15 @@
         dk_ref[...] = jnp.zeros_like(dk_ref)
         dv_ref[...] = jnp.zeros_like(dv_ref)
 
-    start, offset = window(h, kt_ref.shape[0])
-    inside = head_lanes(offset)
-    columns = pl.ds(start, WIN)
-    out_columns = pl.ds(pl.multiple_of(start - base, 128), WIN)
-    first_row = pl.multiple_of((h * HD) // 16 * 16, 16)
-    out_rows = pl.ds(pl.multiple_of(first_row - base_row, 16), HD + 8)
-    row = lax.broadcasted_iota(jnp.int32, (HD + 8, 1), 0) + first_row
-    own_rows = (row >= h * HD) & (row < h * HD + HD)
-
-    def step(rows):
+    def head(h, rows):
+        start, offset = window(h, kt_ref.shape[0])
+        inside = head_lanes(offset)
+        columns = pl.ds(start, WIN)
+        out_columns = pl.ds(pl.multiple_of(start - base, 128), WIN)
+        first_row = pl.multiple_of((h * HD) // 16 * 16, 16)
+        out_rows = pl.ds(pl.multiple_of(first_row - base_row, 16), HD + 8)
+        row = lax.broadcasted_iota(jnp.int32, (HD + 8, 1), 0) + first_row
+        own_rows = (row >= h * HD) & (row < h * HD + HD)
         query = q_ref[rows, columns]
         grad_out = do_ref[rows, columns]
         key = jnp.where(inside, k_ref[rows, columns], 0)
@@ -358,19 +419,19 @@
         turned = nn(kt_ref[pl.ds(first_row, HD + 8), rows], scores) * SCORE_SCALE
         dqt_ref[out_rows, rows] += jnp.where(own_rows, turned, 0.0)
 
-    whole = slots[tokens // TB - 1] == slots[0]
+    whole = slots[tokens // SEG - 1] == slots[0]
+    begin = first + pl.program_id(0) * TOGETHER
 
     @pl.when(whole)
     def _():
-        step(slice(None))
+        for i in range(TOGETHER):
+            head(begin + i, slice(None))
 
     @pl.when(jnp.logical_not(whole))
     def _():
-        def block(i, carry):
-            step(pl.ds(pl.multiple_of(i * TB, TB), TB))
-            return carry
-
-        lax.fori_loop(0, tokens // TB, block, 0)
+        for i in range(TOGETHER):
+            for b in range(tokens // SEG):
+                head(begin + i, slice(b * SEG, (b + 1) * SEG))
 
     @pl.when(pl.program_id(0) == pl.num_programs(0) - 1)
     def _():
@@ -384,6 +445,8 @@
 
 def join_spans(low, high, begin, axis):
     size = low.shape[axis] - begin
+    if size == 0:
+        return jnp.concatenate([low, high], axis=axis)
     cut = lambda arr, start, stop: lax.slice_in_dim(arr, start, stop, axis=axis)
     middle = cut(low, begin, begin + size) + cut(high, 0, size)
     return jnp.concatenate([cut(low, 0, begin), middle, cut(high, size, high.shape[axis])], axis=axis)
@@ -421,7 +484,7 @@
             inverse * (back * gain_ref[index : index + 1, :] - norm * head_spread(mean, spread_ref))
         ).astype(bf16)
         out_ref[...] = grad_raw
-        acc_ref[...] += nn(units_ref[...].reshape(width, TB), grad_raw)
+        acc_ref[...] += nn(units_ref[...].reshape(width, -1), grad_raw)
 
     @pl.when(block == pl.num_programs(0) - 1)
     def _():
@@ -444,12 +507,14 @@
 ):
     width = x_ref.shape[1]
     block = pl.program_id(0)
-    slot = slots[block]
+    here = slots_here(slots, x_ref.shape[0])
     last_block = pl.num_programs(0) - 1
+    segments = pl.num_programs(0) * len(here)
     dmod = nt(gq_ref[...], w_ref[:, :width]) + nt(gk_ref[...], w_ref[:, width : 2 * width])
     dmod = dmod + nt(join_spans(dv0_ref[...], dv1_ref[...], base, 1), w_ref[:, 2 * width :])
     norm, inverse = normed(x_ref[...].astype(f32))
-    grad_x = grad_mid_ref[...] + norm_back(dmod, part(mod_ref, slot, 1, width), norm, inverse)
+    scaled = by_slot(lambda slot, rows: rows * (1.0 + part(mod_ref, slot, 1, width)), here, dmod)
+    grad_x = grad_mid_ref[...] + norm_back(scaled, norm, inverse)
     grad_x_ref[...] = grad_x.astype(bf16)
 
     @pl.when(block == 0)
@@ -457,12 +522,11 @@
         sums_ref[...] = jnp.zeros_like(sums_ref)
 
     for index, term in enumerate((dmod, dmod * norm)):
-        columns = slice(index * width, (index + 1) * width)
-        sums_ref[pl.ds(slot, 1), columns] += jnp.sum(term, axis=0, keepdims=True)
+        add_by_slot(sums_ref, here, index, term)
 
     @pl.when(block == last_block)
     def _():
-        mod = slots[last_block + 2]
+        mod = slots[segments + 1]
         count = sums_ref.shape[0]
         half = 3 * width
         mine = jnp.concatenate([sums_ref[...]] * 2, axis=0)
@@ -482,45 +546,69 @@
     product(units_ref, bits[0], rhs, own_ref)
 
 
-def split_step(bits, ins, outs, *, lead, at, bit, pair_rows):
-    own_ref, got_ref = ins
+def split_step(bits, ins, outs, *, lead, at, bit, pair_rows, cuts):
     send_ref, keep_ref = outs
     mine = bits[bit]
-
-    def total(*index):
-        return own_ref[index].astype(f32) + got_ref[index].astype(f32)
-
-    if at is None:
-        for j in range(max(lead, 1)):
-            index = (j,) if lead else ()
-            value = total(*index) if lead else own_ref[...].astype(f32) + got_ref[...].astype(f32)
-            rows = pair_rows or value.shape[0] // 2
-            for p in range(value.shape[0] // (2 * rows)):
-                first = value[2 * p * rows : (2 * p + 1) * rows]
-                second = value[(2 * p + 1) * rows : (2 * p + 2) * rows]
-                place = index + (slice(p * rows, (p + 1) * rows),)
-                send_ref[place] = jnp.where(mine == 1, first, second).astype(bf16)
-                keep_ref[place] = jnp.where(mine == 1, second, first).astype(keep_ref.dtype)
-        return
-    for j in range(lead // 2):
-        place = (j,) if lead > 2 else (Ellipsis,)
-        away = 1 - mine if lead == 2 else 2 * (1 - mine) + j if at == 0 else 2 * j + 1 - mine
-        own = mine if lead == 2 else 2 * mine + j if at == 0 else 2 * j + mine
-        send_ref[place] = total(away).astype(bf16)
-        keep_ref[place] = total(own).astype(keep_ref.dtype)
-
-
-def merge_step(bits, ins, outs, *, bit):
+    start = 0
+    for own_ref, got_ref, cut in zip(ins[::2], ins[1::2], cuts):
+        columns, target = slice(None), slice(None)
+        if cut:
+            columns, target = slice(*cut), slice(start, start + cut[1] - cut[0])
+            start = target.stop
+
+        def total(*index):
+            place = index + (slice(None), columns)
+            return own_ref[place].astype(f32) + got_ref[place].astype(f32)
+
+        if at is None:
+            for j in range(max(lead, 1)):
+                index = (j,) if lead else ()
+                value = total(*index)
+                rows = pair_rows or value.shape[0] // 2
+                for p in range(value.shape[0] // (2 * rows)):
+                    first = value[2 * p * rows : (2 * p + 1) * rows]
+                    second = value[(2 * p + 1) * rows : (2 * p + 2) * rows]
+                    place = index + (slice(p * rows, (p + 1) * rows), target)
+                    send_ref[place] = jnp.where(mine == 1, first, second).astype(bf16)
+                    keep_ref[place] = jnp.where(mine == 1, second, first).astype(keep_ref.dtype)
+            continue
+        for j in range(lead // 2):
+            place = ((j,) if lead > 2 else ()) + (slice(None), target)
+            away = 1 - mine if lead == 2 else 2 * (1 - mine) + j if at == 0 else 2 * j + 1 - mine
+            own = mine if lead == 2 else 2 * mine + j if at == 0 else 2 * j + mine
+            send_ref[place] = total(away).astype(bf16)
+            keep_ref[place] = total(own).astype(keep_ref.dtype)
+
+
+def merge_step(bits, ins, outs, *, bit, parts):
     send_ref, keep_ref = outs
     start = 0
-    for own_ref, got_ref in zip(ins[::2], ins[1::2]):
+    for own_ref, got_ref, pieces in zip(ins[::2], ins[1::2], parts):
         value = own_ref[...].astype(f32) + got_ref[...].astype(f32)
-        rows = value.shape[0] // 2
-        place = slice(start, start + value.shape[1])
+        rows, columns = value.shape[0] // 2, value.shape[1]
         first, second = value[:rows], value[rows:]
-        send_ref[:, place] = jnp.where(bits[bit] == 1, first, second).astype(bf16)
-        keep_ref[:, place] = jnp.where(bits[bit] == 1, second, first)
-        start += value.shape[1]
+        sent = jnp.where(bits[bit] == 1, first, second).astype(bf16)
+        kept = jnp.where(bits[bit] == 1, second, first)
+        for i in range(pieces):
+            place = slice(start, start + columns)
+            if pieces > 1:
+                send_ref[:, place] = jnp.zeros_like(send_ref[:, place])
+                keep_ref[:, place] = jnp.zeros_like(keep_ref[:, place])
+            taken = slice(i * rows // pieces, (i + 1) * rows // pieces)
+            send_ref[: rows // pieces, place] = sent[taken]
+            keep_ref[: rows // pieces, place] = kept[taken]
+            start += columns
+
+
+def apart_step(bits, ins, outs, *, places):
+    own_ref, got_ref = ins
+    for out, at, start, stop, rows in places:
+        value = own_ref[:, start:stop] + got_ref[:, start:stop].astype(f32)
+        if rows is None:
+            outs[out][:, at : at + stop - start] = value
+        else:
+            count = rows[1] - rows[0]
+            outs[out][rows[0] : rows[1], :] = value[:count]
 
 
 def pair_step(bits, ins, outs):
@@ -648,7 +736,10 @@
             args += inputs
             outs += shapes
         size = sum(arg.size for arg in args)
-        split = all(isinstance(stream, Stream) and stream.own.shape[-1] % 384 == 0 for stream in streams)
+        split = all(
+            isinstance(stream, Stream) and stream.side is None and stream.own.shape[-1] % 384 == 0
+            for stream in streams
+        )
         steps = 3 if split and size > 2**20 else 1
         results = self.call(
             functools.partial(step_kernel, plans=plans),
@@ -687,17 +778,23 @@
         order = ["mod", 1, 2]
         self.steps = order[first:] + order[:first] + list(range(3, reducer.n_dp.bit_length() - 1))
         self.lead = ["mod", 1]
+        self.side = None
         self.got = reducer.swap(sent, 0)
 
     def inputs(self):
-        return [self.own, self.got]
+        return [self.own, self.got] + ([self.side[0].own, self.side[0].got] if self.side else [])
 
     def plan(self):
         bit = self.steps[0]
         dims = self.own.shape
         at = self.lead.index(bit) if bit in self.lead else None
+        cuts = [None]
+        if self.side is not None:
+            cuts = [(0, dims[-1]), self.side[1]]
+            dims = dims[:-1] + (dims[-1] + self.side[1][1] - self.side[1][0],)
         function = functools.partial(
-            split_step, lead=dims[0] if self.lead else 0, at=at, bit=self.r.bit_of(bit), pair_rows=self.pair_rows
+            split_step, lead=dims[0] if self.lead else 0, at=at, bit=self.r.bit_of(bit), pair_rows=self.pair_rows,
+            cuts=cuts,
         )
         if at is None:
             dims = dims[:-2] + (dims[-2] // 2, dims[-1])
@@ -709,17 +806,18 @@
         bit = self.steps.pop(0)
         if bit in self.lead:
             self.lead.remove(bit)
+        self.side = None
         sent, self.own = results
         self.got = self.r.swap(sent, bit)
 
-    def last_plan(self):
-        return last_step, [shape(self.own.shape, f32)]
+    def join(self, stream, cut):
+        self.side = (stream, cut)
 
 
 class Merged:
     def __init__(self, streams):
         self.streams, self.r, self.bit = streams, streams[0].r, streams[0].steps[0]
-        self.own = None
+        self.own = self.places = self.shapes = None
 
     def inputs(self):
         if self.own is not None:
@@ -727,9 +825,10 @@
         return [arr for stream in self.streams for arr in (stream.own, stream.got)]
 
     def plan(self):
-        columns = sum(stream.own.shape[1] for stream in self.streams)
+        parts = [3 if stream.pair_rows else 1 for stream in self.streams]
+        columns = sum(pieces * stream.own.shape[1] for pieces, stream in zip(parts, self.streams))
         dims = (self.streams[0].own.shape[0] // 2, columns)
-        function = functools.partial(merge_step, bit=self.r.bit_of(self.bit))
+        function = functools.partial(merge_step, bit=self.r.bit_of(self.bit), parts=parts)
         return function, [shape(dims, bf16), shape(dims, f32)]
 
     def step(self, results):
@@ -737,7 +836,9 @@
         self.got = self.r.swap(sent, self.bit)
 
     def last_plan(self):
-        return last_step, [shape(self.own.shape, f32)]
+        if self.places is None:
+            return last_step, [shape(self.own.shape, f32)]
+        return functools.partial(apart_step, places=self.places), self.shapes
 
 
 class Gather:
@@ -793,7 +894,7 @@
     mod_index = lax.axis_index("mod")
     x = tokens[0]
     cot = cotangent[0]
-    slots = segments[0, ::TB]
+    slots = segments[0, ::SEG]
     coord = coords[0]
     cos_table, sin_table = (jnp.asarray(t) for t in rope_tables(width))
     gather, spread, head_fold = (jnp.asarray(t) for t in head_tables(width))
@@ -832,18 +933,28 @@
         scalars=slots,
         name="project",
     )
-    attended, lse, attn, mid, ffn_in, grad_ffn, out_units, ffn_units = call(
+    attended, lse_columns = call(
         attend_kernel,
+        (HEADS // TOGETHER,),
+        [fixed((count, width))] * 3,
+        [fixed((count, width)), fixed((count, 128))],
+        [token_f32, shape((count, 128), f32)],
+        (query, key, value),
+        scalars=slots,
+        name="attend",
+    )
+    lse, attn, mid, ffn_in, grad_ffn, out_units, ffn_units = call(
+        mix_kernel,
         (blocks,),
-        [token_spec, token_spec, mod_spec, token_spec] + [fixed((count, width))] * 2 + [square, square],
-        [token_spec, rows_of((128, TB), 1)] + [token_spec] * 4 + [units_spec] * 2,
-        [token_f32, lane_rows, token_f32, token_f32, token_bf16, token_bf16, units, units],
-        (x, cot, modulation, query, key, value, w_out, perm),
+        [token_spec, token_spec, mod_spec, token_spec, rows_of((TB, 128)), square, square],
+        [rows_of((128, TB), 1)] + [token_spec] * 4 + [units_spec] * 2,
+        [lane_rows, token_f32, token_f32, token_bf16, token_bf16, units, units],
+        (x, cot, modulation, attended, lse_columns, w_out, perm),
         scalars=slots,
-        scratch=[pltpu.VMEM((TB, 128), f32)],
-        name="attend",
-    )
-
+        name="mix",
+    )
+
+    anywhere = pl.BlockSpec(memory_space=pl.ANY)
     rows_ff = ff // n_dev
     chunk = 768
     piece = chunk // 8
@@ -853,15 +964,22 @@
     gate_send, gate_own, up_send, up_own, down_send, down_own, ffn, grad_mod_ffn = call(
         functools.partial(ffn_kernel, n_mod=n_mod, rows_ff=rows_ff),
         (ff // chunk,),
-        [fixed((count, width))] * 2 + [fixed(units.shape)]
+        [fixed((count, width)), anywhere, anywhere]
         + [rows_of((width, chunk), 1)] * 2 + [rows_of((chunk, width))],
         [rows_of((4, width // 8, chunk), 2)] * 4
-        + [rows_of((4, 1, piece, width), 1)] * 2 + [fixed((count, width))] * 2,
+        + [rows_of((4, 1, piece, width), 1)] * 2 + [anywhere] * 2,
         [half_units(width // 8, ff)] * 4
         + [shape((4, ff // chunk, piece, width), bf16)] * 2 + [token_f32] * 2,
         (ffn_in, grad_ffn, ffn_units, w_gate, w_up, w_down),
         scalars=reducer.bits,
-        scratch=[pltpu.VMEM((8, piece, count), bf16)],
+        scratch=[
+            pltpu.VMEM((8, piece, count), bf16),
+            pltpu.VMEM((count, width), bf16),
+            pltpu.VMEM(units.shape, bf16),
+            pltpu.VMEM((count, width), f32),
+            pltpu.VMEM((count, width), f32),
+            pltpu.SemaphoreType.DMA((4,)),
+        ],
         name="ffn",
     )
     gate = Stream(reducer, gate_send, gate_own, 0)
@@ -871,11 +989,12 @@
     )
 
     slots_core = jnp.concatenate([slots, reducer.bits[:2]])
+    seg_spec = rows_of((SEG, width))
     output, grad_mid, grad_attended, dot_term, sums_b, out_send, out_own = call(
         middle_kernel,
-        (blocks,),
-        [token_spec] * 6 + [units_spec, mod_spec, square, fixed(gather.shape)],
-        [token_spec] * 3 + [rows_of((128, TB), 1), fixed((slots_n, 4 * width))] + square_send,
+        (count // SEG,),
+        [seg_spec] * 6 + [rows_of((8, width // 8, SEG), 2), mod_spec, square, fixed(gather.shape)],
+        [seg_spec] * 3 + [rows_of((128, SEG), 1), fixed((slots_n, 4 * width))] + square_send,
         [token_bf16, token_f32, token_bf16, lane_rows, shape((slots_n, 4 * width), f32)] + square_shapes,
         (mid, ffn, grad_mod_ffn, cot, attn, attended, out_units, modulation, w_out, gather),
         scalars=slots_core,
@@ -883,7 +1002,10 @@
         name="middle",
     )
     out = Stream(reducer, out_send, out_own, 1)
-    early = [gate, up, down, out]
+    early = [gate, up, down]
+    middle_cut = width // 256 * 128 + 128
+    gate.join(out, (0, middle_cut))
+    up.join(out, (middle_cut, width))
     reducer.fold(early, "early")
 
     def attend_back(first, end, name):
@@ -892,7 +1014,7 @@
         used = fixed((count, stop))
         return call(
             functools.partial(attend_back_kernel, first=first, base=begin, base_row=begin_row),
-            (end - first,),
+            ((end - first) // TOGETHER,),
             [used] * 4 + [fixed((128, count))] * 2 + [fixed((width, count))],
             [fixed((rows, count))] + [fixed((count, columns))] * 2,
             [shape((rows, count), f32), shape((count, columns), f32), shape((count, columns), bf16)],
@@ -902,11 +1024,10 @@
             name=name,
         )
 
-    cut = HEADS // 2 + 1
+    cut = 3 * HEADS // 4
     dqt0, dk0, dv0 = attend_back(0, cut, "attend_back_0")
     reducer.fold(early, "early")
     dqt1, dk1, dv1 = attend_back(cut, HEADS, "attend_back_1")
-    reducer.fold(early, "early")
     base, _, base_row, _ = head_span(cut, HEADS, width)
     v_send, v_own = call(
         functools.partial(value_kernel, base=base),
@@ -919,14 +1040,15 @@
         name="value",
     )
     v_part = Stream(reducer, v_send, v_own, 2)
+    reducer.fold(early, "early")
     grad_q, grad_k, gains_low, q_send, q_own, k_send, k_own = call(
         functools.partial(project_back_kernel, base=base, base_row=base_row),
-        (blocks,),
-        [rows_of((dqt0.shape[0], TB), 1), rows_of((dqt1.shape[0], TB), 1)]
-        + [rows_of((TB, dk0.shape[1])), rows_of((TB, dk1.shape[1]))]
-        + [rows_of((TB, 2 * width)), rows_of((TB, 256)), token_spec, token_spec, units_spec, rows_of((2, TB), 1)]
+        (count // SEG,),
+        [rows_of((dqt0.shape[0], SEG), 1), rows_of((dqt1.shape[0], SEG), 1)]
+        + [rows_of((SEG, dk0.shape[1])), rows_of((SEG, dk1.shape[1]))]
+        + [rows_of((SEG, 2 * width)), rows_of((SEG, 256)), seg_spec, seg_spec, rows_of((8, width // 8, SEG), 2), rows_of((2, SEG), 1)]
         + table_specs + [fixed(head_fold.shape)],
-        [token_spec] * 2 + [fixed((8, 128))] + square_send * 2,
+        [seg_spec] * 2 + [fixed((8, 128))] + square_send * 2,
         [token_bf16] * 2 + [shape((8, 128), bf16)] + square_shapes * 2,
         (dqt0, dqt1, dk0, dk1, raw, inverse, query, key, attn_units, coord) + tables + (head_fold,),
         scalars=reducer.bits,
@@ -944,7 +1066,21 @@
     reducer.fold([v_part], "v")
     for _ in range(extra):
         reducer.fold(early, "early")
-    early = [Merged([gate, up, out]), down]
+    rows_d = width // n_dev
+    merged = Merged([gate, up, down])
+    third = rows_ff // 3
+    gate_end = ff + middle_cut
+    up_end = gate_end + ff + width - middle_cut
+    merged.places = [
+        (0, 0, 0, ff, None),
+        (2, 0, ff, gate_end, None),
+        (1, 0, gate_end, gate_end + ff, None),
+        (2, middle_cut, gate_end + ff, up_end, None),
+    ] + [
+        (3, 0, up_end + i * width, up_end + (i + 1) * width, (i * third, (i + 1) * third)) for i in range(3)
+    ]
+    merged.shapes = [shape((rows_d, ff), f32)] * 2 + [shape((rows_d, width), f32), shape((rows_ff, width), f32)]
+    early = [merged]
     reducer.fold(early, "early")
     reducer.fold([q_part, k_part], "late")
     grad_tokens, mod_own, mod_other = call(
@@ -960,19 +1096,15 @@
         name="input_back",
     )
     every_mod = Gather(reducer, mod_other, mod_own, activated)
+    reducer.fold([every_mod], "pair")
     reducer.fold(late, "late")
-    reducer.fold([every_mod], "pair")
-    summed_early, summed_down = reducer.fold(early, "early_last", last=True)
+    reducer.fold([every_mod], "every")
+    summed_gate, summed_up, summed_out, summed_down = reducer.fold(early, "early_last", last=True)
     for _ in range(1 + extra):
         reducer.fold(late + [every_mod], "late")
     late = [Merged(late)]
     reducer.fold(late + [every_mod], "late")
-    while every_mod.steps:
-        reducer.fold([every_mod], "every")
     summed_qkv, grad_w_ada, gain_grads = reducer.fold(late + [every_mod], "late_last", last=True)
-    summed_gate, summed_up = summed_early[:, :ff], summed_early[:, ff : 2 * ff]
-    summed_out = summed_early[:, 2 * ff :]
-
     grad_activated = jnp.einsum("nc,dc->nd", every_mod.pair[:, width : width + half], w_ada, preferred_element_type=f32)
     grad_activated = grad_activated.reshape(n_mod, slots_n, width)
     own_part = lax.dynamic_index_in_dim(grad_activated, mod_index, 0, keepdims=False)

time: 534 us -> 483 us (0.904); the launches traced: 525 us -> 480 us
  Pallas kernels: 375 us -> 345 us
  waiting for transfers between devices: 55 us -> 48.8 us
    pallas_call x23 -> x24, Pallas kernels: 375 us -> 345 us  [__call__(): pl.pallas_call(body, grid_spec=spec, input_output_aliases=aliases or {},...]
    ppermute x28 -> x25, starting transfers between devices: 40.4 us -> 28.2 us  [swap(): lax.ppermute(arr, 'dp', [(i, i ^ 1 << bit) for i in range(self.n_dp)])]
    ppermute x28 -> x25, waiting for transfers between devices: 54.6 us -> 44.5 us  [swap(): lax.ppermute(arr, 'dp', [(i, i ^ 1 << bit) for i in range(self.n_dp)])]
    ppermute x11 -> x10, starting transfers between devices: 17.9 us -> 25.3 us  [swap(): return lax.ppermute(arr, 'mod', [(i, i ^ 1) for i in range(self.n_mod)])]
    unnamed x86 -> x64, local copies, waits for them, and re-layouts: 15.2 us -> 12.6 us
  transfers between devices with their start and end apart: 39 -> 35, of which waited for: 7 -> 10; matrix products, arithmetic and copies ran while one was open for 2% -> 2% of each run, Pallas kernels for 28% -> 32%
where the time goes in v7:
time: 483 us; the launch traced here: 480 us
  Pallas kernels  345 us (71%)
  starting transfers between devices  53.5 us (11%)
  waiting for transfers between devices  48.8 us (10%)
  local copies, waits for them, and re-layouts  17.4 us (4%)
  matrix products  9.81 us (2%)
    pallas_call x24, Pallas kernels, __call__(): pl.pallas_call(body, grid_spec=spec, input_output_aliases=aliases or {},...  345 us
    ppermute x25, waiting for transfers between devices, swap(): lax.ppermute(arr, 'dp', [(i, i ^ 1 << bit) for i in range(self.n_dp)])  44.5 us
    ppermute x25, starting transfers between devices, swap(): lax.ppermute(arr, 'dp', [(i, i ^ 1 << bit) for i in range(self.n_dp)])  28.2 us
    ppermute x10, starting transfers between devices, swap(): return lax.ppermute(arr, 'mod', [(i, i ^ 1) for i in range(self.n_mod)])  25.3 us
    unnamed x64, local copies, waits for them, and re-layouts  12.6 us
  transfers between devices with their start and end apart: 35, of which 10 were waited for; matrix products, arithmetic and copies ran while one was open for 2% of the time, Pallas kernels for 32%

profile of v7, /device:TPU:0, one launch (start us, length us, event | category | flops | bytes accessed | tf_op | source)
XLA Modules:
  0.0 479.7 jit_solution(9598789251078234983)
XLA Ops:
  0.6 3.0 collective-permute-start
  6.5 4.4 convolution_convert_fusion
  11.0 2.1 collective-permute-start.1
  16.4 28.1 %project.1 = (bf16[8,144,1024]{2,1,0:T(8,128)(2,1)}, f32[1024,2304]{1,0:T(8,128)}, f32[1024,256]{1,0:T(8,128)}, bf16[1024,1152]{1,0:T(8,128)(2,1)}, bf16[1024,11...) custom-call(s32[4]{0:T(128)} %bitcast.49, bf16[1024,1152]{1,0:T(8,128)(2,1)} %bitcast.37, ...), custom_call_target="tpu_custom_call" | custom-call | flops 1 | bytes 1 | tf_op jit(solution)/shard_map/project/pallas_call | solution.py:681
  44.4 15.4 %attend.1 = (f32[1024,1152]{1,0:T(8,128)}, f32[1024,128]{1,0:T(8,128)}) custom-call(s32[4]{0:T(128)} %bitcast.50, bf16[8,144,1024]{2,1,0:T(8,128)(2,1)} %get-tuple-element.115.refs_1_.refs_2_.refs_10_, bf16[1024,1152]{1,0:T(8,128)(2,1)} %get-tuple-element.116.refs_2_.refs_8_, bf16[1024,1152]{1,0:T(8,128)(2,1)} %get-tuple-element.117.refs_3_.refs_9_, ...), custom_call_target="tpu_custom_call" | custom-call | flops 1 | bytes 1 | tf_op jit(solution)/shard_map/attend/pallas_call | solution.py:681
  59.8 20.2 %mix.1 = (f32[128,1024]{1,0:T(8,128)}, f32[1024,1152]{1,0:T(8,128)}, f32[1024,1152]{1,0:T(8,128)}, bf16[1024,1152]{1,0:T(8,128)(2,1)}, bf16[1024,1152]{1,0:T(8,1...) custom-call(s32[4]{0:T(128)} %bitcast.51, ...), custom_call_target="tpu_custom_call" | custom-call | flops 1 | bytes 1 | tf_op jit(solution)/shard_map/mix/pallas_call | solution.py:681
  80.0 95.6 %ffn.1 = (bf16[4,144,3072]{2,1,0:T(8,128)(2,1)}, bf16[4,144,3072]{2,1,0:T(8,128)(2,1)}, bf16[4,144,3072]{2,1,0:T(8,128)(2,1)}, bf16[4,144,3072]{2,1,0:T(8,128)(2...) custom-call(s32[5]{0:T(128)} %stack.48.refs_0_, ...), custom_call_target="tpu_custom_call" | custom-call | flops 1 | bytes 1 | tf_op jit(solution)/shard_map/ffn/pallas_call | solution.py:681
  176.9 25.2 %middle.1 = (bf16[1024,1152]{1,0:T(8,128)(2,1)}, f32[1024,1152]{1,0:T(8,128)}, bf16[1024,1152]{1,0:T(8,128)(2,1)}, f32[128,1024]{1,0:T(8,128)}, f32[4,4608]{1,0:...) custom-call(s32[6]{0:T(128)} %pad_add_fusion.refs_0_, ...), custom_call_target="tpu_custom_call" | custom-call | flops 1 | bytes 1 | tf_op jit(solution)/shard_map/middle/pallas_call | solution.py:681
  202.6 2.9 collective-permute-done.3.refs_5_.refs_9_
  206.6 15.2 %early.4 = (bf16[2,144,3712]{2,1,0:T(8,128)(2,1)}, bf16[2,144,3712]{2,1,0:T(8,128)(2,1)}, bf16[2,144,3584]{2,1,0:T(8,128)(2,1)}, bf16[2,144,3584]{2,1,0:T(8,128)...) custom-call(s32[5]{0:T(128)} %stack.48.refs_0_, bf16[1024,1152]{1,0:T(8,128)(2,1)} %get-tuple-element.131.refs_1_, ...), custom_call_target="tpu_custom_call" | custom-call | flops 1 | bytes 1 | tf_op jit(solution)/shard_map/early/pallas_call | solution.py:681
  221.8 13.1 %collective-permute-start.6 = (bf16[2,144,3712]{2,1,0:T(8,128)(2,1)}, bf16[2,144,3712]{2,1,0:T(8,128)(2,1)S(1)}, u32[]{:S(2)}, u32[]{:S(2)}) collective-permute-start(bf16[2,144,3712]{2,1,0:T(8,128)(2,1)} %get-tuple-element.139.refs_1_), channel_id=1, source_target_pairs={{0,1},{1,0},{2,3},{3,2},{4,5},{5,4},{6,7},{7,6},{8,9},{9,8},{10,11... | collective-permute-start | bytes 6414344 | tf_op jit(solution)/shard_map/ppermute | solution.py:724
  235.2 2.8 collective-permute-start.8
  238.0 23.7 %attend_back_0.1 = (f32[864,1024]{1,0:T(8,128)}, f32[1024,1024]{1,0:T(8,128)}, bf16[1024,1024]{1,0:T(8,128)(2,1)}) custom-call(s32[4]{0:T(128)} %bitcast.52, bf16[2,144,3712]{2,1,0:T(8,128)(2,1)} %get-tuple-element.139.refs_1_, bf16[1024,1152]{1,0:T(8,128)(2,1)} %get-tuple-element.116.refs_2_.refs_8_, bf16[1024,1152]{1,0:T(8,128)(2,1)} %get-tuple-element.117.refs_3_.refs_9_, ...), custom_call_target="tpu_custom_call" | custom-call | flops 1 | bytes 1 | tf_op jit(solution)/shard_map/attend_back_0/pallas_call | solution.py:681
  261.7 15.1 %collective-permute-done.8.refs_7_ = bf16[4,192,1152]{2,1,0:T(8,128)(2,1)S(1)} collective-permute-done((bf16[4,192,1152]{2,1,0:T(8,128)(2,1)}, bf16[4,192,1152]{2,1,0:T(8,128)(2,1)S(1)}, u32[]{:S(2)}, u32[]{:S(2)}) %collective-permute-start.8) | collective-permute-done | bytes 1769504 | tf_op jit(solution)/shard_map/ppermute | solution.py:725
  276.8 5.4 %collective-permute-done.7.refs_5_ = bf16[2,144,3584]{2,1,0:T(8,128)(2,1)} collective-permute-done((bf16[2,144,3584]{2,1,0:T(8,128)(2,1)}, bf16[2,144,3584]{2,1,0:T(8,128)(2,1)}, u32[]{:S(2)}, u32[]{:S(2)}) %collective-permute-start.7) | collective-permute-done | bytes 2064416 | tf_op jit(solution)/shard_map/ppermute | solution.py:725
  282.2 1.4 copy-done.3
  283.6 8.5 %early.5 = (bf16[144,3712]{1,0:T(8,128)(2,1)}, f32[144,3712]{1,0:T(8,128)}, bf16[2,72,3584]{2,1,0:T(8,128)(2,1)}, f32[2,72,3584]{2,1,0:T(8,128)}, bf16[2,192,115...) custom-call(s32[5]{0:T(128)} %stack.48.refs_0_, f32[864,1024]{1,0:T(8,128)} %get-tuple-element.143.refs_1_.refs_2_, ...), custom_call_target="tpu_custom_call" | custom-call | flops 1 | bytes 1 | tf_op jit(solution)/shard_map/early/pallas_call | solution.py:681
  292.1 1.9 collective-permute-start.9
  294.0 1.6 collective-permute-start.10
  296.9 12.0 %attend_back_1.1 = (f32[288,1024]{1,0:T(8,128)}, f32[1024,384]{1,0:T(8,128)}, bf16[1024,384]{1,0:T(8,128)(2,1)}) custom-call(s32[4]{0:T(128)} %bitcast.53, bf16[144,3712]{1,0:T(8,128)(2,1)} %get-tuple-element.149.refs_1_, bf16[1024,1152]{1,0:T(8,128)(2,1)} %get-tuple-element.116.refs_2_.refs_8_, bf16[1024,1152]{1,0:T(8,128)(2,1)} %get-tuple-element.117.refs_3_.refs_9_, ...), custom_call_target="tpu_custom_call" | custom-call | flops 1 | bytes 1 | tf_op jit(solution)/shard_map/attend_back_1/pallas_call | solution.py:681
  308.9 7.4 %value.1 = (bf16[4,144,1152]{2,1,0:T(8,128)(2,1)}, bf16[4,144,1152]{2,1,0:T(8,128)(2,1)}) custom-call(s32[5]{0:T(128)} %stack.48.refs_0_, f32[288,1024]{1,0:T(8,128)} %get-tuple-element.150.refs_1_.refs_3_, bf16[8,144,1024]{2,1,0:T(8,128)(2,1)} %get-tuple-element.115.refs_1_.refs_2_.refs_10_, bf16[1024,1024]{1,0:T(8,128)(2,1)} %get-tuple-element.151.refs_3_.refs_4_, ...), custom_call_target="tpu_custom_call" | custom-call | flops 1 | bytes 1 | tf_op jit(solution)/shard_map/value/pallas_call | solution.py:681
  316.6 1.7 collective-permute-done.10.refs_5_
  319.6 6.3 %early.6 = (bf16[72,3712]{1,0:T(8,128)(2,1)}, f32[72,3712]{1,0:T(8,128)}, bf16[72,3584]{1,0:T(8,128)(2,1)}, f32[72,3584]{1,0:T(8,128)}, bf16[192,1152]{1,0:T(8,128)(2,1)}, /*index=5*/f32[192,1152]{1,0:T(8,128)}) custom-call(s32[5]{0:T(128)} %stack.48.refs_0_, bf16[4,144,1152]{2,1,0:T(8,128)(2,1)} %get-tuple-element.153.refs_1_, ...), custom_call_target="tpu_custom_call" | custom-call | flops 1 | bytes 1 | tf_op jit(solution)/shard_map/early/pallas_call | solution.py:681
  325.9 4.2 collective-permute-start.12
  331.4 27.6 %project_back.1 = (bf16[1024,1152]{1,0:T(8,128)(2,1)}, bf16[1024,1152]{1,0:T(8,128)(2,1)}, bf16[8,128]{1,0:T(8,128)(2,1)}, bf16[4,144,1152]{2,1,0:T(8,128)(2,1)}...) custom-call(s32[5]{0:T(128)} %stack.48.refs_0_, ...), custom_call_target="tpu_custom_call" | custom-call | flops 1 | bytes 1 | tf_op jit(solution)/shard_map/project_back/pallas_call | solution.py:681
  361.1 4.5 v.1
  365.6 1.5 collective-permute-start.22
  367.1 5.1 %early.7 = (bf16[36,10752]{1,0:T(8,128)(2,1)}, f32[36,10752]{1,0:T(8,128)}) custom-call(s32[5]{0:T(128)} %stack.48.refs_0_, bf16[4,72,1152]{2,1,0:T(8,128)(2,1)} %get-tuple-element.172.refs_1_, f32[72,3712]{1,0:T(8,128)} %get-tuple-element.173.refs_2_, bf16[72,3712]{1,0:T(8,128)(2,1)} %get-tuple-element.169.refs_1_.refs_3_, ...), custom_call_target="tpu_custom_call" | custom-call | flops 1 | bytes 1 | tf_op jit(solution)/shard_map/early/pallas_call | solution.py:681
  373.6 5.4 %late.4 = (bf16[2,144,1152]{2,1,0:T(8,128)(2,1)}, bf16[2,144,1152]{2,1,0:T(8,128)(2,1)}, bf16[2,144,1152]{2,1,0:T(8,128)(2,1)}, bf16[2,144,1152]{2,1,0:T(8,128)(2,1)}) custom-call(s32[5]{0:T(128)} %stack.48.refs_0_, bf16[36,10752]{1,0:T(8,128)(2,1)} %get-tuple-element.178.refs_1_, bf16[4,144,1152]{2,1,0:T(8,128)(2,1)} %get-tuple-element.179.refs_2_, ...), custom_call_target="tpu_custom_call" | custom-call | flops 1 | bytes 1 | tf_op jit(solution)/shard_map/late/pallas_call | solution.py:681
  381.2 2.3 collective-permute-start.24
  383.5 21.0 %input_back.1 = (bf16[1024,1152]{1,0:T(8,128)(2,1)}, bf16[8,3584]{1,0:T(8,128)(2,1)}, bf16[8,3584]{1,0:T(8,128)(2,1)}) custom-call(s32[6]{0:T(128)} %pad_add_fusion.refs_0_, bf16[2,144,1152]{2,1,0:T(8,128)(2,1)} %get-tuple-element.183.refs_1_, bf16[1024,1152]{1,0:T(8,128)(2,1)} %get-tuple-element.164.refs_0_.refs_2_, ...), custom_call_target="tpu_custom_call" | custom-call | flops 1 | bytes 1 | tf_op jit(solution)/shard_map/input_back/pallas_call | solution.py:681
  405.4 3.5 collective-permute-done.18.refs_3_
  409.6 2.1 pair.1.refs_1_.refs_2_
  412.8 5.1 %late.5 = (bf16[2,72,1152]{2,1,0:T(8,128)(2,1)}, f32[2,72,1152]{2,1,0:T(8,128)}, bf16[144,1152]{1,0:T(8,128)(2,1)}, f32[144,1152]{1,0:T(8,128)}, bf16[2,72,1152]...) custom-call(s32[5]{0:T(128)} %stack.48.refs_0_, bf16[8,4736]{1,0:T(8,128)(2,1)} %pair.1.refs_1_.refs_2_, ...), custom_call_target="tpu_custom_call" | custom-call | flops 1 | bytes 1 | tf_op jit(solution)/shard_map/late/pallas_call | solution.py:681
  417.9 2.1 collective-permute-start.26
  421.1 6.4 %collective-permute-done.23.refs_3_ = bf16[8,4736]{1,0:T(8,128)(2,1)S(1)} collective-permute-done((bf16[8,4736]{1,0:T(8,128)(2,1)S(1)}, bf16[8,4736]{1,0:T(8,128)(2,1)S(1)}, u32[]{:S(2)}, u32[]{:S(2)}) %collective-permute-start.23) | collective-permute-done | bytes 75808 | tf_op jit(solution)/shard_map/ppermute | solution.py:725
  428.2 2.2 every.1.refs_1_.refs_8_
  430.4 2.2 collective-permute-start.28
  433.5 3.5 early_last.1
  438.1 3.7 late.6
  442.7 1.5 collective-permute-start.31
  444.6 1.4 collective-permute-start.32
  446.0 5.4 %fusion = f32[8,1152]{1,0:T(8,128)S(1)} fusion(bf16[1152,3456]{1,0:T(8,128)(2,1)} %param.23, bf16[8,4736]{1,0:T(8,128)(2,1)S(1)} %copy-done.11), kind=kOutput, calls=%fused_computation.1 | convolution fusion | flops 63700992 | bytes 8054784 | tf_op jit(solution)/shard_map/nc,dc->nd/dot_general | solution.py:1108
  452.4 3.6 late.7
  455.9 1.7 collective-permute-start.19
  457.7 2.1 collective-permute-start.33
  460.4 13.0 %collective-permute-done.33.refs_3_ = bf16[36,3456]{1,0:T(8,128)(2,1)S(1)} collective-permute-done((bf16[36,3456]{1,0:T(8,128)(2,1)}, bf16[36,3456]{1,0:T(8,128)(2,1)S(1)}, u32[]{:S(2)}, u32[]{:S(2)}) %collective-permute-start.33) | collective-permute-done | bytes 248864 | tf_op jit(solution)/shard_map/ppermute | solution.py:725
  474.3 4.0 late_last.1
  (132 shorter events, 30.2 us)
Async XLA Ops:
  0.6 5.0 %collective-permute-start = (f32[4,1152]{1,0:T(4,128)}, f32[4,1152]{1,0:T(4,128)S(1)}, u32[]{:S(2)}, u32[]{:S(2)}) collective-permute-start(f32[4,1152]{1,0:T(4,128)} %bitcast.45), channel_id=1, source_target_pairs={{0,1},{1,0},{2,3},{3,2},{4,5},{5,4},{6,7},{7,6},{8,9},{9,8},{10,11... | collective-permute-start | bytes 55304 | tf_op jit(solution)/shard_map/ppermute | solution.py:724
  6.5 4.4 copy-start.23
  11.0 4.6 collective-permute-start.1
  80.0 96.3 %copy-start.31 = (s32[1,4]{1,0:T(1,128)S(1)}, s32[1,4]{1,0:T(1,128)}, u32[]{:S(2)}) copy-start(s32[1,4]{1,0:T(1,128)} %slice.20) | copy-start | bytes 52
  175.6 29.9 %collective-permute-start.4 = (bf16[4,144,3072]{2,1,0:T(8,128)(2,1)}, bf16[4,144,3072]{2,1,0:T(8,128)(2,1)}, u32[]{:S(2)}, u32[]{:S(2)}) collective-permute-start(bf16[4,144,3072]{2,1,0:T(8,128)(2,1)} %get-tuple-element.136), channel_id=1, source_target_pairs={{0,2},{2,0},{4,6},{6,4},{8,10},{10,8},{12,14},{14,12},{16,18},{18,... | collective-permute-start | bytes 10616840 | tf_op jit(solution)/shard_map/ppermute | solution.py:725
  175.7 29.8 %collective-permute-start.5 = (bf16[4,384,1152]{2,1,0:T(8,128)(2,1)}, bf16[4,384,1152]{2,1,0:T(8,128)(2,1)}, u32[]{:S(2)}, u32[]{:S(2)}) collective-permute-start(bf16[4,384,1152]{2,1,0:T(8,128)(2,1)} %bitcast.56), channel_id=1, source_target_pairs={{0,2},{2,0},{4,6},{6,4},{8,10},{10,8},{12,14},{14,12},{16,18},{18,... | collective-permute-start | bytes 10616840 | tf_op jit(solution)/shard_map/ppermute | solution.py:725
  176.2 29.3 %collective-permute-start.2 = (bf16[4,144,3072]{2,1,0:T(8,128)(2,1)}, bf16[4,144,3072]{2,1,0:T(8,128)(2,1)}, u32[]{:S(2)}, u32[]{:S(2)}) collective-permute-start(bf16[4,144,3072]{2,1,0:T(8,128)(2,1)} %get-tuple-element.125.refs_1_), channel_id=1, source_target_pairs={{0,2},{2,0},{4,6},{6,4},{8,10},{10,8},{12,14},{14,12},{16,18},{18,... | collective-permute-start | bytes 10616840 | tf_op jit(solution)/shard_map/ppermute | solution.py:725
  202.1 3.4 collective-permute-start.3
  221.8 60.4 %collective-permute-start.6 = (bf16[2,144,3712]{2,1,0:T(8,128)(2,1)}, bf16[2,144,3712]{2,1,0:T(8,128)(2,1)S(1)}, u32[]{:S(2)}, u32[]{:S(2)}) collective-permute-start(bf16[2,144,3712]{2,1,0:T(8,128)(2,1)} %get-tuple-element.139.refs_1_), channel_id=1, source_target_pairs={{0,1},{1,0},{2,3},{3,2},{4,5},{5,4},{6,7},{7,6},{8,9},{9,8},{10,11... | collective-permute-start | bytes 6414344 | tf_op jit(solution)/shard_map/ppermute | solution.py:724
  234.9 47.2 %collective-permute-start.7 = (bf16[2,144,3584]{2,1,0:T(8,128)(2,1)}, bf16[2,144,3584]{2,1,0:T(8,128)(2,1)}, u32[]{:S(2)}, u32[]{:S(2)}) collective-permute-start(bf16[2,144,3584]{2,1,0:T(8,128)(2,1)} %get-tuple-element.146), channel_id=1, source_target_pairs={{0,4},{2,6},{4,0},{6,2},{8,12},{10,14},{12,8},{14,10},{16,20},{18,... | collective-permute-start | bytes 6193160 | tf_op jit(solution)/shard_map/ppermute | solution.py:725
  235.2 41.6 %collective-permute-start.8 = (bf16[4,192,1152]{2,1,0:T(8,128)(2,1)}, bf16[4,192,1152]{2,1,0:T(8,128)(2,1)S(1)}, u32[]{:S(2)}, u32[]{:S(2)}) collective-permute-start(bf16[4,192,1152]{2,1,0:T(8,128)(2,1)} %get-tuple-element.148), channel_id=1, source_target_pairs={{0,8},{2,10},{4,12},{6,14},{8,0},{10,2},{12,4},{14,6},{16,24},{18,... | collective-permute-start | bytes 5308424 | tf_op jit(solution)/shard_map/ppermute | solution.py:725
  276.8 5.4 %copy-start.6 = (bf16[4,192,1152]{2,1,0:T(8,128)(2,1)}, bf16[4,192,1152]{2,1,0:T(8,128)(2,1)S(1)}, u32[]{:S(2)}) copy-start(bf16[4,192,1152]{2,1,0:T(8,128)(2,1)S(1)} %collective-permute-done.8.refs_7_) | copy-start | bytes 5308420
  282.2 1.4 copy-start.3
  292.1 26.1 %collective-permute-start.9 = (bf16[144,3712]{1,0:T(8,128)(2,1)}, bf16[144,3712]{1,0:T(8,128)(2,1)S(1)}, u32[]{:S(2)}, u32[]{:S(2)}) collective-permute-start(bf16[144,3712]{1,0:T(8,128)(2,1)} %get-tuple-element.149.refs_1_), channel_id=1, source_target_pairs={{0,4},{2,6},{4,0},{6,2},{8,12},{10,14},{12,8},{14,10},{16,20},{18,... | collective-permute-start | bytes 3207176 | tf_op jit(solution)/shard_map/ppermute | solution.py:725
  294.0 24.2 %collective-permute-start.10 = (bf16[2,72,3584]{2,1,0:T(8,128)(2,1)}, bf16[2,72,3584]{2,1,0:T(8,128)(2,1)S(1)}, u32[]{:S(2)}, u32[]{:S(2)}) collective-permute-start(bf16[2,72,3584]{2,1,0:T(8,128)(2,1)} %get-tuple-element.156), channel_id=1, source_target_pairs={{0,8},{2,10},{4,12},{6,14},{8,0},{10,2},{12,4},{14,6},{16,24},{18,... | collective-permute-start | bytes 3096584 | tf_op jit(solution)/shard_map/ppermute | solution.py:725
  295.6 21.0 %collective-permute-start.11 = (bf16[2,192,1152]{2,1,0:T(8,128)(2,1)}, bf16[2,192,1152]{2,1,0:T(8,128)(2,1)}, u32[]{:S(2)}, u32[]{:S(2)}) collective-permute-start(bf16[2,192,1152]{2,1,0:T(8,128)(2,1)} %get-tuple-element.158), channel_id=1, source_target_pairs={{0,1},{1,0},{2,3},{3,2},{4,5},{5,4},{6,7},{7,6},{8,9},{9,8},{10,11... | collective-permute-start | bytes 2654216 | tf_op jit(solution)/shard_map/ppermute | solution.py:724
  316.3 42.8 %collective-permute-start.15 = (bf16[4,144,1152]{2,1,0:T(8,128)(2,1)}, bf16[4,144,1152]{2,1,0:T(8,128)(2,1)S(1)}, u32[]{:S(2)}, u32[]{:S(2)}) collective-permute-start(bf16[4,144,1152]{2,1,0:T(8,128)(2,1)} %get-tuple-element.153.refs_1_), channel_id=1, source_target_pairs={{0,2},{2,0},{4,6},{6,4},{8,10},{10,8},{12,14},{14,12},{16,18},{18,... | collective-permute-start | bytes 3981320 | tf_op jit(solution)/shard_map/ppermute | solution.py:725
  318.2 1.4 copy-start.9
  325.9 33.2 %collective-permute-start.12 = (bf16[72,3712]{1,0:T(8,128)(2,1)}, bf16[72,3712]{1,0:T(8,128)(2,1)S(1)}, u32[]{:S(2)}, u32[]{:S(2)}) collective-permute-start(bf16[72,3712]{1,0:T(8,128)(2,1)} %get-tuple-element.159.refs_1_), channel_id=1, source_target_pairs={{0,8},{2,10},{4,12},{6,14},{8,0},{10,2},{12,4},{14,6},{16,24},{18,... | collective-permute-start | bytes 1603592 | tf_op jit(solution)/shard_map/ppermute | solution.py:725
  330.1 29.0 %collective-permute-start.13 = (bf16[72,3584]{1,0:T(8,128)(2,1)}, bf16[72,3584]{1,0:T(8,128)(2,1)S(1)}, u32[]{:S(2)}, u32[]{:S(2)}) collective-permute-start(bf16[72,3584]{1,0:T(8,128)(2,1)} %get-tuple-element.165), channel_id=1, source_target_pairs={{0,1},{1,0},{2,3},{3,2},{4,5},{5,4},{6,7},{7,6},{8,9},{9,8},{10,11... | collective-permute-start | bytes 1548296 | tf_op jit(solution)/shard_map/ppermute | solution.py:724
  330.9 28.2 %collective-permute-start.14 = (bf16[192,1152]{1,0:T(8,128)(2,1)}, bf16[192,1152]{1,0:T(8,128)(2,1)S(1)}, u32[]{:S(2)}, u32[]{:S(2)}) collective-permute-start(bf16[192,1152]{1,0:T(8,128)(2,1)} %get-tuple-element.166), channel_id=1, source_target_pairs={{0,4},{2,6},{4,0},{6,2},{8,12},{10,14},{12,8},{14,10},{16,20},{18,... | collective-permute-start | bytes 1327112 | tf_op jit(solution)/shard_map/ppermute | solution.py:725
  359.1 1.2 copy-start.5
  359.1 1.4 copy-start.4
  359.1 1.5 copy-start.2
  360.6 11.5 %collective-permute-start.16 = (bf16[4,144,1152]{2,1,0:T(8,128)(2,1)}, bf16[4,144,1152]{2,1,0:T(8,128)(2,1)S(1)}, u32[]{:S(2)}, u32[]{:S(2)}) collective-permute-start(bf16[4,144,1152]{2,1,0:T(8,128)(2,1)} %get-tuple-element.180), channel_id=1, source_target_pairs={{0,2},{2,0},{4,6},{6,4},{8,10},{10,8},{12,14},{14,12},{16,18},{18,... | collective-permute-start | bytes 3981320 | tf_op jit(solution)/shard_map/ppermute | solution.py:725
  360.6 11.5 %collective-permute-start.17 = (bf16[4,144,1152]{2,1,0:T(8,128)(2,1)}, bf16[4,144,1152]{2,1,0:T(8,128)(2,1)S(1)}, u32[]{:S(2)}, u32[]{:S(2)}) collective-permute-start(bf16[4,144,1152]{2,1,0:T(8,128)(2,1)} %get-tuple-element.182), channel_id=1, source_target_pairs={{0,2},{2,0},{4,6},{6,4},{8,10},{10,8},{12,14},{14,12},{16,18},{18,... | collective-permute-start | bytes 3981320 | tf_op jit(solution)/shard_map/ppermute | solution.py:725
  365.6 46.1 %collective-permute-start.22 = (bf16[4,72,1152]{2,1,0:T(8,128)(2,1)}, bf16[4,72,1152]{2,1,0:T(8,128)(2,1)}, u32[]{:S(2)}, u32[]{:S(2)}) collective-permute-start(bf16[4,72,1152]{2,1,0:T(8,128)(2,1)} %get-tuple-element.172.refs_1_), channel_id=1, source_target_pairs={{0,8},{2,10},{4,12},{6,14},{8,0},{10,2},{12,4},{14,6},{16,24},{18,... | collective-permute-start | bytes 1990664 | tf_op jit(solution)/shard_map/ppermute | solution.py:725
  372.1 1.5 copy-start.8
  373.6 7.6 %copy-start.13 = (bf16[36,10752]{1,0:T(8,128)(2,1)S(1)}, bf16[36,10752]{1,0:T(8,128)(2,1)}, u32[]{:S(2)}) copy-start(bf16[36,10752]{1,0:T(8,128)(2,1)} %get-tuple-element.178.refs_1_) | copy-start | bytes 2322436
  379.1 32.6 %collective-permute-start.21 = (bf16[2,144,1152]{2,1,0:T(8,128)(2,1)}, bf16[2,144,1152]{2,1,0:T(8,128)(2,1)S(1)}, u32[]{:S(2)}, u32[]{:S(2)}) collective-permute-start(bf16[2,144,1152]{2,1,0:T(8,128)(2,1)} %get-tuple-element.193), channel_id=1, source_target_pairs={{0,1},{1,0},{2,3},{3,2},{4,5},{5,4},{6,7},{7,6},{8,9},{9,8},{10,11... | collective-permute-start | bytes 1990664 | tf_op jit(solution)/shard_map/ppermute | solution.py:724
  380.4 31.4 %collective-permute-start.20 = (bf16[2,144,1152]{2,1,0:T(8,128)(2,1)}, bf16[2,144,1152]{2,1,0:T(8,128)(2,1)S(1)}, u32[]{:S(2)}, u32[]{:S(2)}) collective-permute-start(bf16[2,144,1152]{2,1,0:T(8,128)(2,1)} %get-tuple-element.183.refs_1_), channel_id=1, source_target_pairs={{0,4},{2,6},{4,0},{6,2},{8,12},{10,14},{12,8},{14,10},{16,20},{18,... | collective-permute-start | bytes 1990664 | tf_op jit(solution)/shard_map/ppermute | solution.py:725
  381.2 51.4 %collective-permute-start.24 = (bf16[36,10752]{1,0:T(8,128)(2,1)S(1)}, bf16[36,10752]{1,0:T(8,128)(2,1)S(1)}, u32[]{:S(2)}, u32[]{:S(2)}) collective-permute-start(bf16[36,10752]{1,0:T(8,128)(2,1)S(1)} %copy-done.13), channel_id=1, source_target_pairs={{0,16},{2,18},{4,20},{6,22},{8,24},{10,26},{12,28},{14,30},{16,0},... | collective-permute-start | bytes 2322440 | tf_op jit(solution)/shard_map/ppermute | solution.py:725
  404.5 4.5 collective-permute-start.18
  411.7 9.0 %copy-start.10 = (bf16[8,4736]{1,0:T(8,128)(2,1)S(1)}, bf16[8,4736]{1,0:T(8,128)(2,1)}, u32[]{:S(2)}) copy-start(bf16[8,4736]{1,0:T(8,128)(2,1)} %pair.1.refs_1_.refs_2_) | copy-start | bytes 227332
  417.9 19.1 %collective-permute-start.26 = (bf16[144,1152]{1,0:T(8,128)(2,1)}, bf16[144,1152]{1,0:T(8,128)(2,1)S(1)}, u32[]{:S(2)}, u32[]{:S(2)}) collective-permute-start(bf16[144,1152]{1,0:T(8,128)(2,1)} %get-tuple-element.200), channel_id=1, source_target_pairs={{0,4},{2,6},{4,0},{6,2},{8,12},{10,14},{12,8},{14,10},{16,20},{18,... | collective-permute-start | bytes 995336 | tf_op jit(solution)/shard_map/ppermute | solution.py:725
  420.0 17.1 %collective-permute-start.27 = (bf16[2,72,1152]{2,1,0:T(8,128)(2,1)}, bf16[2,72,1152]{2,1,0:T(8,128)(2,1)S(1)}, u32[]{:S(2)}, u32[]{:S(2)}) collective-permute-start(bf16[2,72,1152]{2,1,0:T(8,128)(2,1)} %get-tuple-element.202), channel_id=1, source_target_pairs={{0,1},{1,0},{2,3},{3,2},{4,5},{5,4},{6,7},{7,6},{8,9},{9,8},{10,11... | collective-permute-start | bytes 995336 | tf_op jit(solution)/shard_map/ppermute | solution.py:724
  420.8 16.4 %collective-permute-start.25 = (bf16[2,72,1152]{2,1,0:T(8,128)(2,1)}, bf16[2,72,1152]{2,1,0:T(8,128)(2,1)S(1)}, u32[]{:S(2)}, u32[]{:S(2)}) collective-permute-start(bf16[2,72,1152]{2,1,0:T(8,128)(2,1)} %get-tuple-element.195.refs_1_), channel_id=1, source_target_pairs={{0,8},{2,10},{4,12},{6,14},{8,0},{10,2},{12,4},{14,6},{16,24},{18,... | collective-permute-start | bytes 995336 | tf_op jit(solution)/shard_map/ppermute | solution.py:725
  420.8 6.8 %collective-permute-start.23 = (bf16[8,4736]{1,0:T(8,128)(2,1)S(1)}, bf16[8,4736]{1,0:T(8,128)(2,1)S(1)}, u32[]{:S(2)}, u32[]{:S(2)}) collective-permute-start(bf16[8,4736]{1,0:T(8,128)(2,1)S(1)} %copy-done.10), channel_id=1, source_target_pairs={{0,16},{2,18},{4,20},{6,22},{8,24},{10,26},{12,28},{14,30},{16,0},... | collective-permute-start | bytes 227336 | tf_op jit(solution)/shard_map/ppermute | solution.py:725
  430.4 6.6 %collective-permute-start.28 = (bf16[16,4736]{1,0:T(8,128)(2,1)}, bf16[16,4736]{1,0:T(8,128)(2,1)S(1)}, u32[]{:S(2)}, u32[]{:S(2)}) collective-permute-start(bf16[16,4736]{1,0:T(8,128)(2,1)} %every.1.refs_1_.refs_8_), channel_id=1, source_target_pairs={{0,8},{2,10},{4,12},{6,14},{8,0},{10,2},{12,4},{14,6},{16,24},{18,... | collective-permute-start | bytes 454664 | tf_op jit(solution)/shard_map/ppermute | solution.py:725
  437.1 9.0 %copy-start.11 = (bf16[8,4736]{1,0:T(8,128)(2,1)S(1)}, bf16[8,4736]{1,0:T(8,128)(2,1)}, u32[]{:S(2)}) copy-start(bf16[8,4736]{1,0:T(8,128)(2,1)} %pair.1.refs_1_.refs_2_) | copy-start | bytes 227332
  441.7 9.7 %collective-permute-start.30 = (bf16[72,1152]{1,0:T(8,128)(2,1)}, bf16[72,1152]{1,0:T(8,128)(2,1)S(1)}, u32[]{:S(2)}, u32[]{:S(2)}) collective-permute-start(bf16[72,1152]{1,0:T(8,128)(2,1)} %get-tuple-element.206), channel_id=1, source_target_pairs={{0,8},{2,10},{4,12},{6,14},{8,0},{10,2},{12,4},{14,6},{16,24},{18,... | collective-permute-start | bytes 497672 | tf_op jit(solution)/shard_map/ppermute | solution.py:725
  442.7 8.8 %collective-permute-start.31 = (bf16[72,1152]{1,0:T(8,128)(2,1)}, bf16[72,1152]{1,0:T(8,128)(2,1)S(1)}, u32[]{:S(2)}, u32[]{:S(2)}) collective-permute-start(bf16[72,1152]{1,0:T(8,128)(2,1)} %get-tuple-element.208), channel_id=1, source_target_pairs={{0,4},{2,6},{4,0},{6,2},{8,12},{10,14},{12,8},{14,10},{16,20},{18,... | collective-permute-start | bytes 497672 | tf_op jit(solution)/shard_map/ppermute | solution.py:725
  444.3 7.3 %collective-permute-start.29 = (bf16[72,1152]{1,0:T(8,128)(2,1)}, bf16[72,1152]{1,0:T(8,128)(2,1)S(1)}, u32[]{:S(2)}, u32[]{:S(2)}) collective-permute-start(bf16[72,1152]{1,0:T(8,128)(2,1)} %get-tuple-element.203.refs_1_), channel_id=1, source_target_pairs={{0,1},{1,0},{2,3},{3,2},{4,5},{5,4},{6,7},{7,6},{8,9},{9,8},{10,11... | collective-permute-start | bytes 497672 | tf_op jit(solution)/shard_map/ppermute | solution.py:724
  444.6 7.0 %collective-permute-start.32 = (bf16[32,4736]{1,0:T(8,128)(2,1)}, bf16[32,4736]{1,0:T(8,128)(2,1)S(1)}, u32[]{:S(2)}, u32[]{:S(2)}) collective-permute-start(bf16[32,4736]{1,0:T(8,128)(2,1)} %get-tuple-element.209.refs_8_), channel_id=1, source_target_pairs={{0,4},{2,6},{4,0},{6,2},{8,12},{10,14},{12,8},{14,10},{16,20},{18,... | collective-permute-start | bytes 909320 | tf_op jit(solution)/shard_map/ppermute | solution.py:725
  451.4 8.3 %copy-start.29 = (f32[1,4,1152]{2,1,0:T(4,128)S(1)}, f32[1,4,1152]{2,1,0:T(4,128)}, u32[]{:S(2)}) copy-start(f32[1,4,1152]{2,1,0:T(4,128)} %param.20) | copy-start | bytes 55300
  455.9 17.5 %collective-permute-start.34 = (bf16[64,4736]{1,0:T(8,128)(2,1)}, bf16[64,4736]{1,0:T(8,128)(2,1)S(1)}, u32[]{:S(2)}, u32[]{:S(2)}) collective-permute-start(bf16[64,4736]{1,0:T(8,128)(2,1)} %get-tuple-element.212.refs_4_), channel_id=1, source_target_pairs={{0,2},{2,0},{4,6},{6,4},{8,10},{10,8},{12,14},{14,12},{16,18},{18,... | collective-permute-start | bytes 1818632 | tf_op jit(solution)/shard_map/ppermute | solution.py:725
  455.9 3.8 collective-permute-start.19
  457.7 15.7 %collective-permute-start.33 = (bf16[36,3456]{1,0:T(8,128)(2,1)}, bf16[36,3456]{1,0:T(8,128)(2,1)S(1)}, u32[]{:S(2)}, u32[]{:S(2)}) collective-permute-start(bf16[36,3456]{1,0:T(8,128)(2,1)} %get-tuple-element.210.refs_1_), channel_id=1, source_target_pairs={{0,16},{2,18},{4,20},{6,22},{8,24},{10,26},{12,28},{14,30},{16,0},... | collective-permute-start | bytes 746504 | tf_op jit(solution)/shard_map/ppermute | solution.py:725
  (19 other events, 15.9 us)

commit v8 on v7

--- a/solution.py
+++ b/solution.py
@@ -254,15 +254,16 @@
 
 def mix_kernel(
     slots, x_ref, cot_ref, mod_ref, o_ref, lse_ref, w_out_ref, perm_ref,
-    lse_out_ref, attn_ref, mid_ref, low_ref, gf_ref, att_units_ref, ffn_units_ref,
+    attended_ref, lse_out_ref, attn_ref, mid_ref, low_ref, gf_ref, att_units_ref, ffn_units_ref,
 ):
     width = x_ref.shape[1]
     here = slots_here(slots, x_ref.shape[0])
     lse_out_ref[...] = lse_ref[...].T
     attended = o_ref[...].astype(bf16)
+    attended_ref[...] = attended
     att_units_ref[...] = nt(perm_ref[...], attended).astype(bf16).reshape(att_units_ref.shape)
     attn = nn(attended, w_out_ref[...])
-    attn_ref[...] = attn
+    attn_ref[...] = attn.astype(bf16)
     mid = by_slot(
         lambda slot, x, rows: x.astype(f32) + part(mod_ref, slot, 2, width) * rows, here, x_ref[...], attn
     )
@@ -377,19 +378,19 @@
 
     do = nt(ga, w_out_ref[...]).astype(bf16)
     do_ref[...] = do
-    dot_ref[...] = head_sum(do.astype(f32) * o_ref[...], gather_ref).T
+    dot_ref[...] = head_sum(do.astype(f32) * o_ref[...].astype(f32), gather_ref).T
 
     @pl.when(block == 0)
     def _():
         sums_ref[...] = jnp.zeros_like(sums_ref)
 
-    for index, term in enumerate((grad_mid * attn_ref[...], dmod, dmod * norm, incoming * ffn_ref[...])):
+    for index, term in enumerate((grad_mid * attn_ref[...].astype(f32), dmod, dmod * norm, incoming * ffn_ref[...])):
         add_by_slot(sums_ref, here, index, term)
 
 
 def attend_back_kernel(
     slots, q_ref, k_ref, v_ref, do_ref, lse_ref, dot_ref, kt_ref, dqt_ref, dk_ref, dv_low_ref, dv_ref,
-    *, first, base, base_row,
+    *, first, base, base_row, width,
 ):
     tokens = q_ref.shape[0]
 
@@ -400,12 +401,11 @@
         dv_ref[...] = jnp.zeros_like(dv_ref)
 
     def head(h, rows):
-        start, offset = window(h, kt_ref.shape[0])
+        start, offset = window(h, width)
         inside = head_lanes(offset)
-        columns = pl.ds(start, WIN)
-        out_columns = pl.ds(pl.multiple_of(start - base, 128), WIN)
+        columns = pl.ds(pl.multiple_of(start - base, 128), WIN)
         first_row = pl.multiple_of((h * HD) // 16 * 16, 16)
-        out_rows = pl.ds(pl.multiple_of(first_row - base_row, 16), HD + 8)
+        own_place = pl.ds(pl.multiple_of(first_row - base_row, 16), HD + 8)
         row = lax.broadcasted_iota(jnp.int32, (HD + 8, 1), 0) + first_row
         own_rows = (row >= h * HD) & (row < h * HD + HD)
         query = q_ref[rows, columns]
@@ -414,10 +414,10 @@
         value = jnp.where(inside, v_ref[rows, columns], 0)
         probs = jnp.exp2(nt(key, query) * SCORE_LOG2 - lse_ref[pl.ds(h, 1), rows])
         scores = (probs * (nt(value, grad_out) - dot_ref[pl.ds(h, 1), rows])).astype(bf16)
-        dv_ref[rows, out_columns] += jnp.where(inside, nn(probs.astype(bf16), grad_out), 0.0)
-        dk_ref[rows, out_columns] += jnp.where(inside, nn(scores, query) * SCORE_SCALE, 0.0)
-        turned = nn(kt_ref[pl.ds(first_row, HD + 8), rows], scores) * SCORE_SCALE
-        dqt_ref[out_rows, rows] += jnp.where(own_rows, turned, 0.0)
+        dv_ref[rows, columns] += jnp.where(inside, nn(probs.astype(bf16), grad_out), 0.0)
+        dk_ref[rows, columns] += jnp.where(inside, nn(scores, query) * SCORE_SCALE, 0.0)
+        turned = nn(kt_ref[own_place, rows], scores) * SCORE_SCALE
+        dqt_ref[own_place, rows] += jnp.where(own_rows, turned, 0.0)
 
     whole = slots[tokens // SEG - 1] == slots[0]
     begin = first + pl.program_id(0) * TOGETHER
@@ -493,23 +493,20 @@
         terms = split3(gains_ref[...])
         sums = sum(nn(term.astype(bf16), fold_ref[...]) for term in terms)
         high = sums.astype(bf16).astype(f32)
-        row = lax.broadcasted_iota(jnp.int32, (8, 1), 0)
-        mine = 4 * bits[1]
-        placed = jnp.zeros((8, 128), f32)
+        row = lax.broadcasted_iota(jnp.int32, (4, 1), 0)
+        placed = jnp.zeros((4, 128), f32)
         for index, term in enumerate((high[0:1], (sums - high)[0:1], high[1:2], (sums - high)[1:2])):
-            placed = jnp.where(row == mine + index, term, placed)
+            placed = jnp.where(row == index, term, placed)
         gains_low_ref[...] = placed.astype(bf16)
 
 
 def input_back_kernel(
     slots, gq_ref, gk_ref, dv0_ref, dv1_ref, x_ref, grad_mid_ref, mod_ref, w_ref, other_sums_ref, gains_ref,
-    grad_x_ref, grad_own_ref, grad_other_ref, sums_ref, *, base,
+    activated_ref, grad_x_ref, rows_ref, sums_ref, *, base,
 ):
     width = x_ref.shape[1]
     block = pl.program_id(0)
     here = slots_here(slots, x_ref.shape[0])
-    last_block = pl.num_programs(0) - 1
-    segments = pl.num_programs(0) * len(here)
     dmod = nt(gq_ref[...], w_ref[:, :width]) + nt(gk_ref[...], w_ref[:, width : 2 * width])
     dmod = dmod + nt(join_spans(dv0_ref[...], dv1_ref[...], base, 1), w_ref[:, 2 * width :])
     norm, inverse = normed(x_ref[...].astype(f32))
@@ -524,20 +521,12 @@
     for index, term in enumerate((dmod, dmod * norm)):
         add_by_slot(sums_ref, here, index, term)
 
-    @pl.when(block == last_block)
-    def _():
-        mod = slots[segments + 1]
-        count = sums_ref.shape[0]
-        half = 3 * width
-        mine = jnp.concatenate([sums_ref[...]] * 2, axis=0)
-        rest = jnp.concatenate([other_sums_ref[...]] * 2, axis=0)
-        row = lax.broadcasted_iota(jnp.int32, (2 * count, 1), 0) // count
-        attn_part = jnp.where(row == mod, jnp.concatenate([mine, rest[:, :width]], axis=1), 0.0)
-        ffn_part = jnp.where(row == mod, rest[:, width:], 0.0)
-        grad_own_ref[:, :half] = jnp.where(mod == 0, attn_part, ffn_part).astype(bf16)
-        grad_other_ref[:, :half] = jnp.where(mod == 0, ffn_part, attn_part).astype(bf16)
-        grad_own_ref[:, half:] = gains_ref[...]
-        grad_other_ref[:, half:] = gains_ref[...]
+    @pl.when(block == pl.num_programs(0) - 1)
+    def _():
+        rows_ref[:, : 2 * width] = sums_ref[...].astype(bf16)
+        rows_ref[:, 2 * width : 6 * width] = other_sums_ref[...].astype(bf16)
+        rows_ref[:, 6 * width : 7 * width] = activated_ref[...]
+        rows_ref[:, 7 * width :] = gains_ref[...]
 
 
 def value_kernel(bits, units_ref, dv0_ref, dv1_ref, send_ref, own_ref, *, base):
@@ -611,44 +600,28 @@
             outs[out][rows[0] : rows[1], :] = value[:count]
 
 
-def pair_step(bits, ins, outs):
-    own_ref, got_ref, activated_ref = ins
-    width = activated_ref.shape[1]
-    outs[0][:, :width] = activated_ref[...]
-    outs[0][:, width:] = (own_ref[...].astype(f32) + got_ref[...].astype(f32)).astype(bf16)
-
-
-def joined(ins):
-    return jnp.concatenate([ref[...].astype(f32) for ref in ins], axis=0).astype(bf16)
-
-
-def join_step(bits, ins, outs):
-    outs[0][...] = joined(ins)
-
-
 def last_step(bits, ins, outs):
     outs[0][...] = ins[0][...] + ins[1][...].astype(f32)
 
 
-def ada_step(bits, ins, outs, *, width):
-    rows = outs[0].shape[0]
-    every = joined(ins)
+def ada_kernel(bits, rows_ref, grad_ref, gains_ref, *, width):
+    rows, half = grad_ref.shape
     position = bits[0] + sum(bits[1 + k] * 2**k for k in range(1, (width // rows).bit_length() - 1))
     feature = lax.broadcasted_iota(jnp.int32, (width, 128), 0)
     place = lax.broadcasted_iota(jnp.int32, (width, 128), 1)
     chosen = (feature == position * rows + place) & (place < rows)
-    own = nn(every[:, :width], chosen.astype(f32).astype(bf16)).astype(bf16)
-    half = outs[0].shape[1]
-    outs[0][...] = tn(own, every[:, width : width + half])[:rows]
-    terms = every[:, width + half :].astype(f32)
+    own = nn(rows_ref[:, 6 * width : 7 * width], chosen.astype(f32).astype(bf16)).astype(bf16)
+    channels = pl.ds(pl.multiple_of(bits[1] * half, 128), half)
+    grad_ref[...] = tn(own, rows_ref[:, channels])[:rows]
+    terms = rows_ref[:, 7 * width :].astype(f32)
     kind = lax.broadcasted_iota(jnp.int32, (terms.shape[0], 1), 0) // 2 % 2
     for index in range(2):
-        outs[1][index : index + 1, :] = jnp.sum(jnp.where(kind == index, terms, 0.0), axis=0, keepdims=True)
-
-
-def step_kernel(bits, *refs, plans):
+        gains_ref[index : index + 1, :] = jnp.sum(jnp.where(kind == index, terms, 0.0), axis=0, keepdims=True)
+
+
+def step_kernel(bits, *refs, plans, passed):
     n_in = sum(plan[1] for plan in plans)
-    ins, outs = refs[:n_in], refs[n_in:]
+    ins, outs = refs[:n_in], refs[n_in + passed :]
     for function, takes, gives in plans:
         function(bits, ins[:takes], outs[:gives])
         ins, outs = ins[takes:], outs[gives:]
@@ -727,7 +700,7 @@
     def bit_of(self, bit):
         return 1 if bit == "mod" else bit + 1 if bit else 0
 
-    def fold(self, streams, name, last=False):
+    def fold(self, streams, name, last=False, passed=()):
         plans, args, outs = [], [], []
         for stream in streams:
             function, shapes = stream.last_plan() if last else stream.plan()
@@ -742,18 +715,20 @@
         )
         steps = 3 if split and size > 2**20 else 1
         results = self.call(
-            functools.partial(step_kernel, plans=plans),
+            functools.partial(step_kernel, plans=plans, passed=len(passed)),
             (steps,),
-            [column_parts(arg.shape, steps) for arg in args],
-            [column_parts(out.shape, steps) for out in outs],
-            outs,
-            args,
+            [column_parts(arg.shape, steps) for arg in args] + [pl.BlockSpec(memory_space=pl.ANY)] * len(passed),
+            [column_parts(out.shape, steps) for out in outs] + [pl.BlockSpec(memory_space=pl.ANY)] * len(passed),
+            outs + [shape(arr.shape, arr.dtype) for arr in passed],
+            args + list(passed),
             scalars=self.bits,
             name=name,
+            aliases={2 + len(args) + i: len(outs) + i for i in range(len(passed))},
         )
         results = list(results)
         if last:
             return results
+        self.passed = results[len(outs) :]
         for stream, plan in zip(streams, plans):
             stream.step(results[: plan[2]])
             results = results[plan[2] :]
@@ -839,35 +814,6 @@
         if self.places is None:
             return last_step, [shape(self.own.shape, f32)]
         return functools.partial(apart_step, places=self.places), self.shapes
-
-
-class Gather:
-    def __init__(self, reducer, sent, own, activated):
-        self.r, self.own, self.activated = reducer, own, activated
-        self.steps = list(range(reducer.n_dp.bit_length() - 2, -1, -1))
-        self.got = reducer.swap(sent, "mod")
-        self.pair = None
-
-    def inputs(self):
-        return [self.own, self.got] + ([self.activated] if self.pair is None else [])
-
-    def plan(self):
-        rows, columns = self.own.shape
-        if self.pair is None:
-            return pair_step, [shape((rows, columns + self.activated.shape[1]), bf16)]
-        return join_step, [shape((2 * rows, columns), bf16)]
-
-    def step(self, results):
-        (self.own,) = results
-        if self.pair is None:
-            self.pair = self.own
-        self.got = self.r.swap(self.own, self.steps.pop(0))
-
-    def last_plan(self):
-        width = self.activated.shape[1]
-        function = functools.partial(ada_step, width=width)
-        dims = (width // self.r.n_dp, self.own.shape[1] - width - 128)
-        return function, [shape(dims, f32), shape((2, 128), f32)]
 
 
 def silu_grad(v):
@@ -903,6 +849,7 @@
 
     cond_both = pair_order(cond[0], reducer.swap(cond[0], "mod"), mod_index)
     activated = jax.nn.silu(cond_both).astype(bf16).reshape(-1, width)
+    own_activated = jax.nn.silu(cond[0]).astype(bf16)
     mod_half = jnp.dot(activated, w_ada, preferred_element_type=f32).astype(bf16)
     mod_half = mod_half.reshape(n_mod, slots_n, half)
     own_half = lax.dynamic_index_in_dim(mod_half, mod_index, 0, keepdims=False)
@@ -910,6 +857,7 @@
     pair = pair_order(own_half, reducer.swap(other_half, "mod"), mod_index)
     modulation = jnp.concatenate([pair[0], pair[1]], axis=1).astype(f32)
 
+    anywhere = pl.BlockSpec(memory_space=pl.ANY)
     token_f32 = shape((count, width), f32)
     token_bf16 = shape((count, width), bf16)
     units = shape((8, width // 8, count), bf16)
@@ -943,18 +891,17 @@
         scalars=slots,
         name="attend",
     )
-    lse, attn, mid, ffn_in, grad_ffn, out_units, ffn_units = call(
+    attended, lse, attn, mid, ffn_in, grad_ffn, out_units, ffn_units = call(
         mix_kernel,
         (blocks,),
         [token_spec, token_spec, mod_spec, token_spec, rows_of((TB, 128)), square, square],
-        [rows_of((128, TB), 1)] + [token_spec] * 4 + [units_spec] * 2,
-        [lane_rows, token_f32, token_f32, token_bf16, token_bf16, units, units],
+        [token_spec, rows_of((128, TB), 1)] + [token_spec] * 4 + [units_spec] * 2,
+        [token_bf16, lane_rows, token_bf16, token_f32, token_bf16, token_bf16, units, units],
         (x, cot, modulation, attended, lse_columns, w_out, perm),
         scalars=slots,
         name="mix",
     )
 
-    anywhere = pl.BlockSpec(memory_space=pl.ANY)
     rows_ff = ff // n_dev
     chunk = 768
     piece = chunk // 8
@@ -1011,11 +958,12 @@
     def attend_back(first, end, name):
         begin, stop, begin_row, stop_row = head_span(first, end, width)
         columns, rows = stop - begin, stop_row - begin_row
-        used = fixed((count, stop))
+        used = pl.BlockSpec((count, columns), lambda *_: (0, begin // columns), pipeline_mode=pl.Buffered(1))
+        used_rows = pl.BlockSpec((rows, count), lambda *_: (begin_row // rows, 0), pipeline_mode=pl.Buffered(1))
         return call(
-            functools.partial(attend_back_kernel, first=first, base=begin, base_row=begin_row),
+            functools.partial(attend_back_kernel, first=first, base=begin, base_row=begin_row, width=width),
             ((end - first) // TOGETHER,),
-            [used] * 4 + [fixed((128, count))] * 2 + [fixed((width, count))],
+            [used] * 4 + [fixed((128, count))] * 2 + [used_rows],
             [fixed((rows, count))] + [fixed((count, columns))] * 2,
             [shape((rows, count), f32), shape((count, columns), f32), shape((count, columns), bf16)],
             (query, key, value, grad_attended, lse, dot_term, key_t),
@@ -1048,8 +996,8 @@
         + [rows_of((SEG, dk0.shape[1])), rows_of((SEG, dk1.shape[1]))]
         + [rows_of((SEG, 2 * width)), rows_of((SEG, 256)), seg_spec, seg_spec, rows_of((8, width // 8, SEG), 2), rows_of((2, SEG), 1)]
         + table_specs + [fixed(head_fold.shape)],
-        [seg_spec] * 2 + [fixed((8, 128))] + square_send * 2,
-        [token_bf16] * 2 + [shape((8, 128), bf16)] + square_shapes * 2,
+        [seg_spec] * 2 + [fixed((4, 128))] + square_send * 2,
+        [token_bf16] * 2 + [shape((4, 128), bf16)] + square_shapes * 2,
         (dqt0, dqt1, dk0, dk1, raw, inverse, query, key, attn_units, coord) + tables + (head_fold,),
         scalars=reducer.bits,
         scratch=[pltpu.VMEM((width, width), f32)] * 2 + [pltpu.VMEM((2, width), f32)],
@@ -1064,6 +1012,7 @@
     late = [q_part, k_part, v_part]
     extra = n_dp.bit_length() - 5
     reducer.fold([v_part], "v")
+    reducer.fold([q_part, k_part], "late")
     for _ in range(extra):
         reducer.fold(early, "early")
     rows_d = width // n_dev
@@ -1082,30 +1031,46 @@
     merged.shapes = [shape((rows_d, ff), f32)] * 2 + [shape((rows_d, width), f32), shape((rows_ff, width), f32)]
     early = [merged]
     reducer.fold(early, "early")
-    reducer.fold([q_part, k_part], "late")
-    grad_tokens, mod_own, mod_other = call(
+
+    columns = 7 * width + 128
+    grad_tokens, own_rows = call(
         functools.partial(input_back_kernel, base=base),
         (blocks,),
         [token_spec] * 2 + [rows_of((TB, dv0.shape[1])), rows_of((TB, dv1.shape[1]))] + [token_spec] * 2
-        + [mod_spec, fixed((width, 3 * width)), fixed((slots_n, 4 * width)), fixed((8, 128))],
-        [token_spec] + [fixed((2 * slots_n, half + 128))] * 2,
-        [token_bf16] + [shape((2 * slots_n, half + 128), bf16)] * 2,
-        (grad_q, grad_k, dv0, dv1, x, grad_mid, modulation, w_qkv, sums_b, gains_low),
-        scalars=slots_core,
+        + [mod_spec, fixed((width, 3 * width)), fixed((slots_n, 4 * width)), fixed((4, 128)), fixed((slots_n, width))],
+        [token_spec, fixed((slots_n, columns))],
+        [token_bf16, shape((slots_n, columns), bf16)],
+        (grad_q, grad_k, dv0, dv1, x, grad_mid, modulation, w_qkv, sums_b, gains_low, own_activated),
+        scalars=slots,
         scratch=[pltpu.VMEM((slots_n, 2 * width), f32)],
         name="input_back",
     )
-    every_mod = Gather(reducer, mod_other, mod_own, activated)
-    reducer.fold([every_mod], "pair")
     reducer.fold(late, "late")
-    reducer.fold([every_mod], "every")
     summed_gate, summed_up, summed_out, summed_down = reducer.fold(early, "early_last", last=True)
-    for _ in range(1 + extra):
-        reducer.fold(late + [every_mod], "late")
+    reducer.fold(late, "late", passed=[own_rows])
+    (own_rows,) = reducer.passed
+    every_row = lax.all_gather(own_rows, ("dp", "mod"), axis=0, tiled=True)
+    for _ in range(extra):
+        reducer.fold(late, "late")
     late = [Merged(late)]
-    reducer.fold(late + [every_mod], "late")
-    summed_qkv, grad_w_ada, gain_grads = reducer.fold(late + [every_mod], "late_last", last=True)
-    grad_activated = jnp.einsum("nc,dc->nd", every_mod.pair[:, width : width + half], w_ada, preferred_element_type=f32)
+    reducer.fold(late, "late")
+    (summed_qkv,) = reducer.fold(late, "late_last", last=True)
+    grad_w_ada, gain_grads = call(
+        functools.partial(ada_kernel, width=width),
+        (1,),
+        [whole(every_row.shape)],
+        [whole((width // n_dp, half)), whole((2, 128))],
+        [shape((width // n_dp, half), f32), shape((2, 128), f32)],
+        (every_row,),
+        scalars=reducer.bits,
+        name="ada",
+    )
+
+    halves = own_rows[:, : 6 * width].reshape(slots_n, n_mod, half)
+    own_half = lax.dynamic_index_in_dim(halves, mod_index, 1, keepdims=False)
+    other_half = lax.dynamic_index_in_dim(halves, 1 - mod_index, 1, keepdims=False)
+    both = pair_order(own_half, reducer.swap(other_half, "mod"), mod_index).reshape(-1, half)
+    grad_activated = jnp.einsum("nc,dc->nd", both, w_ada, preferred_element_type=f32)
     grad_activated = grad_activated.reshape(n_mod, slots_n, width)
     own_part = lax.dynamic_index_in_dim(grad_activated, mod_index, 0, keepdims=False)
     other_part = lax.dynamic_index_in_dim(grad_activated, 1 - mod_index, 0, keepdims=False)

time: 483 us -> 519 us (1.075)
  Pallas kernels: 345 us -> 377 us
  starting transfers between devices: 53.5 us -> 31.7 us
  between operations: 1.27 us -> 14.6 us
  waiting for transfers between devices: 48.8 us -> 56.7 us
    pallas_call x24 -> x23, Pallas kernels: 345 us -> 377 us  [__call__(): pl.pallas_call(body, grid_spec=spec, input_output_aliases=aliases or {},...]
    all_gather x0 -> x1, waiting for transfers between devices: none -> 30.3 us  [body(): every_row = lax.all_gather(own_rows, ('dp', 'mod'), axis=0, tiled=True)]
    ppermute x25 -> x21, waiting for transfers between devices: 44.5 us -> 21.5 us  [swap(): lax.ppermute(arr, 'dp', [(i, i ^ 1 << bit) for i in range(self.n_dp)])]
    ppermute x25 -> x21, starting transfers between devices: 28.2 us -> 16.4 us  [swap(): lax.ppermute(arr, 'dp', [(i, i ^ 1 << bit) for i in range(self.n_dp)])]
    ppermute x10, starting transfers between devices: 25.3 us -> 15.3 us  [swap(): return lax.ppermute(arr, 'mod', [(i, i ^ 1) for i in range(self.n_mod)])]
    unnamed x64 -> x49, local copies, waits for them, and re-layouts: 12.6 us -> 15.2 us
  transfers between devices with their start and end apart: 35 -> 32, of which waited for: 10 -> 10; matrix products, arithmetic and copies ran while one was open for 2% -> 3% of each run, Pallas kernels for 32% -> 34%
where the time goes in v8:
time: 519 us; the launch traced here: 515 us
  Pallas kernels  377 us (73%)
  waiting for transfers between devices  56.7 us (11%)
  starting transfers between devices  31.7 us (6%)
  local copies, waits for them, and re-layouts  20.9 us (4%)
  between operations  14.6 us (3%)
  matrix products  9.89 us (2%)
    pallas_call x23, Pallas kernels, __call__(): pl.pallas_call(body, grid_spec=spec, input_output_aliases=aliases or {},...  377 us
    all_gather x1, waiting for transfers between devices, body(): every_row = lax.all_gather(own_rows, ('dp', 'mod'), axis=0, tiled=True)  30.3 us
    ppermute x21, waiting for transfers between devices, swap(): lax.ppermute(arr, 'dp', [(i, i ^ 1 << bit) for i in range(self.n_dp)])  21.5 us
    ppermute x21, starting transfers between devices, swap(): lax.ppermute(arr, 'dp', [(i, i ^ 1 << bit) for i in range(self.n_dp)])  16.4 us
    ppermute x10, starting transfers between devices, swap(): return lax.ppermute(arr, 'mod', [(i, i ^ 1) for i in range(self.n_mod)])  15.3 us
    unnamed x49, local copies, waits for them, and re-layouts  15.2 us
  transfers between devices with their start and end apart: 32, of which 10 were waited for; matrix products, arithmetic and copies ran while one was open for 3% of the time, Pallas kernels for 34%

profile of v8, /device:TPU:0, one launch (start us, length us, event | category | flops | bytes accessed | tf_op | source)
XLA Modules:
  0.0 514.9 jit_solution(10228131137051472525)
XLA Ops:
  7.2 3.0 collective-permute-start
  13.0 4.4 convolution_convert_fusion
  17.5 2.1 collective-permute-start.1
  20.2 1.3 slice.20
  22.9 28.1 %project.1 = (bf16[8,144,1024]{2,1,0:T(8,128)(2,1)}, f32[1024,2304]{1,0:T(8,128)}, f32[1024,256]{1,0:T(8,128)}, bf16[1024,1152]{1,0:T(8,128)(2,1)}, bf16[1024,11...) custom-call(s32[4]{0:T(128)} %bitcast.62, bf16[1024,1152]{1,0:T(8,128)(2,1)} %bitcast.47, ...), custom_call_target="tpu_custom_call" | custom-call | flops 1 | bytes 1 | tf_op jit(solution)/shard_map/project/pallas_call | solution.py:654
  51.0 27.2 %attend.1 = (f32[1024,1152]{1,0:T(8,128)}, f32[1024,128]{1,0:T(8,128)}) custom-call(s32[4]{0:T(128)} %bitcast.63, bf16[8,144,1024]{2,1,0:T(8,128)(2,1)} %get-tuple-element.113.refs_1_.refs_2_.refs_10_, bf16[1024,1152]{1,0:T(8,128)(2,1)} %get-tuple-element.114.refs_2_.refs_8_, bf16[1024,1152]{1,0:T(8,128)(2,1)} %get-tuple-element.115.refs_3_.refs_9_, ...), custom_call_target="tpu_custom_call" | custom-call | flops 1 | bytes 1 | tf_op jit(solution)/shard_map/attend/pallas_call | solution.py:654
  78.2 20.2 %mix.1 = (bf16[1024,1152]{1,0:T(8,128)(2,1)}, f32[128,1024]{1,0:T(8,128)}, bf16[1024,1152]{1,0:T(8,128)(2,1)}, f32[1024,1152]{1,0:T(8,128)}, bf16[1024,1152]{1,0...) custom-call(s32[4]{0:T(128)} %bitcast.64, ...), custom_call_target="tpu_custom_call" | custom-call | flops 1 | bytes 1 | tf_op jit(solution)/shard_map/mix/pallas_call | solution.py:654
  98.4 95.5 %ffn.1 = (bf16[4,144,3072]{2,1,0:T(8,128)(2,1)}, bf16[4,144,3072]{2,1,0:T(8,128)(2,1)}, bf16[4,144,3072]{2,1,0:T(8,128)(2,1)}, bf16[4,144,3072]{2,1,0:T(8,128)(2...) custom-call(s32[5]{0:T(128)} %stack.62.refs_0_, ...), custom_call_target="tpu_custom_call" | custom-call | flops 1 | bytes 1 | tf_op jit(solution)/shard_map/ffn/pallas_call | solution.py:654
  195.2 25.1 %middle.1 = (bf16[1024,1152]{1,0:T(8,128)(2,1)}, f32[1024,1152]{1,0:T(8,128)}, bf16[1024,1152]{1,0:T(8,128)(2,1)}, f32[128,1024]{1,0:T(8,128)}, f32[4,4608]{1,0:...) custom-call(s32[6]{0:T(128)} %pad_add_fusion.refs_0_, ...), custom_call_target="tpu_custom_call" | custom-call | flops 1 | bytes 1 | tf_op jit(solution)/shard_map/middle/pallas_call | solution.py:654
  220.7 2.9 collective-permute-done.3.refs_5_.refs_9_
  224.7 15.2 %early.4 = (bf16[2,144,3712]{2,1,0:T(8,128)(2,1)}, bf16[2,144,3712]{2,1,0:T(8,128)(2,1)}, bf16[2,144,3584]{2,1,0:T(8,128)(2,1)}, bf16[2,144,3584]{2,1,0:T(8,128)...) custom-call(s32[5]{0:T(128)} %stack.62.refs_0_, bf16[1024,1152]{1,0:T(8,128)(2,1)} %get-tuple-element.129.refs_1_, ...), custom_call_target="tpu_custom_call" | custom-call | flops 1 | bytes 1 | tf_op jit(solution)/shard_map/early/pallas_call | solution.py:654
  239.9 1.6 collective-permute-start.7
  241.5 1.4 collective-permute-start.8
  242.8 42.5 %attend_back_0.1 = (f32[864,1024]{1,0:T(8,128)}, f32[1024,1024]{1,0:T(8,128)}, bf16[1024,1024]{1,0:T(8,128)(2,1)}) custom-call(s32[4]{0:T(128)} %bitcast.65, bf16[2,144,3712]{2,1,0:T(8,128)(2,1)} %get-tuple-element.137.refs_1_, bf16[1024,1152]{1,0:T(8,128)(2,1)} %get-tuple-element.114.refs_2_.refs_8_, bf16[1024,1152]{1,0:T(8,128)(2,1)} %get-tuple-element.115.refs_3_.refs_9_, ...), custom_call_target="tpu_custom_call" | custom-call | flops 1 | bytes 1 | tf_op jit(solution)/shard_map/attend_back_0/pallas_call | solution.py:654
  285.3 2.2 collective-permute-done.7.refs_5_
  287.5 1.4 collective-permute-done.6.refs_3_
  288.9 1.3 copy-done.3
  290.2 8.5 %early.5 = (bf16[144,3712]{1,0:T(8,128)(2,1)}, f32[144,3712]{1,0:T(8,128)}, bf16[2,72,3584]{2,1,0:T(8,128)(2,1)}, f32[2,72,3584]{2,1,0:T(8,128)}, bf16[2,192,115...) custom-call(s32[5]{0:T(128)} %stack.62.refs_0_, f32[864,1024]{1,0:T(8,128)} %get-tuple-element.142.refs_1_.refs_2_, ...), custom_call_target="tpu_custom_call" | custom-call | flops 1 | bytes 1 | tf_op jit(solution)/shard_map/early/pallas_call | solution.py:654
  298.8 1.5 collective-permute-start.9
  300.3 1.4 collective-permute-start.11
  301.7 15.8 %attend_back_1.1 = (f32[288,1024]{1,0:T(8,128)}, f32[1024,384]{1,0:T(8,128)}, bf16[1024,384]{1,0:T(8,128)(2,1)}) custom-call(s32[4]{0:T(128)} %bitcast.66, bf16[144,3712]{1,0:T(8,128)(2,1)} %get-tuple-element.148.refs_1_, bf16[1024,1152]{1,0:T(8,128)(2,1)} %get-tuple-element.114.refs_2_.refs_8_, bf16[1024,1152]{1,0:T(8,128)(2,1)} %get-tuple-element.115.refs_3_.refs_9_, ...), custom_call_target="tpu_custom_call" | custom-call | flops 1 | bytes 1 | tf_op jit(solution)/shard_map/attend_back_1/pallas_call | solution.py:654
  317.4 7.4 %value.1 = (bf16[4,144,1152]{2,1,0:T(8,128)(2,1)}, bf16[4,144,1152]{2,1,0:T(8,128)(2,1)}) custom-call(s32[5]{0:T(128)} %stack.62.refs_0_, f32[288,1024]{1,0:T(8,128)} %get-tuple-element.149.refs_1_.refs_3_, bf16[8,144,1024]{2,1,0:T(8,128)(2,1)} %get-tuple-element.113.refs_1_.refs_2_.refs_10_, bf16[1024,1024]{1,0:T(8,128)(2,1)} %get-tuple-element.150.refs_3_.refs_4_, ...), custom_call_target="tpu_custom_call" | custom-call | flops 1 | bytes 1 | tf_op jit(solution)/shard_map/value/pallas_call | solution.py:654
  326.3 6.3 %early.6 = (bf16[72,3712]{1,0:T(8,128)(2,1)}, f32[72,3712]{1,0:T(8,128)}, bf16[72,3584]{1,0:T(8,128)(2,1)}, f32[72,3584]{1,0:T(8,128)}, bf16[192,1152]{1,0:T(8,128)(2,1)}, /*index=5*/f32[192,1152]{1,0:T(8,128)}) custom-call(s32[5]{0:T(128)} %stack.62.refs_0_, bf16[4,144,1152]{2,1,0:T(8,128)(2,1)} %get-tuple-element.152.refs_1_, ...), custom_call_target="tpu_custom_call" | custom-call | flops 1 | bytes 1 | tf_op jit(solution)/shard_map/early/pallas_call | solution.py:654
  332.9 2.4 collective-permute-start.13
  335.7 27.7 %project_back.1 = (bf16[1024,1152]{1,0:T(8,128)(2,1)}, bf16[1024,1152]{1,0:T(8,128)(2,1)}, bf16[4,128]{1,0:T(4,128)(2,1)}, bf16[4,144,1152]{2,1,0:T(8,128)(2,1)}...) custom-call(s32[5]{0:T(128)} %stack.62.refs_0_, ...), custom_call_target="tpu_custom_call" | custom-call | flops 1 | bytes 1 | tf_op jit(solution)/shard_map/project_back/pallas_call | solution.py:654
  365.4 4.5 v.1
  372.4 5.3 %late.4 = (bf16[2,144,1152]{2,1,0:T(8,128)(2,1)}, bf16[2,144,1152]{2,1,0:T(8,128)(2,1)}, bf16[2,144,1152]{2,1,0:T(8,128)(2,1)}, bf16[2,144,1152]{2,1,0:T(8,128)(2,1)}) custom-call(s32[5]{0:T(128)} %stack.62.refs_0_, bf16[4,72,1152]{2,1,0:T(8,128)(2,1)} %get-tuple-element.171.refs_1_, bf16[4,144,1152]{2,1,0:T(8,128)(2,1)} %get-tuple-element.172.refs_2_, ...), custom_call_target="tpu_custom_call" | custom-call | flops 1 | bytes 1 | tf_op jit(solution)/shard_map/late/pallas_call | solution.py:654
  378.3 1.5 collective-permute-start.19
  379.8 5.1 early.7
  385.0 2.7 collective-permute-start.21
  388.3 21.0 %input_back.1 = (bf16[1024,1152]{1,0:T(8,128)(2,1)}, bf16[4,8192]{1,0:T(4,128)(2,1)}) custom-call(s32[4]{0:T(128)} %bitcast.67, bf16[36,10752]{1,0:T(8,128)(2,1)} %get-tuple-element.182.refs_1_, bf16[1024,1152]{1,0:T(8,128)(2,1)} %get-tuple-element.163.refs_0_.refs_2_, bf16[1024,1152]{1,0:T(8,128)(2,1)} %get-tuple-element.183.refs_3_, ...), custom_call_target="tpu_custom_call" | custom-call | flops 1 | bytes 1 | tf_op jit(solution)/shard_map/input_back/pallas_call | solution.py:654
  410.6 5.1 late.5
  418.7 6.4 %collective-permute-done.21.refs_3_ = bf16[36,10752]{1,0:T(8,128)(2,1)S(1)} collective-permute-done((bf16[36,10752]{1,0:T(8,128)(2,1)}, bf16[36,10752]{1,0:T(8,128)(2,1)S(1)}, u32[]{:S(2)}, u32[]{:S(2)}) %collective-permute-start.21) | collective-permute-done | bytes 774176 | tf_op jit(solution)/shard_map/ppermute | solution.py:698
  426.0 3.5 early_last.1
  429.6 2.6 collective-permute-done.22.refs_3_
  433.1 3.5 late.6
  437.5 1.8 collective-permute-start.27
  439.6 1.6 collective-permute-start.25
  441.2 3.0 collective-permute-done.27.refs_3_
  446.1 3.1 late.7
  449.2 2.6 collective-permute-start.30
  451.9 5.5 %fusion = f32[2,4,1152]{2,1,0:T(4,128)S(1)} fusion(bf16[1152,3456]{1,0:T(8,128)(2,1)} %param.23, bf16[1,4,3456]{2,1,0:T(4,128)(2,1)S(1)} %bitcast.60, bf16[1,4,3456]{2,1,0:T(4,128)(2,1)S(1)} %get-tuple-element.215, pred[]{:T(512)S(6)} %eq.2), kind=kOutput, calls=%fused_computation | convolution fusion | flops 63949824 | bytes 8054785 | tf_op jit(solution)/shard_map/nc,dc->nd/dot_general | solution.py:1073
  458.2 6.3 %collective-permute-done.30.refs_3_ = bf16[36,3456]{1,0:T(8,128)(2,1)S(1)} collective-permute-done((bf16[36,3456]{1,0:T(8,128)(2,1)}, bf16[36,3456]{1,0:T(8,128)(2,1)S(1)}, u32[]{:S(2)}, u32[]{:S(2)}) %collective-permute-start.30) | collective-permute-done | bytes 248864 | tf_op jit(solution)/shard_map/ppermute | solution.py:698
  465.2 2.7 late_last.1.refs_1_
  467.9 30.3 %all-gather.3.cloned.1.call-done = bf16[32,4,8192]{2,1,0:T(4,128)(2,1)} async-done(((bf16[1,4,8192]{2,1,0:T(4,128)(2,1)}), bf16[32,4,8192]{2,1,0:T(4,128)(2,1)}) %all-gather.3.cloned.1.call-update) | async-done | bytes 2097168 | tf_op jit(solution)/shard_map/all_gather | solution.py:1052
  498.2 4.0 reshape.53.refs_2_
  502.7 3.9 ada.1
  506.6 1.3 slice_bitcast_fusion.2
  (112 shorter events, 26.9 us)
Async XLA Ops:
  7.2 491.0 %all-gather.3.cloned.1.call-start = ((), (), s32[]{:S(2)}) async-start(), calls=%async_computation | async-start | bytes 2162688 | tf_op jit(solution)/shard_map/all_gather | solution.py:1052
  7.2 5.0 collective-permute-start
  17.5 4.6 collective-permute-start.1
  98.4 96.2 %copy-start.23 = (s32[1,4]{1,0:T(1,128)S(1)}, s32[1,4]{1,0:T(1,128)}, u32[]{:S(2)}) copy-start(s32[1,4]{1,0:T(1,128)} %slice.20) | copy-start | bytes 52
  193.9 29.7 %collective-permute-start.2 = (bf16[4,144,3072]{2,1,0:T(8,128)(2,1)}, bf16[4,144,3072]{2,1,0:T(8,128)(2,1)}, u32[]{:S(2)}, u32[]{:S(2)}) collective-permute-start(bf16[4,144,3072]{2,1,0:T(8,128)(2,1)} %get-tuple-element.123.refs_1_), channel_id=1, source_target_pairs={{0,2},{2,0},{4,6},{6,4},{8,10},{10,8},{12,14},{14,12},{16,18},{18,... | collective-permute-start | bytes 10616840 | tf_op jit(solution)/shard_map/ppermute | solution.py:698
  194.0 29.6 %collective-permute-start.4 = (bf16[4,144,3072]{2,1,0:T(8,128)(2,1)}, bf16[4,144,3072]{2,1,0:T(8,128)(2,1)}, u32[]{:S(2)}, u32[]{:S(2)}) collective-permute-start(bf16[4,144,3072]{2,1,0:T(8,128)(2,1)} %get-tuple-element.134), channel_id=1, source_target_pairs={{0,2},{2,0},{4,6},{6,4},{8,10},{10,8},{12,14},{14,12},{16,18},{18,... | collective-permute-start | bytes 10616840 | tf_op jit(solution)/shard_map/ppermute | solution.py:698
  194.5 29.1 %collective-permute-start.5 = (bf16[4,384,1152]{2,1,0:T(8,128)(2,1)}, bf16[4,384,1152]{2,1,0:T(8,128)(2,1)}, u32[]{:S(2)}, u32[]{:S(2)}) collective-permute-start(bf16[4,384,1152]{2,1,0:T(8,128)(2,1)} %bitcast.70), channel_id=1, source_target_pairs={{0,2},{2,0},{4,6},{6,4},{8,10},{10,8},{12,14},{14,12},{16,18},{18,... | collective-permute-start | bytes 10616840 | tf_op jit(solution)/shard_map/ppermute | solution.py:698
  220.2 3.4 collective-permute-start.3
  223.6 1.1 copy-start.1
  239.9 49.0 %collective-permute-start.6 = (bf16[2,144,3712]{2,1,0:T(8,128)(2,1)}, bf16[2,144,3712]{2,1,0:T(8,128)(2,1)S(1)}, u32[]{:S(2)}, u32[]{:S(2)}) collective-permute-start(bf16[2,144,3712]{2,1,0:T(8,128)(2,1)} %get-tuple-element.137.refs_1_), channel_id=1, source_target_pairs={{0,1},{1,0},{2,3},{3,2},{4,5},{5,4},{6,7},{7,6},{8,9},{9,8},{10,11... | collective-permute-start | bytes 6414344 | tf_op jit(solution)/shard_map/ppermute | solution.py:697
  239.9 47.6 %collective-permute-start.7 = (bf16[2,144,3584]{2,1,0:T(8,128)(2,1)}, bf16[2,144,3584]{2,1,0:T(8,128)(2,1)}, u32[]{:S(2)}, u32[]{:S(2)}) collective-permute-start(bf16[2,144,3584]{2,1,0:T(8,128)(2,1)} %get-tuple-element.145), channel_id=1, source_target_pairs={{0,4},{2,6},{4,0},{6,2},{8,12},{10,14},{12,8},{14,10},{16,20},{18,... | collective-permute-start | bytes 6193160 | tf_op jit(solution)/shard_map/ppermute | solution.py:698
  241.5 43.8 %collective-permute-start.8 = (bf16[4,192,1152]{2,1,0:T(8,128)(2,1)}, bf16[4,192,1152]{2,1,0:T(8,128)(2,1)S(1)}, u32[]{:S(2)}, u32[]{:S(2)}) collective-permute-start(bf16[4,192,1152]{2,1,0:T(8,128)(2,1)} %get-tuple-element.147), channel_id=1, source_target_pairs={{0,8},{2,10},{4,12},{6,14},{8,0},{10,2},{12,4},{14,6},{16,24},{18,... | collective-permute-start | bytes 5308424 | tf_op jit(solution)/shard_map/ppermute | solution.py:698
  285.3 3.6 copy-start.6
  288.9 1.4 copy-start.3
  298.8 26.1 %collective-permute-start.9 = (bf16[144,3712]{1,0:T(8,128)(2,1)}, bf16[144,3712]{1,0:T(8,128)(2,1)S(1)}, u32[]{:S(2)}, u32[]{:S(2)}) collective-permute-start(bf16[144,3712]{1,0:T(8,128)(2,1)} %get-tuple-element.148.refs_1_), channel_id=1, source_target_pairs={{0,4},{2,6},{4,0},{6,2},{8,12},{10,14},{12,8},{14,10},{16,20},{18,... | collective-permute-start | bytes 3207176 | tf_op jit(solution)/shard_map/ppermute | solution.py:698
  300.3 24.6 %collective-permute-start.10 = (bf16[2,72,3584]{2,1,0:T(8,128)(2,1)}, bf16[2,72,3584]{2,1,0:T(8,128)(2,1)S(1)}, u32[]{:S(2)}, u32[]{:S(2)}) collective-permute-start(bf16[2,72,3584]{2,1,0:T(8,128)(2,1)} %get-tuple-element.155), channel_id=1, source_target_pairs={{0,8},{2,10},{4,12},{6,14},{8,0},{10,2},{12,4},{14,6},{16,24},{18,... | collective-permute-start | bytes 3096584 | tf_op jit(solution)/shard_map/ppermute | solution.py:698
  300.3 24.6 %collective-permute-start.11 = (bf16[2,192,1152]{2,1,0:T(8,128)(2,1)}, bf16[2,192,1152]{2,1,0:T(8,128)(2,1)}, u32[]{:S(2)}, u32[]{:S(2)}) collective-permute-start(bf16[2,192,1152]{2,1,0:T(8,128)(2,1)} %get-tuple-element.157), channel_id=1, source_target_pairs={{0,1},{1,0},{2,3},{3,2},{4,5},{5,4},{6,7},{7,6},{8,9},{9,8},{10,11... | collective-permute-start | bytes 2654216 | tf_op jit(solution)/shard_map/ppermute | solution.py:697
  324.8 38.5 %collective-permute-start.15 = (bf16[4,144,1152]{2,1,0:T(8,128)(2,1)}, bf16[4,144,1152]{2,1,0:T(8,128)(2,1)S(1)}, u32[]{:S(2)}, u32[]{:S(2)}) collective-permute-start(bf16[4,144,1152]{2,1,0:T(8,128)(2,1)} %get-tuple-element.152.refs_1_), channel_id=1, source_target_pairs={{0,2},{2,0},{4,6},{6,4},{8,10},{10,8},{12,14},{14,12},{16,18},{18,... | collective-permute-start | bytes 3981320 | tf_op jit(solution)/shard_map/ppermute | solution.py:698
  324.9 1.1 copy-start.10
  324.9 1.4 copy-start.9
  332.6 30.8 %collective-permute-start.12 = (bf16[72,3712]{1,0:T(8,128)(2,1)}, bf16[72,3712]{1,0:T(8,128)(2,1)S(1)}, u32[]{:S(2)}, u32[]{:S(2)}) collective-permute-start(bf16[72,3712]{1,0:T(8,128)(2,1)} %get-tuple-element.158.refs_1_), channel_id=1, source_target_pairs={{0,8},{2,10},{4,12},{6,14},{8,0},{10,2},{12,4},{14,6},{16,24},{18,... | collective-permute-start | bytes 1603592 | tf_op jit(solution)/shard_map/ppermute | solution.py:698
  332.9 30.5 %collective-permute-start.13 = (bf16[72,3584]{1,0:T(8,128)(2,1)}, bf16[72,3584]{1,0:T(8,128)(2,1)S(1)}, u32[]{:S(2)}, u32[]{:S(2)}) collective-permute-start(bf16[72,3584]{1,0:T(8,128)(2,1)} %get-tuple-element.164), channel_id=1, source_target_pairs={{0,1},{1,0},{2,3},{3,2},{4,5},{5,4},{6,7},{7,6},{8,9},{9,8},{10,11... | collective-permute-start | bytes 1548296 | tf_op jit(solution)/shard_map/ppermute | solution.py:697
  335.2 28.1 %collective-permute-start.14 = (bf16[192,1152]{1,0:T(8,128)(2,1)}, bf16[192,1152]{1,0:T(8,128)(2,1)S(1)}, u32[]{:S(2)}, u32[]{:S(2)}) collective-permute-start(bf16[192,1152]{1,0:T(8,128)(2,1)} %get-tuple-element.165), channel_id=1, source_target_pairs={{0,4},{2,6},{4,0},{6,2},{8,12},{10,14},{12,8},{14,10},{16,20},{18,... | collective-permute-start | bytes 1327112 | tf_op jit(solution)/shard_map/ppermute | solution.py:698
  363.4 1.1 copy-start
  363.4 1.2 copy-start.5
  363.4 1.3 copy-start.4
  363.4 1.5 copy-start.2
  364.9 6.0 %collective-permute-start.16 = (bf16[4,144,1152]{2,1,0:T(8,128)(2,1)}, bf16[4,144,1152]{2,1,0:T(8,128)(2,1)S(1)}, u32[]{:S(2)}, u32[]{:S(2)}) collective-permute-start(bf16[4,144,1152]{2,1,0:T(8,128)(2,1)} %get-tuple-element.173), channel_id=1, source_target_pairs={{0,2},{2,0},{4,6},{6,4},{8,10},{10,8},{12,14},{14,12},{16,18},{18,... | collective-permute-start | bytes 3981320 | tf_op jit(solution)/shard_map/ppermute | solution.py:698
  364.9 6.0 %collective-permute-start.17 = (bf16[4,144,1152]{2,1,0:T(8,128)(2,1)}, bf16[4,144,1152]{2,1,0:T(8,128)(2,1)S(1)}, u32[]{:S(2)}, u32[]{:S(2)}) collective-permute-start(bf16[4,144,1152]{2,1,0:T(8,128)(2,1)} %get-tuple-element.175), channel_id=1, source_target_pairs={{0,2},{2,0},{4,6},{6,4},{8,10},{10,8},{12,14},{14,12},{16,18},{18,... | collective-permute-start | bytes 3981320 | tf_op jit(solution)/shard_map/ppermute | solution.py:698
  369.9 39.4 %collective-permute-start.20 = (bf16[4,72,1152]{2,1,0:T(8,128)(2,1)}, bf16[4,72,1152]{2,1,0:T(8,128)(2,1)S(1)}, u32[]{:S(2)}, u32[]{:S(2)}) collective-permute-start(bf16[4,72,1152]{2,1,0:T(8,128)(2,1)} %get-tuple-element.171.refs_1_), channel_id=1, source_target_pairs={{0,8},{2,10},{4,12},{6,14},{8,0},{10,2},{12,4},{14,6},{16,24},{18,... | collective-permute-start | bytes 1990664 | tf_op jit(solution)/shard_map/ppermute | solution.py:698
  370.9 1.1 copy-start.7
  370.9 1.5 copy-start.8
  377.7 31.6 %collective-permute-start.18 = (bf16[2,144,1152]{2,1,0:T(8,128)(2,1)}, bf16[2,144,1152]{2,1,0:T(8,128)(2,1)S(1)}, u32[]{:S(2)}, u32[]{:S(2)}) collective-permute-start(bf16[2,144,1152]{2,1,0:T(8,128)(2,1)} %get-tuple-element.176.refs_1_), channel_id=1, source_target_pairs={{0,4},{2,6},{4,0},{6,2},{8,12},{10,14},{12,8},{14,10},{16,20},{18,... | collective-permute-start | bytes 1990664 | tf_op jit(solution)/shard_map/ppermute | solution.py:698
  378.3 31.0 %collective-permute-start.19 = (bf16[2,144,1152]{2,1,0:T(8,128)(2,1)}, bf16[2,144,1152]{2,1,0:T(8,128)(2,1)S(1)}, u32[]{:S(2)}, u32[]{:S(2)}) collective-permute-start(bf16[2,144,1152]{2,1,0:T(8,128)(2,1)} %get-tuple-element.190), channel_id=1, source_target_pairs={{0,1},{1,0},{2,3},{3,2},{4,5},{5,4},{6,7},{7,6},{8,9},{9,8},{10,11... | collective-permute-start | bytes 1990664 | tf_op jit(solution)/shard_map/ppermute | solution.py:697
  379.8 7.9 %copy-start.22 = (f32[1,4,1152]{2,1,0:T(4,128)S(1)}, f32[1,4,1152]{2,1,0:T(4,128)}, u32[]{:S(2)}) copy-start(f32[1,4,1152]{2,1,0:T(4,128)} %param.20) | copy-start | bytes 55300
  385.0 40.1 %collective-permute-start.21 = (bf16[36,10752]{1,0:T(8,128)(2,1)}, bf16[36,10752]{1,0:T(8,128)(2,1)S(1)}, u32[]{:S(2)}, u32[]{:S(2)}) collective-permute-start(bf16[36,10752]{1,0:T(8,128)(2,1)} %get-tuple-element.182.refs_1_), channel_id=1, source_target_pairs={{0,16},{2,18},{4,20},{6,22},{8,24},{10,26},{12,28},{14,30},{16,0},... | collective-permute-start | bytes 2322440 | tf_op jit(solution)/shard_map/ppermute | solution.py:698
  409.3 1.0 copy-start.13
  409.3 1.2 copy-start.14
  415.7 16.4 %collective-permute-start.22 = (bf16[2,72,1152]{2,1,0:T(8,128)(2,1)}, bf16[2,72,1152]{2,1,0:T(8,128)(2,1)S(1)}, u32[]{:S(2)}, u32[]{:S(2)}) collective-permute-start(bf16[2,72,1152]{2,1,0:T(8,128)(2,1)} %get-tuple-element.192.refs_1_), channel_id=1, source_target_pairs={{0,8},{2,10},{4,12},{6,14},{8,0},{10,2},{12,4},{14,6},{16,24},{18,... | collective-permute-start | bytes 995336 | tf_op jit(solution)/shard_map/ppermute | solution.py:698
  416.8 15.3 %collective-permute-start.23 = (bf16[144,1152]{1,0:T(8,128)(2,1)}, bf16[144,1152]{1,0:T(8,128)(2,1)S(1)}, u32[]{:S(2)}, u32[]{:S(2)}) collective-permute-start(bf16[144,1152]{1,0:T(8,128)(2,1)} %get-tuple-element.197), channel_id=1, source_target_pairs={{0,4},{2,6},{4,0},{6,2},{8,12},{10,14},{12,8},{14,10},{16,20},{18,... | collective-permute-start | bytes 995336 | tf_op jit(solution)/shard_map/ppermute | solution.py:698
  418.0 14.1 %collective-permute-start.24 = (bf16[2,72,1152]{2,1,0:T(8,128)(2,1)}, bf16[2,72,1152]{2,1,0:T(8,128)(2,1)S(1)}, u32[]{:S(2)}, u32[]{:S(2)}) collective-permute-start(bf16[2,72,1152]{2,1,0:T(8,128)(2,1)} %get-tuple-element.199), channel_id=1, source_target_pairs={{0,1},{1,0},{2,3},{3,2},{4,5},{5,4},{6,7},{7,6},{8,9},{9,8},{10,11... | collective-permute-start | bytes 995336 | tf_op jit(solution)/shard_map/ppermute | solution.py:697
  437.5 6.7 %collective-permute-start.27 = (bf16[72,1152]{1,0:T(8,128)(2,1)}, bf16[72,1152]{1,0:T(8,128)(2,1)S(1)}, u32[]{:S(2)}, u32[]{:S(2)}) collective-permute-start(bf16[72,1152]{1,0:T(8,128)(2,1)} %get-tuple-element.202.refs_1_), channel_id=1, source_target_pairs={{0,1},{1,0},{2,3},{3,2},{4,5},{5,4},{6,7},{7,6},{8,9},{9,8},{10,11... | collective-permute-start | bytes 497672 | tf_op jit(solution)/shard_map/ppermute | solution.py:697
  439.3 6.1 %collective-permute-start.28 = (bf16[72,1152]{1,0:T(8,128)(2,1)}, bf16[72,1152]{1,0:T(8,128)(2,1)S(1)}, u32[]{:S(2)}, u32[]{:S(2)}) collective-permute-start(bf16[72,1152]{1,0:T(8,128)(2,1)} %get-tuple-element.205), channel_id=1, source_target_pairs={{0,8},{2,10},{4,12},{6,14},{8,0},{10,2},{12,4},{14,6},{16,24},{18,... | collective-permute-start | bytes 497672 | tf_op jit(solution)/shard_map/ppermute | solution.py:698
  439.3 6.1 %collective-permute-start.29 = (bf16[72,1152]{1,0:T(8,128)(2,1)}, bf16[72,1152]{1,0:T(8,128)(2,1)S(1)}, u32[]{:S(2)}, u32[]{:S(2)}) collective-permute-start(bf16[72,1152]{1,0:T(8,128)(2,1)} %get-tuple-element.207), channel_id=1, source_target_pairs={{0,4},{2,6},{4,0},{6,2},{8,12},{10,14},{12,8},{14,10},{16,20},{18,... | collective-permute-start | bytes 497672 | tf_op jit(solution)/shard_map/ppermute | solution.py:698
  439.6 12.2 %collective-permute-start.25 = (bf16[4,3456]{1,0:T(4,128)(2,1)S(1)}, bf16[4,3456]{1,0:T(4,128)(2,1)S(1)}, u32[]{:S(2)}, u32[]{:S(2)}) collective-permute-start(bf16[4,3456]{1,0:T(4,128)(2,1)S(1)} %get-tuple-element.216), channel_id=1, source_target_pairs={{0,1},{1,0},{2,3},{3,2},{4,5},{5,4},{6,7},{7,6},{8,9},{9,8},{10,11... | collective-permute-start | bytes 82952 | tf_op jit(solution)/shard_map/ppermute | solution.py:697
  444.2 1.2 copy-start.19
  449.2 15.2 %collective-permute-start.30 = (bf16[36,3456]{1,0:T(8,128)(2,1)}, bf16[36,3456]{1,0:T(8,128)(2,1)S(1)}, u32[]{:S(2)}, u32[]{:S(2)}) collective-permute-start(bf16[36,3456]{1,0:T(8,128)(2,1)} %get-tuple-element.208.refs_1_), channel_id=1, source_target_pairs={{0,16},{2,18},{4,20},{6,22},{8,24},{10,26},{12,28},{14,30},{16,0},... | collective-permute-start | bytes 746504 | tf_op jit(solution)/shard_map/ppermute | solution.py:698
  457.4 44.7 %collective-permute-start.26 = (bf16[4,1152]{1,0:T(4,128)(2,1)S(1)}, bf16[4,1152]{1,0:T(4,128)(2,1)S(1)}, u32[]{:S(2)}, u32[]{:S(2)}) collective-permute-start(bf16[4,1152]{1,0:T(4,128)(2,1)S(1)} %fusion.10), channel_id=1, source_target_pairs={{0,1},{1,0},{2,3},{3,2},{4,5},{5,4},{6,7},{7,6},{8,9},{9,8},{10,11... | collective-permute-start | bytes 27656 | tf_op jit(solution)/shard_map/ppermute | solution.py:697
  (8 other events, 6.4 us)
Sparse Core Ops, SparseCore 0:
  436.7 61.3 all-gather.2

commit v9 on v7

--- a/solution.py
+++ b/solution.py
@@ -254,15 +254,16 @@
 
 def mix_kernel(
     slots, x_ref, cot_ref, mod_ref, o_ref, lse_ref, w_out_ref, perm_ref,
-    lse_out_ref, attn_ref, mid_ref, low_ref, gf_ref, att_units_ref, ffn_units_ref,
+    attended_ref, lse_out_ref, attn_ref, mid_ref, low_ref, gf_ref, att_units_ref, ffn_units_ref,
 ):
     width = x_ref.shape[1]
     here = slots_here(slots, x_ref.shape[0])
     lse_out_ref[...] = lse_ref[...].T
     attended = o_ref[...].astype(bf16)
+    attended_ref[...] = attended
     att_units_ref[...] = nt(perm_ref[...], attended).astype(bf16).reshape(att_units_ref.shape)
     attn = nn(attended, w_out_ref[...])
-    attn_ref[...] = attn
+    attn_ref[...] = attn.astype(bf16)
     mid = by_slot(
         lambda slot, x, rows: x.astype(f32) + part(mod_ref, slot, 2, width) * rows, here, x_ref[...], attn
     )
@@ -377,19 +378,19 @@
 
     do = nt(ga, w_out_ref[...]).astype(bf16)
     do_ref[...] = do
-    dot_ref[...] = head_sum(do.astype(f32) * o_ref[...], gather_ref).T
+    dot_ref[...] = head_sum(do.astype(f32) * o_ref[...].astype(f32), gather_ref).T
 
     @pl.when(block == 0)
     def _():
         sums_ref[...] = jnp.zeros_like(sums_ref)
 
-    for index, term in enumerate((grad_mid * attn_ref[...], dmod, dmod * norm, incoming * ffn_ref[...])):
+    for index, term in enumerate((grad_mid * attn_ref[...].astype(f32), dmod, dmod * norm, incoming * ffn_ref[...])):
         add_by_slot(sums_ref, here, index, term)
 
 
 def attend_back_kernel(
     slots, q_ref, k_ref, v_ref, do_ref, lse_ref, dot_ref, kt_ref, dqt_ref, dk_ref, dv_low_ref, dv_ref,
-    *, first, base, base_row,
+    *, first, base, base_row, width,
 ):
     tokens = q_ref.shape[0]
 
@@ -400,12 +401,11 @@
         dv_ref[...] = jnp.zeros_like(dv_ref)
 
     def head(h, rows):
-        start, offset = window(h, kt_ref.shape[0])
+        start, offset = window(h, width)
         inside = head_lanes(offset)
-        columns = pl.ds(start, WIN)
-        out_columns = pl.ds(pl.multiple_of(start - base, 128), WIN)
+        columns = pl.ds(pl.multiple_of(start - base, 128), WIN)
         first_row = pl.multiple_of((h * HD) // 16 * 16, 16)
-        out_rows = pl.ds(pl.multiple_of(first_row - base_row, 16), HD + 8)
+        own_place = pl.ds(pl.multiple_of(first_row - base_row, 16), HD + 8)
         row = lax.broadcasted_iota(jnp.int32, (HD + 8, 1), 0) + first_row
         own_rows = (row >= h * HD) & (row < h * HD + HD)
         query = q_ref[rows, columns]
@@ -414,10 +414,10 @@
         value = jnp.where(inside, v_ref[rows, columns], 0)
         probs = jnp.exp2(nt(key, query) * SCORE_LOG2 - lse_ref[pl.ds(h, 1), rows])
         scores = (probs * (nt(value, grad_out) - dot_ref[pl.ds(h, 1), rows])).astype(bf16)
-        dv_ref[rows, out_columns] += jnp.where(inside, nn(probs.astype(bf16), grad_out), 0.0)
-        dk_ref[rows, out_columns] += jnp.where(inside, nn(scores, query) * SCORE_SCALE, 0.0)
-        turned = nn(kt_ref[pl.ds(first_row, HD + 8), rows], scores) * SCORE_SCALE
-        dqt_ref[out_rows, rows] += jnp.where(own_rows, turned, 0.0)
+        dv_ref[rows, columns] += jnp.where(inside, nn(probs.astype(bf16), grad_out), 0.0)
+        dk_ref[rows, columns] += jnp.where(inside, nn(scores, query) * SCORE_SCALE, 0.0)
+        turned = nn(kt_ref[own_place, rows], scores) * SCORE_SCALE
+        dqt_ref[own_place, rows] += jnp.where(own_rows, turned, 0.0)
 
     whole = slots[tokens // SEG - 1] == slots[0]
     begin = first + pl.program_id(0) * TOGETHER
@@ -844,7 +844,7 @@
 class Gather:
     def __init__(self, reducer, sent, own, activated):
         self.r, self.own, self.activated = reducer, own, activated
-        self.steps = list(range(reducer.n_dp.bit_length() - 2, -1, -1))
+        self.steps = [1] + list(range(reducer.n_dp.bit_length() - 2, 1, -1)) + [0]
         self.got = reducer.swap(sent, "mod")
         self.pair = None
 
@@ -910,6 +910,7 @@
     pair = pair_order(own_half, reducer.swap(other_half, "mod"), mod_index)
     modulation = jnp.concatenate([pair[0], pair[1]], axis=1).astype(f32)
 
+    anywhere = pl.BlockSpec(memory_space=pl.ANY)
     token_f32 = shape((count, width), f32)
     token_bf16 = shape((count, width), bf16)
     units = shape((8, width // 8, count), bf16)
@@ -943,18 +944,17 @@
         scalars=slots,
         name="attend",
     )
-    lse, attn, mid, ffn_in, grad_ffn, out_units, ffn_units = call(
+    attended, lse, attn, mid, ffn_in, grad_ffn, out_units, ffn_units = call(
         mix_kernel,
         (blocks,),
         [token_spec, token_spec, mod_spec, token_spec, rows_of((TB, 128)), square, square],
-        [rows_of((128, TB), 1)] + [token_spec] * 4 + [units_spec] * 2,
-        [lane_rows, token_f32, token_f32, token_bf16, token_bf16, units, units],
+        [token_spec, rows_of((128, TB), 1)] + [token_spec] * 4 + [units_spec] * 2,
+        [token_bf16, lane_rows, token_bf16, token_f32, token_bf16, token_bf16, units, units],
         (x, cot, modulation, attended, lse_columns, w_out, perm),
         scalars=slots,
         name="mix",
     )
 
-    anywhere = pl.BlockSpec(memory_space=pl.ANY)
     rows_ff = ff // n_dev
     chunk = 768
     piece = chunk // 8
@@ -1011,11 +1011,12 @@
     def attend_back(first, end, name):
         begin, stop, begin_row, stop_row = head_span(first, end, width)
         columns, rows = stop - begin, stop_row - begin_row
-        used = fixed((count, stop))
+        used = pl.BlockSpec((count, columns), lambda *_: (0, begin // columns), pipeline_mode=pl.Buffered(1))
+        used_rows = pl.BlockSpec((rows, count), lambda *_: (begin_row // rows, 0), pipeline_mode=pl.Buffered(1))
         return call(
-            functools.partial(attend_back_kernel, first=first, base=begin, base_row=begin_row),
+            functools.partial(attend_back_kernel, first=first, base=begin, base_row=begin_row, width=width),
             ((end - first) // TOGETHER,),
-            [used] * 4 + [fixed((128, count))] * 2 + [fixed((width, count))],
+            [used] * 4 + [fixed((128, count))] * 2 + [used_rows],
             [fixed((rows, count))] + [fixed((count, columns))] * 2,
             [shape((rows, count), f32), shape((count, columns), f32), shape((count, columns), bf16)],
             (query, key, value, grad_attended, lse, dot_term, key_t),
@@ -1064,6 +1065,7 @@
     late = [q_part, k_part, v_part]
     extra = n_dp.bit_length() - 5
     reducer.fold([v_part], "v")
+    reducer.fold([q_part, k_part], "late")
     for _ in range(extra):
         reducer.fold(early, "early")
     rows_d = width // n_dev
@@ -1082,7 +1084,7 @@
     merged.shapes = [shape((rows_d, ff), f32)] * 2 + [shape((rows_d, width), f32), shape((rows_ff, width), f32)]
     early = [merged]
     reducer.fold(early, "early")
-    reducer.fold([q_part, k_part], "late")
+
     grad_tokens, mod_own, mod_other = call(
         functools.partial(input_back_kernel, base=base),
         (blocks,),
@@ -1096,15 +1098,18 @@
         name="input_back",
     )
     every_mod = Gather(reducer, mod_other, mod_own, activated)
+    reducer.fold([v_part], "v")
     reducer.fold([every_mod], "pair")
-    reducer.fold(late, "late")
+    reducer.fold([q_part], "q")
     reducer.fold([every_mod], "every")
+    reducer.fold([k_part], "k")
     summed_gate, summed_up, summed_out, summed_down = reducer.fold(early, "early_last", last=True)
     for _ in range(1 + extra):
         reducer.fold(late + [every_mod], "late")
     late = [Merged(late)]
     reducer.fold(late + [every_mod], "late")
     summed_qkv, grad_w_ada, gain_grads = reducer.fold(late + [every_mod], "late_last", last=True)
+
     grad_activated = jnp.einsum("nc,dc->nd", every_mod.pair[:, width : width + half], w_ada, preferred_element_type=f32)
     grad_activated = grad_activated.reshape(n_mod, slots_n, width)
     own_part = lax.dynamic_index_in_dim(grad_activated, mod_index, 0, keepdims=False)

time: 483 us -> 481 us (level)
  starting transfers between devices: 53.5 us -> 47.1 us
    unnamed x64 -> x62, local copies, waits for them, and re-layouts: 12.6 us -> 13.9 us
    pallas_call x24 -> x26, Pallas kernels: 345 us -> 346 us  [__call__(): pl.pallas_call(body, grid_spec=spec, input_output_aliases=aliases or {},...]
  transfers between devices with their start and end apart: 35 -> 35, of which waited for: 10 -> 11; matrix products, arithmetic and copies ran while one was open for 2% -> 2% of each run, Pallas kernels for 32% -> 32%
where the time goes in v9:
time: 481 us; the launch traced here: 477 us
  Pallas kernels  346 us (72%)
  waiting for transfers between devices  50.9 us (11%)
  starting transfers between devices  47.1 us (10%)
  local copies, waits for them, and re-layouts  18.6 us (4%)
  matrix products  9.81 us (2%)
    pallas_call x26, Pallas kernels, __call__(): pl.pallas_call(body, grid_spec=spec, input_output_aliases=aliases or {},...  346 us
    ppermute x25, waiting for transfers between devices, swap(): lax.ppermute(arr, 'dp', [(i, i ^ 1 << bit) for i in range(self.n_dp)])  45 us
    ppermute x10, starting transfers between devices, swap(): return lax.ppermute(arr, 'mod', [(i, i ^ 1) for i in range(self.n_mod)])  23.7 us
    ppermute x25, starting transfers between devices, swap(): lax.ppermute(arr, 'dp', [(i, i ^ 1 << bit) for i in range(self.n_dp)])  23.4 us
    unnamed x62, local copies, waits for them, and re-layouts  13.9 us
  transfers between devices with their start and end apart: 35, of which 11 were waited for; matrix products, arithmetic and copies ran while one was open for 2% of the time, Pallas kernels for 32%

profile of v9, /device:TPU:0, one launch (start us, length us, event | category | flops | bytes accessed | tf_op | source)
XLA Modules:
  0.0 477.2 jit_solution(12991167205339038114)
XLA Ops:
  0.6 3.0 collective-permute-start
  6.5 4.4 convolution_convert_fusion
  11.0 2.1 collective-permute-start.1
  16.3 28.1 %project.1 = (bf16[8,144,1024]{2,1,0:T(8,128)(2,1)}, f32[1024,2304]{1,0:T(8,128)}, f32[1024,256]{1,0:T(8,128)}, bf16[1024,1152]{1,0:T(8,128)(2,1)}, bf16[1024,11...) custom-call(s32[4]{0:T(128)} %bitcast.49, bf16[1024,1152]{1,0:T(8,128)(2,1)} %bitcast.37, ...), custom_call_target="tpu_custom_call" | custom-call | flops 1 | bytes 1 | tf_op jit(solution)/shard_map/project/pallas_call | solution.py:681
  44.4 15.4 %attend.1 = (f32[1024,1152]{1,0:T(8,128)}, f32[1024,128]{1,0:T(8,128)}) custom-call(s32[4]{0:T(128)} %bitcast.50, bf16[8,144,1024]{2,1,0:T(8,128)(2,1)} %get-tuple-element.116.refs_1_.refs_2_.refs_10_, bf16[1024,1152]{1,0:T(8,128)(2,1)} %get-tuple-element.117.refs_2_.refs_8_, bf16[1024,1152]{1,0:T(8,128)(2,1)} %get-tuple-element.118.refs_3_.refs_9_, ...), custom_call_target="tpu_custom_call" | custom-call | flops 1 | bytes 1 | tf_op jit(solution)/shard_map/attend/pallas_call | solution.py:681
  59.8 20.2 %mix.1 = (bf16[1024,1152]{1,0:T(8,128)(2,1)}, f32[128,1024]{1,0:T(8,128)}, bf16[1024,1152]{1,0:T(8,128)(2,1)}, f32[1024,1152]{1,0:T(8,128)}, bf16[1024,1152]{1,0...) custom-call(s32[4]{0:T(128)} %bitcast.51, ...), custom_call_target="tpu_custom_call" | custom-call | flops 1 | bytes 1 | tf_op jit(solution)/shard_map/mix/pallas_call | solution.py:681
  80.0 95.5 %ffn.1 = (bf16[4,144,3072]{2,1,0:T(8,128)(2,1)}, bf16[4,144,3072]{2,1,0:T(8,128)(2,1)}, bf16[4,144,3072]{2,1,0:T(8,128)(2,1)}, bf16[4,144,3072]{2,1,0:T(8,128)(2...) custom-call(s32[5]{0:T(128)} %stack.48.refs_0_, ...), custom_call_target="tpu_custom_call" | custom-call | flops 1 | bytes 1 | tf_op jit(solution)/shard_map/ffn/pallas_call | solution.py:681
  176.8 24.9 %middle.1 = (bf16[1024,1152]{1,0:T(8,128)(2,1)}, f32[1024,1152]{1,0:T(8,128)}, bf16[1024,1152]{1,0:T(8,128)(2,1)}, f32[128,1024]{1,0:T(8,128)}, f32[4,4608]{1,0:...) custom-call(s32[6]{0:T(128)} %pad_add_fusion.refs_0_, ...), custom_call_target="tpu_custom_call" | custom-call | flops 1 | bytes 1 | tf_op jit(solution)/shard_map/middle/pallas_call | solution.py:681
  202.2 2.9 collective-permute-done.3.refs_5_.refs_9_
  206.1 15.1 %early.4 = (bf16[2,144,3712]{2,1,0:T(8,128)(2,1)}, bf16[2,144,3712]{2,1,0:T(8,128)(2,1)}, bf16[2,144,3584]{2,1,0:T(8,128)(2,1)}, bf16[2,144,3584]{2,1,0:T(8,128)...) custom-call(s32[5]{0:T(128)} %stack.48.refs_0_, bf16[1024,1152]{1,0:T(8,128)(2,1)} %get-tuple-element.132.refs_1_, ...), custom_call_target="tpu_custom_call" | custom-call | flops 1 | bytes 1 | tf_op jit(solution)/shard_map/early/pallas_call | solution.py:681
  221.2 13.2 %collective-permute-start.6 = (bf16[2,144,3712]{2,1,0:T(8,128)(2,1)}, bf16[2,144,3712]{2,1,0:T(8,128)(2,1)S(1)}, u32[]{:S(2)}, u32[]{:S(2)}) collective-permute-start(bf16[2,144,3712]{2,1,0:T(8,128)(2,1)} %get-tuple-element.140.refs_1_), channel_id=1, source_target_pairs={{0,1},{1,0},{2,3},{3,2},{4,5},{5,4},{6,7},{7,6},{8,9},{9,8},{10,11... | collective-permute-start | bytes 6414344 | tf_op jit(solution)/shard_map/ppermute | solution.py:724
  234.4 1.7 collective-permute-start.8
  236.1 23.5 %attend_back_0.1 = (f32[864,1024]{1,0:T(8,128)}, f32[1024,1024]{1,0:T(8,128)}, bf16[1024,1024]{1,0:T(8,128)(2,1)}) custom-call(s32[4]{0:T(128)} %bitcast.52, bf16[2,144,3712]{2,1,0:T(8,128)(2,1)} %get-tuple-element.140.refs_1_, bf16[1024,1152]{1,0:T(8,128)(2,1)} %get-tuple-element.117.refs_2_.refs_8_, bf16[1024,1152]{1,0:T(8,128)(2,1)} %get-tuple-element.118.refs_3_.refs_9_, ...), custom_call_target="tpu_custom_call" | custom-call | flops 1 | bytes 1 | tf_op jit(solution)/shard_map/attend_back_0/pallas_call | solution.py:681
  259.6 15.6 %collective-permute-done.8.refs_7_ = bf16[4,192,1152]{2,1,0:T(8,128)(2,1)S(1)} collective-permute-done((bf16[4,192,1152]{2,1,0:T(8,128)(2,1)}, bf16[4,192,1152]{2,1,0:T(8,128)(2,1)S(1)}, u32[]{:S(2)}, u32[]{:S(2)}) %collective-permute-start.8) | collective-permute-done | bytes 1769504 | tf_op jit(solution)/shard_map/ppermute | solution.py:725
  275.2 6.4 %collective-permute-done.7.refs_5_ = bf16[2,144,3584]{2,1,0:T(8,128)(2,1)} collective-permute-done((bf16[2,144,3584]{2,1,0:T(8,128)(2,1)}, bf16[2,144,3584]{2,1,0:T(8,128)(2,1)}, u32[]{:S(2)}, u32[]{:S(2)}) %collective-permute-start.7) | collective-permute-done | bytes 2064416 | tf_op jit(solution)/shard_map/ppermute | solution.py:725
  283.0 8.5 %early.5 = (bf16[144,3712]{1,0:T(8,128)(2,1)}, f32[144,3712]{1,0:T(8,128)}, bf16[2,72,3584]{2,1,0:T(8,128)(2,1)}, f32[2,72,3584]{2,1,0:T(8,128)}, bf16[2,192,115...) custom-call(s32[5]{0:T(128)} %stack.48.refs_0_, f32[864,1024]{1,0:T(8,128)} %get-tuple-element.145.refs_1_.refs_2_, ...), custom_call_target="tpu_custom_call" | custom-call | flops 1 | bytes 1 | tf_op jit(solution)/shard_map/early/pallas_call | solution.py:681
  291.8 3.1 collective-permute-start.10
  295.2 9.6 %attend_back_1.1 = (f32[288,1024]{1,0:T(8,128)}, f32[1024,384]{1,0:T(8,128)}, bf16[1024,384]{1,0:T(8,128)(2,1)}) custom-call(s32[4]{0:T(128)} %bitcast.53, bf16[144,3712]{1,0:T(8,128)(2,1)} %get-tuple-element.151.refs_1_, bf16[1024,1152]{1,0:T(8,128)(2,1)} %get-tuple-element.117.refs_2_.refs_8_, bf16[1024,1152]{1,0:T(8,128)(2,1)} %get-tuple-element.118.refs_3_.refs_9_, ...), custom_call_target="tpu_custom_call" | custom-call | flops 1 | bytes 1 | tf_op jit(solution)/shard_map/attend_back_1/pallas_call | solution.py:681
  304.9 7.4 %value.1 = (bf16[4,144,1152]{2,1,0:T(8,128)(2,1)}, bf16[4,144,1152]{2,1,0:T(8,128)(2,1)}) custom-call(s32[5]{0:T(128)} %stack.48.refs_0_, f32[288,1024]{1,0:T(8,128)} %get-tuple-element.152.refs_1_.refs_3_, bf16[8,144,1024]{2,1,0:T(8,128)(2,1)} %get-tuple-element.116.refs_1_.refs_2_.refs_10_, bf16[1024,1024]{1,0:T(8,128)(2,1)} %get-tuple-element.153.refs_3_.refs_4_, ...), custom_call_target="tpu_custom_call" | custom-call | flops 1 | bytes 1 | tf_op jit(solution)/shard_map/value/pallas_call | solution.py:681
  312.3 3.5 collective-permute-done.11.refs_7_
  315.8 1.6 collective-permute-done.10.refs_5_
  318.8 6.3 %early.6 = (bf16[72,3712]{1,0:T(8,128)(2,1)}, f32[72,3712]{1,0:T(8,128)}, bf16[72,3584]{1,0:T(8,128)(2,1)}, f32[72,3584]{1,0:T(8,128)}, bf16[192,1152]{1,0:T(8,128)(2,1)}, /*index=5*/f32[192,1152]{1,0:T(8,128)}) custom-call(s32[5]{0:T(128)} %stack.48.refs_0_, bf16[4,144,1152]{2,1,0:T(8,128)(2,1)} %get-tuple-element.155.refs_1_, ...), custom_call_target="tpu_custom_call" | custom-call | flops 1 | bytes 1 | tf_op jit(solution)/shard_map/early/pallas_call | solution.py:681
  325.2 1.7 collective-permute-start.12
  328.3 27.6 %project_back.1 = (bf16[1024,1152]{1,0:T(8,128)(2,1)}, bf16[1024,1152]{1,0:T(8,128)(2,1)}, bf16[8,128]{1,0:T(8,128)(2,1)}, bf16[4,144,1152]{2,1,0:T(8,128)(2,1)}...) custom-call(s32[5]{0:T(128)} %stack.48.refs_0_, ...), custom_call_target="tpu_custom_call" | custom-call | flops 1 | bytes 1 | tf_op jit(solution)/shard_map/project_back/pallas_call | solution.py:681
  358.0 4.4 v.2
  362.4 1.7 collective-permute-start.18
  365.6 5.4 %late.3 = (bf16[2,144,1152]{2,1,0:T(8,128)(2,1)}, bf16[2,144,1152]{2,1,0:T(8,128)(2,1)}, bf16[2,144,1152]{2,1,0:T(8,128)(2,1)}, bf16[2,144,1152]{2,1,0:T(8,128)(2,1)}) custom-call(s32[5]{0:T(128)} %stack.48.refs_0_, bf16[4,72,1152]{2,1,0:T(8,128)(2,1)} %get-tuple-element.174.refs_1_, bf16[4,144,1152]{2,1,0:T(8,128)(2,1)} %get-tuple-element.175.refs_2_, ...), custom_call_target="tpu_custom_call" | custom-call | flops 1 | bytes 1 | tf_op jit(solution)/shard_map/late/pallas_call | solution.py:681
  371.0 2.0 collective-permute-start.21
  373.0 5.0 %early.7 = (bf16[36,10752]{1,0:T(8,128)(2,1)}, f32[36,10752]{1,0:T(8,128)}) custom-call(s32[5]{0:T(128)} %stack.48.refs_0_, bf16[2,144,1152]{2,1,0:T(8,128)(2,1)} %get-tuple-element.179.refs_1_, f32[72,3712]{1,0:T(8,128)} %get-tuple-element.180.refs_2_, bf16[72,3712]{1,0:T(8,128)(2,1)} %get-tuple-element.171.refs_1_.refs_3_, ...), custom_call_target="tpu_custom_call" | custom-call | flops 1 | bytes 1 | tf_op jit(solution)/shard_map/early/pallas_call | solution.py:681
  378.0 2.4 collective-permute-start.24
  380.4 21.0 %input_back.1 = (bf16[1024,1152]{1,0:T(8,128)(2,1)}, bf16[8,3584]{1,0:T(8,128)(2,1)}, bf16[8,3584]{1,0:T(8,128)(2,1)}) custom-call(s32[6]{0:T(128)} %pad_add_fusion.refs_0_, bf16[36,10752]{1,0:T(8,128)(2,1)} %get-tuple-element.185.refs_1_, bf16[1024,1152]{1,0:T(8,128)(2,1)} %get-tuple-element.166.refs_0_.refs_2_, ...), custom_call_target="tpu_custom_call" | custom-call | flops 1 | bytes 1 | tf_op jit(solution)/shard_map/input_back/pallas_call | solution.py:681
  403.3 2.9 v.3
  406.9 2.2 pair.1.refs_1_.refs_2_
  409.0 1.7 collective-permute-start.22
  412.5 3.1 q.1
  416.2 2.2 every.1.refs_1_.refs_8_
  419.3 3.0 k.1
  422.8 2.0 collective-permute-start.25
  425.7 3.5 early_last.1
  429.2 4.1 collective-permute-done.28.refs_9_
  434.7 3.7 late.4
  441.3 1.6 collective-permute-start.32
  442.9 5.4 %fusion = f32[8,1152]{1,0:T(8,128)S(1)} fusion(bf16[1152,3456]{1,0:T(8,128)(2,1)} %param.23, bf16[8,4736]{1,0:T(8,128)(2,1)S(1)} %copy-done.10), kind=kOutput, calls=%fused_computation.1 | convolution fusion | flops 63700992 | bytes 8054784 | tf_op jit(solution)/shard_map/nc,dc->nd/dot_general | solution.py:1113
  448.4 1.5 collective-permute-done.32.refs_9_
  450.6 3.6 late.5
  456.0 1.9 collective-permute-done.20
  458.5 12.3 %collective-permute-done.33.refs_3_ = bf16[36,3456]{1,0:T(8,128)(2,1)S(1)} collective-permute-done((bf16[36,3456]{1,0:T(8,128)(2,1)}, bf16[36,3456]{1,0:T(8,128)(2,1)S(1)}, u32[]{:S(2)}, u32[]{:S(2)}) %collective-permute-start.33) | collective-permute-done | bytes 248864 | tf_op jit(solution)/shard_map/ppermute | solution.py:725
  471.8 4.0 late_last.1
  (132 shorter events, 34.0 us)
Async XLA Ops:
  0.6 5.0 %collective-permute-start = (f32[4,1152]{1,0:T(4,128)}, f32[4,1152]{1,0:T(4,128)S(1)}, u32[]{:S(2)}, u32[]{:S(2)}) collective-permute-start(f32[4,1152]{1,0:T(4,128)} %bitcast.45), channel_id=1, source_target_pairs={{0,1},{1,0},{2,3},{3,2},{4,5},{5,4},{6,7},{7,6},{8,9},{9,8},{10,11... | collective-permute-start | bytes 55304 | tf_op jit(solution)/shard_map/ppermute | solution.py:724
  6.5 4.4 copy-start.22
  11.0 4.5 collective-permute-start.1
  80.0 96.2 %copy-start.30 = (s32[1,4]{1,0:T(1,128)S(1)}, s32[1,4]{1,0:T(1,128)}, u32[]{:S(2)}) copy-start(s32[1,4]{1,0:T(1,128)} %slice.20) | copy-start | bytes 52
  175.5 29.6 %collective-permute-start.4 = (bf16[4,144,3072]{2,1,0:T(8,128)(2,1)}, bf16[4,144,3072]{2,1,0:T(8,128)(2,1)}, u32[]{:S(2)}, u32[]{:S(2)}) collective-permute-start(bf16[4,144,3072]{2,1,0:T(8,128)(2,1)} %get-tuple-element.137), channel_id=1, source_target_pairs={{0,2},{2,0},{4,6},{6,4},{8,10},{10,8},{12,14},{14,12},{16,18},{18,... | collective-permute-start | bytes 10616840 | tf_op jit(solution)/shard_map/ppermute | solution.py:725
  175.6 29.5 %collective-permute-start.5 = (bf16[4,384,1152]{2,1,0:T(8,128)(2,1)}, bf16[4,384,1152]{2,1,0:T(8,128)(2,1)}, u32[]{:S(2)}, u32[]{:S(2)}) collective-permute-start(bf16[4,384,1152]{2,1,0:T(8,128)(2,1)} %bitcast.56), channel_id=1, source_target_pairs={{0,2},{2,0},{4,6},{6,4},{8,10},{10,8},{12,14},{14,12},{16,18},{18,... | collective-permute-start | bytes 10616840 | tf_op jit(solution)/shard_map/ppermute | solution.py:725
  176.1 29.0 %collective-permute-start.2 = (bf16[4,144,3072]{2,1,0:T(8,128)(2,1)}, bf16[4,144,3072]{2,1,0:T(8,128)(2,1)}, u32[]{:S(2)}, u32[]{:S(2)}) collective-permute-start(bf16[4,144,3072]{2,1,0:T(8,128)(2,1)} %get-tuple-element.126.refs_1_), channel_id=1, source_target_pairs={{0,2},{2,0},{4,6},{6,4},{8,10},{10,8},{12,14},{14,12},{16,18},{18,... | collective-permute-start | bytes 10616840 | tf_op jit(solution)/shard_map/ppermute | solution.py:725
  201.7 3.4 collective-permute-start.3
  221.2 60.5 %collective-permute-start.6 = (bf16[2,144,3712]{2,1,0:T(8,128)(2,1)}, bf16[2,144,3712]{2,1,0:T(8,128)(2,1)S(1)}, u32[]{:S(2)}, u32[]{:S(2)}) collective-permute-start(bf16[2,144,3712]{2,1,0:T(8,128)(2,1)} %get-tuple-element.140.refs_1_), channel_id=1, source_target_pairs={{0,1},{1,0},{2,3},{3,2},{4,5},{5,4},{6,7},{7,6},{8,9},{9,8},{10,11... | collective-permute-start | bytes 6414344 | tf_op jit(solution)/shard_map/ppermute | solution.py:724
  234.4 47.2 %collective-permute-start.7 = (bf16[2,144,3584]{2,1,0:T(8,128)(2,1)}, bf16[2,144,3584]{2,1,0:T(8,128)(2,1)}, u32[]{:S(2)}, u32[]{:S(2)}) collective-permute-start(bf16[2,144,3584]{2,1,0:T(8,128)(2,1)} %get-tuple-element.148), channel_id=1, source_target_pairs={{0,4},{2,6},{4,0},{6,2},{8,12},{10,14},{12,8},{14,10},{16,20},{18,... | collective-permute-start | bytes 6193160 | tf_op jit(solution)/shard_map/ppermute | solution.py:725
  234.4 40.8 %collective-permute-start.8 = (bf16[4,192,1152]{2,1,0:T(8,128)(2,1)}, bf16[4,192,1152]{2,1,0:T(8,128)(2,1)S(1)}, u32[]{:S(2)}, u32[]{:S(2)}) collective-permute-start(bf16[4,192,1152]{2,1,0:T(8,128)(2,1)} %get-tuple-element.150), channel_id=1, source_target_pairs={{0,8},{2,10},{4,12},{6,14},{8,0},{10,2},{12,4},{14,6},{16,24},{18,... | collective-permute-start | bytes 5308424 | tf_op jit(solution)/shard_map/ppermute | solution.py:725
  275.2 6.4 %copy-start.6 = (bf16[4,192,1152]{2,1,0:T(8,128)(2,1)}, bf16[4,192,1152]{2,1,0:T(8,128)(2,1)S(1)}, u32[]{:S(2)}) copy-start(bf16[4,192,1152]{2,1,0:T(8,128)(2,1)S(1)} %collective-permute-done.8.refs_7_) | copy-start | bytes 5308420
  281.6 1.4 copy-start.3
  291.5 25.9 %collective-permute-start.9 = (bf16[144,3712]{1,0:T(8,128)(2,1)}, bf16[144,3712]{1,0:T(8,128)(2,1)S(1)}, u32[]{:S(2)}, u32[]{:S(2)}) collective-permute-start(bf16[144,3712]{1,0:T(8,128)(2,1)} %get-tuple-element.151.refs_1_), channel_id=1, source_target_pairs={{0,4},{2,6},{4,0},{6,2},{8,12},{10,14},{12,8},{14,10},{16,20},{18,... | collective-permute-start | bytes 3207176 | tf_op jit(solution)/shard_map/ppermute | solution.py:725
  291.8 25.6 %collective-permute-start.10 = (bf16[2,72,3584]{2,1,0:T(8,128)(2,1)}, bf16[2,72,3584]{2,1,0:T(8,128)(2,1)S(1)}, u32[]{:S(2)}, u32[]{:S(2)}) collective-permute-start(bf16[2,72,3584]{2,1,0:T(8,128)(2,1)} %get-tuple-element.158), channel_id=1, source_target_pairs={{0,8},{2,10},{4,12},{6,14},{8,0},{10,2},{12,4},{14,6},{16,24},{18,... | collective-permute-start | bytes 3096584 | tf_op jit(solution)/shard_map/ppermute | solution.py:725
  294.9 20.9 %collective-permute-start.11 = (bf16[2,192,1152]{2,1,0:T(8,128)(2,1)}, bf16[2,192,1152]{2,1,0:T(8,128)(2,1)}, u32[]{:S(2)}, u32[]{:S(2)}) collective-permute-start(bf16[2,192,1152]{2,1,0:T(8,128)(2,1)} %get-tuple-element.160), channel_id=1, source_target_pairs={{0,1},{1,0},{2,3},{3,2},{4,5},{5,4},{6,7},{7,6},{8,9},{9,8},{10,11... | collective-permute-start | bytes 2654216 | tf_op jit(solution)/shard_map/ppermute | solution.py:724
  312.3 43.6 %collective-permute-start.15 = (bf16[4,144,1152]{2,1,0:T(8,128)(2,1)}, bf16[4,144,1152]{2,1,0:T(8,128)(2,1)S(1)}, u32[]{:S(2)}, u32[]{:S(2)}) collective-permute-start(bf16[4,144,1152]{2,1,0:T(8,128)(2,1)} %get-tuple-element.155.refs_1_), channel_id=1, source_target_pairs={{0,2},{2,0},{4,6},{6,4},{8,10},{10,8},{12,14},{14,12},{16,18},{18,... | collective-permute-start | bytes 3981320 | tf_op jit(solution)/shard_map/ppermute | solution.py:725
  317.4 1.4 copy-start.9
  325.2 30.8 %collective-permute-start.12 = (bf16[72,3712]{1,0:T(8,128)(2,1)}, bf16[72,3712]{1,0:T(8,128)(2,1)S(1)}, u32[]{:S(2)}, u32[]{:S(2)}) collective-permute-start(bf16[72,3712]{1,0:T(8,128)(2,1)} %get-tuple-element.161.refs_1_), channel_id=1, source_target_pairs={{0,8},{2,10},{4,12},{6,14},{8,0},{10,2},{12,4},{14,6},{16,24},{18,... | collective-permute-start | bytes 1603592 | tf_op jit(solution)/shard_map/ppermute | solution.py:725
  326.9 29.0 %collective-permute-start.13 = (bf16[72,3584]{1,0:T(8,128)(2,1)}, bf16[72,3584]{1,0:T(8,128)(2,1)S(1)}, u32[]{:S(2)}, u32[]{:S(2)}) collective-permute-start(bf16[72,3584]{1,0:T(8,128)(2,1)} %get-tuple-element.167), channel_id=1, source_target_pairs={{0,1},{1,0},{2,3},{3,2},{4,5},{5,4},{6,7},{7,6},{8,9},{9,8},{10,11... | collective-permute-start | bytes 1548296 | tf_op jit(solution)/shard_map/ppermute | solution.py:724
  327.9 28.0 %collective-permute-start.14 = (bf16[192,1152]{1,0:T(8,128)(2,1)}, bf16[192,1152]{1,0:T(8,128)(2,1)S(1)}, u32[]{:S(2)}, u32[]{:S(2)}) collective-permute-start(bf16[192,1152]{1,0:T(8,128)(2,1)} %get-tuple-element.168), channel_id=1, source_target_pairs={{0,4},{2,6},{4,0},{6,2},{8,12},{10,14},{12,8},{14,10},{16,20},{18,... | collective-permute-start | bytes 1327112 | tf_op jit(solution)/shard_map/ppermute | solution.py:725
  356.0 1.5 copy-start.2
  357.5 6.6 %collective-permute-start.16 = (bf16[4,144,1152]{2,1,0:T(8,128)(2,1)}, bf16[4,144,1152]{2,1,0:T(8,128)(2,1)S(1)}, u32[]{:S(2)}, u32[]{:S(2)}) collective-permute-start(bf16[4,144,1152]{2,1,0:T(8,128)(2,1)} %get-tuple-element.176), channel_id=1, source_target_pairs={{0,2},{2,0},{4,6},{6,4},{8,10},{10,8},{12,14},{14,12},{16,18},{18,... | collective-permute-start | bytes 3981320 | tf_op jit(solution)/shard_map/ppermute | solution.py:725
  357.5 6.6 %collective-permute-start.17 = (bf16[4,144,1152]{2,1,0:T(8,128)(2,1)}, bf16[4,144,1152]{2,1,0:T(8,128)(2,1)S(1)}, u32[]{:S(2)}, u32[]{:S(2)}) collective-permute-start(bf16[4,144,1152]{2,1,0:T(8,128)(2,1)} %get-tuple-element.178), channel_id=1, source_target_pairs={{0,2},{2,0},{4,6},{6,4},{8,10},{10,8},{12,14},{14,12},{16,18},{18,... | collective-permute-start | bytes 3981320 | tf_op jit(solution)/shard_map/ppermute | solution.py:725
  362.4 40.1 %collective-permute-start.18 = (bf16[4,72,1152]{2,1,0:T(8,128)(2,1)}, bf16[4,72,1152]{2,1,0:T(8,128)(2,1)S(1)}, u32[]{:S(2)}, u32[]{:S(2)}) collective-permute-start(bf16[4,72,1152]{2,1,0:T(8,128)(2,1)} %get-tuple-element.174.refs_1_), channel_id=1, source_target_pairs={{0,8},{2,10},{4,12},{6,14},{8,0},{10,2},{12,4},{14,6},{16,24},{18,... | collective-permute-start | bytes 1990664 | tf_op jit(solution)/shard_map/ppermute | solution.py:725
  364.1 1.5 copy-start.8
  371.0 40.6 %collective-permute-start.21 = (bf16[2,144,1152]{2,1,0:T(8,128)(2,1)}, bf16[2,144,1152]{2,1,0:T(8,128)(2,1)S(1)}, u32[]{:S(2)}, u32[]{:S(2)}) collective-permute-start(bf16[2,144,1152]{2,1,0:T(8,128)(2,1)} %get-tuple-element.179.refs_1_), channel_id=1, source_target_pairs={{0,4},{2,6},{4,0},{6,2},{8,12},{10,14},{12,8},{14,10},{16,20},{18,... | collective-permute-start | bytes 1990664 | tf_op jit(solution)/shard_map/ppermute | solution.py:725
  373.0 45.5 %collective-permute-start.23 = (bf16[2,144,1152]{2,1,0:T(8,128)(2,1)}, bf16[2,144,1152]{2,1,0:T(8,128)(2,1)S(1)}, u32[]{:S(2)}, u32[]{:S(2)}) collective-permute-start(bf16[2,144,1152]{2,1,0:T(8,128)(2,1)} %get-tuple-element.198), channel_id=1, source_target_pairs={{0,1},{1,0},{2,3},{3,2},{4,5},{5,4},{6,7},{7,6},{8,9},{9,8},{10,11... | collective-permute-start | bytes 1990664 | tf_op jit(solution)/shard_map/ppermute | solution.py:724
  378.0 46.8 %collective-permute-start.24 = (bf16[36,10752]{1,0:T(8,128)(2,1)}, bf16[36,10752]{1,0:T(8,128)(2,1)S(1)}, u32[]{:S(2)}, u32[]{:S(2)}) collective-permute-start(bf16[36,10752]{1,0:T(8,128)(2,1)} %get-tuple-element.185.refs_1_), channel_id=1, source_target_pairs={{0,16},{2,18},{4,20},{6,22},{8,24},{10,26},{12,28},{14,30},{16,0},... | collective-permute-start | bytes 2322440 | tf_op jit(solution)/shard_map/ppermute | solution.py:725
  401.4 4.8 %collective-permute-start.19 = (bf16[8,3584]{1,0:T(8,128)(2,1)}, bf16[8,3584]{1,0:T(8,128)(2,1)S(1)}, u32[]{:S(2)}, u32[]{:S(2)}) collective-permute-start(bf16[8,3584]{1,0:T(8,128)(2,1)} %get-tuple-element.194), channel_id=1, source_target_pairs={{0,1},{1,0},{2,3},{3,2},{4,5},{5,4},{6,7},{7,6},{8,9},{9,8},{10,11... | collective-permute-start | bytes 172040 | tf_op jit(solution)/shard_map/ppermute | solution.py:724
  409.0 6.6 %collective-permute-start.22 = (bf16[8,4736]{1,0:T(8,128)(2,1)}, bf16[8,4736]{1,0:T(8,128)(2,1)S(1)}, u32[]{:S(2)}, u32[]{:S(2)}) collective-permute-start(bf16[8,4736]{1,0:T(8,128)(2,1)} %pair.1.refs_1_.refs_2_), channel_id=1, source_target_pairs={{0,4},{2,6},{4,0},{6,2},{8,12},{10,14},{12,8},{14,10},{16,20},{18,... | collective-permute-start | bytes 227336 | tf_op jit(solution)/shard_map/ppermute | solution.py:725
  410.7 18.5 %collective-permute-start.27 = (bf16[2,72,1152]{2,1,0:T(8,128)(2,1)}, bf16[2,72,1152]{2,1,0:T(8,128)(2,1)S(1)}, u32[]{:S(2)}, u32[]{:S(2)}) collective-permute-start(bf16[2,72,1152]{2,1,0:T(8,128)(2,1)} %get-tuple-element.192.refs_1_), channel_id=1, source_target_pairs={{0,1},{1,0},{2,3},{3,2},{4,5},{5,4},{6,7},{7,6},{8,9},{9,8},{10,11... | collective-permute-start | bytes 995336 | tf_op jit(solution)/shard_map/ppermute | solution.py:724
  422.3 11.0 %collective-permute-start.26 = (bf16[144,1152]{1,0:T(8,128)(2,1)}, bf16[144,1152]{1,0:T(8,128)(2,1)S(1)}, u32[]{:S(2)}, u32[]{:S(2)}) collective-permute-start(bf16[144,1152]{1,0:T(8,128)(2,1)} %get-tuple-element.199.refs_1_), channel_id=1, source_target_pairs={{0,4},{2,6},{4,0},{6,2},{8,12},{10,14},{12,8},{14,10},{16,20},{18,... | collective-permute-start | bytes 995336 | tf_op jit(solution)/shard_map/ppermute | solution.py:725
  422.8 11.2 %collective-permute-start.25 = (bf16[2,72,1152]{2,1,0:T(8,128)(2,1)}, bf16[2,72,1152]{2,1,0:T(8,128)(2,1)S(1)}, u32[]{:S(2)}, u32[]{:S(2)}) collective-permute-start(bf16[2,72,1152]{2,1,0:T(8,128)(2,1)} %get-tuple-element.196.refs_1_), channel_id=1, source_target_pairs={{0,8},{2,10},{4,12},{6,14},{8,0},{10,2},{12,4},{14,6},{16,24},{18,... | collective-permute-start | bytes 995336 | tf_op jit(solution)/shard_map/ppermute | solution.py:725
  424.8 8.6 %collective-permute-start.28 = (bf16[16,4736]{1,0:T(8,128)(2,1)}, bf16[16,4736]{1,0:T(8,128)(2,1)S(1)}, u32[]{:S(2)}, u32[]{:S(2)}) collective-permute-start(bf16[16,4736]{1,0:T(8,128)(2,1)} %every.1.refs_1_.refs_8_), channel_id=1, source_target_pairs={{0,16},{2,18},{4,20},{6,22},{8,24},{10,26},{12,28},{14,30},{16,0},... | collective-permute-start | bytes 454664 | tf_op jit(solution)/shard_map/ppermute | solution.py:725
  429.2 13.6 %copy-start.10 = (bf16[8,4736]{1,0:T(8,128)(2,1)S(1)}, bf16[8,4736]{1,0:T(8,128)(2,1)}, u32[]{:S(2)}) copy-start(bf16[8,4736]{1,0:T(8,128)(2,1)} %pair.1.refs_1_.refs_2_) | copy-start | bytes 227332
  429.2 4.7 copy-start.17
  438.4 9.9 %collective-permute-start.30 = (bf16[72,1152]{1,0:T(8,128)(2,1)}, bf16[72,1152]{1,0:T(8,128)(2,1)S(1)}, u32[]{:S(2)}, u32[]{:S(2)}) collective-permute-start(bf16[72,1152]{1,0:T(8,128)(2,1)} %get-tuple-element.208), channel_id=1, source_target_pairs={{0,8},{2,10},{4,12},{6,14},{8,0},{10,2},{12,4},{14,6},{16,24},{18,... | collective-permute-start | bytes 497672 | tf_op jit(solution)/shard_map/ppermute | solution.py:725
  439.1 9.3 %collective-permute-start.31 = (bf16[72,1152]{1,0:T(8,128)(2,1)}, bf16[72,1152]{1,0:T(8,128)(2,1)S(1)}, u32[]{:S(2)}, u32[]{:S(2)}) collective-permute-start(bf16[72,1152]{1,0:T(8,128)(2,1)} %get-tuple-element.210), channel_id=1, source_target_pairs={{0,4},{2,6},{4,0},{6,2},{8,12},{10,14},{12,8},{14,10},{16,20},{18,... | collective-permute-start | bytes 497672 | tf_op jit(solution)/shard_map/ppermute | solution.py:725
  440.1 8.2 %collective-permute-start.29 = (bf16[72,1152]{1,0:T(8,128)(2,1)}, bf16[72,1152]{1,0:T(8,128)(2,1)S(1)}, u32[]{:S(2)}, u32[]{:S(2)}) collective-permute-start(bf16[72,1152]{1,0:T(8,128)(2,1)} %get-tuple-element.205.refs_1_), channel_id=1, source_target_pairs={{0,1},{1,0},{2,3},{3,2},{4,5},{5,4},{6,7},{7,6},{8,9},{9,8},{10,11... | collective-permute-start | bytes 497672 | tf_op jit(solution)/shard_map/ppermute | solution.py:724
  441.3 8.6 %collective-permute-start.32 = (bf16[32,4736]{1,0:T(8,128)(2,1)}, bf16[32,4736]{1,0:T(8,128)(2,1)S(1)}, u32[]{:S(2)}, u32[]{:S(2)}) collective-permute-start(bf16[32,4736]{1,0:T(8,128)(2,1)} %get-tuple-element.211.refs_8_), channel_id=1, source_target_pairs={{0,8},{2,10},{4,12},{6,14},{8,0},{10,2},{12,4},{14,6},{16,24},{18,... | collective-permute-start | bytes 909320 | tf_op jit(solution)/shard_map/ppermute | solution.py:725
  448.3 9.6 %copy-start.28 = (f32[1,4,1152]{2,1,0:T(4,128)S(1)}, f32[1,4,1152]{2,1,0:T(4,128)}, u32[]{:S(2)}) copy-start(f32[1,4,1152]{2,1,0:T(4,128)} %param.20) | copy-start | bytes 55300
  448.3 1.6 copy-start.23
  448.3 1.6 copy-start.24
  448.4 1.5 copy-start.25
  454.2 16.7 %collective-permute-start.34 = (bf16[64,4736]{1,0:T(8,128)(2,1)}, bf16[64,4736]{1,0:T(8,128)(2,1)S(1)}, u32[]{:S(2)}, u32[]{:S(2)}) collective-permute-start(bf16[64,4736]{1,0:T(8,128)(2,1)} %get-tuple-element.214.refs_4_), channel_id=1, source_target_pairs={{0,2},{2,0},{4,6},{6,4},{8,10},{10,8},{12,14},{14,12},{16,18},{18,... | collective-permute-start | bytes 1818632 | tf_op jit(solution)/shard_map/ppermute | solution.py:725
  454.2 3.7 collective-permute-start.20
  455.1 15.7 %collective-permute-start.33 = (bf16[36,3456]{1,0:T(8,128)(2,1)}, bf16[36,3456]{1,0:T(8,128)(2,1)S(1)}, u32[]{:S(2)}, u32[]{:S(2)}) collective-permute-start(bf16[36,3456]{1,0:T(8,128)(2,1)} %get-tuple-element.212.refs_1_), channel_id=1, source_target_pairs={{0,16},{2,18},{4,20},{6,22},{8,24},{10,26},{12,28},{14,30},{16,0},... | collective-permute-start | bytes 746504 | tf_op jit(solution)/shard_map/ppermute | solution.py:725
  (18 other events, 15.9 us)

commit v10 on v9

--- a/solution.py
+++ b/solution.py
@@ -17,6 +17,7 @@
 TB = 512
 WIN = 256
 TOGETHER = 4
+CHUNKS = 3
 SCORE_SCALE = float(HD**-0.5)
 SCORE_LOG2 = float(np.log2(np.e) * HD**-0.5)
 VMEM = 60 * 2**20
@@ -737,10 +738,9 @@
             outs += shapes
         size = sum(arg.size for arg in args)
         split = all(
-            isinstance(stream, Stream) and stream.side is None and stream.own.shape[-1] % 384 == 0
-            for stream in streams
+            isinstance(stream, Stream) and stream.own.shape[-1] % (CHUNKS * 128) == 0 for stream in streams
         )
-        steps = 3 if split and size > 2**20 else 1
+        steps = CHUNKS if split and size > 2**20 else 1
         results = self.call(
             functools.partial(step_kernel, plans=plans),
             (steps,),
@@ -790,8 +790,9 @@
         at = self.lead.index(bit) if bit in self.lead else None
         cuts = [None]
         if self.side is not None:
-            cuts = [(0, dims[-1]), self.side[1]]
-            dims = dims[:-1] + (dims[-1] + self.side[1][1] - self.side[1][0],)
+            cut = self.side[1]
+            cuts = [(0, dims[-1] // CHUNKS), cut]
+            dims = dims[:-1] + (dims[-1] + CHUNKS * (cut[1] - cut[0]),)
         function = functools.partial(
             split_step, lead=dims[0] if self.lead else 0, at=at, bit=self.r.bit_of(bit), pair_rows=self.pair_rows,
             cuts=cuts,
@@ -992,9 +993,9 @@
     seg_spec = rows_of((SEG, width))
     output, grad_mid, grad_attended, dot_term, sums_b, out_send, out_own = call(
         middle_kernel,
-        (count // SEG,),
-        [seg_spec] * 6 + [rows_of((8, width // 8, SEG), 2), mod_spec, square, fixed(gather.shape)],
-        [seg_spec] * 3 + [rows_of((128, SEG), 1), fixed((slots_n, 4 * width))] + square_send,
+        (blocks,),
+        [token_spec] * 6 + [units_spec, mod_spec, square, fixed(gather.shape)],
+        [token_spec] * 3 + [rows_of((128, TB), 1), fixed((slots_n, 4 * width))] + square_send,
         [token_bf16, token_f32, token_bf16, lane_rows, shape((slots_n, 4 * width), f32)] + square_shapes,
         (mid, ffn, grad_mod_ffn, cot, attn, attended, out_units, modulation, w_out, gather),
         scalars=slots_core,
@@ -1003,9 +1004,9 @@
     )
     out = Stream(reducer, out_send, out_own, 1)
     early = [gate, up, down]
-    middle_cut = width // 256 * 128 + 128
-    gate.join(out, (0, middle_cut))
-    up.join(out, (middle_cut, width))
+    out_chunk = width // CHUNKS
+    gate.join(out, (0, 128))
+    up.join(out, (128, out_chunk))
     reducer.fold(early, "early")
 
     def attend_back(first, end, name):
@@ -1071,16 +1072,19 @@
     rows_d = width // n_dev
     merged = Merged([gate, up, down])
     third = rows_ff // 3
-    gate_end = ff + middle_cut
-    up_end = gate_end + ff + width - middle_cut
+    ff_chunk = ff // CHUNKS
+    gate_end = ff + CHUNKS * 128
+    up_end = gate_end + ff + width - CHUNKS * 128
     merged.places = [
-        (0, 0, 0, ff, None),
-        (2, 0, ff, gate_end, None),
-        (1, 0, gate_end, gate_end + ff, None),
-        (2, middle_cut, gate_end + ff, up_end, None),
-    ] + [
         (3, 0, up_end + i * width, up_end + (i + 1) * width, (i * third, (i + 1) * third)) for i in range(3)
     ]
+    for j in range(CHUNKS):
+        at = j * (gate_end // CHUNKS)
+        merged.places.append((0, j * ff_chunk, at, at + ff_chunk, None))
+        merged.places.append((2, j * out_chunk, at + ff_chunk, at + ff_chunk + 128, None))
+        at = gate_end + j * ((up_end - gate_end) // CHUNKS)
+        merged.places.append((1, j * ff_chunk, at, at + ff_chunk, None))
+        merged.places.append((2, j * out_chunk + 128, at + ff_chunk, at + ff_chunk + out_chunk - 128, None))
     merged.shapes = [shape((rows_d, ff), f32)] * 2 + [shape((rows_d, width), f32), shape((rows_ff, width), f32)]
     early = [merged]
     reducer.fold(early, "early")

time: 481 us -> 485 us (level)
    ppermute x25, starting transfers between devices: 23.4 us -> 36.6 us  [swap(): lax.ppermute(arr, 'dp', [(i, i ^ 1 << bit) for i in range(self.n_dp)])]
    ppermute x10, starting transfers between devices: 23.7 us -> 14.8 us  [swap(): return lax.ppermute(arr, 'mod', [(i, i ^ 1) for i in range(self.n_mod)])]
where the time goes in v10:
time: 485 us; the launch traced here: 481 us
  Pallas kernels  348 us (72%)
  starting transfers between devices  51.4 us (11%)
  waiting for transfers between devices  48.9 us (10%)
  local copies, waits for them, and re-layouts  18.2 us (4%)
  matrix products  9.81 us (2%)
    pallas_call x26, Pallas kernels, __call__(): pl.pallas_call(body, grid_spec=spec, input_output_aliases=aliases or {},...  348 us
    ppermute x25, waiting for transfers between devices, swap(): lax.ppermute(arr, 'dp', [(i, i ^ 1 << bit) for i in range(self.n_dp)])  43 us
    ppermute x25, starting transfers between devices, swap(): lax.ppermute(arr, 'dp', [(i, i ^ 1 << bit) for i in range(self.n_dp)])  36.6 us
    ppermute x10, starting transfers between devices, swap(): return lax.ppermute(arr, 'mod', [(i, i ^ 1) for i in range(self.n_mod)])  14.8 us
    unnamed x62, local copies, waits for them, and re-layouts  13.6 us
  transfers between devices with their start and end apart: 35, of which 11 were waited for; matrix products, arithmetic and copies ran while one was open for 2% of the time, Pallas kernels for 32%

profile of v10, /device:TPU:0, one launch (start us, length us, event | category | flops | bytes accessed | tf_op | source)
XLA Modules:
  0.0 480.6 jit_solution(4192399676245659492)
XLA Ops:
  0.6 3.0 collective-permute-start
  6.5 4.4 convolution_convert_fusion
  11.0 2.1 collective-permute-start.1
  16.3 28.1 %project.1 = (bf16[8,144,1024]{2,1,0:T(8,128)(2,1)}, f32[1024,2304]{1,0:T(8,128)}, f32[1024,256]{1,0:T(8,128)}, bf16[1024,1152]{1,0:T(8,128)(2,1)}, bf16[1024,11...) custom-call(s32[4]{0:T(128)} %bitcast.49, bf16[1024,1152]{1,0:T(8,128)(2,1)} %bitcast.37, ...), custom_call_target="tpu_custom_call" | custom-call | flops 1 | bytes 1 | tf_op jit(solution)/shard_map/project/pallas_call | solution.py:682
  44.4 15.4 %attend.1 = (f32[1024,1152]{1,0:T(8,128)}, f32[1024,128]{1,0:T(8,128)}) custom-call(s32[4]{0:T(128)} %bitcast.50, bf16[8,144,1024]{2,1,0:T(8,128)(2,1)} %get-tuple-element.116.refs_1_.refs_2_.refs_10_, bf16[1024,1152]{1,0:T(8,128)(2,1)} %get-tuple-element.117.refs_2_.refs_8_, bf16[1024,1152]{1,0:T(8,128)(2,1)} %get-tuple-element.118.refs_3_.refs_9_, ...), custom_call_target="tpu_custom_call" | custom-call | flops 1 | bytes 1 | tf_op jit(solution)/shard_map/attend/pallas_call | solution.py:682
  59.8 20.2 %mix.1 = (bf16[1024,1152]{1,0:T(8,128)(2,1)}, f32[128,1024]{1,0:T(8,128)}, bf16[1024,1152]{1,0:T(8,128)(2,1)}, f32[1024,1152]{1,0:T(8,128)}, bf16[1024,1152]{1,0...) custom-call(s32[4]{0:T(128)} %bitcast.51, ...), custom_call_target="tpu_custom_call" | custom-call | flops 1 | bytes 1 | tf_op jit(solution)/shard_map/mix/pallas_call | solution.py:682
  80.0 95.5 %ffn.1 = (bf16[4,144,3072]{2,1,0:T(8,128)(2,1)}, bf16[4,144,3072]{2,1,0:T(8,128)(2,1)}, bf16[4,144,3072]{2,1,0:T(8,128)(2,1)}, bf16[4,144,3072]{2,1,0:T(8,128)(2...) custom-call(s32[5]{0:T(128)} %stack.48.refs_0_, ...), custom_call_target="tpu_custom_call" | custom-call | flops 1 | bytes 1 | tf_op jit(solution)/shard_map/ffn/pallas_call | solution.py:682
  175.5 10.3 %collective-permute-start.4 = (bf16[4,144,3072]{2,1,0:T(8,128)(2,1)}, bf16[4,144,3072]{2,1,0:T(8,128)(2,1)}, u32[]{:S(2)}, u32[]{:S(2)}) collective-permute-start(bf16[4,144,3072]{2,1,0:T(8,128)(2,1)} %get-tuple-element.137), channel_id=1, source_target_pairs={{0,2},{2,0},{4,6},{6,4},{8,10},{10,8},{12,14},{14,12},{16,18},{18,... | collective-permute-start | bytes 10616840 | tf_op jit(solution)/shard_map/ppermute | solution.py:726
  186.9 25.3 %middle.1 = (bf16[1024,1152]{1,0:T(8,128)(2,1)}, f32[1024,1152]{1,0:T(8,128)}, bf16[1024,1152]{1,0:T(8,128)(2,1)}, f32[128,1024]{1,0:T(8,128)}, f32[4,4608]{1,0:...) custom-call(s32[6]{0:T(128)} %pad_add_fusion.refs_0_, ...), custom_call_target="tpu_custom_call" | custom-call | flops 1 | bytes 1 | tf_op jit(solution)/shard_map/middle/pallas_call | solution.py:682
  212.4 3.2 collective-permute-done.3.refs_5_.refs_9_
  216.7 15.1 %early.4 = (bf16[2,144,3456]{2,1,0:T(8,128)(2,1)}, bf16[2,144,3456]{2,1,0:T(8,128)(2,1)}, bf16[2,144,3840]{2,1,0:T(8,128)(2,1)}, bf16[2,144,3840]{2,1,0:T(8,128)...) custom-call(s32[5]{0:T(128)} %stack.48.refs_0_, bf16[1024,1152]{1,0:T(8,128)(2,1)} %get-tuple-element.132.refs_1_, ...), custom_call_target="tpu_custom_call" | custom-call | flops 1 | bytes 1 | tf_op jit(solution)/shard_map/early/pallas_call | solution.py:682
  231.8 3.3 collective-permute-start.7
  235.1 1.4 collective-permute-start.6
  236.5 23.5 %attend_back_0.1 = (f32[864,1024]{1,0:T(8,128)}, f32[1024,1024]{1,0:T(8,128)}, bf16[1024,1024]{1,0:T(8,128)(2,1)}) custom-call(s32[4]{0:T(128)} %bitcast.52, bf16[2,144,3456]{2,1,0:T(8,128)(2,1)} %get-tuple-element.140.refs_1_, bf16[1024,1152]{1,0:T(8,128)(2,1)} %get-tuple-element.117.refs_2_.refs_8_, bf16[1024,1152]{1,0:T(8,128)(2,1)} %get-tuple-element.118.refs_3_.refs_9_, ...), custom_call_target="tpu_custom_call" | custom-call | flops 1 | bytes 1 | tf_op jit(solution)/shard_map/attend_back_0/pallas_call | solution.py:682
  260.0 17.0 %collective-permute-done.8.refs_7_ = bf16[4,192,1152]{2,1,0:T(8,128)(2,1)S(1)} collective-permute-done((bf16[4,192,1152]{2,1,0:T(8,128)(2,1)}, bf16[4,192,1152]{2,1,0:T(8,128)(2,1)S(1)}, u32[]{:S(2)}, u32[]{:S(2)}) %collective-permute-start.8) | collective-permute-done | bytes 1769504 | tf_op jit(solution)/shard_map/ppermute | solution.py:726
  277.0 3.7 collective-permute-done.6.refs_3_
  280.7 3.2 collective-permute-done.7.refs_5_
  283.9 1.4 copy-done.4
  285.3 9.1 %early.5 = (bf16[144,3456]{1,0:T(8,128)(2,1)}, f32[144,3456]{1,0:T(8,128)}, bf16[2,72,3840]{2,1,0:T(8,128)(2,1)}, f32[2,72,3840]{2,1,0:T(8,128)}, bf16[2,192,115...) custom-call(s32[5]{0:T(128)} %stack.48.refs_0_, f32[864,1024]{1,0:T(8,128)} %get-tuple-element.145.refs_1_.refs_2_, ...), custom_call_target="tpu_custom_call" | custom-call | flops 1 | bytes 1 | tf_op jit(solution)/shard_map/early/pallas_call | solution.py:682
  294.4 1.9 collective-permute-start.10
  297.7 9.6 %attend_back_1.1 = (f32[288,1024]{1,0:T(8,128)}, f32[1024,384]{1,0:T(8,128)}, bf16[1024,384]{1,0:T(8,128)(2,1)}) custom-call(s32[4]{0:T(128)} %bitcast.53, bf16[144,3456]{1,0:T(8,128)(2,1)} %get-tuple-element.151.refs_1_, bf16[1024,1152]{1,0:T(8,128)(2,1)} %get-tuple-element.117.refs_2_.refs_8_, bf16[1024,1152]{1,0:T(8,128)(2,1)} %get-tuple-element.118.refs_3_.refs_9_, ...), custom_call_target="tpu_custom_call" | custom-call | flops 1 | bytes 1 | tf_op jit(solution)/shard_map/attend_back_1/pallas_call | solution.py:682
  307.4 7.4 %value.1 = (bf16[4,144,1152]{2,1,0:T(8,128)(2,1)}, bf16[4,144,1152]{2,1,0:T(8,128)(2,1)}) custom-call(s32[5]{0:T(128)} %stack.48.refs_0_, f32[288,1024]{1,0:T(8,128)} %get-tuple-element.152.refs_1_.refs_3_, bf16[8,144,1024]{2,1,0:T(8,128)(2,1)} %get-tuple-element.116.refs_1_.refs_2_.refs_10_, bf16[1024,1024]{1,0:T(8,128)(2,1)} %get-tuple-element.153.refs_3_.refs_4_, ...), custom_call_target="tpu_custom_call" | custom-call | flops 1 | bytes 1 | tf_op jit(solution)/shard_map/value/pallas_call | solution.py:682
  314.8 5.1 %collective-permute-start.15 = (bf16[4,144,1152]{2,1,0:T(8,128)(2,1)}, bf16[4,144,1152]{2,1,0:T(8,128)(2,1)S(1)}, u32[]{:S(2)}, u32[]{:S(2)}) collective-permute-start(bf16[4,144,1152]{2,1,0:T(8,128)(2,1)} %get-tuple-element.155.refs_1_), channel_id=1, source_target_pairs={{0,2},{2,0},{4,6},{6,4},{8,10},{10,8},{12,14},{14,12},{16,18},{18,... | collective-permute-start | bytes 3981320 | tf_op jit(solution)/shard_map/ppermute | solution.py:726
  321.8 6.7 %early.6 = (bf16[72,3456]{1,0:T(8,128)(2,1)}, f32[72,3456]{1,0:T(8,128)}, bf16[72,3840]{1,0:T(8,128)(2,1)}, f32[72,3840]{1,0:T(8,128)}, bf16[192,1152]{1,0:T(8,128)(2,1)}, /*index=5*/f32[192,1152]{1,0:T(8,128)}) custom-call(s32[5]{0:T(128)} %stack.48.refs_0_, bf16[4,144,1152]{2,1,0:T(8,128)(2,1)} %get-tuple-element.155.refs_1_, ...), custom_call_target="tpu_custom_call" | custom-call | flops 1 | bytes 1 | tf_op jit(solution)/shard_map/early/pallas_call | solution.py:682
  328.5 1.4 collective-permute-start.13
  331.8 27.7 %project_back.1 = (bf16[1024,1152]{1,0:T(8,128)(2,1)}, bf16[1024,1152]{1,0:T(8,128)(2,1)}, bf16[8,128]{1,0:T(8,128)(2,1)}, bf16[4,144,1152]{2,1,0:T(8,128)(2,1)}...) custom-call(s32[5]{0:T(128)} %stack.48.refs_0_, ...), custom_call_target="tpu_custom_call" | custom-call | flops 1 | bytes 1 | tf_op jit(solution)/shard_map/project_back/pallas_call | solution.py:682
  361.5 4.5 v.2
  366.0 1.9 collective-permute-start.18
  369.4 5.3 %late.3 = (bf16[2,144,1152]{2,1,0:T(8,128)(2,1)}, bf16[2,144,1152]{2,1,0:T(8,128)(2,1)}, bf16[2,144,1152]{2,1,0:T(8,128)(2,1)}, bf16[2,144,1152]{2,1,0:T(8,128)(2,1)}) custom-call(s32[5]{0:T(128)} %stack.48.refs_0_, bf16[4,72,1152]{2,1,0:T(8,128)(2,1)} %get-tuple-element.174.refs_1_, bf16[4,144,1152]{2,1,0:T(8,128)(2,1)} %get-tuple-element.175.refs_2_, ...), custom_call_target="tpu_custom_call" | custom-call | flops 1 | bytes 1 | tf_op jit(solution)/shard_map/late/pallas_call | solution.py:682
  376.1 5.0 %early.7 = (bf16[36,10752]{1,0:T(8,128)(2,1)}, f32[36,10752]{1,0:T(8,128)}) custom-call(s32[5]{0:T(128)} %stack.48.refs_0_, bf16[2,144,1152]{2,1,0:T(8,128)(2,1)} %get-tuple-element.179.refs_1_, f32[72,3456]{1,0:T(8,128)} %get-tuple-element.180.refs_2_, bf16[72,3456]{1,0:T(8,128)(2,1)} %get-tuple-element.171.refs_1_.refs_3_, ...), custom_call_target="tpu_custom_call" | custom-call | flops 1 | bytes 1 | tf_op jit(solution)/shard_map/early/pallas_call | solution.py:682
  381.2 2.9 collective-permute-start.24
  384.0 21.0 %input_back.1 = (bf16[1024,1152]{1,0:T(8,128)(2,1)}, bf16[8,3584]{1,0:T(8,128)(2,1)}, bf16[8,3584]{1,0:T(8,128)(2,1)}) custom-call(s32[6]{0:T(128)} %pad_add_fusion.refs_0_, bf16[36,10752]{1,0:T(8,128)(2,1)} %get-tuple-element.185.refs_1_, bf16[1024,1152]{1,0:T(8,128)(2,1)} %get-tuple-element.166.refs_0_.refs_2_, ...), custom_call_target="tpu_custom_call" | custom-call | flops 1 | bytes 1 | tf_op jit(solution)/shard_map/input_back/pallas_call | solution.py:682
  407.2 2.9 v.3
  410.7 2.2 pair.1.refs_1_.refs_2_
  415.2 3.1 q.1
  418.9 2.2 every.1.refs_1_.refs_8_
  422.0 3.0 k.1
  429.4 3.5 early_last.1
  432.9 2.6 collective-permute-done.28.refs_9_
  435.6 1.8 collective-permute-done.25.refs_3_
  438.1 3.7 late.4
  443.1 1.6 collective-permute-start.29
  445.9 5.4 %fusion = f32[8,1152]{1,0:T(8,128)S(1)} fusion(bf16[1152,3456]{1,0:T(8,128)(2,1)} %param.23, bf16[8,4736]{1,0:T(8,128)(2,1)S(1)} %copy-done.10), kind=kOutput, calls=%fused_computation.1 | convolution fusion | flops 63700992 | bytes 8054784 | tf_op jit(solution)/shard_map/nc,dc->nd/dot_general | solution.py:1117
  451.4 1.7 collective-permute-done.32.refs_9_
  453.8 3.6 late.5
  459.4 1.7 collective-permute-done.20
  461.7 12.5 %collective-permute-done.33.refs_3_ = bf16[36,3456]{1,0:T(8,128)(2,1)S(1)} collective-permute-done((bf16[36,3456]{1,0:T(8,128)(2,1)}, bf16[36,3456]{1,0:T(8,128)(2,1)S(1)}, u32[]{:S(2)}, u32[]{:S(2)}) %collective-permute-start.33) | collective-permute-done | bytes 248864 | tf_op jit(solution)/shard_map/ppermute | solution.py:726
  475.2 4.0 late_last.1
  (132 shorter events, 38.2 us)
Async XLA Ops:
  0.6 5.0 %collective-permute-start = (f32[4,1152]{1,0:T(4,128)}, f32[4,1152]{1,0:T(4,128)S(1)}, u32[]{:S(2)}, u32[]{:S(2)}) collective-permute-start(f32[4,1152]{1,0:T(4,128)} %bitcast.45), channel_id=1, source_target_pairs={{0,1},{1,0},{2,3},{3,2},{4,5},{5,4},{6,7},{7,6},{8,9},{9,8},{10,11... | collective-permute-start | bytes 55304 | tf_op jit(solution)/shard_map/ppermute | solution.py:725
  6.5 4.4 copy-start.22
  11.0 4.5 collective-permute-start.1
  80.0 106.3 %copy-start.30 = (s32[1,4]{1,0:T(1,128)S(1)}, s32[1,4]{1,0:T(1,128)}, u32[]{:S(2)}) copy-start(s32[1,4]{1,0:T(1,128)} %slice.20) | copy-start | bytes 52
  175.5 40.1 %collective-permute-start.4 = (bf16[4,144,3072]{2,1,0:T(8,128)(2,1)}, bf16[4,144,3072]{2,1,0:T(8,128)(2,1)}, u32[]{:S(2)}, u32[]{:S(2)}) collective-permute-start(bf16[4,144,3072]{2,1,0:T(8,128)(2,1)} %get-tuple-element.137), channel_id=1, source_target_pairs={{0,2},{2,0},{4,6},{6,4},{8,10},{10,8},{12,14},{14,12},{16,18},{18,... | collective-permute-start | bytes 10616840 | tf_op jit(solution)/shard_map/ppermute | solution.py:726
  185.8 29.8 %collective-permute-start.5 = (bf16[4,384,1152]{2,1,0:T(8,128)(2,1)}, bf16[4,384,1152]{2,1,0:T(8,128)(2,1)}, u32[]{:S(2)}, u32[]{:S(2)}) collective-permute-start(bf16[4,384,1152]{2,1,0:T(8,128)(2,1)} %bitcast.56), channel_id=1, source_target_pairs={{0,2},{2,0},{4,6},{6,4},{8,10},{10,8},{12,14},{14,12},{16,18},{18,... | collective-permute-start | bytes 10616840 | tf_op jit(solution)/shard_map/ppermute | solution.py:726
  185.8 29.8 %collective-permute-start.2 = (bf16[4,144,3072]{2,1,0:T(8,128)(2,1)}, bf16[4,144,3072]{2,1,0:T(8,128)(2,1)}, u32[]{:S(2)}, u32[]{:S(2)}) collective-permute-start(bf16[4,144,3072]{2,1,0:T(8,128)(2,1)} %get-tuple-element.126.refs_1_), channel_id=1, source_target_pairs={{0,2},{2,0},{4,6},{6,4},{8,10},{10,8},{12,14},{14,12},{16,18},{18,... | collective-permute-start | bytes 10616840 | tf_op jit(solution)/shard_map/ppermute | solution.py:726
  212.3 3.3 collective-permute-start.3
  231.8 52.1 %collective-permute-start.7 = (bf16[2,144,3840]{2,1,0:T(8,128)(2,1)}, bf16[2,144,3840]{2,1,0:T(8,128)(2,1)S(1)}, u32[]{:S(2)}, u32[]{:S(2)}) collective-permute-start(bf16[2,144,3840]{2,1,0:T(8,128)(2,1)} %get-tuple-element.148), channel_id=1, source_target_pairs={{0,4},{2,6},{4,0},{6,2},{8,12},{10,14},{12,8},{14,10},{16,20},{18,... | collective-permute-start | bytes 6635528 | tf_op jit(solution)/shard_map/ppermute | solution.py:726
  235.1 45.6 %collective-permute-start.6 = (bf16[2,144,3456]{2,1,0:T(8,128)(2,1)}, bf16[2,144,3456]{2,1,0:T(8,128)(2,1)}, u32[]{:S(2)}, u32[]{:S(2)}) collective-permute-start(bf16[2,144,3456]{2,1,0:T(8,128)(2,1)} %get-tuple-element.140.refs_1_), channel_id=1, source_target_pairs={{0,1},{1,0},{2,3},{3,2},{4,5},{5,4},{6,7},{7,6},{8,9},{9,8},{10,11... | collective-permute-start | bytes 5971976 | tf_op jit(solution)/shard_map/ppermute | solution.py:725
  236.5 40.5 %collective-permute-start.8 = (bf16[4,192,1152]{2,1,0:T(8,128)(2,1)}, bf16[4,192,1152]{2,1,0:T(8,128)(2,1)S(1)}, u32[]{:S(2)}, u32[]{:S(2)}) collective-permute-start(bf16[4,192,1152]{2,1,0:T(8,128)(2,1)} %get-tuple-element.150), channel_id=1, source_target_pairs={{0,8},{2,10},{4,12},{6,14},{8,0},{10,2},{12,4},{14,6},{16,24},{18,... | collective-permute-start | bytes 5308424 | tf_op jit(solution)/shard_map/ppermute | solution.py:726
  277.0 6.9 %copy-start.6 = (bf16[4,192,1152]{2,1,0:T(8,128)(2,1)}, bf16[4,192,1152]{2,1,0:T(8,128)(2,1)S(1)}, u32[]{:S(2)}) copy-start(bf16[4,192,1152]{2,1,0:T(8,128)(2,1)S(1)} %collective-permute-done.8.refs_7_) | copy-start | bytes 5308420
  294.4 26.4 %collective-permute-start.10 = (bf16[2,72,3840]{2,1,0:T(8,128)(2,1)}, bf16[2,72,3840]{2,1,0:T(8,128)(2,1)S(1)}, u32[]{:S(2)}, u32[]{:S(2)}) collective-permute-start(bf16[2,72,3840]{2,1,0:T(8,128)(2,1)} %get-tuple-element.158), channel_id=1, source_target_pairs={{0,8},{2,10},{4,12},{6,14},{8,0},{10,2},{12,4},{14,6},{16,24},{18,... | collective-permute-start | bytes 3317768 | tf_op jit(solution)/shard_map/ppermute | solution.py:726
  296.3 23.6 %collective-permute-start.9 = (bf16[144,3456]{1,0:T(8,128)(2,1)}, bf16[144,3456]{1,0:T(8,128)(2,1)S(1)}, u32[]{:S(2)}, u32[]{:S(2)}) collective-permute-start(bf16[144,3456]{1,0:T(8,128)(2,1)} %get-tuple-element.151.refs_1_), channel_id=1, source_target_pairs={{0,4},{2,6},{4,0},{6,2},{8,12},{10,14},{12,8},{14,10},{16,20},{18,... | collective-permute-start | bytes 2985992 | tf_op jit(solution)/shard_map/ppermute | solution.py:726
  296.6 23.3 %collective-permute-start.11 = (bf16[2,192,1152]{2,1,0:T(8,128)(2,1)}, bf16[2,192,1152]{2,1,0:T(8,128)(2,1)}, u32[]{:S(2)}, u32[]{:S(2)}) collective-permute-start(bf16[2,192,1152]{2,1,0:T(8,128)(2,1)} %get-tuple-element.160), channel_id=1, source_target_pairs={{0,1},{1,0},{2,3},{3,2},{4,5},{5,4},{6,7},{7,6},{8,9},{9,8},{10,11... | collective-permute-start | bytes 2654216 | tf_op jit(solution)/shard_map/ppermute | solution.py:725
  314.8 44.7 %collective-permute-start.15 = (bf16[4,144,1152]{2,1,0:T(8,128)(2,1)}, bf16[4,144,1152]{2,1,0:T(8,128)(2,1)S(1)}, u32[]{:S(2)}, u32[]{:S(2)}) collective-permute-start(bf16[4,144,1152]{2,1,0:T(8,128)(2,1)} %get-tuple-element.155.refs_1_), channel_id=1, source_target_pairs={{0,2},{2,0},{4,6},{6,4},{8,10},{10,8},{12,14},{14,12},{16,18},{18,... | collective-permute-start | bytes 3981320 | tf_op jit(solution)/shard_map/ppermute | solution.py:726
  328.5 31.0 %collective-permute-start.13 = (bf16[72,3840]{1,0:T(8,128)(2,1)}, bf16[72,3840]{1,0:T(8,128)(2,1)S(1)}, u32[]{:S(2)}, u32[]{:S(2)}) collective-permute-start(bf16[72,3840]{1,0:T(8,128)(2,1)} %get-tuple-element.167), channel_id=1, source_target_pairs={{0,1},{1,0},{2,3},{3,2},{4,5},{5,4},{6,7},{7,6},{8,9},{9,8},{10,11... | collective-permute-start | bytes 1658888 | tf_op jit(solution)/shard_map/ppermute | solution.py:725
  330.0 29.5 %collective-permute-start.12 = (bf16[72,3456]{1,0:T(8,128)(2,1)}, bf16[72,3456]{1,0:T(8,128)(2,1)S(1)}, u32[]{:S(2)}, u32[]{:S(2)}) collective-permute-start(bf16[72,3456]{1,0:T(8,128)(2,1)} %get-tuple-element.161.refs_1_), channel_id=1, source_target_pairs={{0,8},{2,10},{4,12},{6,14},{8,0},{10,2},{12,4},{14,6},{16,24},{18,... | collective-permute-start | bytes 1493000 | tf_op jit(solution)/shard_map/ppermute | solution.py:726
  331.0 28.4 %collective-permute-start.14 = (bf16[192,1152]{1,0:T(8,128)(2,1)}, bf16[192,1152]{1,0:T(8,128)(2,1)S(1)}, u32[]{:S(2)}, u32[]{:S(2)}) collective-permute-start(bf16[192,1152]{1,0:T(8,128)(2,1)} %get-tuple-element.168), channel_id=1, source_target_pairs={{0,4},{2,6},{4,0},{6,2},{8,12},{10,14},{12,8},{14,10},{16,20},{18,... | collective-permute-start | bytes 1327112 | tf_op jit(solution)/shard_map/ppermute | solution.py:726
  359.5 1.5 copy-start.3
  361.0 6.9 %collective-permute-start.16 = (bf16[4,144,1152]{2,1,0:T(8,128)(2,1)}, bf16[4,144,1152]{2,1,0:T(8,128)(2,1)S(1)}, u32[]{:S(2)}, u32[]{:S(2)}) collective-permute-start(bf16[4,144,1152]{2,1,0:T(8,128)(2,1)} %get-tuple-element.176), channel_id=1, source_target_pairs={{0,2},{2,0},{4,6},{6,4},{8,10},{10,8},{12,14},{14,12},{16,18},{18,... | collective-permute-start | bytes 3981320 | tf_op jit(solution)/shard_map/ppermute | solution.py:726
  361.0 6.9 %collective-permute-start.17 = (bf16[4,144,1152]{2,1,0:T(8,128)(2,1)}, bf16[4,144,1152]{2,1,0:T(8,128)(2,1)S(1)}, u32[]{:S(2)}, u32[]{:S(2)}) collective-permute-start(bf16[4,144,1152]{2,1,0:T(8,128)(2,1)} %get-tuple-element.178), channel_id=1, source_target_pairs={{0,2},{2,0},{4,6},{6,4},{8,10},{10,8},{12,14},{14,12},{16,18},{18,... | collective-permute-start | bytes 3981320 | tf_op jit(solution)/shard_map/ppermute | solution.py:726
  366.0 40.4 %collective-permute-start.18 = (bf16[4,72,1152]{2,1,0:T(8,128)(2,1)}, bf16[4,72,1152]{2,1,0:T(8,128)(2,1)S(1)}, u32[]{:S(2)}, u32[]{:S(2)}) collective-permute-start(bf16[4,72,1152]{2,1,0:T(8,128)(2,1)} %get-tuple-element.174.refs_1_), channel_id=1, source_target_pairs={{0,8},{2,10},{4,12},{6,14},{8,0},{10,2},{12,4},{14,6},{16,24},{18,... | collective-permute-start | bytes 1990664 | tf_op jit(solution)/shard_map/ppermute | solution.py:726
  367.9 1.5 copy-start.8
  374.8 39.5 %collective-permute-start.21 = (bf16[2,144,1152]{2,1,0:T(8,128)(2,1)}, bf16[2,144,1152]{2,1,0:T(8,128)(2,1)S(1)}, u32[]{:S(2)}, u32[]{:S(2)}) collective-permute-start(bf16[2,144,1152]{2,1,0:T(8,128)(2,1)} %get-tuple-element.179.refs_1_), channel_id=1, source_target_pairs={{0,4},{2,6},{4,0},{6,2},{8,12},{10,14},{12,8},{14,10},{16,20},{18,... | collective-permute-start | bytes 1990664 | tf_op jit(solution)/shard_map/ppermute | solution.py:726
  375.1 46.1 %collective-permute-start.23 = (bf16[2,144,1152]{2,1,0:T(8,128)(2,1)}, bf16[2,144,1152]{2,1,0:T(8,128)(2,1)S(1)}, u32[]{:S(2)}, u32[]{:S(2)}) collective-permute-start(bf16[2,144,1152]{2,1,0:T(8,128)(2,1)} %get-tuple-element.198), channel_id=1, source_target_pairs={{0,1},{1,0},{2,3},{3,2},{4,5},{5,4},{6,7},{7,6},{8,9},{9,8},{10,11... | collective-permute-start | bytes 1990664 | tf_op jit(solution)/shard_map/ppermute | solution.py:725
  381.2 47.3 %collective-permute-start.24 = (bf16[36,10752]{1,0:T(8,128)(2,1)}, bf16[36,10752]{1,0:T(8,128)(2,1)S(1)}, u32[]{:S(2)}, u32[]{:S(2)}) collective-permute-start(bf16[36,10752]{1,0:T(8,128)(2,1)} %get-tuple-element.185.refs_1_), channel_id=1, source_target_pairs={{0,16},{2,18},{4,20},{6,22},{8,24},{10,26},{12,28},{14,30},{16,0},... | collective-permute-start | bytes 2322440 | tf_op jit(solution)/shard_map/ppermute | solution.py:726
  405.0 5.1 %collective-permute-start.19 = (bf16[8,3584]{1,0:T(8,128)(2,1)}, bf16[8,3584]{1,0:T(8,128)(2,1)S(1)}, u32[]{:S(2)}, u32[]{:S(2)}) collective-permute-start(bf16[8,3584]{1,0:T(8,128)(2,1)} %get-tuple-element.194), channel_id=1, source_target_pairs={{0,1},{1,0},{2,3},{3,2},{4,5},{5,4},{6,7},{7,6},{8,9},{9,8},{10,11... | collective-permute-start | bytes 172040 | tf_op jit(solution)/shard_map/ppermute | solution.py:725
  412.9 5.4 %collective-permute-start.22 = (bf16[8,4736]{1,0:T(8,128)(2,1)}, bf16[8,4736]{1,0:T(8,128)(2,1)S(1)}, u32[]{:S(2)}, u32[]{:S(2)}) collective-permute-start(bf16[8,4736]{1,0:T(8,128)(2,1)} %pair.1.refs_1_.refs_2_), channel_id=1, source_target_pairs={{0,4},{2,6},{4,0},{6,2},{8,12},{10,14},{12,8},{14,10},{16,20},{18,... | collective-permute-start | bytes 227336 | tf_op jit(solution)/shard_map/ppermute | solution.py:726
  413.7 19.2 %collective-permute-start.27 = (bf16[2,72,1152]{2,1,0:T(8,128)(2,1)}, bf16[2,72,1152]{2,1,0:T(8,128)(2,1)S(1)}, u32[]{:S(2)}, u32[]{:S(2)}) collective-permute-start(bf16[2,72,1152]{2,1,0:T(8,128)(2,1)} %get-tuple-element.192.refs_1_), channel_id=1, source_target_pairs={{0,1},{1,0},{2,3},{3,2},{4,5},{5,4},{6,7},{7,6},{8,9},{9,8},{10,11... | collective-permute-start | bytes 995336 | tf_op jit(solution)/shard_map/ppermute | solution.py:725
  425.1 10.5 %collective-permute-start.26 = (bf16[144,1152]{1,0:T(8,128)(2,1)}, bf16[144,1152]{1,0:T(8,128)(2,1)S(1)}, u32[]{:S(2)}, u32[]{:S(2)}) collective-permute-start(bf16[144,1152]{1,0:T(8,128)(2,1)} %get-tuple-element.199.refs_1_), channel_id=1, source_target_pairs={{0,4},{2,6},{4,0},{6,2},{8,12},{10,14},{12,8},{14,10},{16,20},{18,... | collective-permute-start | bytes 995336 | tf_op jit(solution)/shard_map/ppermute | solution.py:726
  426.4 10.9 %collective-permute-start.25 = (bf16[2,72,1152]{2,1,0:T(8,128)(2,1)}, bf16[2,72,1152]{2,1,0:T(8,128)(2,1)S(1)}, u32[]{:S(2)}, u32[]{:S(2)}) collective-permute-start(bf16[2,72,1152]{2,1,0:T(8,128)(2,1)} %get-tuple-element.196.refs_1_), channel_id=1, source_target_pairs={{0,8},{2,10},{4,12},{6,14},{8,0},{10,2},{12,4},{14,6},{16,24},{18,... | collective-permute-start | bytes 995336 | tf_op jit(solution)/shard_map/ppermute | solution.py:726
  427.3 8.2 %collective-permute-start.28 = (bf16[16,4736]{1,0:T(8,128)(2,1)}, bf16[16,4736]{1,0:T(8,128)(2,1)S(1)}, u32[]{:S(2)}, u32[]{:S(2)}) collective-permute-start(bf16[16,4736]{1,0:T(8,128)(2,1)} %every.1.refs_1_.refs_8_), channel_id=1, source_target_pairs={{0,16},{2,18},{4,20},{6,22},{8,24},{10,26},{12,28},{14,30},{16,0},... | collective-permute-start | bytes 454664 | tf_op jit(solution)/shard_map/ppermute | solution.py:726
  432.9 13.0 %copy-start.10 = (bf16[8,4736]{1,0:T(8,128)(2,1)S(1)}, bf16[8,4736]{1,0:T(8,128)(2,1)}, u32[]{:S(2)}) copy-start(bf16[8,4736]{1,0:T(8,128)(2,1)} %pair.1.refs_1_.refs_2_) | copy-start | bytes 227332
  432.9 4.4 copy-start.17
  435.6 1.8 copy-start.26
  435.6 1.8 copy-start.18
  441.8 9.6 %collective-permute-start.30 = (bf16[72,1152]{1,0:T(8,128)(2,1)}, bf16[72,1152]{1,0:T(8,128)(2,1)S(1)}, u32[]{:S(2)}, u32[]{:S(2)}) collective-permute-start(bf16[72,1152]{1,0:T(8,128)(2,1)} %get-tuple-element.208), channel_id=1, source_target_pairs={{0,8},{2,10},{4,12},{6,14},{8,0},{10,2},{12,4},{14,6},{16,24},{18,... | collective-permute-start | bytes 497672 | tf_op jit(solution)/shard_map/ppermute | solution.py:726
  442.3 9.1 %collective-permute-start.31 = (bf16[72,1152]{1,0:T(8,128)(2,1)}, bf16[72,1152]{1,0:T(8,128)(2,1)S(1)}, u32[]{:S(2)}, u32[]{:S(2)}) collective-permute-start(bf16[72,1152]{1,0:T(8,128)(2,1)} %get-tuple-element.210), channel_id=1, source_target_pairs={{0,4},{2,6},{4,0},{6,2},{8,12},{10,14},{12,8},{14,10},{16,20},{18,... | collective-permute-start | bytes 497672 | tf_op jit(solution)/shard_map/ppermute | solution.py:726
  443.1 8.2 %collective-permute-start.29 = (bf16[72,1152]{1,0:T(8,128)(2,1)}, bf16[72,1152]{1,0:T(8,128)(2,1)S(1)}, u32[]{:S(2)}, u32[]{:S(2)}) collective-permute-start(bf16[72,1152]{1,0:T(8,128)(2,1)} %get-tuple-element.205.refs_1_), channel_id=1, source_target_pairs={{0,1},{1,0},{2,3},{3,2},{4,5},{5,4},{6,7},{7,6},{8,9},{9,8},{10,11... | collective-permute-start | bytes 497672 | tf_op jit(solution)/shard_map/ppermute | solution.py:725
  444.7 8.4 %collective-permute-start.32 = (bf16[32,4736]{1,0:T(8,128)(2,1)}, bf16[32,4736]{1,0:T(8,128)(2,1)S(1)}, u32[]{:S(2)}, u32[]{:S(2)}) collective-permute-start(bf16[32,4736]{1,0:T(8,128)(2,1)} %get-tuple-element.211.refs_8_), channel_id=1, source_target_pairs={{0,8},{2,10},{4,12},{6,14},{8,0},{10,2},{12,4},{14,6},{16,24},{18,... | collective-permute-start | bytes 909320 | tf_op jit(solution)/shard_map/ppermute | solution.py:726
  451.3 9.8 %copy-start.28 = (f32[1,4,1152]{2,1,0:T(4,128)S(1)}, f32[1,4,1152]{2,1,0:T(4,128)}, u32[]{:S(2)}) copy-start(f32[1,4,1152]{2,1,0:T(4,128)} %param.20) | copy-start | bytes 55300
  451.4 1.7 copy-start.23
  451.4 1.7 copy-start.24
  451.4 1.7 copy-start.25
  457.4 16.9 %collective-permute-start.34 = (bf16[64,4736]{1,0:T(8,128)(2,1)}, bf16[64,4736]{1,0:T(8,128)(2,1)S(1)}, u32[]{:S(2)}, u32[]{:S(2)}) collective-permute-start(bf16[64,4736]{1,0:T(8,128)(2,1)} %get-tuple-element.214.refs_4_), channel_id=1, source_target_pairs={{0,2},{2,0},{4,6},{6,4},{8,10},{10,8},{12,14},{14,12},{16,18},{18,... | collective-permute-start | bytes 1818632 | tf_op jit(solution)/shard_map/ppermute | solution.py:726
  457.4 3.7 collective-permute-start.20
  458.5 15.7 %collective-permute-start.33 = (bf16[36,3456]{1,0:T(8,128)(2,1)}, bf16[36,3456]{1,0:T(8,128)(2,1)S(1)}, u32[]{:S(2)}, u32[]{:S(2)}) collective-permute-start(bf16[36,3456]{1,0:T(8,128)(2,1)} %get-tuple-element.212.refs_1_), channel_id=1, source_target_pairs={{0,16},{2,18},{4,20},{6,22},{8,24},{10,26},{12,28},{14,30},{16,0},... | collective-permute-start | bytes 746504 | tf_op jit(solution)/shard_map/ppermute | solution.py:726
  (18 other events, 16.9 us)

commit v11 on v9

--- a/solution.py
+++ b/solution.py
@@ -17,6 +17,7 @@
 TB = 512
 WIN = 256
 TOGETHER = 4
+FIRST = 384
 SCORE_SCALE = float(HD**-0.5)
 SCORE_LOG2 = float(np.log2(np.e) * HD**-0.5)
 VMEM = 60 * 2**20
@@ -214,9 +215,39 @@
     v_ref[...] = nn(low, w_ref[:, 2 * width :]).astype(bf16)
 
 
-def attend_kernel(slots, q_ref, k_ref, v_ref, o_ref, lse_ref):
+def load_parts(sources, targets, sems, base, cut):
+    columns = targets[0].shape[1]
+    spans = [(0, cut), (cut, columns)] if cut else [(0, columns)]
+    loads = [
+        [
+            pltpu.make_async_copy(
+                source.at[:, pl.ds(base + start, stop - start)],
+                target.at[:, pl.ds(start, stop - start)],
+                sems.at[part, i],
+            )
+            for i, (source, target) in enumerate(zip(sources, targets))
+        ]
+        for part, (start, stop) in enumerate(spans)
+    ]
+
+    @pl.when(pl.program_id(0) == 0)
+    def _():
+        for part in loads:
+            for load in part:
+                load.start()
+
+    for step, part in enumerate(loads):
+
+        @pl.when(pl.program_id(0) == step)
+        def _(part=part):
+            for load in part:
+                load.wait()
+
+
+def attend_kernel(slots, q_hbm, k_hbm, v_hbm, o_ref, lse_ref, q_ref, k_ref, v_ref, sems):
     step = pl.program_id(0)
     tokens, width = q_ref.shape
+    load_parts((q_hbm, k_hbm, v_hbm), (q_ref, k_ref, v_ref), sems, 0, FIRST)
     lane128 = lax.broadcasted_iota(jnp.int32, (1, 128), 1)
     lane = lax.broadcasted_iota(jnp.int32, (1, WIN), 1)
 
@@ -389,10 +420,11 @@
 
 
 def attend_back_kernel(
-    slots, q_ref, k_ref, v_ref, do_ref, lse_ref, dot_ref, kt_ref, dqt_ref, dk_ref, dv_low_ref, dv_ref,
-    *, first, base, base_row, width,
+    slots, q_hbm, k_hbm, v_hbm, do_hbm, lse_ref, dot_ref, kt_ref, dqt_ref, dk_ref, dv_low_ref, dv_ref,
+    q_ref, k_ref, v_ref, do_ref, sems, *, first, base, base_row, width, cut,
 ):
     tokens = q_ref.shape[0]
+    load_parts((q_hbm, k_hbm, v_hbm, do_hbm), (q_ref, k_ref, v_ref, do_ref), sems, base, cut)
 
     @pl.when(pl.program_id(0) == 0)
     def _():
@@ -937,11 +969,12 @@
     attended, lse_columns = call(
         attend_kernel,
         (HEADS // TOGETHER,),
-        [fixed((count, width))] * 3,
+        [anywhere] * 3,
         [fixed((count, width)), fixed((count, 128))],
         [token_f32, shape((count, 128), f32)],
         (query, key, value),
         scalars=slots,
+        scratch=[pltpu.VMEM((count, width), bf16)] * 3 + [pltpu.SemaphoreType.DMA((2, 3))],
         name="attend",
     )
     attended, lse, attn, mid, ffn_in, grad_ffn, out_units, ffn_units = call(
@@ -1011,16 +1044,17 @@
     def attend_back(first, end, name):
         begin, stop, begin_row, stop_row = head_span(first, end, width)
         columns, rows = stop - begin, stop_row - begin_row
-        used = pl.BlockSpec((count, columns), lambda *_: (0, begin // columns), pipeline_mode=pl.Buffered(1))
         used_rows = pl.BlockSpec((rows, count), lambda *_: (begin_row // rows, 0), pipeline_mode=pl.Buffered(1))
         return call(
-            functools.partial(attend_back_kernel, first=first, base=begin, base_row=begin_row, width=width),
+            functools.partial(attend_back_kernel, first=first, base=begin, base_row=begin_row, width=width,
+                              cut=FIRST if first == 0 else 0),
             ((end - first) // TOGETHER,),
-            [used] * 4 + [fixed((128, count))] * 2 + [used_rows],
+            [anywhere] * 4 + [fixed((128, count))] * 2 + [used_rows],
             [fixed((rows, count))] + [fixed((count, columns))] * 2,
             [shape((rows, count), f32), shape((count, columns), f32), shape((count, columns), bf16)],
             (query, key, value, grad_attended, lse, dot_term, key_t),
-            scratch=[pltpu.VMEM((count, columns), f32)],
+            scratch=[pltpu.VMEM((count, columns), f32)]
+            + [pltpu.VMEM((count, columns), bf16)] * 4 + [pltpu.SemaphoreType.DMA((2, 4))],
             scalars=slots,
             name=name,
         )

time: 481 us -> 481 us (level)
  no operation moved by 1% of the time
where the time goes in v11:
time: 481 us; the launch traced here: 478 us
  Pallas kernels  345 us (72%)
  waiting for transfers between devices  52.6 us (11%)
  starting transfers between devices  46.8 us (10%)
  local copies, waits for them, and re-layouts  18.6 us (4%)
  matrix products  9.81 us (2%)
    pallas_call x26, Pallas kernels, __call__(): pl.pallas_call(body, grid_spec=spec, input_output_aliases=aliases or {},...  345 us
    ppermute x25, waiting for transfers between devices, swap(): lax.ppermute(arr, 'dp', [(i, i ^ 1 << bit) for i in range(self.n_dp)])  46.6 us
    ppermute x25, starting transfers between devices, swap(): lax.ppermute(arr, 'dp', [(i, i ^ 1 << bit) for i in range(self.n_dp)])  26.5 us
    ppermute x10, starting transfers between devices, swap(): return lax.ppermute(arr, 'mod', [(i, i ^ 1) for i in range(self.n_mod)])  20.4 us
    unnamed x62, local copies, waits for them, and re-layouts  13.9 us
  transfers between devices with their start and end apart: 35, of which 11 were waited for; matrix products, arithmetic and copies ran while one was open for 2% of the time, Pallas kernels for 32%

profile of v11, /device:TPU:0, one launch (start us, length us, event | category | flops | bytes accessed | tf_op | source)
XLA Modules:
  0.0 477.7 jit_solution(14828049029212351700)
XLA Ops:
  0.6 3.0 collective-permute-start
  6.5 4.4 convolution_convert_fusion
  11.0 2.1 collective-permute-start.1
  16.3 28.1 %project.1 = (bf16[8,144,1024]{2,1,0:T(8,128)(2,1)}, f32[1024,2304]{1,0:T(8,128)}, f32[1024,256]{1,0:T(8,128)}, bf16[1024,1152]{1,0:T(8,128)(2,1)}, bf16[1024,11...) custom-call(s32[4]{0:T(128)} %bitcast.49, bf16[1024,1152]{1,0:T(8,128)(2,1)} %bitcast.37, ...), custom_call_target="tpu_custom_call" | custom-call | flops 1 | bytes 1 | tf_op jit(solution)/shard_map/project/pallas_call | solution.py:713
  44.4 14.0 %attend.1 = (f32[1024,1152]{1,0:T(8,128)}, f32[1024,128]{1,0:T(8,128)}) custom-call(s32[4]{0:T(128)} %bitcast.50, bf16[8,144,1024]{2,1,0:T(8,128)(2,1)} %get-tuple-element.116.refs_1_.refs_2_.refs_10_, bf16[1024,1152]{1,0:T(8,128)(2,1)} %get-tuple-element.117.refs_2_.refs_8_, bf16[1024,1152]{1,0:T(8,128)(2,1)} %get-tuple-element.118.refs_3_.refs_9_, ...), custom_call_target="tpu_custom_call" | custom-call | flops 1 | bytes 1 | tf_op jit(solution)/shard_map/attend/pallas_call | solution.py:713
  58.4 20.2 %mix.1 = (bf16[1024,1152]{1,0:T(8,128)(2,1)}, f32[128,1024]{1,0:T(8,128)}, bf16[1024,1152]{1,0:T(8,128)(2,1)}, f32[1024,1152]{1,0:T(8,128)}, bf16[1024,1152]{1,0...) custom-call(s32[4]{0:T(128)} %bitcast.51, ...), custom_call_target="tpu_custom_call" | custom-call | flops 1 | bytes 1 | tf_op jit(solution)/shard_map/mix/pallas_call | solution.py:713
  78.6 95.5 %ffn.1 = (bf16[4,144,3072]{2,1,0:T(8,128)(2,1)}, bf16[4,144,3072]{2,1,0:T(8,128)(2,1)}, bf16[4,144,3072]{2,1,0:T(8,128)(2,1)}, bf16[4,144,3072]{2,1,0:T(8,128)(2...) custom-call(s32[5]{0:T(128)} %stack.48.refs_0_, ...), custom_call_target="tpu_custom_call" | custom-call | flops 1 | bytes 1 | tf_op jit(solution)/shard_map/ffn/pallas_call | solution.py:713
  175.4 24.9 %middle.1 = (bf16[1024,1152]{1,0:T(8,128)(2,1)}, f32[1024,1152]{1,0:T(8,128)}, bf16[1024,1152]{1,0:T(8,128)(2,1)}, f32[128,1024]{1,0:T(8,128)}, f32[4,4608]{1,0:...) custom-call(s32[6]{0:T(128)} %pad_add_fusion.refs_0_, ...), custom_call_target="tpu_custom_call" | custom-call | flops 1 | bytes 1 | tf_op jit(solution)/shard_map/middle/pallas_call | solution.py:713
  200.8 2.9 collective-permute-done.3.refs_5_.refs_9_
  204.7 15.1 %early.4 = (bf16[2,144,3712]{2,1,0:T(8,128)(2,1)}, bf16[2,144,3712]{2,1,0:T(8,128)(2,1)}, bf16[2,144,3584]{2,1,0:T(8,128)(2,1)}, bf16[2,144,3584]{2,1,0:T(8,128)...) custom-call(s32[5]{0:T(128)} %stack.48.refs_0_, bf16[1024,1152]{1,0:T(8,128)(2,1)} %get-tuple-element.132.refs_1_, ...), custom_call_target="tpu_custom_call" | custom-call | flops 1 | bytes 1 | tf_op jit(solution)/shard_map/early/pallas_call | solution.py:713
  219.8 10.6 %collective-permute-start.6 = (bf16[2,144,3712]{2,1,0:T(8,128)(2,1)}, bf16[2,144,3712]{2,1,0:T(8,128)(2,1)S(1)}, u32[]{:S(2)}, u32[]{:S(2)}) collective-permute-start(bf16[2,144,3712]{2,1,0:T(8,128)(2,1)} %get-tuple-element.140.refs_1_), channel_id=1, source_target_pairs={{0,1},{1,0},{2,3},{3,2},{4,5},{5,4},{6,7},{7,6},{8,9},{9,8},{10,11... | collective-permute-start | bytes 6414344 | tf_op jit(solution)/shard_map/ppermute | solution.py:756
  230.4 2.8 collective-permute-start.7
  233.2 1.6 collective-permute-start.8
  234.8 23.0 %attend_back_0.1 = (f32[864,1024]{1,0:T(8,128)}, f32[1024,1024]{1,0:T(8,128)}, bf16[1024,1024]{1,0:T(8,128)(2,1)}) custom-call(s32[4]{0:T(128)} %bitcast.52, bf16[2,144,3712]{2,1,0:T(8,128)(2,1)} %get-tuple-element.140.refs_1_, bf16[1024,1152]{1,0:T(8,128)(2,1)} %get-tuple-element.117.refs_2_.refs_8_, bf16[1024,1152]{1,0:T(8,128)(2,1)} %get-tuple-element.118.refs_3_.refs_9_, ...), custom_call_target="tpu_custom_call" | custom-call | flops 1 | bytes 1 | tf_op jit(solution)/shard_map/attend_back_0/pallas_call | solution.py:713
  257.8 16.2 %collective-permute-done.8.refs_7_ = bf16[4,192,1152]{2,1,0:T(8,128)(2,1)S(1)} collective-permute-done((bf16[4,192,1152]{2,1,0:T(8,128)(2,1)}, bf16[4,192,1152]{2,1,0:T(8,128)(2,1)S(1)}, u32[]{:S(2)}, u32[]{:S(2)}) %collective-permute-start.8) | collective-permute-done | bytes 1769504 | tf_op jit(solution)/shard_map/ppermute | solution.py:757
  274.0 5.0 %collective-permute-done.7.refs_5_ = bf16[2,144,3584]{2,1,0:T(8,128)(2,1)} collective-permute-done((bf16[2,144,3584]{2,1,0:T(8,128)(2,1)}, bf16[2,144,3584]{2,1,0:T(8,128)(2,1)}, u32[]{:S(2)}, u32[]{:S(2)}) %collective-permute-start.7) | collective-permute-done | bytes 2064416 | tf_op jit(solution)/shard_map/ppermute | solution.py:757
  280.3 8.5 %early.5 = (bf16[144,3712]{1,0:T(8,128)(2,1)}, f32[144,3712]{1,0:T(8,128)}, bf16[2,72,3584]{2,1,0:T(8,128)(2,1)}, f32[2,72,3584]{2,1,0:T(8,128)}, bf16[2,192,115...) custom-call(s32[5]{0:T(128)} %stack.48.refs_0_, f32[864,1024]{1,0:T(8,128)} %get-tuple-element.145.refs_1_.refs_2_, ...), custom_call_target="tpu_custom_call" | custom-call | flops 1 | bytes 1 | tf_op jit(solution)/shard_map/early/pallas_call | solution.py:713
  288.8 3.1 collective-permute-start.9
  292.0 1.6 collective-permute-start.10
  293.8 10.6 %attend_back_1.1 = (f32[288,1024]{1,0:T(8,128)}, f32[1024,384]{1,0:T(8,128)}, bf16[1024,384]{1,0:T(8,128)(2,1)}) custom-call(s32[4]{0:T(128)} %bitcast.53, bf16[144,3712]{1,0:T(8,128)(2,1)} %get-tuple-element.151.refs_1_, bf16[1024,1152]{1,0:T(8,128)(2,1)} %get-tuple-element.117.refs_2_.refs_8_, bf16[1024,1152]{1,0:T(8,128)(2,1)} %get-tuple-element.118.refs_3_.refs_9_, ...), custom_call_target="tpu_custom_call" | custom-call | flops 1 | bytes 1 | tf_op jit(solution)/shard_map/attend_back_1/pallas_call | solution.py:713
  304.4 7.4 %value.1 = (bf16[4,144,1152]{2,1,0:T(8,128)(2,1)}, bf16[4,144,1152]{2,1,0:T(8,128)(2,1)}) custom-call(s32[5]{0:T(128)} %stack.48.refs_0_, f32[288,1024]{1,0:T(8,128)} %get-tuple-element.152.refs_1_.refs_3_, bf16[8,144,1024]{2,1,0:T(8,128)(2,1)} %get-tuple-element.116.refs_1_.refs_2_.refs_10_, bf16[1024,1024]{1,0:T(8,128)(2,1)} %get-tuple-element.153.refs_3_.refs_4_, ...), custom_call_target="tpu_custom_call" | custom-call | flops 1 | bytes 1 | tf_op jit(solution)/shard_map/value/pallas_call | solution.py:713
  311.9 2.5 collective-permute-done.11.refs_7_
  314.4 1.8 collective-permute-done.10.refs_5_
  317.6 6.3 %early.6 = (bf16[72,3712]{1,0:T(8,128)(2,1)}, f32[72,3712]{1,0:T(8,128)}, bf16[72,3584]{1,0:T(8,128)(2,1)}, f32[72,3584]{1,0:T(8,128)}, bf16[192,1152]{1,0:T(8,128)(2,1)}, /*index=5*/f32[192,1152]{1,0:T(8,128)}) custom-call(s32[5]{0:T(128)} %stack.48.refs_0_, bf16[4,144,1152]{2,1,0:T(8,128)(2,1)} %get-tuple-element.155.refs_1_, ...), custom_call_target="tpu_custom_call" | custom-call | flops 1 | bytes 1 | tf_op jit(solution)/shard_map/early/pallas_call | solution.py:713
  326.9 27.6 %project_back.1 = (bf16[1024,1152]{1,0:T(8,128)(2,1)}, bf16[1024,1152]{1,0:T(8,128)(2,1)}, bf16[8,128]{1,0:T(8,128)(2,1)}, bf16[4,144,1152]{2,1,0:T(8,128)(2,1)}...) custom-call(s32[5]{0:T(128)} %stack.48.refs_0_, ...), custom_call_target="tpu_custom_call" | custom-call | flops 1 | bytes 1 | tf_op jit(solution)/shard_map/project_back/pallas_call | solution.py:713
  356.7 4.4 v.2
  363.9 5.4 %late.3 = (bf16[2,144,1152]{2,1,0:T(8,128)(2,1)}, bf16[2,144,1152]{2,1,0:T(8,128)(2,1)}, bf16[2,144,1152]{2,1,0:T(8,128)(2,1)}, bf16[2,144,1152]{2,1,0:T(8,128)(2,1)}) custom-call(s32[5]{0:T(128)} %stack.48.refs_0_, bf16[4,72,1152]{2,1,0:T(8,128)(2,1)} %get-tuple-element.174.refs_1_, bf16[4,144,1152]{2,1,0:T(8,128)(2,1)} %get-tuple-element.175.refs_2_, ...), custom_call_target="tpu_custom_call" | custom-call | flops 1 | bytes 1 | tf_op jit(solution)/shard_map/late/pallas_call | solution.py:713
  369.3 2.0 collective-permute-start.21
  371.3 5.0 %early.7 = (bf16[36,10752]{1,0:T(8,128)(2,1)}, f32[36,10752]{1,0:T(8,128)}) custom-call(s32[5]{0:T(128)} %stack.48.refs_0_, bf16[2,144,1152]{2,1,0:T(8,128)(2,1)} %get-tuple-element.179.refs_1_, f32[72,3712]{1,0:T(8,128)} %get-tuple-element.180.refs_2_, bf16[72,3712]{1,0:T(8,128)(2,1)} %get-tuple-element.171.refs_1_.refs_3_, ...), custom_call_target="tpu_custom_call" | custom-call | flops 1 | bytes 1 | tf_op jit(solution)/shard_map/early/pallas_call | solution.py:713
  376.3 5.2 %collective-permute-start.24 = (bf16[36,10752]{1,0:T(8,128)(2,1)}, bf16[36,10752]{1,0:T(8,128)(2,1)S(1)}, u32[]{:S(2)}, u32[]{:S(2)}) collective-permute-start(bf16[36,10752]{1,0:T(8,128)(2,1)} %get-tuple-element.185.refs_1_), channel_id=1, source_target_pairs={{0,16},{2,18},{4,20},{6,22},{8,24},{10,26},{12,28},{14,30},{16,0},... | collective-permute-start | bytes 2322440 | tf_op jit(solution)/shard_map/ppermute | solution.py:757
  381.6 21.0 %input_back.1 = (bf16[1024,1152]{1,0:T(8,128)(2,1)}, bf16[8,3584]{1,0:T(8,128)(2,1)}, bf16[8,3584]{1,0:T(8,128)(2,1)}) custom-call(s32[6]{0:T(128)} %pad_add_fusion.refs_0_, bf16[36,10752]{1,0:T(8,128)(2,1)} %get-tuple-element.185.refs_1_, bf16[1024,1152]{1,0:T(8,128)(2,1)} %get-tuple-element.166.refs_0_.refs_2_, ...), custom_call_target="tpu_custom_call" | custom-call | flops 1 | bytes 1 | tf_op jit(solution)/shard_map/input_back/pallas_call | solution.py:713
  404.1 2.9 v.3
  407.6 2.2 pair.1.refs_1_.refs_2_
  412.1 3.1 q.1
  415.9 2.2 every.1.refs_1_.refs_8_
  418.9 3.0 k.1
  421.9 2.0 collective-permute-start.26
  425.3 3.5 early_last.1
  428.8 4.1 collective-permute-done.28.refs_9_
  432.9 1.9 collective-permute-done.25.refs_3_
  435.5 3.7 late.4
  440.8 1.6 collective-permute-start.32
  442.4 5.4 %fusion = f32[8,1152]{1,0:T(8,128)S(1)} fusion(bf16[1152,3456]{1,0:T(8,128)(2,1)} %param.23, bf16[8,4736]{1,0:T(8,128)(2,1)S(1)} %copy-done.10), kind=kOutput, calls=%fused_computation.1 | convolution fusion | flops 63700992 | bytes 8054784 | tf_op jit(solution)/shard_map/nc,dc->nd/dot_general | solution.py:1147
  447.9 2.6 collective-permute-done.32.refs_9_
  451.3 3.6 late.5
  455.6 3.0 collective-permute-done.20
  459.2 12.1 %collective-permute-done.33.refs_3_ = bf16[36,3456]{1,0:T(8,128)(2,1)S(1)} collective-permute-done((bf16[36,3456]{1,0:T(8,128)(2,1)}, bf16[36,3456]{1,0:T(8,128)(2,1)S(1)}, u32[]{:S(2)}, u32[]{:S(2)}) %collective-permute-start.33) | collective-permute-done | bytes 248864 | tf_op jit(solution)/shard_map/ppermute | solution.py:757
  472.2 4.0 late_last.1
  (132 shorter events, 33.8 us)
Async XLA Ops:
  0.6 5.0 %collective-permute-start = (f32[4,1152]{1,0:T(4,128)}, f32[4,1152]{1,0:T(4,128)S(1)}, u32[]{:S(2)}, u32[]{:S(2)}) collective-permute-start(f32[4,1152]{1,0:T(4,128)} %bitcast.45), channel_id=1, source_target_pairs={{0,1},{1,0},{2,3},{3,2},{4,5},{5,4},{6,7},{7,6},{8,9},{9,8},{10,11... | collective-permute-start | bytes 55304 | tf_op jit(solution)/shard_map/ppermute | solution.py:756
  6.5 4.4 copy-start.22
  11.0 4.5 collective-permute-start.1
  78.6 96.2 %copy-start.30 = (s32[1,4]{1,0:T(1,128)S(1)}, s32[1,4]{1,0:T(1,128)}, u32[]{:S(2)}) copy-start(s32[1,4]{1,0:T(1,128)} %slice.20) | copy-start | bytes 52
  174.1 29.6 %collective-permute-start.4 = (bf16[4,144,3072]{2,1,0:T(8,128)(2,1)}, bf16[4,144,3072]{2,1,0:T(8,128)(2,1)}, u32[]{:S(2)}, u32[]{:S(2)}) collective-permute-start(bf16[4,144,3072]{2,1,0:T(8,128)(2,1)} %get-tuple-element.137), channel_id=1, source_target_pairs={{0,2},{2,0},{4,6},{6,4},{8,10},{10,8},{12,14},{14,12},{16,18},{18,... | collective-permute-start | bytes 10616840 | tf_op jit(solution)/shard_map/ppermute | solution.py:757
  174.2 29.5 %collective-permute-start.5 = (bf16[4,384,1152]{2,1,0:T(8,128)(2,1)}, bf16[4,384,1152]{2,1,0:T(8,128)(2,1)}, u32[]{:S(2)}, u32[]{:S(2)}) collective-permute-start(bf16[4,384,1152]{2,1,0:T(8,128)(2,1)} %bitcast.56), channel_id=1, source_target_pairs={{0,2},{2,0},{4,6},{6,4},{8,10},{10,8},{12,14},{14,12},{16,18},{18,... | collective-permute-start | bytes 10616840 | tf_op jit(solution)/shard_map/ppermute | solution.py:757
  174.7 29.0 %collective-permute-start.2 = (bf16[4,144,3072]{2,1,0:T(8,128)(2,1)}, bf16[4,144,3072]{2,1,0:T(8,128)(2,1)}, u32[]{:S(2)}, u32[]{:S(2)}) collective-permute-start(bf16[4,144,3072]{2,1,0:T(8,128)(2,1)} %get-tuple-element.126.refs_1_), channel_id=1, source_target_pairs={{0,2},{2,0},{4,6},{6,4},{8,10},{10,8},{12,14},{14,12},{16,18},{18,... | collective-permute-start | bytes 10616840 | tf_op jit(solution)/shard_map/ppermute | solution.py:757
  200.3 3.4 collective-permute-start.3
  219.8 59.2 %collective-permute-start.6 = (bf16[2,144,3712]{2,1,0:T(8,128)(2,1)}, bf16[2,144,3712]{2,1,0:T(8,128)(2,1)S(1)}, u32[]{:S(2)}, u32[]{:S(2)}) collective-permute-start(bf16[2,144,3712]{2,1,0:T(8,128)(2,1)} %get-tuple-element.140.refs_1_), channel_id=1, source_target_pairs={{0,1},{1,0},{2,3},{3,2},{4,5},{5,4},{6,7},{7,6},{8,9},{9,8},{10,11... | collective-permute-start | bytes 6414344 | tf_op jit(solution)/shard_map/ppermute | solution.py:756
  230.4 48.5 %collective-permute-start.7 = (bf16[2,144,3584]{2,1,0:T(8,128)(2,1)}, bf16[2,144,3584]{2,1,0:T(8,128)(2,1)}, u32[]{:S(2)}, u32[]{:S(2)}) collective-permute-start(bf16[2,144,3584]{2,1,0:T(8,128)(2,1)} %get-tuple-element.148), channel_id=1, source_target_pairs={{0,4},{2,6},{4,0},{6,2},{8,12},{10,14},{12,8},{14,10},{16,20},{18,... | collective-permute-start | bytes 6193160 | tf_op jit(solution)/shard_map/ppermute | solution.py:757
  233.2 40.8 %collective-permute-start.8 = (bf16[4,192,1152]{2,1,0:T(8,128)(2,1)}, bf16[4,192,1152]{2,1,0:T(8,128)(2,1)S(1)}, u32[]{:S(2)}, u32[]{:S(2)}) collective-permute-start(bf16[4,192,1152]{2,1,0:T(8,128)(2,1)} %get-tuple-element.150), channel_id=1, source_target_pairs={{0,8},{2,10},{4,12},{6,14},{8,0},{10,2},{12,4},{14,6},{16,24},{18,... | collective-permute-start | bytes 5308424 | tf_op jit(solution)/shard_map/ppermute | solution.py:757
  274.0 5.0 %copy-start.6 = (bf16[4,192,1152]{2,1,0:T(8,128)(2,1)}, bf16[4,192,1152]{2,1,0:T(8,128)(2,1)S(1)}, u32[]{:S(2)}) copy-start(bf16[4,192,1152]{2,1,0:T(8,128)(2,1)S(1)} %collective-permute-done.8.refs_7_) | copy-start | bytes 5308420
  288.8 27.4 %collective-permute-start.9 = (bf16[144,3712]{1,0:T(8,128)(2,1)}, bf16[144,3712]{1,0:T(8,128)(2,1)S(1)}, u32[]{:S(2)}, u32[]{:S(2)}) collective-permute-start(bf16[144,3712]{1,0:T(8,128)(2,1)} %get-tuple-element.151.refs_1_), channel_id=1, source_target_pairs={{0,4},{2,6},{4,0},{6,2},{8,12},{10,14},{12,8},{14,10},{16,20},{18,... | collective-permute-start | bytes 3207176 | tf_op jit(solution)/shard_map/ppermute | solution.py:757
  292.0 24.2 %collective-permute-start.10 = (bf16[2,72,3584]{2,1,0:T(8,128)(2,1)}, bf16[2,72,3584]{2,1,0:T(8,128)(2,1)S(1)}, u32[]{:S(2)}, u32[]{:S(2)}) collective-permute-start(bf16[2,72,3584]{2,1,0:T(8,128)(2,1)} %get-tuple-element.158), channel_id=1, source_target_pairs={{0,8},{2,10},{4,12},{6,14},{8,0},{10,2},{12,4},{14,6},{16,24},{18,... | collective-permute-start | bytes 3096584 | tf_op jit(solution)/shard_map/ppermute | solution.py:757
  293.6 20.9 %collective-permute-start.11 = (bf16[2,192,1152]{2,1,0:T(8,128)(2,1)}, bf16[2,192,1152]{2,1,0:T(8,128)(2,1)}, u32[]{:S(2)}, u32[]{:S(2)}) collective-permute-start(bf16[2,192,1152]{2,1,0:T(8,128)(2,1)} %get-tuple-element.160), channel_id=1, source_target_pairs={{0,1},{1,0},{2,3},{3,2},{4,5},{5,4},{6,7},{7,6},{8,9},{9,8},{10,11... | collective-permute-start | bytes 2654216 | tf_op jit(solution)/shard_map/ppermute | solution.py:756
  311.9 42.7 %collective-permute-start.15 = (bf16[4,144,1152]{2,1,0:T(8,128)(2,1)}, bf16[4,144,1152]{2,1,0:T(8,128)(2,1)S(1)}, u32[]{:S(2)}, u32[]{:S(2)}) collective-permute-start(bf16[4,144,1152]{2,1,0:T(8,128)(2,1)} %get-tuple-element.155.refs_1_), channel_id=1, source_target_pairs={{0,2},{2,0},{4,6},{6,4},{8,10},{10,8},{12,14},{14,12},{16,18},{18,... | collective-permute-start | bytes 3981320 | tf_op jit(solution)/shard_map/ppermute | solution.py:757
  323.9 30.7 %collective-permute-start.12 = (bf16[72,3712]{1,0:T(8,128)(2,1)}, bf16[72,3712]{1,0:T(8,128)(2,1)S(1)}, u32[]{:S(2)}, u32[]{:S(2)}) collective-permute-start(bf16[72,3712]{1,0:T(8,128)(2,1)} %get-tuple-element.161.refs_1_), channel_id=1, source_target_pairs={{0,8},{2,10},{4,12},{6,14},{8,0},{10,2},{12,4},{14,6},{16,24},{18,... | collective-permute-start | bytes 1603592 | tf_op jit(solution)/shard_map/ppermute | solution.py:757
  325.5 29.1 %collective-permute-start.13 = (bf16[72,3584]{1,0:T(8,128)(2,1)}, bf16[72,3584]{1,0:T(8,128)(2,1)S(1)}, u32[]{:S(2)}, u32[]{:S(2)}) collective-permute-start(bf16[72,3584]{1,0:T(8,128)(2,1)} %get-tuple-element.167), channel_id=1, source_target_pairs={{0,1},{1,0},{2,3},{3,2},{4,5},{5,4},{6,7},{7,6},{8,9},{9,8},{10,11... | collective-permute-start | bytes 1548296 | tf_op jit(solution)/shard_map/ppermute | solution.py:756
  326.7 28.0 %collective-permute-start.14 = (bf16[192,1152]{1,0:T(8,128)(2,1)}, bf16[192,1152]{1,0:T(8,128)(2,1)S(1)}, u32[]{:S(2)}, u32[]{:S(2)}) collective-permute-start(bf16[192,1152]{1,0:T(8,128)(2,1)} %get-tuple-element.168), channel_id=1, source_target_pairs={{0,4},{2,6},{4,0},{6,2},{8,12},{10,14},{12,8},{14,10},{16,20},{18,... | collective-permute-start | bytes 1327112 | tf_op jit(solution)/shard_map/ppermute | solution.py:757
  354.7 1.5 copy-start.2
  356.1 6.2 %collective-permute-start.16 = (bf16[4,144,1152]{2,1,0:T(8,128)(2,1)}, bf16[4,144,1152]{2,1,0:T(8,128)(2,1)S(1)}, u32[]{:S(2)}, u32[]{:S(2)}) collective-permute-start(bf16[4,144,1152]{2,1,0:T(8,128)(2,1)} %get-tuple-element.176), channel_id=1, source_target_pairs={{0,2},{2,0},{4,6},{6,4},{8,10},{10,8},{12,14},{14,12},{16,18},{18,... | collective-permute-start | bytes 3981320 | tf_op jit(solution)/shard_map/ppermute | solution.py:757
  356.1 6.2 %collective-permute-start.17 = (bf16[4,144,1152]{2,1,0:T(8,128)(2,1)}, bf16[4,144,1152]{2,1,0:T(8,128)(2,1)S(1)}, u32[]{:S(2)}, u32[]{:S(2)}) collective-permute-start(bf16[4,144,1152]{2,1,0:T(8,128)(2,1)} %get-tuple-element.178), channel_id=1, source_target_pairs={{0,2},{2,0},{4,6},{6,4},{8,10},{10,8},{12,14},{14,12},{16,18},{18,... | collective-permute-start | bytes 3981320 | tf_op jit(solution)/shard_map/ppermute | solution.py:757
  361.1 42.2 %collective-permute-start.18 = (bf16[4,72,1152]{2,1,0:T(8,128)(2,1)}, bf16[4,72,1152]{2,1,0:T(8,128)(2,1)S(1)}, u32[]{:S(2)}, u32[]{:S(2)}) collective-permute-start(bf16[4,72,1152]{2,1,0:T(8,128)(2,1)} %get-tuple-element.174.refs_1_), channel_id=1, source_target_pairs={{0,8},{2,10},{4,12},{6,14},{8,0},{10,2},{12,4},{14,6},{16,24},{18,... | collective-permute-start | bytes 1990664 | tf_op jit(solution)/shard_map/ppermute | solution.py:757
  362.4 1.5 copy-start.8
  369.3 41.9 %collective-permute-start.21 = (bf16[2,144,1152]{2,1,0:T(8,128)(2,1)}, bf16[2,144,1152]{2,1,0:T(8,128)(2,1)S(1)}, u32[]{:S(2)}, u32[]{:S(2)}) collective-permute-start(bf16[2,144,1152]{2,1,0:T(8,128)(2,1)} %get-tuple-element.179.refs_1_), channel_id=1, source_target_pairs={{0,4},{2,6},{4,0},{6,2},{8,12},{10,14},{12,8},{14,10},{16,20},{18,... | collective-permute-start | bytes 1990664 | tf_op jit(solution)/shard_map/ppermute | solution.py:757
  371.3 46.8 %collective-permute-start.23 = (bf16[2,144,1152]{2,1,0:T(8,128)(2,1)}, bf16[2,144,1152]{2,1,0:T(8,128)(2,1)S(1)}, u32[]{:S(2)}, u32[]{:S(2)}) collective-permute-start(bf16[2,144,1152]{2,1,0:T(8,128)(2,1)} %get-tuple-element.198), channel_id=1, source_target_pairs={{0,1},{1,0},{2,3},{3,2},{4,5},{5,4},{6,7},{7,6},{8,9},{9,8},{10,11... | collective-permute-start | bytes 1990664 | tf_op jit(solution)/shard_map/ppermute | solution.py:756
  376.3 48.0 %collective-permute-start.24 = (bf16[36,10752]{1,0:T(8,128)(2,1)}, bf16[36,10752]{1,0:T(8,128)(2,1)S(1)}, u32[]{:S(2)}, u32[]{:S(2)}) collective-permute-start(bf16[36,10752]{1,0:T(8,128)(2,1)} %get-tuple-element.185.refs_1_), channel_id=1, source_target_pairs={{0,16},{2,18},{4,20},{6,22},{8,24},{10,26},{12,28},{14,30},{16,0},... | collective-permute-start | bytes 2322440 | tf_op jit(solution)/shard_map/ppermute | solution.py:757
  402.5 4.5 collective-permute-start.19
  409.8 5.4 %collective-permute-start.22 = (bf16[8,4736]{1,0:T(8,128)(2,1)}, bf16[8,4736]{1,0:T(8,128)(2,1)S(1)}, u32[]{:S(2)}, u32[]{:S(2)}) collective-permute-start(bf16[8,4736]{1,0:T(8,128)(2,1)} %pair.1.refs_1_.refs_2_), channel_id=1, source_target_pairs={{0,4},{2,6},{4,0},{6,2},{8,12},{10,14},{12,8},{14,10},{16,20},{18,... | collective-permute-start | bytes 227336 | tf_op jit(solution)/shard_map/ppermute | solution.py:757
  410.3 18.5 %collective-permute-start.27 = (bf16[2,72,1152]{2,1,0:T(8,128)(2,1)}, bf16[2,72,1152]{2,1,0:T(8,128)(2,1)S(1)}, u32[]{:S(2)}, u32[]{:S(2)}) collective-permute-start(bf16[2,72,1152]{2,1,0:T(8,128)(2,1)} %get-tuple-element.192.refs_1_), channel_id=1, source_target_pairs={{0,1},{1,0},{2,3},{3,2},{4,5},{5,4},{6,7},{7,6},{8,9},{9,8},{10,11... | collective-permute-start | bytes 995336 | tf_op jit(solution)/shard_map/ppermute | solution.py:756
  421.9 11.0 %collective-permute-start.26 = (bf16[144,1152]{1,0:T(8,128)(2,1)}, bf16[144,1152]{1,0:T(8,128)(2,1)S(1)}, u32[]{:S(2)}, u32[]{:S(2)}) collective-permute-start(bf16[144,1152]{1,0:T(8,128)(2,1)} %get-tuple-element.199.refs_1_), channel_id=1, source_target_pairs={{0,4},{2,6},{4,0},{6,2},{8,12},{10,14},{12,8},{14,10},{16,20},{18,... | collective-permute-start | bytes 995336 | tf_op jit(solution)/shard_map/ppermute | solution.py:757
  423.9 10.9 %collective-permute-start.25 = (bf16[2,72,1152]{2,1,0:T(8,128)(2,1)}, bf16[2,72,1152]{2,1,0:T(8,128)(2,1)S(1)}, u32[]{:S(2)}, u32[]{:S(2)}) collective-permute-start(bf16[2,72,1152]{2,1,0:T(8,128)(2,1)} %get-tuple-element.196.refs_1_), channel_id=1, source_target_pairs={{0,8},{2,10},{4,12},{6,14},{8,0},{10,2},{12,4},{14,6},{16,24},{18,... | collective-permute-start | bytes 995336 | tf_op jit(solution)/shard_map/ppermute | solution.py:757
  424.3 8.6 %collective-permute-start.28 = (bf16[16,4736]{1,0:T(8,128)(2,1)}, bf16[16,4736]{1,0:T(8,128)(2,1)S(1)}, u32[]{:S(2)}, u32[]{:S(2)}) collective-permute-start(bf16[16,4736]{1,0:T(8,128)(2,1)} %every.1.refs_1_.refs_8_), channel_id=1, source_target_pairs={{0,16},{2,18},{4,20},{6,22},{8,24},{10,26},{12,28},{14,30},{16,0},... | collective-permute-start | bytes 454664 | tf_op jit(solution)/shard_map/ppermute | solution.py:757
  428.8 13.6 %copy-start.10 = (bf16[8,4736]{1,0:T(8,128)(2,1)S(1)}, bf16[8,4736]{1,0:T(8,128)(2,1)}, u32[]{:S(2)}) copy-start(bf16[8,4736]{1,0:T(8,128)(2,1)} %pair.1.refs_1_.refs_2_) | copy-start | bytes 227332
  428.8 6.0 %copy-start.17 = (bf16[2,72,1152]{2,1,0:T(8,128)(2,1)}, bf16[2,72,1152]{2,1,0:T(8,128)(2,1)S(1)}, u32[]{:S(2)}) copy-start(bf16[2,72,1152]{2,1,0:T(8,128)(2,1)S(1)} %collective-permute-done.27.refs_7_) | copy-start | bytes 995332
  432.9 1.9 copy-start.26
  432.9 1.9 copy-start.18
  439.2 8.7 %collective-permute-start.30 = (bf16[72,1152]{1,0:T(8,128)(2,1)}, bf16[72,1152]{1,0:T(8,128)(2,1)S(1)}, u32[]{:S(2)}, u32[]{:S(2)}) collective-permute-start(bf16[72,1152]{1,0:T(8,128)(2,1)} %get-tuple-element.208), channel_id=1, source_target_pairs={{0,8},{2,10},{4,12},{6,14},{8,0},{10,2},{12,4},{14,6},{16,24},{18,... | collective-permute-start | bytes 497672 | tf_op jit(solution)/shard_map/ppermute | solution.py:757
  439.6 8.2 %collective-permute-start.31 = (bf16[72,1152]{1,0:T(8,128)(2,1)}, bf16[72,1152]{1,0:T(8,128)(2,1)S(1)}, u32[]{:S(2)}, u32[]{:S(2)}) collective-permute-start(bf16[72,1152]{1,0:T(8,128)(2,1)} %get-tuple-element.210), channel_id=1, source_target_pairs={{0,4},{2,6},{4,0},{6,2},{8,12},{10,14},{12,8},{14,10},{16,20},{18,... | collective-permute-start | bytes 497672 | tf_op jit(solution)/shard_map/ppermute | solution.py:757
  440.0 7.9 %collective-permute-start.29 = (bf16[72,1152]{1,0:T(8,128)(2,1)}, bf16[72,1152]{1,0:T(8,128)(2,1)S(1)}, u32[]{:S(2)}, u32[]{:S(2)}) collective-permute-start(bf16[72,1152]{1,0:T(8,128)(2,1)} %get-tuple-element.205.refs_1_), channel_id=1, source_target_pairs={{0,1},{1,0},{2,3},{3,2},{4,5},{5,4},{6,7},{7,6},{8,9},{9,8},{10,11... | collective-permute-start | bytes 497672 | tf_op jit(solution)/shard_map/ppermute | solution.py:756
  440.8 9.7 %collective-permute-start.32 = (bf16[32,4736]{1,0:T(8,128)(2,1)}, bf16[32,4736]{1,0:T(8,128)(2,1)S(1)}, u32[]{:S(2)}, u32[]{:S(2)}) collective-permute-start(bf16[32,4736]{1,0:T(8,128)(2,1)} %get-tuple-element.211.refs_8_), channel_id=1, source_target_pairs={{0,8},{2,10},{4,12},{6,14},{8,0},{10,2},{12,4},{14,6},{16,24},{18,... | collective-permute-start | bytes 909320 | tf_op jit(solution)/shard_map/ppermute | solution.py:757
  447.8 10.7 %copy-start.28 = (f32[1,4,1152]{2,1,0:T(4,128)S(1)}, f32[1,4,1152]{2,1,0:T(4,128)}, u32[]{:S(2)}) copy-start(f32[1,4,1152]{2,1,0:T(4,128)} %param.20) | copy-start | bytes 55300
  447.9 2.7 copy-start.23
  447.9 2.6 copy-start.24
  447.9 2.6 copy-start.25
  454.8 16.5 %collective-permute-start.34 = (bf16[64,4736]{1,0:T(8,128)(2,1)}, bf16[64,4736]{1,0:T(8,128)(2,1)S(1)}, u32[]{:S(2)}, u32[]{:S(2)}) collective-permute-start(bf16[64,4736]{1,0:T(8,128)(2,1)} %get-tuple-element.214.refs_4_), channel_id=1, source_target_pairs={{0,2},{2,0},{4,6},{6,4},{8,10},{10,8},{12,14},{14,12},{16,18},{18,... | collective-permute-start | bytes 1818632 | tf_op jit(solution)/shard_map/ppermute | solution.py:757
  454.8 3.7 collective-permute-start.20
  455.6 15.7 %collective-permute-start.33 = (bf16[36,3456]{1,0:T(8,128)(2,1)}, bf16[36,3456]{1,0:T(8,128)(2,1)S(1)}, u32[]{:S(2)}, u32[]{:S(2)}) collective-permute-start(bf16[36,3456]{1,0:T(8,128)(2,1)} %get-tuple-element.212.refs_1_), channel_id=1, source_target_pairs={{0,16},{2,18},{4,20},{6,22},{8,24},{10,26},{12,28},{14,30},{16,0},... | collective-permute-start | bytes 746504 | tf_op jit(solution)/shard_map/ppermute | solution.py:757
  (18 other events, 17.3 us)
